TPU v7x, 32 devices: a whole 2x2x4 slice. The times are simulated.
32 devices in a mesh: layer: 4 (over x, core), row: 2 (over y), col: 4 (over z).
Axes of the slice: x: 2, y: 2, z: 4, core: 2. Of those that a mesh axis runs over, the one named last changes fastest.
Arguments:
- a_blocks: bfloat16 [32, 8, 128, 128], P(('layer', 'row', 'col'))
- a_rows: int32 [32, 8], P(('layer', 'row', 'col')), may hold values from 0 to 15, as said below
- a_count: int32 [32], P(('layer', 'row', 'col')), may hold values from 1 to 8, as said below
- b_panel: bfloat16 [2048, 512], P(('layer', 'row'), 'col'), may hold values from -6 to 6
Outputs:
- flow_out: float32 [2, 2048, 512], P('row', 'layer', 'col')
Inputs may be any that keep to these rules, and one draw needn't show every extreme that they name: `a_rows`: within one panel the listed block rows are distinct. `a_count`: some panel's list is full in every draw.
All inputs are finite; a program needn't handle non-finite values.
Results may differ from a plain program's by a relative error of at most 0.0003.
Values may be sent and summed in bfloat16 or wider, within the bound.
No kernel may reach another device: no remote copies, remote signals or barrier semaphores. Data moves between devices by JAX's collectives and lax.ppermute only.
A program may use at most 64 MiB of HBM per device.

v0:
```python
import jax
import jax.numpy as jnp
from jax import lax
from jax.sharding import PartitionSpec as P

IB = 16


def body(a_blocks, a_rows, a_count, b_panel):
    capacity = a_blocks.shape[1]
    block_size = a_blocks.shape[-1]
    width = b_panel.shape[1]
    block_rows = IB
    inner_rows = lax.all_gather(b_panel, "row", axis=0, tiled=True)
    inner_blocks = inner_rows.reshape(-1, block_size, width)
    empty = jnp.zeros((block_rows, block_size, width), jnp.float32)
    blocks = lax.all_gather(a_blocks, "col", axis=0, tiled=True)
    row_ids = lax.all_gather(a_rows, "col", axis=0, tiled=True)
    counts = lax.all_gather(a_count, "col", axis=0, tiled=True)
    is_valid = jnp.arange(capacity, dtype=jnp.int32)[None, :] < counts[:, None]
    products = jnp.einsum(
        "snab,sbc->snac", blocks, inner_blocks, preferred_element_type=jnp.float32
    )
    products = products * is_valid[:, :, None, None].astype(jnp.float32)
    partial_sum = empty.at[row_ids.reshape(-1)].add(products.reshape(-1, block_size, width))
    partial_sum = partial_sum.reshape(block_rows * block_size, width)
    share_rows = partial_sum.shape[0] // lax.axis_size("layer")
    rows_total = lax.axis_size("row") * partial_sum.shape[0]
    expanded = lax.psum(partial_sum, "layer")
    squares = expanded * expanded
    col_sums = lax.psum(jnp.sum(squares, axis=0), "row")
    my_squares = lax.dynamic_slice_in_dim(
        squares, lax.axis_index("layer") * share_rows, share_rows, 0
    )
    flow_out = my_squares / (col_sums / rows_total + 1e-06)
    return flow_out[None]


def solution(mesh):
    return jax.shard_map(
        body,
        mesh=mesh,
        in_specs=(
            P(("layer", "row", "col"), None, None, None),
            P(("layer", "row", "col"), None),
            P(("layer", "row", "col")),
            P(("layer", "row"), "col"),
        ),
        out_specs=P("row", "layer", "col"),
        check_vma=False,
    )
```

profile of v0, /device:TPU:0, one launch (start us, length us, event | category | flops | bytes accessed | tf_op | source)
XLA Modules:
  0.0 94.9 jit_solution(17536458132945903601)
XLA Ops:
  6.5 0.0 all-gather.3.cloned.1.call-start
  6.5 0.7 all-gather.3.cloned.1.call-update
  7.3 0.0 all-reduce.3.cloned.1.call-start
  8.0 1.2 %dynamic-slice = u32[1]{0:T(128)} dynamic-slice(u32[32]{0:T(128)} %constant.27, u32[]{:T(128)S(6)} %add.33), dynamic_slice_sizes={1} | dynamic-slice | bytes 12
  9.2 0.8 dynamic-update-slice
  10.0 9.9 %all-reduce = s32[4]{0:T(128)S(1)} all-reduce(s32[4]{0:T(128)S(1)} %dynamic-update-slice), channel_id=1, replica_groups=mesh['layer'=4,'row'=2,'col'=4] {'col'}, use_global_device_ids=true, to_apply=%add | all-reduce | flops 4 | bytes 32
  19.8 9.4 %all-gather = s32[4,1,8]{2,1,0:T(1,128)S(1)} all-gather(s32[1,1,8]{2,1,0:T(1,128)} %bitcast.18), channel_id=1, replica_groups=mesh['layer'=4,'row'=2,'col'=4] {'col'}, dimensions={0}, use_global_device_ids=true | all-gather | bytes 160 | tf_op jit(solution)/shard_map/all_gather | solution.py:18
  29.2 0.5 broadcast.34
  29.7 0.7 reduce.3
  30.4 0.1 reshape.64
  30.5 5.1 %all_gather.14 = bf16[512,128]{1,0:T(8,128)(2,1)S(1)} all-gather(bf16[256,128]{1,0:T(8,128)(2,1)} %param.7), channel_id=1, replica_groups=mesh['layer'=4,'row'=2,'col'=4] {'row'}, dimensions={0}, use_global_device_ids=true | all-gather | bytes 196608 | tf_op jit(solution)/shard_map/all_gather | solution.py:14
  35.6 0.1 fusion
  35.7 3.9 %all-gather.3.cloned.1.call-done = bf16[4,8,128,128]{3,2,1,0:T(8,128)(2,1)} async-done(((bf16[1,8,128,128]{3,2,1,0:T(8,128)(2,1)}), bf16[4,8,128,128]{3,2,1,0:T(8,128)(2,1)}) %all-gather.3.cloned.1.call-update) | async-done | bytes 1048592 | tf_op jit(solution)/shard_map/all_gather | solution.py:17
  39.6 1.6 %convolution_multiply_fusion = f32[4,8,128,128]{3,2,1,0:T(8,128)S(1)} fusion(bf16[4,8,128,128]{3,2,1,0:T(8,128)(2,1)} %all-gather.3.cloned.1.call-done, bf16[4,128,128,1]{2,1,3,0:T(8,128)(2,1)S(1)} %bitcast.17, f32[4,8]{1,0:T(4,128)S(1)} %fusion), kind=kOutput, calls=%fused_computation.1 | convolution fusion | flops 134742016 | bytes 3276928 | tf_op jit(solution)/shard_map/snab,sbc->snac/dot_general | solution.py:21
  41.3 0.1 broadcast_in_dim.4
  41.4 2.7 %scatter_fusion = f32[16,128,128]{2,1,0:T(8,128)S(1)} fusion(f32[16,128,128]{2,1,0:T(8,128)S(1)} %broadcast_in_dim.4, s32[32]{0:T(128)S(1)} %fusion.1, f32[32,128,128]{2,1,0:T(8,128)S(1)} %bitcast.16), kind=kCustom, calls=%fused_computation | custom fusion | flops 524288 | bytes 6291584 | tf_op jit(solution)/shard_map/scatter-add | solution.py:25
  44.0 0.0 copy-start
  44.0 1.0 %copy-done = f32[16,128,128]{2,1,0:T(8,128)} copy-done((f32[16,128,128]{2,1,0:T(8,128)}, f32[16,128,128]{2,1,0:T(8,128)S(1)}, u32[]{:S(2)}) %copy-start) | copy-done | bytes 1048600
  45.1 0.0 all-reduce.3.cloned.1.call-update
  45.1 35.8 %all-reduce.3.cloned.1.call-done = f32[2048,128]{1,0:T(8,128)} async-done(((f32[2048,128]{1,0:T(8,128)}), f32[2048,128]{1,0:T(8,128)}) %all-reduce.3.cloned.1.call-update) | async-done | bytes 1048592 | tf_op jit(solution)/shard_map/psum | solution.py:29
  80.9 1.5 %multiply_reduce_fusion = (f32[128]{0:T(128)S(1)}, f32[2048,128]{1,0:T(8,128)S(1)}) fusion(f32[2048,128]{1,0:T(8,128)} %all-reduce.3.cloned.1.call-done), kind=kLoop, calls=%fused_computation.8 | loop fusion | flops 524160 | bytes 2097664 | tf_op jit(solution)/shard_map/reduce_sum | solution.py:31
  82.4 4.9 %psum.15 = f32[128]{0:T(128)S(1)} all-reduce(f32[128]{0:T(128)S(1)} %get-tuple-element.5), channel_id=1, replica_groups=mesh['layer'=4,'row'=2,'col'=4] {'row'}, use_global_device_ids=true, to_apply=%region_3.0 | all-reduce | flops 128 | bytes 1024 | tf_op jit(solution)/shard_map/psum | solution.py:31
  87.3 0.7 divide_bitcast_fusion
  (3 shorter events, 0.0 us)
Async XLA Ops:
  6.5 33.1 %all-gather.3.cloned.1.call-start = ((), (), s32[]{:S(2)}) async-start(), calls=%async_computation | async-start | bytes 1310720 | tf_op jit(solution)/shard_map/all_gather | solution.py:17
  7.3 73.6 %all-reduce.3.cloned.1.call-start = ((), (), s32[]{:S(2)}) async-start(), calls=%async_computation.1 | async-start | bytes 2097152 | tf_op jit(solution)/shard_map/psum | solution.py:29
  44.0 1.0 %copy-start = (f32[16,128,128]{2,1,0:T(8,128)}, f32[16,128,128]{2,1,0:T(8,128)S(1)}, u32[]{:S(2)}) copy-start(f32[16,128,128]{2,1,0:T(8,128)S(1)} %scatter_fusion) | copy-start | bytes 3145732
Sparse Core Ops, SparseCore 0:
  8.9 30.6 all-gather.2
  45.2 35.5 all-reduce.2
where the time goes:
time: 95.1 us; the launch traced here: 94.9 us
  waiting for transfers between devices  40.4 us (42%)
  blocking collectives  29.3 us (31%)
  between operations  14.1 us (15%)
  other arithmetic  5.65 us (6%)
  local copies, waits for them, and re-layouts  3.72 us (4%)
  matrix products  1.64 us (2%)
    psum x1, waiting for transfers between devices, body(): expanded = lax.psum(partial_sum, 'layer')  35.8 us
    unnamed x1, blocking collectives  9.89 us
    all_gather x1, blocking collectives, body(): row_ids = lax.all_gather(a_rows, 'col', axis=0, tiled=True)  9.35 us
    all_gather x1, blocking collectives, body(): inner_rows = lax.all_gather(b_panel, 'row', axis=0, tiled=True)  5.14 us
    psum x1, blocking collectives, body(): col_sums = lax.psum(jnp.sum(squares, axis=0), 'row')  4.93 us
    all_gather x1, waiting for transfers between devices, body(): blocks = lax.all_gather(a_blocks, 'col', axis=0, tiled=True)  3.93 us
    unnamed x5, local copies, waits for them, and re-layouts  3.03 us
    scatter-add x1, other arithmetic, body(): empty.at[row_ids.reshape(-1)].add(products.reshape(-1, block_size, width))  2.67 us
  transfers between devices with their start and end apart: 2, of which 2 were waited for; matrix products, arithmetic and copies ran while one was open for 4% of the time, Pallas kernels for 0%

commit v1 on v0

v1 whole, which is shorter than its diff:
```python
import functools

import jax
import jax.numpy as jnp
from jax import lax
from jax.experimental import pallas as pl
from jax.experimental.pallas import tpu as pltpu
from jax.sharding import PartitionSpec as P

IB = 16
CHUNKS = 2
VMEM = pl.BlockSpec(memory_space=pltpu.VMEM)
SMEM = pl.BlockSpec(memory_space=pltpu.SMEM)


def xor_permute(x, axis, mask):
    return lax.ppermute(x, axis, [(i, i ^ mask) for i in range(lax.axis_size(axis))])


def grid_permute(x, layer_mask, row_mask):
    n, m = lax.axis_size("layer"), lax.axis_size("row")
    pairs = [
        (i * m + j, (i ^ layer_mask) * m + (j ^ row_mask)) for i in range(n) for j in range(m)
    ]
    return lax.ppermute(x, ("layer", "row"), pairs)


def partial_kernel(masks, n_layer, place_ref, ids_ref, b_ref, *refs):
    a_refs, (keep_ref, send_ref) = refs[: len(masks)], refs[len(masks) :]
    keep_ref[...] = jnp.zeros_like(keep_ref)
    send_ref[...] = jnp.zeros_like(send_ref)
    layer, col = place_ref[0], place_ref[1]
    per = IB // n_layer
    capacity, rows, depth = a_refs[0].shape
    for mask, a_ref in zip(masks, a_refs, strict=True):
        panel = col ^ mask
        b = b_ref[pl.ds(pl.multiple_of(panel * depth, depth), depth), :]
        a = a_ref[...].reshape(capacity * rows, depth)
        prod = jnp.dot(a, b, preferred_element_type=jnp.float32).reshape(capacity, rows, -1)
        for n in range(capacity):
            block_row = ids_ref[panel, n]
            target = (block_row // per) ^ layer
            slot, sub = target // 2, block_row % per
            is_valid = block_row < IB

            @pl.when(is_valid & (target % 2 == 0))
            def _():
                keep_ref[slot, sub] += prod[n]

            @pl.when(is_valid & (target % 2 == 1))
            def _():
                send_ref[slot, sub] += prod[n]


def square_kernel(n_terms, chunks, *refs):
    ins, (sq_ref, sum_ref) = refs[: n_terms * chunks], refs[n_terms * chunks :]
    total = jnp.zeros(sum_ref.shape, jnp.float32)
    rows = sq_ref.shape[1] // chunks
    for h in range(chunks):
        e = ins[h * n_terms][...]
        for t in range(1, n_terms):
            e = e + ins[h * n_terms + t][...]
        sq = e * e
        sq_ref[:, h * rows : (h + 1) * rows, :] = sq
        total = total + jnp.sum(sq, axis=(0, 1))[None]
    sum_ref[...] = total


def body(a_blocks, a_rows, a_count, b_panel):
    n_layer, n_row, n_col = (lax.axis_size(a) for a in ("layer", "row", "col"))
    _, capacity, block, depth = a_blocks.shape
    width = b_panel.shape[1]
    rows = block // CHUNKS
    a = a_blocks[0]

    parts = [a[:, h * rows : (h + 1) * rows, :] for h in range(CHUNKS)]
    masks = [0]
    held = [[p] for p in parts]
    bit = n_col // 2
    while bit:
        for h in range(CHUNKS):
            held[h] = held[h] + [xor_permute(p, "col", bit) for p in held[h]]
        masks = masks + [m ^ bit for m in masks]
        bit //= 2

    valid = jnp.arange(capacity, dtype=jnp.int32)[None, :] < a_count[:, None]
    ids = lax.all_gather(jnp.where(valid, a_rows, IB), "col", axis=0, tiled=True)
    b_rows = lax.all_gather(b_panel, "row", axis=0, tiled=True)
    place = jnp.stack([lax.axis_index("layer"), lax.axis_index("col")]).astype(jnp.int32)

    per = IB // n_layer
    half = jax.ShapeDtypeStruct((n_layer // 2, per, rows, width), jnp.float32)
    terms = []
    for h in range(CHUNKS):
        keep, send = pl.pallas_call(
            functools.partial(partial_kernel, masks, n_layer),
            out_shape=(half, half),
            in_specs=[SMEM, SMEM] + [VMEM] * (1 + len(masks)),
            out_specs=(VMEM, VMEM),
            name="partial_rows",
        )(place, ids, b_rows, *held[h])
        got = xor_permute(send, "layer", 1)
        mine = [keep[0], got[0]]
        others = [keep[k] + got[k] for k in range(1, n_layer // 2)]
        bit = n_layer // 2
        n_slots = n_layer // 2
        slots = {k: others[k - 1] for k in range(1, n_slots)}
        step = n_slots // 2
        while step:
            got = {k: xor_permute(slots[k], "layer", 2 * step) for k in range(step, 2 * step)}
            mine.append(got[step])
            slots = {k: slots[k] + got[k + step] for k in range(1, step)}
            step //= 2
        terms += mine
    n_terms = len(terms) // CHUNKS

    sq, col_sum = pl.pallas_call(
        functools.partial(square_kernel, n_terms, CHUNKS),
        out_shape=(
            jax.ShapeDtypeStruct((per, block, width), jnp.float32),
            jax.ShapeDtypeStruct((1, width), jnp.float32),
        ),
        in_specs=[VMEM] * len(terms),
        out_specs=(VMEM, VMEM),
        name="squares",
    )(*terms)

    col_sum = col_sum + xor_permute(col_sum, "layer", 1)
    others = [
        grid_permute(col_sum, i, j)
        for i in range(0, n_layer, 2)
        for j in range(n_row)
        if i or j
    ]
    for other in others:
        col_sum = col_sum + other
    scale = 1.0 / (col_sum * (1.0 / (n_row * IB * block)) + 1e-06)
    return (sq * scale).reshape(1, per * block, width)


def solution(mesh):
    return jax.shard_map(
        body,
        mesh=mesh,
        in_specs=(
            P(("layer", "row", "col"), None, None, None),
            P(("layer", "row", "col"), None),
            P(("layer", "row", "col")),
            P(("layer", "row"), "col"),
        ),
        out_specs=P("row", "layer", "col"),
        check_vma=False,
    )
```

time: 95.1 us -> 65.8 us (0.69)
  waiting for transfers between devices: 40.4 us -> 17.4 us
  starting transfers between devices: 0.04 us -> 14.2 us
  between operations: 14.1 us -> 0.77 us
  blocking collectives: 29.3 us -> 16 us
  Pallas kernels: 0 us -> 9.04 us
  other arithmetic: 5.65 us -> 3.8 us
  matrix products: 1.64 us -> 0 us
    psum x1 -> x0, waiting for transfers between devices: 35.8 us -> none  [body(): expanded = lax.psum(partial_sum, 'layer')]
    ppermute x0 -> x14, waiting for transfers between devices: none -> 17.4 us  [the longest x11 13.4 us: xor_permute(): lax.ppermute(x, axis, [(i, i ^ mask) for i in range(lax.axis_size(axis))])]
    ppermute x0 -> x14, starting transfers between devices: none -> 14.2 us  [the longest x11 10.7 us: xor_permute(): lax.ppermute(x, axis, [(i, i ^ mask) for i in range(lax.axis_size(axis))])]
    unnamed x1 -> x0, blocking collectives: 9.89 us -> none
    pallas_call x0 -> x3, Pallas kernels: none -> 9.04 us  [the longest x2 7.1 us: body(): pl.pallas_call(functools.partial(partial_kernel, masks, n_layer), out_sha...]
    psum x1 -> x0, blocking collectives: 4.93 us -> none  [body(): col_sums = lax.psum(jnp.sum(squares, axis=0), 'row')]
    all_gather x1 -> x0, waiting for transfers between devices: 3.93 us -> none  [body(): blocks = lax.all_gather(a_blocks, 'col', axis=0, tiled=True)]
    scatter-add x1 -> x0, other arithmetic: 2.67 us -> none  [body(): empty.at[row_ids.reshape(-1)].add(products.reshape(-1, block_size, width))]
  transfers between devices with their start and end apart: 2 -> 14, of which waited for: 2 -> 8; matrix products, arithmetic and copies ran while one was open for 4% -> 3% of each run, Pallas kernels for 0% -> 11%
where the time goes in v1:
time: 65.8 us; the launch traced here: 65.5 us
  waiting for transfers between devices  17.4 us (26%)
  blocking collectives  16 us (24%)
  starting transfers between devices  14.2 us (22%)
  Pallas kernels  9.04 us (14%)
  local copies, waits for them, and re-layouts  4.29 us (7%)
  other arithmetic  3.8 us (6%)
  between operations  0.77 us (1%)
    ppermute x11, waiting for transfers between devices, xor_permute(): lax.ppermute(x, axis, [(i, i ^ mask) for i in range(lax.axis_size(axis))])  13.4 us
    all_gather x1, blocking collectives, body(): lax.all_gather(jnp.where(valid, a_rows, IB), 'col', axis=0, tiled=True)  11 us
    ppermute x11, starting transfers between devices, xor_permute(): lax.ppermute(x, axis, [(i, i ^ mask) for i in range(lax.axis_size(axis))])  10.7 us
    pallas_call x2, Pallas kernels, body(): pl.pallas_call(functools.partial(partial_kernel, masks, n_layer), out_sha...  7.1 us
    all_gather x1, blocking collectives, body(): b_rows = lax.all_gather(b_panel, 'row', axis=0, tiled=True)  5.04 us
    ppermute x3, waiting for transfers between devices, grid_permute(): return lax.ppermute(x, ('layer', 'row'), pairs)  3.98 us
    ppermute x3, starting transfers between devices, grid_permute(): return lax.ppermute(x, ('layer', 'row'), pairs)  3.49 us
    unnamed x30, local copies, waits for them, and re-layouts  3.27 us
  transfers between devices with their start and end apart: 14, of which 8 were waited for; matrix products, arithmetic and copies ran while one was open for 3% of the time, Pallas kernels for 11%

profile of v1, /device:TPU:0, one launch (start us, length us, event | category | flops | bytes accessed | tf_op | source)
XLA Modules:
  0.0 65.5 jit_solution(7954887193984746774)
XLA Ops:
  0.0 1.0 %fusion.3 = (bf16[8,64,128]{2,1,0:T(8,128)(2,1)S(1)}, bf16[8,64,128]{2,1,0:T(8,128)(2,1)S(1)}) fusion(bf16[8,128,128]{2,1,0:T(8,128)(2,1)} %bitcast.23), kind=kLoop, calls=%fused_computation.13 | loop fusion | bytes 524288 | tf_op jit(solution)/shard_map/slice | solution.py:76
  1.0 0.0 copy-start.1
  1.0 4.1 %collective-permute-start.5 = (bf16[8,64,128]{2,1,0:T(8,128)(2,1)S(1)}, bf16[8,64,128]{2,1,0:T(8,128)(2,1)S(1)}, u32[]{:S(2)}, u32[]{:S(2)}) collective-permute-start(bf16[8,64,128]{2,1,0:T(8,128)(2,1)S(1)} %get-tuple-element.20.refs_0_), channel_id=1, source_target_pairs={{0,2},{1,3},{2,0},{3,1},{4,6},{5,7},{6,4},{7,5},{8,10},{9,11},{10,... | collective-permute-start | bytes 393224 | tf_op jit(solution)/shard_map/ppermute | solution.py:17
  5.1 1.6 %collective-permute-start.6 = (bf16[8,64,128]{2,1,0:T(8,128)(2,1)S(1)}, bf16[8,64,128]{2,1,0:T(8,128)(2,1)S(1)}, u32[]{:S(2)}, u32[]{:S(2)}) collective-permute-start(bf16[8,64,128]{2,1,0:T(8,128)(2,1)S(1)} %get-tuple-element.20.refs_0_), channel_id=1, source_target_pairs={{0,1},{1,0},{2,3},{3,2},{4,5},{5,4},{6,7},{7,6},{8,9},{9,8},{10,11... | collective-permute-start | bytes 393224 | tf_op jit(solution)/shard_map/ppermute | solution.py:17
  7.4 0.0 copy-start.13
  7.4 0.6 copy-done.13
  8.0 0.3 collective-permute-start
  8.4 11.0 %all-gather = s32[4,1,8]{2,1,0:T(1,128)} all-gather(s32[1,1,8]{2,1,0:T(1,128)S(1)} %fusion.2), channel_id=1, replica_groups=mesh['layer'=4,'row'=2,'col'=4] {'col'}, dimensions={0}, use_global_device_ids=true | all-gather | bytes 160 | tf_op jit(solution)/shard_map/all_gather | solution.py:87
  19.4 0.0 collective-permute-done.5.refs_1_
  19.4 0.1 collective-permute-start.7
  19.4 0.6 pad_add_fusion.place_ref
  20.1 5.0 %all_gather.7.b_ref = bf16[512,128]{1,0:T(8,128)(2,1)} all-gather(bf16[256,128]{1,0:T(8,128)(2,1)S(1)} %copy-done.12), channel_id=1, replica_groups=mesh['layer'=4,'row'=2,'col'=4] {'row'}, dimensions={0}, use_global_device_ids=true | all-gather | bytes 196608 | tf_op jit(solution)/shard_map/all_gather | solution.py:88
  25.1 0.0 collective-permute-done.6.refs_2_
  25.1 0.0 collective-permute-done.7.refs_3_
  25.2 0.6 copy-done.6
  25.8 0.1 copy-done.10
  25.8 3.6 %partial_rows.3 = (f32[2,4,64,128]{3,2,1,0:T(8,128)}, f32[2,4,64,128]{3,2,1,0:T(8,128)}) custom-call(s32[2]{0:T(128)} %pad_add_fusion.place_ref, s32[4,8]{1,0:T(4,128)} %bitcast.24, bf16[512,128]{1,0:T(8,128)(2,1)} %all_gather.7.b_ref, bf16[8,64,128]{2,1,0:T(8,128)(2,1)} %copy-done.1, bf16[8,64,128]{2,1,0:T(8,128)(2,1)} %copy-done.5, ...), custom_call_target="tpu_custom_call" | custom-call | tf_op jit(solution)/shard_map/partial_rows/pallas_call | solution.py:95
  29.4 0.0 collective-permute-start.8
  29.4 2.0 %collective-permute-start.1 = (bf16[8,64,128]{2,1,0:T(8,128)(2,1)S(1)}, bf16[8,64,128]{2,1,0:T(8,128)(2,1)S(1)}, u32[]{:S(2)}, u32[]{:S(2)}) collective-permute-start(bf16[8,64,128]{2,1,0:T(8,128)(2,1)S(1)} %get-tuple-element.21.refs_0_), channel_id=1, source_target_pairs={{0,1},{1,0},{2,3},{3,2},{4,5},{5,4},{6,7},{7,6},{8,9},{9,8},{10,11... | collective-permute-start | bytes 393224 | tf_op jit(solution)/shard_map/ppermute | solution.py:17
  31.4 0.0 collective-permute-done.refs_1_
  31.4 0.1 collective-permute-start.2
  31.5 4.3 %collective-permute-done.1.refs_2_ = bf16[8,64,128]{2,1,0:T(8,128)(2,1)S(1)} collective-permute-done((bf16[8,64,128]{2,1,0:T(8,128)(2,1)S(1)}, bf16[8,64,128]{2,1,0:T(8,128)(2,1)S(1)}, u32[]{:S(2)}, u32[]{:S(2)}) %collective-permute-start.1) | collective-permute-done | bytes 131104 | tf_op jit(solution)/shard_map/ppermute | solution.py:17
  35.8 2.5 %collective-permute-done.2.refs_3_ = bf16[8,64,128]{2,1,0:T(8,128)(2,1)S(1)} collective-permute-done((bf16[8,64,128]{2,1,0:T(8,128)(2,1)S(1)}, bf16[8,64,128]{2,1,0:T(8,128)(2,1)S(1)}, u32[]{:S(2)}, u32[]{:S(2)}) %collective-permute-start.2) | collective-permute-done | bytes 131104 | tf_op jit(solution)/shard_map/ppermute | solution.py:17
  38.3 0.7 copy-done.11
  39.0 3.5 %partial_rows.2 = (f32[2,4,64,128]{3,2,1,0:T(8,128)}, f32[2,4,64,128]{3,2,1,0:T(8,128)}) custom-call(s32[2]{0:T(128)} %pad_add_fusion.place_ref, s32[4,8]{1,0:T(4,128)} %bitcast.25, bf16[512,128]{1,0:T(8,128)(2,1)} %all_gather.7.b_ref, bf16[8,64,128]{2,1,0:T(8,128)(2,1)} %copy-done, bf16[8,64,128]{2,1,0:T(8,128)(2,1)} %copy-done.4, ...), custom_call_target="tpu_custom_call" | custom-call | tf_op jit(solution)/shard_map/partial_rows/pallas_call | solution.py:95
  42.5 0.0 collective-permute-start.3
  42.5 0.0 collective-permute-done.8
  42.6 0.0 copy-start.3
  42.6 0.7 %fusion = (f32[4,64,128]{2,1,0:T(8,128)S(1)}, f32[4,64,128]{2,1,0:T(8,128)}, f32[4,64,128]{2,1,0:T(8,128)}) fusion(f32[2,4,64,128]{3,2,1,0:T(8,128)S(1)} %collective-permute-done.8, f32[2,4,64,128]{3,2,1,0:T(8,128)S(1)} %copy-done.2), kind=kLoop, calls=%fused_computation.1 | loop fusion | flops 32768 | bytes 917504 | tf_op jit(solution)/shard_map/add | solution.py:104
  43.3 1.5 %collective-permute-start.9 = (f32[4,64,128]{2,1,0:T(8,128)S(1)}, f32[4,64,128]{2,1,0:T(8,128)S(1)}, u32[]{:S(2)}, u32[]{:S(2)}) collective-permute-start(f32[4,64,128]{2,1,0:T(8,128)S(1)} %get-tuple-element.17), channel_id=1, source_target_pairs={{0,16},{8,24},{16,0},{24,8},{1,17},{9,25},{17,1},{25,9},{2,18},{10... | collective-permute-start | bytes 393224 | tf_op jit(solution)/shard_map/ppermute | solution.py:17
  44.8 0.0 collective-permute-done.3
  44.8 0.7 %fusion.1 = (f32[4,64,128]{2,1,0:T(8,128)S(1)}, f32[4,64,128]{2,1,0:T(8,128)}, f32[4,64,128]{2,1,0:T(8,128)}) fusion(f32[2,4,64,128]{3,2,1,0:T(8,128)S(1)} %collective-permute-done.3, f32[2,4,64,128]{3,2,1,0:T(8,128)S(1)} %copy-done.3), kind=kLoop, calls=%fused_computation.4 | loop fusion | flops 32768 | bytes 917504 | tf_op jit(solution)/shard_map/add | solution.py:104
  45.6 1.0 %collective-permute-start.4 = (f32[4,64,128]{2,1,0:T(8,128)S(1)}, f32[4,64,128]{2,1,0:T(8,128)S(1)}, u32[]{:S(2)}, u32[]{:S(2)}) collective-permute-start(f32[4,64,128]{2,1,0:T(8,128)S(1)} %get-tuple-element.22), channel_id=1, source_target_pairs={{0,16},{8,24},{16,0},{24,8},{1,17},{9,25},{17,1},{25,9},{2,18},{10... | collective-permute-start | bytes 393224 | tf_op jit(solution)/shard_map/ppermute | solution.py:17
  46.5 3.1 %collective-permute-done.9.refs_5_ = f32[4,64,128]{2,1,0:T(8,128)S(1)} collective-permute-done((f32[4,64,128]{2,1,0:T(8,128)S(1)}, f32[4,64,128]{2,1,0:T(8,128)S(1)}, u32[]{:S(2)}, u32[]{:S(2)}) %collective-permute-start.9) | collective-permute-done | bytes 131104 | tf_op jit(solution)/shard_map/ppermute | solution.py:17
  49.6 2.4 %collective-permute-done.4.refs_2_ = f32[4,64,128]{2,1,0:T(8,128)S(1)} collective-permute-done((f32[4,64,128]{2,1,0:T(8,128)S(1)}, f32[4,64,128]{2,1,0:T(8,128)S(1)}, u32[]{:S(2)}, u32[]{:S(2)}) %collective-permute-start.4) | collective-permute-done | bytes 131104 | tf_op jit(solution)/shard_map/ppermute | solution.py:17
  52.0 0.0 copy-done.7
  52.0 0.6 copy-done.9
  52.6 1.9 %squares.1 = (f32[4,128,128]{2,1,0:T(8,128)}, f32[1,128]{1,0:T(1,128)}) custom-call(f32[4,64,128]{2,1,0:T(8,128)} %get-tuple-element.23.refs_0_, f32[4,64,128]{2,1,0:T(8,128)} %get-tuple-element.24.refs_1_, f32[4,64,128]{2,1,0:T(8,128)} %copy-done.9, f32[4,64,128]{2,1,0:T(8,128)} %get-tuple-element.18.refs_3_, f32[4,64,128]{2,1,0:T(8,128)} %get-tuple-element.19.refs_4_, ...), custom_call_target="tpu_custom_call" | custom-call | tf_op jit(solution)/shard_map/squares/pallas_call | solution.py:117
  54.6 0.6 copy-done.14
  55.2 0.0 collective-permute-start.10
  55.2 1.1 %collective-permute-done.10 = f32[1,128]{1,0:T(1,128)S(1)} collective-permute-done((f32[1,128]{1,0:T(1,128)S(1)}, f32[1,128]{1,0:T(1,128)S(1)}, u32[]{:S(2)}, u32[]{:S(2)}) %collective-permute-start.10) | collective-permute-done | bytes 544 | tf_op jit(solution)/shard_map/ppermute | solution.py:17
  56.3 1.5 %collective-permute-start.11 = (f32[1,128]{1,0:T(1,128)S(1)}, f32[1,128]{1,0:T(1,128)S(1)}, u32[]{:S(2)}, u32[]{:S(2)}) collective-permute-start(f32[1,128]{1,0:T(1,128)S(1)} %add.34), channel_id=1, source_target_pairs={{0,4},{4,0},{8,12},{12,8},{16,20},{20,16},{24,28},{28,24},{1,5},{5... | collective-permute-start | bytes 1544 | tf_op jit(solution)/shard_map/ppermute | solution.py:25
  57.9 1.5 %collective-permute-start.12 = (f32[1,128]{1,0:T(1,128)S(1)}, f32[1,128]{1,0:T(1,128)S(1)}, u32[]{:S(2)}, u32[]{:S(2)}) collective-permute-start(f32[1,128]{1,0:T(1,128)S(1)} %add.34), channel_id=1, source_target_pairs={{0,16},{4,20},{8,24},{12,28},{16,0},{20,4},{24,8},{28,12},{1,17},{... | collective-permute-start | bytes 1544 | tf_op jit(solution)/shard_map/ppermute | solution.py:25
  59.4 0.5 collective-permute-start.13
  59.8 0.1 collective-permute-done.11
  59.9 1.5 %collective-permute-done.12 = f32[1,128]{1,0:T(1,128)S(1)} collective-permute-done((f32[1,128]{1,0:T(1,128)S(1)}, f32[1,128]{1,0:T(1,128)S(1)}, u32[]{:S(2)}, u32[]{:S(2)}) %collective-permute-start.12) | collective-permute-done | bytes 544 | tf_op jit(solution)/shard_map/ppermute | solution.py:25
  61.4 2.4 %collective-permute-done.13 = f32[1,128]{1,0:T(1,128)S(1)} collective-permute-done((f32[1,128]{1,0:T(1,128)S(1)}, f32[1,128]{1,0:T(1,128)S(1)}, u32[]{:S(2)}, u32[]{:S(2)}) %collective-permute-start.13) | collective-permute-done | bytes 544 | tf_op jit(solution)/shard_map/ppermute | solution.py:25
  63.8 1.7 %broadcast_multiply_fusion = f32[4,128,128]{2,1,0:T(8,128)} fusion(f32[4,128,128]{2,1,0:T(8,128)} %get-tuple-element.15, f32[128]{0:T(128)S(1)} %divide_bitcast_fusion), kind=kLoop, calls=%fused_computation.6 | loop fusion | flops 65536 | bytes 524800 | tf_op jit(solution)/shard_map/mul | solution.py:138
  (23 shorter events, 0.1 us)
Async XLA Ops:
  0.0 20.1 %copy-start.12 = (bf16[256,128]{1,0:T(8,128)(2,1)S(1)}, bf16[256,128]{1,0:T(8,128)(2,1)}, u32[]{:S(2)}) copy-start(bf16[256,128]{1,0:T(8,128)(2,1)} %param.7) | copy-start | bytes 196612
  1.0 24.1 %copy-start.1 = (bf16[8,64,128]{2,1,0:T(8,128)(2,1)}, bf16[8,64,128]{2,1,0:T(8,128)(2,1)S(1)}, u32[]{:S(2)}) copy-start(bf16[8,64,128]{2,1,0:T(8,128)(2,1)S(1)} %get-tuple-element.20.refs_0_) | copy-start | bytes 393220
  1.0 28.4 %copy-start = (bf16[8,64,128]{2,1,0:T(8,128)(2,1)}, bf16[8,64,128]{2,1,0:T(8,128)(2,1)S(1)}, u32[]{:S(2)}) copy-start(bf16[8,64,128]{2,1,0:T(8,128)(2,1)S(1)} %get-tuple-element.21.refs_0_) | copy-start | bytes 393220
  1.0 18.3 %collective-permute-start.5 = (bf16[8,64,128]{2,1,0:T(8,128)(2,1)S(1)}, bf16[8,64,128]{2,1,0:T(8,128)(2,1)S(1)}, u32[]{:S(2)}, u32[]{:S(2)}) collective-permute-start(bf16[8,64,128]{2,1,0:T(8,128)(2,1)S(1)} %get-tuple-element.20.refs_0_), channel_id=1, source_target_pairs={{0,2},{1,3},{2,0},{3,1},{4,6},{5,7},{6,4},{7,5},{8,10},{9,11},{10,... | collective-permute-start | bytes 393224 | tf_op jit(solution)/shard_map/ppermute | solution.py:17
  5.1 20.0 %collective-permute-start.6 = (bf16[8,64,128]{2,1,0:T(8,128)(2,1)S(1)}, bf16[8,64,128]{2,1,0:T(8,128)(2,1)S(1)}, u32[]{:S(2)}, u32[]{:S(2)}) collective-permute-start(bf16[8,64,128]{2,1,0:T(8,128)(2,1)S(1)} %get-tuple-element.20.refs_0_), channel_id=1, source_target_pairs={{0,1},{1,0},{2,3},{3,2},{4,5},{5,4},{6,7},{7,6},{8,9},{9,8},{10,11... | collective-permute-start | bytes 393224 | tf_op jit(solution)/shard_map/ppermute | solution.py:17
  7.4 0.7 %copy-start.13 = (s32[1,8]{1,0:T(1,128)S(1)}, s32[1,8]{1,0:T(1,128)}, u32[]{:S(2)}) copy-start(s32[1,8]{1,0:T(1,128)} %param.5) | copy-start | bytes 100
  8.0 23.4 %collective-permute-start = (bf16[8,64,128]{2,1,0:T(8,128)(2,1)S(1)}, bf16[8,64,128]{2,1,0:T(8,128)(2,1)S(1)}, u32[]{:S(2)}, u32[]{:S(2)}) collective-permute-start(bf16[8,64,128]{2,1,0:T(8,128)(2,1)S(1)} %get-tuple-element.21.refs_0_), channel_id=1, source_target_pairs={{0,2},{1,3},{2,0},{3,1},{4,6},{5,7},{6,4},{7,5},{8,10},{9,11},{10,... | collective-permute-start | bytes 393224 | tf_op jit(solution)/shard_map/ppermute | solution.py:17
  19.4 5.8 %copy-start.5 = (bf16[8,64,128]{2,1,0:T(8,128)(2,1)}, bf16[8,64,128]{2,1,0:T(8,128)(2,1)S(1)}, u32[]{:S(2)}) copy-start(bf16[8,64,128]{2,1,0:T(8,128)(2,1)S(1)} %collective-permute-done.5.refs_1_) | copy-start | bytes 393220
  19.4 5.7 %collective-permute-start.7 = (bf16[8,64,128]{2,1,0:T(8,128)(2,1)S(1)}, bf16[8,64,128]{2,1,0:T(8,128)(2,1)S(1)}, u32[]{:S(2)}, u32[]{:S(2)}) collective-permute-start(bf16[8,64,128]{2,1,0:T(8,128)(2,1)S(1)} %collective-permute-done.5.refs_1_), channel_id=1, source_target_pairs={{0,1},{1,0},{2,3},{3,2},{4,5},{5,4},{6,7},{7,6},{8,9},{9,8},{10,11... | collective-permute-start | bytes 393224 | tf_op jit(solution)/shard_map/ppermute | solution.py:17
  25.1 0.7 %copy-start.6 = (bf16[8,64,128]{2,1,0:T(8,128)(2,1)}, bf16[8,64,128]{2,1,0:T(8,128)(2,1)S(1)}, u32[]{:S(2)}) copy-start(bf16[8,64,128]{2,1,0:T(8,128)(2,1)S(1)} %collective-permute-done.6.refs_2_) | copy-start | bytes 393220
  25.1 0.7 %copy-start.10 = (bf16[8,64,128]{2,1,0:T(8,128)(2,1)}, bf16[8,64,128]{2,1,0:T(8,128)(2,1)S(1)}, u32[]{:S(2)}) copy-start(bf16[8,64,128]{2,1,0:T(8,128)(2,1)S(1)} %collective-permute-done.7.refs_3_) | copy-start | bytes 393220
  29.4 13.2 %copy-start.2 = (f32[2,4,64,128]{3,2,1,0:T(8,128)S(1)}, f32[2,4,64,128]{3,2,1,0:T(8,128)}, u32[]{:S(2)}) copy-start(f32[2,4,64,128]{3,2,1,0:T(8,128)} %get-tuple-element.13) | copy-start | bytes 786436
  29.4 13.2 %collective-permute-start.8 = (f32[2,4,64,128]{3,2,1,0:T(8,128)}, f32[2,4,64,128]{3,2,1,0:T(8,128)S(1)}, u32[]{:S(2)}, u32[]{:S(2)}) collective-permute-start(f32[2,4,64,128]{3,2,1,0:T(8,128)} %get-tuple-element.14), channel_id=1, source_target_pairs={{0,8},{8,0},{16,24},{24,16},{1,9},{9,1},{17,25},{25,17},{2,10},{10... | collective-permute-start | bytes 786440 | tf_op jit(solution)/shard_map/ppermute | solution.py:17
  29.4 6.4 %collective-permute-start.1 = (bf16[8,64,128]{2,1,0:T(8,128)(2,1)S(1)}, bf16[8,64,128]{2,1,0:T(8,128)(2,1)S(1)}, u32[]{:S(2)}, u32[]{:S(2)}) collective-permute-start(bf16[8,64,128]{2,1,0:T(8,128)(2,1)S(1)} %get-tuple-element.21.refs_0_), channel_id=1, source_target_pairs={{0,1},{1,0},{2,3},{3,2},{4,5},{5,4},{6,7},{7,6},{8,9},{9,8},{10,11... | collective-permute-start | bytes 393224 | tf_op jit(solution)/shard_map/ppermute | solution.py:17
  31.4 6.9 %copy-start.4 = (bf16[8,64,128]{2,1,0:T(8,128)(2,1)}, bf16[8,64,128]{2,1,0:T(8,128)(2,1)S(1)}, u32[]{:S(2)}) copy-start(bf16[8,64,128]{2,1,0:T(8,128)(2,1)S(1)} %collective-permute-done.refs_1_) | copy-start | bytes 393220
  31.4 6.9 %collective-permute-start.2 = (bf16[8,64,128]{2,1,0:T(8,128)(2,1)S(1)}, bf16[8,64,128]{2,1,0:T(8,128)(2,1)S(1)}, u32[]{:S(2)}, u32[]{:S(2)}) collective-permute-start(bf16[8,64,128]{2,1,0:T(8,128)(2,1)S(1)} %collective-permute-done.refs_1_), channel_id=1, source_target_pairs={{0,1},{1,0},{2,3},{3,2},{4,5},{5,4},{6,7},{7,6},{8,9},{9,8},{10,11... | collective-permute-start | bytes 393224 | tf_op jit(solution)/shard_map/ppermute | solution.py:17
  35.8 2.5 %copy-start.8 = (bf16[8,64,128]{2,1,0:T(8,128)(2,1)}, bf16[8,64,128]{2,1,0:T(8,128)(2,1)S(1)}, u32[]{:S(2)}) copy-start(bf16[8,64,128]{2,1,0:T(8,128)(2,1)S(1)} %collective-permute-done.1.refs_2_) | copy-start | bytes 393220
  38.3 0.7 copy-start.11
  42.5 2.3 %collective-permute-start.3 = (f32[2,4,64,128]{3,2,1,0:T(8,128)}, f32[2,4,64,128]{3,2,1,0:T(8,128)S(1)}, u32[]{:S(2)}, u32[]{:S(2)}) collective-permute-start(f32[2,4,64,128]{3,2,1,0:T(8,128)} %get-tuple-element.12), channel_id=1, source_target_pairs={{0,8},{8,0},{16,24},{24,16},{1,9},{9,1},{17,25},{25,17},{2,10},{10... | collective-permute-start | bytes 786440 | tf_op jit(solution)/shard_map/ppermute | solution.py:17
  42.6 2.3 %copy-start.3 = (f32[2,4,64,128]{3,2,1,0:T(8,128)S(1)}, f32[2,4,64,128]{3,2,1,0:T(8,128)}, u32[]{:S(2)}) copy-start(f32[2,4,64,128]{3,2,1,0:T(8,128)} %get-tuple-element.11) | copy-start | bytes 786436
  43.3 6.3 %collective-permute-start.9 = (f32[4,64,128]{2,1,0:T(8,128)S(1)}, f32[4,64,128]{2,1,0:T(8,128)S(1)}, u32[]{:S(2)}, u32[]{:S(2)}) collective-permute-start(f32[4,64,128]{2,1,0:T(8,128)S(1)} %get-tuple-element.17), channel_id=1, source_target_pairs={{0,16},{8,24},{16,0},{24,8},{1,17},{9,25},{17,1},{25,9},{2,18},{10... | collective-permute-start | bytes 393224 | tf_op jit(solution)/shard_map/ppermute | solution.py:17
  45.6 6.4 %collective-permute-start.4 = (f32[4,64,128]{2,1,0:T(8,128)S(1)}, f32[4,64,128]{2,1,0:T(8,128)S(1)}, u32[]{:S(2)}, u32[]{:S(2)}) collective-permute-start(f32[4,64,128]{2,1,0:T(8,128)S(1)} %get-tuple-element.22), channel_id=1, source_target_pairs={{0,16},{8,24},{16,0},{24,8},{1,17},{9,25},{17,1},{25,9},{2,18},{10... | collective-permute-start | bytes 393224 | tf_op jit(solution)/shard_map/ppermute | solution.py:17
  49.6 2.4 %copy-start.7 = (f32[4,64,128]{2,1,0:T(8,128)}, f32[4,64,128]{2,1,0:T(8,128)S(1)}, u32[]{:S(2)}) copy-start(f32[4,64,128]{2,1,0:T(8,128)S(1)} %collective-permute-done.9.refs_5_) | copy-start | bytes 393220
  52.0 0.7 copy-start.9
  54.6 0.6 copy-start.14
  55.2 1.1 %collective-permute-start.10 = (f32[1,128]{1,0:T(1,128)S(1)}, f32[1,128]{1,0:T(1,128)S(1)}, u32[]{:S(2)}, u32[]{:S(2)}) collective-permute-start(f32[1,128]{1,0:T(1,128)S(1)} %copy-done.14), channel_id=1, source_target_pairs={{0,8},{8,0},{16,24},{24,16},{1,9},{9,1},{17,25},{25,17},{2,10},{10... | collective-permute-start | bytes 1544 | tf_op jit(solution)/shard_map/ppermute | solution.py:17
  56.3 3.5 %collective-permute-start.11 = (f32[1,128]{1,0:T(1,128)S(1)}, f32[1,128]{1,0:T(1,128)S(1)}, u32[]{:S(2)}, u32[]{:S(2)}) collective-permute-start(f32[1,128]{1,0:T(1,128)S(1)} %add.34), channel_id=1, source_target_pairs={{0,4},{4,0},{8,12},{12,8},{16,20},{20,16},{24,28},{28,24},{1,5},{5... | collective-permute-start | bytes 1544 | tf_op jit(solution)/shard_map/ppermute | solution.py:25
  57.9 3.5 %collective-permute-start.12 = (f32[1,128]{1,0:T(1,128)S(1)}, f32[1,128]{1,0:T(1,128)S(1)}, u32[]{:S(2)}, u32[]{:S(2)}) collective-permute-start(f32[1,128]{1,0:T(1,128)S(1)} %add.34), channel_id=1, source_target_pairs={{0,16},{4,20},{8,24},{12,28},{16,0},{20,4},{24,8},{28,12},{1,17},{... | collective-permute-start | bytes 1544 | tf_op jit(solution)/shard_map/ppermute | solution.py:25
  59.4 4.4 %collective-permute-start.13 = (f32[1,128]{1,0:T(1,128)S(1)}, f32[1,128]{1,0:T(1,128)S(1)}, u32[]{:S(2)}, u32[]{:S(2)}) collective-permute-start(f32[1,128]{1,0:T(1,128)S(1)} %add.34), channel_id=1, source_target_pairs={{0,20},{4,16},{8,28},{12,24},{16,4},{20,0},{24,12},{28,8},{1,21},{... | collective-permute-start | bytes 1544 | tf_op jit(solution)/shard_map/ppermute | solution.py:25

commit v2 on v0

v2 whole, which is shorter than its diff:
```python
import functools

import jax
import jax.numpy as jnp
from jax import lax
from jax.experimental import pallas as pl
from jax.experimental.pallas import tpu as pltpu
from jax.sharding import PartitionSpec as P

IB = 16
CUTS = (32, 96)
PAD = 16
VMEM = pl.BlockSpec(memory_space=pltpu.VMEM)
SMEM = pl.BlockSpec(memory_space=pltpu.SMEM)


def pin(x):
    return pltpu.with_memory_space_constraint(x, pltpu.VMEM)


def xor_permute(x, axis, mask):
    return lax.ppermute(x, axis, [(i, i ^ mask) for i in range(lax.axis_size(axis))])


def grid_permute(x, layer_mask, row_mask):
    n, m = lax.axis_size("layer"), lax.axis_size("row")
    pairs = [
        (i * m + j, (i ^ layer_mask) * m + (j ^ row_mask)) for i in range(n) for j in range(m)
    ]
    return lax.ppermute(x, ("layer", "row"), pairs)


def product_kernel(masks, n_layer, n_row, capacity, rows, depth, ids_ref, *refs):
    n_slots, n_held = n_layer // 2, 2 * len(masks)
    b_refs, a_refs = refs[:2], refs[2 : 2 + n_held]
    out_refs = refs[2 + n_held : 2 + n_held + n_slots]
    where_ref, lhs_ref = refs[2 + n_held + n_slots :]
    layer, row, col = (lax.axis_index(n) for n in ("layer", "row", "col"))
    per, per_row = IB // n_layer, len(masks) // n_row
    for k in range(n_held):
        for i in range(IB + 1):
            where_ref[k, i] = -1
        for n in range(capacity):
            where_ref[k, ids_ref[k, n]] = n
    rhs = []
    for k in range(n_held):
        panel = col ^ masks[k // 2]
        start = (((panel // per_row) ^ row) * per_row + panel % per_row) * depth
        rhs.append(b_refs[k % 2][pl.ds(pl.multiple_of(start, depth), depth), :])
    rhs = jnp.concatenate(rhs, axis=0)
    for slot in range(n_slots):
        for sub in range(per):
            block_row = (layer ^ (2 * slot)) * per + sub
            for k in range(n_held):
                n = where_ref[k, block_row]
                start = pl.multiple_of(jnp.maximum(n, 0) * rows, rows)
                a = a_refs[k][pl.ds(start, rows), :]
                lhs_ref[sub * rows : (sub + 1) * rows, k * depth : (k + 1) * depth] = jnp.where(
                    n >= 0, a, jnp.zeros_like(a)
                )
        out_refs[slot][...] = jnp.dot(
            lhs_ref[...], rhs, preferred_element_type=jnp.float32
        ).reshape(out_refs[slot].shape)


def body(a_blocks, a_rows, a_count, b_panel):
    n_layer, n_row, n_col = (lax.axis_size(a) for a in ("layer", "row", "col"))
    _, capacity, block, depth = a_blocks.shape
    width = b_panel.shape[1]
    a = a_blocks[0]

    valid = jnp.arange(capacity, dtype=jnp.int32)[None, :] < a_count[:, None]
    own_ids = jnp.where(valid, a_rows, IB).astype(a.dtype)
    own_ids = jnp.pad(own_ids, ((0, PAD - 1), (0, depth - capacity)))
    parts, start = [], 0
    for h, rows in enumerate(CUTS):
        part = a[:, start : start + rows, :].reshape(capacity * rows, depth)
        parts.append(part if h else jnp.concatenate([part, own_ids]))
        start += rows

    masks = [0]
    held = [[p] for p in parts]
    bit = n_col // 2
    while bit:
        for h in range(len(CUTS)):
            held[h] = held[h] + [xor_permute(p, "col", bit) for p in held[h]]
        masks = masks + [m ^ bit for m in masks]
        bit //= 2

    b_rows = [b_panel]
    bit = 1
    while bit < n_row:
        b_rows = b_rows + [xor_permute(b, "row", bit) for b in b_rows]
        bit *= 2
    b_rows = jnp.concatenate(b_rows)
    b_other = xor_permute(b_rows, "layer", 1)

    pairs = [[q for p in held[h] for q in (p, xor_permute(p, "layer", 1))] for h in range(len(CUTS))]
    ids = jnp.stack([p[capacity * CUTS[0], :capacity] for p in pairs[0]]).astype(jnp.int32)

    per, n_slots = IB // n_layer, n_layer // 2
    terms = []
    for h, rows in enumerate(CUTS):
        slots = pl.pallas_call(
            functools.partial(
                product_kernel, masks, n_layer, n_row, capacity, rows, depth
            ),
            out_shape=[pltpu.VMEM((per, rows, width), jnp.float32)] * n_slots,
            in_specs=[SMEM] + [VMEM] * (2 + len(pairs[h])),
            out_specs=[VMEM] * n_slots,
            scratch_shapes=[
                pltpu.SMEM((len(pairs[h]), IB + 1), jnp.int32),
                pltpu.VMEM((per * rows, len(pairs[h]) * depth), jnp.bfloat16),
            ],
            name="partial_rows",
        )(ids, *(pin(x) for x in (b_rows, b_other, *pairs[h])))
        step = n_slots // 2
        mine = [slots[0]]
        while step:
            got = [xor_permute(s, "layer", 2 * step) for s in slots[step : 2 * step]]
            mine.append(got[0])
            slots = [None] + [s + g for s, g in zip(slots[1:step], got[1:])]
            step //= 2
        terms += mine
    n_terms = len(terms) // len(CUTS)

    expanded = [sum(terms[h * n_terms : (h + 1) * n_terms]) for h in range(len(CUTS))]
    sq = jnp.concatenate([e * e for e in expanded], axis=1)
    col_sum = jnp.sum(sq, axis=(0, 1))[None]

    col_sum = col_sum + xor_permute(col_sum, "layer", 1)
    others = [
        grid_permute(col_sum, i, j)
        for i in range(0, n_layer, 2)
        for j in range(n_row)
        if i or j
    ]
    for other in others:
        col_sum = col_sum + other
    scale = 1.0 / (col_sum * (1.0 / (n_row * IB * block)) + 1e-06)
    return (sq * scale).reshape(1, per * block, width)


def solution(mesh):
    return jax.shard_map(
        body,
        mesh=mesh,
        in_specs=(
            P(("layer", "row", "col"), None, None, None),
            P(("layer", "row", "col"), None),
            P(("layer", "row", "col")),
            P(("layer", "row"), "col"),
        ),
        out_specs=P("row", "layer", "col"),
        check_vma=False,
    )
```

time: 95.1 us -> 49.1 us (0.52)
  blocking collectives: 29.3 us -> 0 us
  waiting for transfers between devices: 40.4 us -> 21.4 us
  starting transfers between devices: 0.04 us -> 18.7 us
  between operations: 14.1 us -> 0.79 us
  other arithmetic: 5.65 us -> 1.49 us
  Pallas kernels: 0 us -> 3.12 us
  matrix products: 1.64 us -> 0 us
    psum x1 -> x0, waiting for transfers between devices: 35.8 us -> none  [body(): expanded = lax.psum(partial_sum, 'layer')]
    ppermute x0 -> x22, waiting for transfers between devices: none -> 21.4 us  [the longest x19 18.6 us: xor_permute(): lax.ppermute(x, axis, [(i, i ^ mask) for i in range(lax.axis_size(axis))])]
    ppermute x0 -> x22, starting transfers between devices: none -> 18.7 us  [the longest x19 15.3 us: xor_permute(): lax.ppermute(x, axis, [(i, i ^ mask) for i in range(lax.axis_size(axis))])]
    all_gather x2 -> x0, blocking collectives: 14.5 us -> none  [the longest x1 9.35 us: body(): row_ids = lax.all_gather(a_rows, 'col', axis=0, tiled=True)]
    unnamed x1 -> x0, blocking collectives: 9.89 us -> none
    psum x1 -> x0, blocking collectives: 4.93 us -> none  [body(): col_sums = lax.psum(jnp.sum(squares, axis=0), 'row')]
    all_gather x1 -> x0, waiting for transfers between devices: 3.93 us -> none  [body(): blocks = lax.all_gather(a_blocks, 'col', axis=0, tiled=True)]
    pallas_call x0 -> x2, Pallas kernels: none -> 3.12 us  [body(): pl.pallas_call(functools.partial(product_kernel, masks, n_layer, n_row, c...]
  transfers between devices with their start and end apart: 2 -> 22, of which waited for: 2 -> 11; matrix products, arithmetic and copies ran while one was open for 4% -> 3% of each run, Pallas kernels for 0% -> 6%
where the time goes in v2:
time: 49.1 us; the launch traced here: 48.8 us
  waiting for transfers between devices  21.4 us (44%)
  starting transfers between devices  18.7 us (38%)
  local copies, waits for them, and re-layouts  3.25 us (7%)
  Pallas kernels  3.12 us (6%)
  other arithmetic  1.49 us (3%)
  between operations  0.79 us (2%)
    ppermute x19, waiting for transfers between devices, xor_permute(): lax.ppermute(x, axis, [(i, i ^ mask) for i in range(lax.axis_size(axis))])  18.6 us
    ppermute x19, starting transfers between devices, xor_permute(): lax.ppermute(x, axis, [(i, i ^ mask) for i in range(lax.axis_size(axis))])  15.3 us
    ppermute x3, starting transfers between devices, grid_permute(): return lax.ppermute(x, ('layer', 'row'), pairs)  3.49 us
    pallas_call x2, Pallas kernels, body(): pl.pallas_call(functools.partial(product_kernel, masks, n_layer, n_row, c...  3.12 us
    ppermute x3, waiting for transfers between devices, grid_permute(): return lax.ppermute(x, ('layer', 'row'), pairs)  2.82 us
    slice x2, local copies, waits for them, and re-layouts, body(): part = a[:, start:start + rows, :].reshape(capacity * rows, depth)  1.79 us
    unnamed x5, local copies, waits for them, and re-layouts  1.41 us
  transfers between devices with their start and end apart: 22, of which 11 were waited for; matrix products, arithmetic and copies ran while one was open for 3% of the time, Pallas kernels for 6%

profile of v2, /device:TPU:0, one launch (start us, length us, event | category | flops | bytes accessed | tf_op | source)
XLA Modules:
  0.0 48.8 jit_solution(12527234139634360174)
XLA Ops:
  0.0 0.9 %slice.45 = bf16[8,96,128]{2,1,0:T(8,128)(2,1)S(1)} slice(bf16[8,128,128]{2,1,0:T(8,128)(2,1)} %bitcast.17), slice={[0:8], [32:128], [0:128]} | slice | bytes 393216 | tf_op jit(solution)/shard_map/slice | solution.py:77
  0.9 4.1 %collective-permute-start.11 = (bf16[768,128]{1,0:T(8,128)(2,1)S(1)}, bf16[768,128]{1,0:T(8,128)(2,1)S(1)}, u32[]{:S(2)}, u32[]{:S(2)}) collective-permute-start(bf16[768,128]{1,0:T(8,128)(2,1)S(1)} %bitcast.12), channel_id=1, source_target_pairs={{0,2},{1,3},{2,0},{3,1},{4,6},{5,7},{6,4},{7,5},{8,10},{9,11},{10,... | collective-permute-start | bytes 589832 | tf_op jit(solution)/shard_map/ppermute | solution.py:22
  5.7 0.0 copy-start.1
  5.7 0.6 %copy-done.1 = s32[1,8]{1,0:T(1,128)S(1)} copy-done((s32[1,8]{1,0:T(1,128)S(1)}, s32[1,8]{1,0:T(1,128)}, u32[]{:S(2)}) %copy-start.1) | copy-done | bytes 56
  6.4 0.8 %slice.37 = bf16[8,32,128]{2,1,0:T(8,128)(2,1)S(1)} slice(bf16[8,128,128]{2,1,0:T(8,128)(2,1)} %bitcast.18), slice={[0:8], [0:32], [0:128]} | slice | bytes 131072 | tf_op jit(solution)/shard_map/slice | solution.py:77
  7.2 0.1 collective-permute-start.1
  7.3 0.7 %copy-done = bf16[256,128]{1,0:T(8,128)(2,1)S(1)} copy-done((bf16[256,128]{1,0:T(8,128)(2,1)S(1)}, bf16[256,128]{1,0:T(8,128)(2,1)}, u32[]{:S(2)}) %copy-start) | copy-done | bytes 65560
  8.0 1.5 %collective-permute-start.7 = (bf16[256,128]{1,0:T(8,128)(2,1)S(1)}, bf16[256,128]{1,0:T(8,128)(2,1)S(1)}, u32[]{:S(2)}, u32[]{:S(2)}) collective-permute-start(bf16[256,128]{1,0:T(8,128)(2,1)S(1)} %copy-done), channel_id=1, source_target_pairs={{0,4},{4,0},{1,5},{5,1},{2,6},{6,2},{3,7},{7,3},{8,12},{12,8},{9,1... | collective-permute-start | bytes 196616 | tf_op jit(solution)/shard_map/ppermute | solution.py:22
  9.6 1.6 %collective-permute-start.3 = (bf16[272,128]{1,0:T(8,128)(2,1)S(1)}, bf16[272,128]{1,0:T(8,128)(2,1)S(1)}, u32[]{:S(2)}, u32[]{:S(2)}) collective-permute-start(bf16[272,128]{1,0:T(8,128)(2,1)S(1)} %fusion.1.refs_2_), channel_id=1, source_target_pairs={{0,1},{1,0},{2,3},{3,2},{4,5},{5,4},{6,7},{7,6},{8,9},{9,8},{10,11... | collective-permute-start | bytes 208904 | tf_op jit(solution)/shard_map/ppermute | solution.py:22
  11.1 0.0 collective-permute-start
  11.1 1.2 %collective-permute-done.7 = bf16[256,128]{1,0:T(8,128)(2,1)S(1)} collective-permute-done((bf16[256,128]{1,0:T(8,128)(2,1)S(1)}, bf16[256,128]{1,0:T(8,128)(2,1)S(1)}, u32[]{:S(2)}, u32[]{:S(2)}) %collective-permute-start.7) | collective-permute-done | bytes 65568 | tf_op jit(solution)/shard_map/ppermute | solution.py:22
  12.3 1.6 %collective-permute-start.13 = (bf16[768,128]{1,0:T(8,128)(2,1)S(1)}, bf16[768,128]{1,0:T(8,128)(2,1)S(1)}, u32[]{:S(2)}, u32[]{:S(2)}) collective-permute-start(bf16[768,128]{1,0:T(8,128)(2,1)S(1)} %bitcast.13), channel_id=1, source_target_pairs={{0,1},{1,0},{2,3},{3,2},{4,5},{5,4},{6,7},{7,6},{8,9},{9,8},{10,11... | collective-permute-start | bytes 589832 | tf_op jit(solution)/shard_map/ppermute | solution.py:22
  13.9 3.3 %collective-permute-done.1.refs_4_ = bf16[272,128]{1,0:T(8,128)(2,1)S(1)} collective-permute-done((bf16[272,128]{1,0:T(8,128)(2,1)S(1)}, bf16[272,128]{1,0:T(8,128)(2,1)S(1)}, u32[]{:S(2)}, u32[]{:S(2)}) %collective-permute-start.1) | collective-permute-done | bytes 69664 | tf_op jit(solution)/shard_map/ppermute | solution.py:22
  17.2 0.7 %collective-permute-start.5 = (bf16[272,128]{1,0:T(8,128)(2,1)S(1)}, bf16[272,128]{1,0:T(8,128)(2,1)S(1)}, u32[]{:S(2)}, u32[]{:S(2)}) collective-permute-start(bf16[272,128]{1,0:T(8,128)(2,1)S(1)} %collective-permute-done.1.refs_4_), channel_id=1, source_target_pairs={{0,1},{1,0},{2,3},{3,2},{4,5},{5,4},{6,7},{7,6},{8,9},{9,8},{10,11... | collective-permute-start | bytes 208904 | tf_op jit(solution)/shard_map/ppermute | solution.py:22
  17.9 0.0 collective-permute-done.11.refs_4_
  17.9 1.3 %collective-permute-start.15 = (bf16[768,128]{1,0:T(8,128)(2,1)S(1)}, bf16[768,128]{1,0:T(8,128)(2,1)S(1)}, u32[]{:S(2)}, u32[]{:S(2)}) collective-permute-start(bf16[768,128]{1,0:T(8,128)(2,1)S(1)} %collective-permute-done.11.refs_4_), channel_id=1, source_target_pairs={{0,1},{1,0},{2,3},{3,2},{4,5},{5,4},{6,7},{7,6},{8,9},{9,8},{10,11... | collective-permute-start | bytes 589832 | tf_op jit(solution)/shard_map/ppermute | solution.py:22
  19.2 0.0 collective-permute-done.3.refs_6_
  19.2 0.1 collective-permute-start.2
  19.3 0.5 %collective-permute-start.4 = (bf16[272,128]{1,0:T(8,128)(2,1)S(1)}, bf16[272,128]{1,0:T(8,128)(2,1)S(1)}, u32[]{:S(2)}, u32[]{:S(2)}) collective-permute-start(bf16[272,128]{1,0:T(8,128)(2,1)S(1)} %collective-permute-done.3.refs_6_), channel_id=1, source_target_pairs={{0,8},{8,0},{16,24},{24,16},{1,9},{9,1},{17,25},{25,17},{2,10},{10... | collective-permute-start | bytes 208904 | tf_op jit(solution)/shard_map/ppermute | solution.py:22
  19.8 3.4 %collective-permute-done.5.refs_8_ = bf16[272,128]{1,0:T(8,128)(2,1)S(1)} collective-permute-done((bf16[272,128]{1,0:T(8,128)(2,1)S(1)}, bf16[272,128]{1,0:T(8,128)(2,1)S(1)}, u32[]{:S(2)}, u32[]{:S(2)}) %collective-permute-start.5) | collective-permute-done | bytes 69664 | tf_op jit(solution)/shard_map/ppermute | solution.py:22
  23.2 0.0 collective-permute-start.6
  23.2 0.0 collective-permute-done.4.refs_7_
  23.2 0.6 %collective-permute-start.10 = (bf16[768,128]{1,0:T(8,128)(2,1)S(1)}, bf16[768,128]{1,0:T(8,128)(2,1)S(1)}, u32[]{:S(2)}, u32[]{:S(2)}) collective-permute-start(bf16[768,128]{1,0:T(8,128)(2,1)S(1)} %bitcast.14), channel_id=1, source_target_pairs={{0,8},{8,0},{16,24},{24,16},{1,9},{9,1},{17,25},{25,17},{2,10},{10... | collective-permute-start | bytes 589832 | tf_op jit(solution)/shard_map/ppermute | solution.py:22
  23.8 0.1 collective-permute-start.12
  23.9 0.0 collective-permute-done.13.refs_6_
  23.9 0.4 collective-permute-start.14
  24.3 2.9 %collective-permute-done.15.refs_8_ = bf16[768,128]{1,0:T(8,128)(2,1)S(1)} collective-permute-done((bf16[768,128]{1,0:T(8,128)(2,1)S(1)}, bf16[768,128]{1,0:T(8,128)(2,1)S(1)}, u32[]{:S(2)}, u32[]{:S(2)}) %collective-permute-start.15) | collective-permute-done | bytes 196640 | tf_op jit(solution)/shard_map/ppermute | solution.py:22
  27.2 0.0 collective-permute-start.16
  27.3 0.0 collective-permute-done.6.refs_9_
  27.3 0.5 %collective-permute-start.8 = (bf16[512,128]{1,0:T(8,128)(2,1)S(1)}, bf16[512,128]{1,0:T(8,128)(2,1)S(1)}, u32[]{:S(2)}, u32[]{:S(2)}) collective-permute-start(bf16[512,128]{1,0:T(8,128)(2,1)S(1)} %constant_dynamic-update-slice_fusion.refs_0_), channel_id=1, source_target_pairs={{0,8},{8,0},{16,24},{24,16},{1,9},{9,1},{17,25},{25,17},{2,10},{10... | collective-permute-start | bytes 393224 | tf_op jit(solution)/shard_map/ppermute | solution.py:22
  27.8 0.6 %convert_element_type.9.ids_ref = s32[8,8]{1,0:T(8,128)} convert(bf16[8,8]{1,0:T(8,128)(2,1)S(1)} %stack.3) | non-fusion elementwise | flops 64 | bytes 384 | tf_op jit(solution)/shard_map/convert_element_type | solution.py:99
  28.4 0.4 collective-permute-done.8.refs_1_
  28.9 1.4 %partial_rows.2 = (f32[4,32,128]{2,1,0:T(8,128)S(1)}, f32[4,32,128]{2,1,0:T(8,128)S(1)}) custom-call(s32[8,8]{1,0:T(8,128)} %convert_element_type.9.ids_ref, bf16[512,128]{1,0:T(8,128)(2,1)S(1)} %constant_dynamic-update-slice_fusion.refs_0_, bf16[512,128]{1,0:T(8,128)(2,1)S(1)} %collective-permute-done.8.refs_1_, bf16[272,128]{1,0:T(8,128)(2,1)S(1)} %fusion.1.refs_2_, ...), custom_call_target="tpu_custom_call" | custom-call | tf_op jit(solution)/shard_map/partial_rows/pallas_call | solution.py:104
  30.3 1.6 %collective-permute-start.9 = (f32[4,32,128]{2,1,0:T(8,128)S(1)}, f32[4,32,128]{2,1,0:T(8,128)S(1)}, u32[]{:S(2)}, u32[]{:S(2)}) collective-permute-start(f32[4,32,128]{2,1,0:T(8,128)S(1)} %get-tuple-element.10), channel_id=1, source_target_pairs={{0,16},{8,24},{16,0},{24,8},{1,17},{9,25},{17,1},{25,9},{2,18},{10... | collective-permute-start | bytes 196616 | tf_op jit(solution)/shard_map/ppermute | solution.py:22
  31.9 1.7 %partial_rows.3 = (f32[4,96,128]{2,1,0:T(8,128)S(1)}, f32[4,96,128]{2,1,0:T(8,128)S(1)}) custom-call(s32[8,8]{1,0:T(8,128)} %convert_element_type.9.ids_ref, bf16[512,128]{1,0:T(8,128)(2,1)S(1)} %constant_dynamic-update-slice_fusion.refs_0_, bf16[512,128]{1,0:T(8,128)(2,1)S(1)} %collective-permute-done.8.refs_1_, bf16[768,128]{1,0:T(8,128)(2,1)S(1)} %bitcast.15, ...), custom_call_target="tpu_custom_call" | custom-call | tf_op jit(solution)/shard_map/partial_rows/pallas_call | solution.py:104
  33.6 0.6 %collective-permute-start.17 = (f32[4,96,128]{2,1,0:T(8,128)S(1)}, f32[4,96,128]{2,1,0:T(8,128)S(1)}, u32[]{:S(2)}, u32[]{:S(2)}) collective-permute-start(f32[4,96,128]{2,1,0:T(8,128)S(1)} %get-tuple-element.12), channel_id=1, source_target_pairs={{0,16},{8,24},{16,0},{24,8},{1,17},{9,25},{17,1},{25,9},{2,18},{10... | collective-permute-start | bytes 589832 | tf_op jit(solution)/shard_map/ppermute | solution.py:22
  34.2 0.4 collective-permute-done.9
  34.7 5.8 %collective-permute-done.17 = f32[4,96,128]{2,1,0:T(8,128)S(1)} collective-permute-done((f32[4,96,128]{2,1,0:T(8,128)S(1)}, f32[4,96,128]{2,1,0:T(8,128)S(1)}, u32[]{:S(2)}, u32[]{:S(2)}) %collective-permute-start.17) | collective-permute-done | bytes 196640 | tf_op jit(solution)/shard_map/ppermute | solution.py:22
  40.5 0.1 fusion.3
  40.6 0.1 collective-permute-start.18
  40.6 1.1 %collective-permute-done.18 = f32[1,128]{1,0:T(1,128)S(1)} collective-permute-done((f32[1,128]{1,0:T(1,128)S(1)}, f32[1,128]{1,0:T(1,128)S(1)}, u32[]{:S(2)}, u32[]{:S(2)}) %collective-permute-start.18) | collective-permute-done | bytes 544 | tf_op jit(solution)/shard_map/ppermute | solution.py:22
  41.7 1.3 %collective-permute-start.21 = (f32[1,128]{1,0:T(1,128)S(1)}, f32[1,128]{1,0:T(1,128)S(1)}, u32[]{:S(2)}, u32[]{:S(2)}) collective-permute-start(f32[1,128]{1,0:T(1,128)S(1)} %add.28), channel_id=1, source_target_pairs={{0,20},{4,16},{8,28},{12,24},{16,4},{20,0},{24,12},{28,8},{1,21},{... | collective-permute-start | bytes 1544 | tf_op jit(solution)/shard_map/ppermute | solution.py:30
  43.0 1.5 %collective-permute-start.20 = (f32[1,128]{1,0:T(1,128)S(1)}, f32[1,128]{1,0:T(1,128)S(1)}, u32[]{:S(2)}, u32[]{:S(2)}) collective-permute-start(f32[1,128]{1,0:T(1,128)S(1)} %add.28), channel_id=1, source_target_pairs={{0,16},{4,20},{8,24},{12,28},{16,0},{20,4},{24,8},{28,12},{1,17},{... | collective-permute-start | bytes 1544 | tf_op jit(solution)/shard_map/ppermute | solution.py:30
  44.5 0.7 %collective-permute-start.19 = (f32[1,128]{1,0:T(1,128)S(1)}, f32[1,128]{1,0:T(1,128)S(1)}, u32[]{:S(2)}, u32[]{:S(2)}) collective-permute-start(f32[1,128]{1,0:T(1,128)S(1)} %add.28), channel_id=1, source_target_pairs={{0,4},{4,0},{8,12},{12,8},{16,20},{20,16},{24,28},{28,24},{1,5},{5... | collective-permute-start | bytes 1544 | tf_op jit(solution)/shard_map/ppermute | solution.py:30
  45.2 0.9 %collective-permute-done.21 = f32[1,128]{1,0:T(1,128)S(1)} collective-permute-done((f32[1,128]{1,0:T(1,128)S(1)}, f32[1,128]{1,0:T(1,128)S(1)}, u32[]{:S(2)}, u32[]{:S(2)}) %collective-permute-start.21) | collective-permute-done | bytes 544 | tf_op jit(solution)/shard_map/ppermute | solution.py:30
  46.2 0.4 collective-permute-done.20
  46.6 1.5 %collective-permute-done.19 = f32[1,128]{1,0:T(1,128)S(1)} collective-permute-done((f32[1,128]{1,0:T(1,128)S(1)}, f32[1,128]{1,0:T(1,128)S(1)}, u32[]{:S(2)}, u32[]{:S(2)}) %collective-permute-start.19) | collective-permute-done | bytes 544 | tf_op jit(solution)/shard_map/ppermute | solution.py:30
  48.1 0.7 %bitcast_multiply_fusion = f32[1,512,128]{2,1,0:T(8,128)} fusion(f32[128]{0:T(128)S(1)} %divide_bitcast_fusion, f32[1,512,128]{2,1,0:T(8,128)S(1)} %bitcast.16), kind=kLoop, calls=%fused_computation.1 | loop fusion | flops 65536 | bytes 524800 | tf_op jit(solution)/shard_map/mul | solution.py:141
  (24 shorter events, 0.2 us)
Async XLA Ops:
  0.9 17.0 %collective-permute-start.11 = (bf16[768,128]{1,0:T(8,128)(2,1)S(1)}, bf16[768,128]{1,0:T(8,128)(2,1)S(1)}, u32[]{:S(2)}, u32[]{:S(2)}) collective-permute-start(bf16[768,128]{1,0:T(8,128)(2,1)S(1)} %bitcast.12), channel_id=1, source_target_pairs={{0,2},{1,3},{2,0},{3,1},{4,6},{5,7},{6,4},{7,5},{8,10},{9,11},{10,... | collective-permute-start | bytes 589832 | tf_op jit(solution)/shard_map/ppermute | solution.py:22
  5.7 0.7 %copy-start.1 = (s32[1,8]{1,0:T(1,128)S(1)}, s32[1,8]{1,0:T(1,128)}, u32[]{:S(2)}) copy-start(s32[1,8]{1,0:T(1,128)} %param.5) | copy-start | bytes 100
  7.2 0.8 %copy-start = (bf16[256,128]{1,0:T(8,128)(2,1)S(1)}, bf16[256,128]{1,0:T(8,128)(2,1)}, u32[]{:S(2)}) copy-start(bf16[256,128]{1,0:T(8,128)(2,1)} %param.7) | copy-start | bytes 196612
  7.2 10.0 %collective-permute-start.1 = (bf16[272,128]{1,0:T(8,128)(2,1)S(1)}, bf16[272,128]{1,0:T(8,128)(2,1)S(1)}, u32[]{:S(2)}, u32[]{:S(2)}) collective-permute-start(bf16[272,128]{1,0:T(8,128)(2,1)S(1)} %fusion.1.refs_2_), channel_id=1, source_target_pairs={{0,2},{1,3},{2,0},{3,1},{4,6},{5,7},{6,4},{7,5},{8,10},{9,11},{10,... | collective-permute-start | bytes 208904 | tf_op jit(solution)/shard_map/ppermute | solution.py:22
  8.0 4.3 %collective-permute-start.7 = (bf16[256,128]{1,0:T(8,128)(2,1)S(1)}, bf16[256,128]{1,0:T(8,128)(2,1)S(1)}, u32[]{:S(2)}, u32[]{:S(2)}) collective-permute-start(bf16[256,128]{1,0:T(8,128)(2,1)S(1)} %copy-done), channel_id=1, source_target_pairs={{0,4},{4,0},{1,5},{5,1},{2,6},{6,2},{3,7},{7,3},{8,12},{12,8},{9,1... | collective-permute-start | bytes 196616 | tf_op jit(solution)/shard_map/ppermute | solution.py:22
  9.6 9.7 %collective-permute-start.3 = (bf16[272,128]{1,0:T(8,128)(2,1)S(1)}, bf16[272,128]{1,0:T(8,128)(2,1)S(1)}, u32[]{:S(2)}, u32[]{:S(2)}) collective-permute-start(bf16[272,128]{1,0:T(8,128)(2,1)S(1)} %fusion.1.refs_2_), channel_id=1, source_target_pairs={{0,1},{1,0},{2,3},{3,2},{4,5},{5,4},{6,7},{7,6},{8,9},{9,8},{10,11... | collective-permute-start | bytes 208904 | tf_op jit(solution)/shard_map/ppermute | solution.py:22
  11.1 8.2 %collective-permute-start = (bf16[272,128]{1,0:T(8,128)(2,1)S(1)}, bf16[272,128]{1,0:T(8,128)(2,1)S(1)}, u32[]{:S(2)}, u32[]{:S(2)}) collective-permute-start(bf16[272,128]{1,0:T(8,128)(2,1)S(1)} %fusion.1.refs_2_), channel_id=1, source_target_pairs={{0,8},{8,0},{16,24},{24,16},{1,9},{9,1},{17,25},{25,17},{2,10},{10... | collective-permute-start | bytes 208904 | tf_op jit(solution)/shard_map/ppermute | solution.py:22
  12.3 11.6 %collective-permute-start.13 = (bf16[768,128]{1,0:T(8,128)(2,1)S(1)}, bf16[768,128]{1,0:T(8,128)(2,1)S(1)}, u32[]{:S(2)}, u32[]{:S(2)}) collective-permute-start(bf16[768,128]{1,0:T(8,128)(2,1)S(1)} %bitcast.13), channel_id=1, source_target_pairs={{0,1},{1,0},{2,3},{3,2},{4,5},{5,4},{6,7},{7,6},{8,9},{9,8},{10,11... | collective-permute-start | bytes 589832 | tf_op jit(solution)/shard_map/ppermute | solution.py:22
  17.2 6.0 %collective-permute-start.5 = (bf16[272,128]{1,0:T(8,128)(2,1)S(1)}, bf16[272,128]{1,0:T(8,128)(2,1)S(1)}, u32[]{:S(2)}, u32[]{:S(2)}) collective-permute-start(bf16[272,128]{1,0:T(8,128)(2,1)S(1)} %collective-permute-done.1.refs_4_), channel_id=1, source_target_pairs={{0,1},{1,0},{2,3},{3,2},{4,5},{5,4},{6,7},{7,6},{8,9},{9,8},{10,11... | collective-permute-start | bytes 208904 | tf_op jit(solution)/shard_map/ppermute | solution.py:22
  17.9 9.3 %collective-permute-start.15 = (bf16[768,128]{1,0:T(8,128)(2,1)S(1)}, bf16[768,128]{1,0:T(8,128)(2,1)S(1)}, u32[]{:S(2)}, u32[]{:S(2)}) collective-permute-start(bf16[768,128]{1,0:T(8,128)(2,1)S(1)} %collective-permute-done.11.refs_4_), channel_id=1, source_target_pairs={{0,1},{1,0},{2,3},{3,2},{4,5},{5,4},{6,7},{7,6},{8,9},{9,8},{10,11... | collective-permute-start | bytes 589832 | tf_op jit(solution)/shard_map/ppermute | solution.py:22
  19.2 4.6 %collective-permute-start.2 = (bf16[272,128]{1,0:T(8,128)(2,1)S(1)}, bf16[272,128]{1,0:T(8,128)(2,1)S(1)}, u32[]{:S(2)}, u32[]{:S(2)}) collective-permute-start(bf16[272,128]{1,0:T(8,128)(2,1)S(1)} %collective-permute-done.1.refs_4_), channel_id=1, source_target_pairs={{0,8},{8,0},{16,24},{24,16},{1,9},{9,1},{17,25},{25,17},{2,10},{10... | collective-permute-start | bytes 208904 | tf_op jit(solution)/shard_map/ppermute | solution.py:22
  19.3 3.9 %collective-permute-start.4 = (bf16[272,128]{1,0:T(8,128)(2,1)S(1)}, bf16[272,128]{1,0:T(8,128)(2,1)S(1)}, u32[]{:S(2)}, u32[]{:S(2)}) collective-permute-start(bf16[272,128]{1,0:T(8,128)(2,1)S(1)} %collective-permute-done.3.refs_6_), channel_id=1, source_target_pairs={{0,8},{8,0},{16,24},{24,16},{1,9},{9,1},{17,25},{25,17},{2,10},{10... | collective-permute-start | bytes 208904 | tf_op jit(solution)/shard_map/ppermute | solution.py:22
  23.2 4.1 %collective-permute-start.6 = (bf16[272,128]{1,0:T(8,128)(2,1)S(1)}, bf16[272,128]{1,0:T(8,128)(2,1)S(1)}, u32[]{:S(2)}, u32[]{:S(2)}) collective-permute-start(bf16[272,128]{1,0:T(8,128)(2,1)S(1)} %collective-permute-done.5.refs_8_), channel_id=1, source_target_pairs={{0,8},{8,0},{16,24},{24,16},{1,9},{9,1},{17,25},{25,17},{2,10},{10... | collective-permute-start | bytes 208904 | tf_op jit(solution)/shard_map/ppermute | solution.py:22
  23.2 8.7 %collective-permute-start.10 = (bf16[768,128]{1,0:T(8,128)(2,1)S(1)}, bf16[768,128]{1,0:T(8,128)(2,1)S(1)}, u32[]{:S(2)}, u32[]{:S(2)}) collective-permute-start(bf16[768,128]{1,0:T(8,128)(2,1)S(1)} %bitcast.14), channel_id=1, source_target_pairs={{0,8},{8,0},{16,24},{24,16},{1,9},{9,1},{17,25},{25,17},{2,10},{10... | collective-permute-start | bytes 589832 | tf_op jit(solution)/shard_map/ppermute | solution.py:22
  23.8 8.1 %collective-permute-start.12 = (bf16[768,128]{1,0:T(8,128)(2,1)S(1)}, bf16[768,128]{1,0:T(8,128)(2,1)S(1)}, u32[]{:S(2)}, u32[]{:S(2)}) collective-permute-start(bf16[768,128]{1,0:T(8,128)(2,1)S(1)} %collective-permute-done.11.refs_4_), channel_id=1, source_target_pairs={{0,8},{8,0},{16,24},{24,16},{1,9},{9,1},{17,25},{25,17},{2,10},{10... | collective-permute-start | bytes 589832 | tf_op jit(solution)/shard_map/ppermute | solution.py:22
  23.9 8.0 %collective-permute-start.14 = (bf16[768,128]{1,0:T(8,128)(2,1)S(1)}, bf16[768,128]{1,0:T(8,128)(2,1)S(1)}, u32[]{:S(2)}, u32[]{:S(2)}) collective-permute-start(bf16[768,128]{1,0:T(8,128)(2,1)S(1)} %collective-permute-done.13.refs_6_), channel_id=1, source_target_pairs={{0,8},{8,0},{16,24},{24,16},{1,9},{9,1},{17,25},{25,17},{2,10},{10... | collective-permute-start | bytes 589832 | tf_op jit(solution)/shard_map/ppermute | solution.py:22
  27.2 4.7 %collective-permute-start.16 = (bf16[768,128]{1,0:T(8,128)(2,1)S(1)}, bf16[768,128]{1,0:T(8,128)(2,1)S(1)}, u32[]{:S(2)}, u32[]{:S(2)}) collective-permute-start(bf16[768,128]{1,0:T(8,128)(2,1)S(1)} %collective-permute-done.15.refs_8_), channel_id=1, source_target_pairs={{0,8},{8,0},{16,24},{24,16},{1,9},{9,1},{17,25},{25,17},{2,10},{10... | collective-permute-start | bytes 589832 | tf_op jit(solution)/shard_map/ppermute | solution.py:22
  27.3 1.6 %collective-permute-start.8 = (bf16[512,128]{1,0:T(8,128)(2,1)S(1)}, bf16[512,128]{1,0:T(8,128)(2,1)S(1)}, u32[]{:S(2)}, u32[]{:S(2)}) collective-permute-start(bf16[512,128]{1,0:T(8,128)(2,1)S(1)} %constant_dynamic-update-slice_fusion.refs_0_), channel_id=1, source_target_pairs={{0,8},{8,0},{16,24},{24,16},{1,9},{9,1},{17,25},{25,17},{2,10},{10... | collective-permute-start | bytes 393224 | tf_op jit(solution)/shard_map/ppermute | solution.py:22
  30.3 4.3 %collective-permute-start.9 = (f32[4,32,128]{2,1,0:T(8,128)S(1)}, f32[4,32,128]{2,1,0:T(8,128)S(1)}, u32[]{:S(2)}, u32[]{:S(2)}) collective-permute-start(f32[4,32,128]{2,1,0:T(8,128)S(1)} %get-tuple-element.10), channel_id=1, source_target_pairs={{0,16},{8,24},{16,0},{24,8},{1,17},{9,25},{17,1},{25,9},{2,18},{10... | collective-permute-start | bytes 196616 | tf_op jit(solution)/shard_map/ppermute | solution.py:22
  33.6 6.8 %collective-permute-start.17 = (f32[4,96,128]{2,1,0:T(8,128)S(1)}, f32[4,96,128]{2,1,0:T(8,128)S(1)}, u32[]{:S(2)}, u32[]{:S(2)}) collective-permute-start(f32[4,96,128]{2,1,0:T(8,128)S(1)} %get-tuple-element.12), channel_id=1, source_target_pairs={{0,16},{8,24},{16,0},{24,8},{1,17},{9,25},{17,1},{25,9},{2,18},{10... | collective-permute-start | bytes 589832 | tf_op jit(solution)/shard_map/ppermute | solution.py:22
  40.6 1.2 %collective-permute-start.18 = (f32[1,128]{1,0:T(1,128)S(1)}, f32[1,128]{1,0:T(1,128)S(1)}, u32[]{:S(2)}, u32[]{:S(2)}) collective-permute-start(f32[1,128]{1,0:T(1,128)S(1)} %add_bitcast_fusion), channel_id=1, source_target_pairs={{0,8},{8,0},{16,24},{24,16},{1,9},{9,1},{17,25},{25,17},{2,10},{10... | collective-permute-start | bytes 1544 | tf_op jit(solution)/shard_map/ppermute | solution.py:22
  41.7 4.4 %collective-permute-start.21 = (f32[1,128]{1,0:T(1,128)S(1)}, f32[1,128]{1,0:T(1,128)S(1)}, u32[]{:S(2)}, u32[]{:S(2)}) collective-permute-start(f32[1,128]{1,0:T(1,128)S(1)} %add.28), channel_id=1, source_target_pairs={{0,20},{4,16},{8,28},{12,24},{16,4},{20,0},{24,12},{28,8},{1,21},{... | collective-permute-start | bytes 1544 | tf_op jit(solution)/shard_map/ppermute | solution.py:30
  43.0 3.5 %collective-permute-start.20 = (f32[1,128]{1,0:T(1,128)S(1)}, f32[1,128]{1,0:T(1,128)S(1)}, u32[]{:S(2)}, u32[]{:S(2)}) collective-permute-start(f32[1,128]{1,0:T(1,128)S(1)} %add.28), channel_id=1, source_target_pairs={{0,16},{4,20},{8,24},{12,28},{16,0},{20,4},{24,8},{28,12},{1,17},{... | collective-permute-start | bytes 1544 | tf_op jit(solution)/shard_map/ppermute | solution.py:30
  44.5 3.5 %collective-permute-start.19 = (f32[1,128]{1,0:T(1,128)S(1)}, f32[1,128]{1,0:T(1,128)S(1)}, u32[]{:S(2)}, u32[]{:S(2)}) collective-permute-start(f32[1,128]{1,0:T(1,128)S(1)} %add.28), channel_id=1, source_target_pairs={{0,4},{4,0},{8,12},{12,8},{16,20},{20,16},{24,28},{28,24},{1,5},{5... | collective-permute-start | bytes 1544 | tf_op jit(solution)/shard_map/ppermute | solution.py:30

commit v3 on v0

v3 whole, which is shorter than its diff:
```python
import functools

import jax
import jax.numpy as jnp
from jax import lax
from jax.experimental import pallas as pl
from jax.experimental.pallas import tpu as pltpu
from jax.sharding import PartitionSpec as P

IB = 16
VMEM = pl.BlockSpec(memory_space=pltpu.VMEM)
SMEM = pl.BlockSpec(memory_space=pltpu.SMEM)


def pin(x):
    return pltpu.with_memory_space_constraint(x, pltpu.VMEM)


def xor_permute(x, axis, mask):
    return lax.ppermute(x, axis, [(i, i ^ mask) for i in range(lax.axis_size(axis))])


def grid_permute(x, layer_mask, row_mask, col_mask):
    n, m, c = (lax.axis_size(a) for a in ("layer", "row", "col"))
    pairs = [
        ((i * m + j) * c + k, ((i ^ layer_mask) * m + (j ^ row_mask)) * c + (k ^ col_mask))
        for i in range(n)
        for j in range(m)
        for k in range(c)
    ]
    return lax.ppermute(x, ("layer", "row", "col"), pairs)


def product_kernel(masks, n_layer, n_row, n_col, ids_ref, *refs):
    n_slots, n_held = n_layer // 2, 2 * len(masks)
    b_refs, a_refs = refs[:4], refs[4 : 4 + n_held]
    out_refs = refs[4 + n_held : -2]
    where_ref, lhs_ref = refs[-2:]
    layer, row, col = (lax.axis_index(n) for n in ("layer", "row", "col"))
    per, per_row = IB // n_layer, n_col // n_row // 2
    capacity, block, depth = a_refs[0].shape
    rhs = []
    for k in range(n_held):
        other, place = k % 2, k // 2
        for i in range(IB + 1):
            where_ref[k, i] = -1
        for n in range(capacity):
            where_ref[k, ids_ref[k, n]] = n
        pair = (col ^ masks[place]) // 2
        start = (((pair // per_row) ^ row) * per_row + pair % per_row) * depth
        at = pl.ds(pl.multiple_of(start, depth), depth)
        rhs.append(jnp.concatenate([b_refs[2 * m + other][at, :] for m in range(2)], axis=1))
    rhs = jnp.concatenate(rhs, axis=0)
    width = rhs.shape[1] // 2
    for slot in range(n_slots):
        for sub in range(per):
            block_row = (layer ^ (2 * slot)) * per + sub
            for k in range(n_held):
                n = where_ref[k, block_row]
                a = a_refs[k][jnp.maximum(n, 0)]
                lhs_ref[slot, sub * block : (sub + 1) * block, k * depth : (k + 1) * depth] = (
                    jnp.where(n >= 0, a, jnp.zeros_like(a))
                )
        out = jnp.dot(lhs_ref[slot], rhs, preferred_element_type=jnp.float32)
        for m in range(2):
            out_refs[2 * slot + m][...] = out[:, m * width : (m + 1) * width]


def products(masks, ids, b_refs, panels):
    n_layer, n_row, n_col = (lax.axis_size(a) for a in ("layer", "row", "col"))
    _, block, depth = panels[0].shape
    rows, n_slots, width = IB // n_layer * block, n_layer // 2, b_refs[0].shape[1]
    ins = [*b_refs, *panels]
    return pl.pallas_call(
        functools.partial(product_kernel, masks, n_layer, n_row, n_col),
        out_shape=[pltpu.VMEM((rows, width), jnp.float32)] * (2 * n_slots),
        in_specs=[SMEM] + [VMEM] * len(ins),
        out_specs=[VMEM] * (2 * n_slots),
        scratch_shapes=[
            pltpu.SMEM((len(panels), IB + 1), jnp.int32),
            pltpu.VMEM((n_slots, rows, len(panels) * depth), jnp.bfloat16),
        ],
        name="partial_rows",
    )(ids, *(pin(x) for x in ins))


def body(a_blocks, a_rows, a_count, b_panel):
    n_layer, n_row, n_col = (lax.axis_size(a) for a in ("layer", "row", "col"))
    _, capacity, block, _ = a_blocks.shape

    def other(x):
        return xor_permute(x, "layer", 1)

    masks, panels = [0], [a_blocks[0]]
    valid = jnp.arange(capacity, dtype=jnp.int32)[None, :] < a_count[:, None]
    ids = jnp.where(valid, a_rows, IB)
    ids = jnp.concatenate([ids, other(ids)])
    bit = n_col // 2
    while bit > 1:
        panels = panels + [xor_permute(p, "col", bit) for p in panels]
        ids = jnp.concatenate([ids, xor_permute(ids, "col", bit)])
        masks = masks + [m ^ bit for m in masks]
        bit //= 2

    b_rows = [b_panel]
    bit = 1
    while bit < n_row:
        b_rows = b_rows + [xor_permute(b, "row", bit) for b in b_rows]
        bit *= 2
    b_rows = jnp.concatenate(b_rows).reshape(-1, 2, *b_panel.shape[-1:] * 2)
    parity = lax.axis_index("col") % 2
    b_mine, b_near = (
        lax.dynamic_index_in_dim(b_rows, p, 1, False).reshape(-1, b_panel.shape[1])
        for p in (parity, 1 - parity)
    )
    b_refs = [b_mine, other(b_mine), xor_permute(b_near, "col", 1)]

    far, ids, b_refs = lax.optimization_barrier((panels[1:], ids, b_refs))
    panels[1:] = far
    b_refs.append(other(b_refs[2]))
    panels = [x for p in panels for x in (p, other(p))]
    parts = products(masks, ids, b_refs, panels)

    expanded = parts[0]
    for k in range(1, n_layer):
        expanded = expanded + grid_permute(parts[k], 2 * (k // 2), 0, k % 2)
    sq = expanded * expanded
    col_sum = jnp.sum(sq, axis=0)[None]

    col_sum = col_sum + xor_permute(col_sum, "layer", 1)
    others = [
        grid_permute(col_sum, i, j, 0)
        for i in range(0, n_layer, 2)
        for j in range(n_row)
        if i or j
    ]
    for other in others:
        col_sum = col_sum + other
    scale = 1.0 / (col_sum * (1.0 / (n_row * IB * block)) + 1e-06)
    return (sq * scale)[None]


def solution(mesh):
    return jax.shard_map(
        body,
        mesh=mesh,
        in_specs=(
            P(("layer", "row", "col"), None, None, None),
            P(("layer", "row", "col"), None),
            P(("layer", "row", "col")),
            P(("layer", "row"), "col"),
        ),
        out_specs=P("row", "layer", "col"),
        check_vma=False,
    )
```

time: 95.1 us -> 45 us (0.47)
  blocking collectives: 29.3 us -> 0 us
  waiting for transfers between devices: 40.4 us -> 24.4 us
  starting transfers between devices: 0.04 us -> 15.4 us
  between operations: 14.1 us -> 0.71 us
  other arithmetic: 5.65 us -> 2.31 us
  local copies, waits for them, and re-layouts: 3.72 us -> 0.67 us
  matrix products: 1.64 us -> 0 us
  Pallas kernels: 0 us -> 1.3 us
    psum x1 -> x0, waiting for transfers between devices: 35.8 us -> none  [body(): expanded = lax.psum(partial_sum, 'layer')]
    ppermute x0 -> x16, waiting for transfers between devices: none -> 24.4 us  [the longest x6 14.5 us: grid_permute(): return lax.ppermute(x, ('layer', 'row', 'col'), pairs)]
    ppermute x0 -> x16, starting transfers between devices: none -> 15.4 us  [the longest x10 8.4 us: xor_permute(): lax.ppermute(x, axis, [(i, i ^ mask) for i in range(lax.axis_size(axis))])]
    all_gather x2 -> x0, blocking collectives: 14.5 us -> none  [the longest x1 9.35 us: body(): row_ids = lax.all_gather(a_rows, 'col', axis=0, tiled=True)]
    unnamed x1 -> x0, blocking collectives: 9.89 us -> none
    psum x1 -> x0, blocking collectives: 4.93 us -> none  [body(): col_sums = lax.psum(jnp.sum(squares, axis=0), 'row')]
    all_gather x1 -> x0, waiting for transfers between devices: 3.93 us -> none  [body(): blocks = lax.all_gather(a_blocks, 'col', axis=0, tiled=True)]
    scatter-add x1 -> x0, other arithmetic: 2.67 us -> none  [body(): empty.at[row_ids.reshape(-1)].add(products.reshape(-1, block_size, width))]
  transfers between devices with their start and end apart: 2 -> 16, of which waited for: 2 -> 10; matrix products, arithmetic and copies ran while one was open for 4% -> 3% of each run, Pallas kernels for 0% -> 0%
where the time goes in v3:
time: 45 us; the launch traced here: 44.8 us
  waiting for transfers between devices  24.4 us (54%)
  starting transfers between devices  15.4 us (34%)
  other arithmetic  2.31 us (5%)
  Pallas kernels  1.3 us (3%)
  between operations  0.71 us (2%)
  local copies, waits for them, and re-layouts  0.67 us (1%)
    ppermute x6, waiting for transfers between devices, grid_permute(): return lax.ppermute(x, ('layer', 'row', 'col'), pairs)  14.5 us
    ppermute x10, waiting for transfers between devices, xor_permute(): lax.ppermute(x, axis, [(i, i ^ mask) for i in range(lax.axis_size(axis))])  9.89 us
    ppermute x10, starting transfers between devices, xor_permute(): lax.ppermute(x, axis, [(i, i ^ mask) for i in range(lax.axis_size(axis))])  8.4 us
    ppermute x6, starting transfers between devices, grid_permute(): return lax.ppermute(x, ('layer', 'row', 'col'), pairs)  7.04 us
    pallas_call x1, Pallas kernels, products(): pl.pallas_call(functools.partial(product_kernel, masks, n_layer, n_row, n...  1.3 us
  transfers between devices with their start and end apart: 16, of which 10 were waited for; matrix products, arithmetic and copies ran while one was open for 3% of the time, Pallas kernels for 0%

profile of v3, /device:TPU:0, one launch (start us, length us, event | category | flops | bytes accessed | tf_op | source)
XLA Modules:
  0.0 44.8 jit_solution(11499712252555220550)
XLA Ops:
  0.0 0.5 %collective-permute-start.7 = (bf16[8,128,128]{2,1,0:T(8,128)(2,1)}, bf16[8,128,128]{2,1,0:T(8,128)(2,1)S(1)}, u32[]{:S(2)}, u32[]{:S(2)}) collective-permute-start(bf16[8,128,128]{2,1,0:T(8,128)(2,1)} %bitcast.16), channel_id=1, source_target_pairs={{0,8},{8,0},{16,24},{24,16},{1,9},{9,1},{17,25},{25,17},{2,10},{10... | collective-permute-start | bytes 786440 | tf_op jit(solution)/shard_map/ppermute | solution.py:20
  0.5 3.6 %collective-permute-start = (bf16[8,128,128]{2,1,0:T(8,128)(2,1)}, bf16[8,128,128]{2,1,0:T(8,128)(2,1)S(1)}, u32[]{:S(2)}, u32[]{:S(2)}) collective-permute-start(bf16[8,128,128]{2,1,0:T(8,128)(2,1)} %bitcast.17), channel_id=1, source_target_pairs={{0,2},{1,3},{2,0},{3,1},{4,6},{5,7},{6,4},{7,5},{8,10},{9,11},{10,... | collective-permute-start | bytes 786440 | tf_op jit(solution)/shard_map/ppermute | solution.py:20
  4.7 0.0 copy-start.1
  4.7 0.6 %copy-done.1 = s32[1,8]{1,0:T(1,128)S(1)} copy-done((s32[1,8]{1,0:T(1,128)S(1)}, s32[1,8]{1,0:T(1,128)}, u32[]{:S(2)}) %copy-start.1) | copy-done | bytes 56
  5.4 0.2 collective-permute-start.1
  5.6 1.5 %collective-permute-start.3 = (bf16[256,128]{1,0:T(8,128)(2,1)}, bf16[256,128]{1,0:T(8,128)(2,1)S(1)}, u32[]{:S(2)}, u32[]{:S(2)}) collective-permute-start(bf16[256,128]{1,0:T(8,128)(2,1)} %param.7), channel_id=1, source_target_pairs={{0,4},{4,0},{1,5},{5,1},{2,6},{6,2},{3,7},{7,3},{8,12},{12,8},{9,1... | collective-permute-start | bytes 196616 | tf_op jit(solution)/shard_map/ppermute | solution.py:20
  7.1 0.0 collective-permute-done.1
  7.1 0.0 copy-start
  7.1 0.4 collective-permute-start.2
  7.5 2.5 %collective-permute-done.3 = bf16[256,128]{1,0:T(8,128)(2,1)S(1)} collective-permute-done((bf16[256,128]{1,0:T(8,128)(2,1)}, bf16[256,128]{1,0:T(8,128)(2,1)S(1)}, u32[]{:S(2)}, u32[]{:S(2)}) %collective-permute-start.3) | collective-permute-done | bytes 65568 | tf_op jit(solution)/shard_map/ppermute | solution.py:20
  10.1 0.8 %pad_maximum_fusion = bf16[512,128]{1,0:T(8,128)(2,1)S(1)} fusion(bf16[256,128]{1,0:T(8,128)(2,1)S(1)} %collective-permute-done.3, bf16[256,128]{1,0:T(8,128)(2,1)} %param.7), kind=kLoop, calls=%fused_computation.2 | loop fusion | flops 262144 | bytes 262144 | tf_op jit(solution)/shard_map/concatenate | solution.py:110
  11.0 1.6 %collective-permute-start.5 = (bf16[256,128]{1,0:T(8,128)(2,1)S(1)}, bf16[256,128]{1,0:T(8,128)(2,1)S(1)}, u32[]{:S(2)}, u32[]{:S(2)}) collective-permute-start(bf16[256,128]{1,0:T(8,128)(2,1)S(1)} %bitcast.22), channel_id=1, source_target_pairs={{0,1},{1,0},{2,3},{3,2},{4,5},{5,4},{6,7},{7,6},{8,9},{9,8},{10,11... | collective-permute-start | bytes 196616 | tf_op jit(solution)/shard_map/ppermute | solution.py:20
  12.6 0.0 collective-permute-start.4
  12.6 4.4 %collective-permute-done.2 = s32[2,8]{1,0:T(2,128)S(1)} collective-permute-done((s32[2,8]{1,0:T(2,128)S(1)}, s32[2,8]{1,0:T(2,128)S(1)}, u32[]{:S(2)}, u32[]{:S(2)}) %collective-permute-start.2) | collective-permute-done | bytes 96 | tf_op jit(solution)/shard_map/ppermute | solution.py:20
  17.0 0.6 %pad_add_fusion.ids_ref = s32[4,8]{1,0:T(4,128)} fusion(s32[2,8]{1,0:T(2,128)S(1)} %collective-permute-done.2, s32[1,8]{1,0:T(1,128)S(1)} %collective-permute-done.1, s32[1,8]{1,0:T(1,128)S(1)} %compare_select_fusion), kind=kLoop, calls=%fused_computation.3 | loop fusion | flops 64 | bytes 256 | tf_op jit(solution)/shard_map/concatenate | solution.py:101
  17.6 0.7 %collective-permute-done.5.refs_2_ = bf16[256,128]{1,0:T(8,128)(2,1)S(1)} collective-permute-done((bf16[256,128]{1,0:T(8,128)(2,1)S(1)}, bf16[256,128]{1,0:T(8,128)(2,1)S(1)}, u32[]{:S(2)}, u32[]{:S(2)}) %collective-permute-start.5) | collective-permute-done | bytes 65568 | tf_op jit(solution)/shard_map/ppermute | solution.py:20
  18.3 0.0 collective-permute-done.4.refs_1_
  18.3 0.0 collective-permute-done.refs_6_
  18.3 0.0 collective-permute-start.8
  18.3 0.5 %collective-permute-start.6 = (bf16[256,128]{1,0:T(8,128)(2,1)S(1)}, bf16[256,128]{1,0:T(8,128)(2,1)S(1)}, u32[]{:S(2)}, u32[]{:S(2)}) collective-permute-start(bf16[256,128]{1,0:T(8,128)(2,1)S(1)} %collective-permute-done.5.refs_2_), channel_id=1, source_target_pairs={{0,8},{8,0},{16,24},{24,16},{1,9},{9,1},{17,25},{25,17},{2,10},{10... | collective-permute-start | bytes 196616 | tf_op jit(solution)/shard_map/ppermute | solution.py:20
  18.8 0.0 collective-permute-done.7.refs_5_
  18.8 1.1 %collective-permute-done.6.refs_3_ = bf16[256,128]{1,0:T(8,128)(2,1)S(1)} collective-permute-done((bf16[256,128]{1,0:T(8,128)(2,1)S(1)}, bf16[256,128]{1,0:T(8,128)(2,1)S(1)}, u32[]{:S(2)}, u32[]{:S(2)}) %collective-permute-start.6) | collective-permute-done | bytes 65568 | tf_op jit(solution)/shard_map/ppermute | solution.py:20
  19.9 0.0 collective-permute-done.8.refs_7_
  19.9 0.0 copy-done
  19.9 1.3 %partial_rows.1 = (f32[512,128]{1,0:T(8,128)S(1)}, f32[512,128]{1,0:T(8,128)S(1)}, f32[512,128]{1,0:T(8,128)S(1)}, f32[512,128]{1,0:T(8,128)S(1)}) custom-call(s32[4,8]{1,0:T(4,128)} %pad_add_fusion.ids_ref, bf16[256,128]{1,0:T(8,128)(2,1)S(1)} %bitcast.20, bf16[256,128]{1,0:T(8,128)(2,1)S(1)} %collective-permute-done.4.refs_1_, ...), custom_call_target="tpu_custom_call" | custom-call | tf_op jit(solution)/shard_map/partial_rows/pallas_call | solution.py:74
  21.2 0.2 collective-permute-start.9
  21.4 1.5 %collective-permute-start.10 = (f32[512,128]{1,0:T(8,128)S(1)}, f32[512,128]{1,0:T(8,128)S(1)}, u32[]{:S(2)}, u32[]{:S(2)}) collective-permute-start(f32[512,128]{1,0:T(8,128)S(1)} %get-tuple-element.21), channel_id=1, source_target_pairs={{0,16},{1,17},{2,18},{3,19},{4,20},{5,21},{6,22},{7,23},{8,24},{9,... | collective-permute-start | bytes 786440 | tf_op jit(solution)/shard_map/ppermute | solution.py:31
  22.9 1.9 %collective-permute-start.11 = (f32[512,128]{1,0:T(8,128)S(1)}, f32[512,128]{1,0:T(8,128)S(1)}, u32[]{:S(2)}, u32[]{:S(2)}) collective-permute-start(f32[512,128]{1,0:T(8,128)S(1)} %get-tuple-element.22), channel_id=1, source_target_pairs={{0,17},{1,16},{2,19},{3,18},{4,21},{5,20},{6,23},{7,22},{8,25},{9,... | collective-permute-start | bytes 786440 | tf_op jit(solution)/shard_map/ppermute | solution.py:31
  24.8 5.7 %collective-permute-done.9 = f32[512,128]{1,0:T(8,128)S(1)} collective-permute-done((f32[512,128]{1,0:T(8,128)S(1)}, f32[512,128]{1,0:T(8,128)S(1)}, u32[]{:S(2)}, u32[]{:S(2)}) %collective-permute-start.9) | collective-permute-done | bytes 262176 | tf_op jit(solution)/shard_map/ppermute | solution.py:31
  30.5 0.0 collective-permute-done.10
  30.5 5.8 %collective-permute-done.11 = f32[512,128]{1,0:T(8,128)S(1)} collective-permute-done((f32[512,128]{1,0:T(8,128)S(1)}, f32[512,128]{1,0:T(8,128)S(1)}, u32[]{:S(2)}, u32[]{:S(2)}) %collective-permute-start.11) | collective-permute-done | bytes 262176 | tf_op jit(solution)/shard_map/ppermute | solution.py:31
  36.3 0.1 fusion
  36.4 0.1 collective-permute-start.12
  36.4 1.1 %collective-permute-done.12 = f32[1,128]{1,0:T(1,128)S(1)} collective-permute-done((f32[1,128]{1,0:T(1,128)S(1)}, f32[1,128]{1,0:T(1,128)S(1)}, u32[]{:S(2)}, u32[]{:S(2)}) %collective-permute-start.12) | collective-permute-done | bytes 544 | tf_op jit(solution)/shard_map/ppermute | solution.py:20
  37.6 1.6 %collective-permute-start.15 = (f32[1,128]{1,0:T(1,128)S(1)}, f32[1,128]{1,0:T(1,128)S(1)}, u32[]{:S(2)}, u32[]{:S(2)}) collective-permute-start(f32[1,128]{1,0:T(1,128)S(1)} %bitcast_add_fusion), channel_id=1, source_target_pairs={{0,20},{1,21},{2,22},{3,23},{4,16},{5,17},{6,18},{7,19},{8,28},{9,... | collective-permute-start | bytes 1544 | tf_op jit(solution)/shard_map/ppermute | solution.py:31
  39.1 1.4 %collective-permute-start.14 = (f32[1,128]{1,0:T(1,128)S(1)}, f32[1,128]{1,0:T(1,128)S(1)}, u32[]{:S(2)}, u32[]{:S(2)}) collective-permute-start(f32[1,128]{1,0:T(1,128)S(1)} %bitcast_add_fusion), channel_id=1, source_target_pairs={{0,16},{1,17},{2,18},{3,19},{4,20},{5,21},{6,22},{7,23},{8,24},{9,... | collective-permute-start | bytes 1544 | tf_op jit(solution)/shard_map/ppermute | solution.py:31
  40.5 0.5 %collective-permute-start.13 = (f32[1,128]{1,0:T(1,128)S(1)}, f32[1,128]{1,0:T(1,128)S(1)}, u32[]{:S(2)}, u32[]{:S(2)}) collective-permute-start(f32[1,128]{1,0:T(1,128)S(1)} %bitcast_add_fusion), channel_id=1, source_target_pairs={{0,4},{1,5},{2,6},{3,7},{4,0},{5,1},{6,2},{7,3},{8,12},{9,13},{10,... | collective-permute-start | bytes 1544 | tf_op jit(solution)/shard_map/ppermute | solution.py:31
  41.0 0.9 %collective-permute-done.15 = f32[1,128]{1,0:T(1,128)S(1)} collective-permute-done((f32[1,128]{1,0:T(1,128)S(1)}, f32[1,128]{1,0:T(1,128)S(1)}, u32[]{:S(2)}, u32[]{:S(2)}) %collective-permute-start.15) | collective-permute-done | bytes 544 | tf_op jit(solution)/shard_map/ppermute | solution.py:31
  42.0 0.7 %collective-permute-done.14 = f32[1,128]{1,0:T(1,128)S(1)} collective-permute-done((f32[1,128]{1,0:T(1,128)S(1)}, f32[1,128]{1,0:T(1,128)S(1)}, u32[]{:S(2)}, u32[]{:S(2)}) %collective-permute-start.14) | collective-permute-done | bytes 544 | tf_op jit(solution)/shard_map/ppermute | solution.py:31
  42.7 1.4 %collective-permute-done.13 = f32[1,128]{1,0:T(1,128)S(1)} collective-permute-done((f32[1,128]{1,0:T(1,128)S(1)}, f32[1,128]{1,0:T(1,128)S(1)}, u32[]{:S(2)}, u32[]{:S(2)}) %collective-permute-start.13) | collective-permute-done | bytes 544 | tf_op jit(solution)/shard_map/ppermute | solution.py:31
  44.1 0.7 %multiply_bitcast_fusion = f32[1,512,128]{2,1,0:T(8,128)} fusion(f32[512,128]{1,0:T(8,128)S(1)} %get-tuple-element.24, f32[128]{0:T(128)S(1)} %divide_bitcast_fusion), kind=kLoop, calls=%fused_computation | loop fusion | flops 65536 | bytes 524800 | tf_op jit(solution)/shard_map/broadcast_in_dim | solution.py:140
  (5 shorter events, 0.0 us)
Async XLA Ops:
  0.0 18.8 %collective-permute-start.7 = (bf16[8,128,128]{2,1,0:T(8,128)(2,1)}, bf16[8,128,128]{2,1,0:T(8,128)(2,1)S(1)}, u32[]{:S(2)}, u32[]{:S(2)}) collective-permute-start(bf16[8,128,128]{2,1,0:T(8,128)(2,1)} %bitcast.16), channel_id=1, source_target_pairs={{0,8},{8,0},{16,24},{24,16},{1,9},{9,1},{17,25},{25,17},{2,10},{10... | collective-permute-start | bytes 786440 | tf_op jit(solution)/shard_map/ppermute | solution.py:20
  0.5 17.8 %collective-permute-start = (bf16[8,128,128]{2,1,0:T(8,128)(2,1)}, bf16[8,128,128]{2,1,0:T(8,128)(2,1)S(1)}, u32[]{:S(2)}, u32[]{:S(2)}) collective-permute-start(bf16[8,128,128]{2,1,0:T(8,128)(2,1)} %bitcast.17), channel_id=1, source_target_pairs={{0,2},{1,3},{2,0},{3,1},{4,6},{5,7},{6,4},{7,5},{8,10},{9,11},{10,... | collective-permute-start | bytes 786440 | tf_op jit(solution)/shard_map/ppermute | solution.py:20
  4.7 0.7 %copy-start.1 = (s32[1,8]{1,0:T(1,128)S(1)}, s32[1,8]{1,0:T(1,128)}, u32[]{:S(2)}) copy-start(s32[1,8]{1,0:T(1,128)} %param.5) | copy-start | bytes 100
  5.4 1.8 %collective-permute-start.1 = (s32[1,8]{1,0:T(1,128)S(1)}, s32[1,8]{1,0:T(1,128)S(1)}, u32[]{:S(2)}, u32[]{:S(2)}) collective-permute-start(s32[1,8]{1,0:T(1,128)S(1)} %compare_select_fusion), channel_id=1, source_target_pairs={{0,8},{8,0},{16,24},{24,16},{1,9},{9,1},{17,25},{25,17},{2,10},{10... | collective-permute-start | bytes 104 | tf_op jit(solution)/shard_map/ppermute | solution.py:20
  5.6 4.5 %collective-permute-start.3 = (bf16[256,128]{1,0:T(8,128)(2,1)}, bf16[256,128]{1,0:T(8,128)(2,1)S(1)}, u32[]{:S(2)}, u32[]{:S(2)}) collective-permute-start(bf16[256,128]{1,0:T(8,128)(2,1)} %param.7), channel_id=1, source_target_pairs={{0,4},{4,0},{1,5},{5,1},{2,6},{6,2},{3,7},{7,3},{8,12},{12,8},{9,1... | collective-permute-start | bytes 196616 | tf_op jit(solution)/shard_map/ppermute | solution.py:20
  7.1 12.8 %copy-start = (bf16[1,8,128,128]{3,2,1,0:T(8,128)(2,1)S(1)}, bf16[1,8,128,128]{3,2,1,0:T(8,128)(2,1)}, u32[]{:S(2)}) copy-start(bf16[1,8,128,128]{3,2,1,0:T(8,128)(2,1)} %param.4) | copy-start | bytes 786436
  7.1 9.9 %collective-permute-start.2 = (s32[2,8]{1,0:T(2,128)S(1)}, s32[2,8]{1,0:T(2,128)S(1)}, u32[]{:S(2)}, u32[]{:S(2)}) collective-permute-start(s32[2,8]{1,0:T(2,128)S(1)} %pad_add_fusion.1), channel_id=1, source_target_pairs={{0,2},{1,3},{2,0},{3,1},{4,6},{5,7},{6,4},{7,5},{8,10},{9,11},{10,... | collective-permute-start | bytes 200 | tf_op jit(solution)/shard_map/ppermute | solution.py:20
  11.0 7.3 %collective-permute-start.5 = (bf16[256,128]{1,0:T(8,128)(2,1)S(1)}, bf16[256,128]{1,0:T(8,128)(2,1)S(1)}, u32[]{:S(2)}, u32[]{:S(2)}) collective-permute-start(bf16[256,128]{1,0:T(8,128)(2,1)S(1)} %bitcast.22), channel_id=1, source_target_pairs={{0,1},{1,0},{2,3},{3,2},{4,5},{5,4},{6,7},{7,6},{8,9},{9,8},{10,11... | collective-permute-start | bytes 196616 | tf_op jit(solution)/shard_map/ppermute | solution.py:20
  12.6 5.7 %collective-permute-start.4 = (bf16[256,128]{1,0:T(8,128)(2,1)S(1)}, bf16[256,128]{1,0:T(8,128)(2,1)S(1)}, u32[]{:S(2)}, u32[]{:S(2)}) collective-permute-start(bf16[256,128]{1,0:T(8,128)(2,1)S(1)} %bitcast.19), channel_id=1, source_target_pairs={{0,8},{8,0},{16,24},{24,16},{1,9},{9,1},{17,25},{25,17},{2,10},{10... | collective-permute-start | bytes 196616 | tf_op jit(solution)/shard_map/ppermute | solution.py:20
  18.3 1.6 %collective-permute-start.8 = (bf16[8,128,128]{2,1,0:T(8,128)(2,1)S(1)}, bf16[8,128,128]{2,1,0:T(8,128)(2,1)S(1)}, u32[]{:S(2)}, u32[]{:S(2)}) collective-permute-start(bf16[8,128,128]{2,1,0:T(8,128)(2,1)S(1)} %collective-permute-done.refs_6_), channel_id=1, source_target_pairs={{0,8},{8,0},{16,24},{24,16},{1,9},{9,1},{17,25},{25,17},{2,10},{10... | collective-permute-start | bytes 786440 | tf_op jit(solution)/shard_map/ppermute | solution.py:20
  18.3 1.6 %collective-permute-start.6 = (bf16[256,128]{1,0:T(8,128)(2,1)S(1)}, bf16[256,128]{1,0:T(8,128)(2,1)S(1)}, u32[]{:S(2)}, u32[]{:S(2)}) collective-permute-start(bf16[256,128]{1,0:T(8,128)(2,1)S(1)} %collective-permute-done.5.refs_2_), channel_id=1, source_target_pairs={{0,8},{8,0},{16,24},{24,16},{1,9},{9,1},{17,25},{25,17},{2,10},{10... | collective-permute-start | bytes 196616 | tf_op jit(solution)/shard_map/ppermute | solution.py:20
  21.2 9.2 %collective-permute-start.9 = (f32[512,128]{1,0:T(8,128)S(1)}, f32[512,128]{1,0:T(8,128)S(1)}, u32[]{:S(2)}, u32[]{:S(2)}) collective-permute-start(f32[512,128]{1,0:T(8,128)S(1)} %get-tuple-element.20), channel_id=1, source_target_pairs={{0,1},{1,0},{2,3},{3,2},{4,5},{5,4},{6,7},{7,6},{8,9},{9,8},{10,11... | collective-permute-start | bytes 786440 | tf_op jit(solution)/shard_map/ppermute | solution.py:31
  21.4 9.0 %collective-permute-start.10 = (f32[512,128]{1,0:T(8,128)S(1)}, f32[512,128]{1,0:T(8,128)S(1)}, u32[]{:S(2)}, u32[]{:S(2)}) collective-permute-start(f32[512,128]{1,0:T(8,128)S(1)} %get-tuple-element.21), channel_id=1, source_target_pairs={{0,16},{1,17},{2,18},{3,19},{4,20},{5,21},{6,22},{7,23},{8,24},{9,... | collective-permute-start | bytes 786440 | tf_op jit(solution)/shard_map/ppermute | solution.py:31
  22.9 13.3 %collective-permute-start.11 = (f32[512,128]{1,0:T(8,128)S(1)}, f32[512,128]{1,0:T(8,128)S(1)}, u32[]{:S(2)}, u32[]{:S(2)}) collective-permute-start(f32[512,128]{1,0:T(8,128)S(1)} %get-tuple-element.22), channel_id=1, source_target_pairs={{0,17},{1,16},{2,19},{3,18},{4,21},{5,20},{6,23},{7,22},{8,25},{9,... | collective-permute-start | bytes 786440 | tf_op jit(solution)/shard_map/ppermute | solution.py:31
  36.4 1.2 %collective-permute-start.12 = (f32[1,128]{1,0:T(1,128)S(1)}, f32[1,128]{1,0:T(1,128)S(1)}, u32[]{:S(2)}, u32[]{:S(2)}) collective-permute-start(f32[1,128]{1,0:T(1,128)S(1)} %bitcast.23), channel_id=1, source_target_pairs={{0,8},{8,0},{16,24},{24,16},{1,9},{9,1},{17,25},{25,17},{2,10},{10... | collective-permute-start | bytes 1544 | tf_op jit(solution)/shard_map/ppermute | solution.py:20
  37.6 4.4 %collective-permute-start.15 = (f32[1,128]{1,0:T(1,128)S(1)}, f32[1,128]{1,0:T(1,128)S(1)}, u32[]{:S(2)}, u32[]{:S(2)}) collective-permute-start(f32[1,128]{1,0:T(1,128)S(1)} %bitcast_add_fusion), channel_id=1, source_target_pairs={{0,20},{1,21},{2,22},{3,23},{4,16},{5,17},{6,18},{7,19},{8,28},{9,... | collective-permute-start | bytes 1544 | tf_op jit(solution)/shard_map/ppermute | solution.py:31
  39.1 3.5 %collective-permute-start.14 = (f32[1,128]{1,0:T(1,128)S(1)}, f32[1,128]{1,0:T(1,128)S(1)}, u32[]{:S(2)}, u32[]{:S(2)}) collective-permute-start(f32[1,128]{1,0:T(1,128)S(1)} %bitcast_add_fusion), channel_id=1, source_target_pairs={{0,16},{1,17},{2,18},{3,19},{4,20},{5,21},{6,22},{7,23},{8,24},{9,... | collective-permute-start | bytes 1544 | tf_op jit(solution)/shard_map/ppermute | solution.py:31
  40.5 3.5 %collective-permute-start.13 = (f32[1,128]{1,0:T(1,128)S(1)}, f32[1,128]{1,0:T(1,128)S(1)}, u32[]{:S(2)}, u32[]{:S(2)}) collective-permute-start(f32[1,128]{1,0:T(1,128)S(1)} %bitcast_add_fusion), channel_id=1, source_target_pairs={{0,4},{1,5},{2,6},{3,7},{4,0},{5,1},{6,2},{7,3},{8,12},{9,13},{10,... | collective-permute-start | bytes 1544 | tf_op jit(solution)/shard_map/ppermute | solution.py:31

commit v4 on v3

--- a/solution.py
+++ b/solution.py
@@ -8,6 +8,7 @@
 from jax.sharding import PartitionSpec as P
 
 IB = 16
+BITS = 24
 VMEM = pl.BlockSpec(memory_space=pltpu.VMEM)
 SMEM = pl.BlockSpec(memory_space=pltpu.SMEM)
 
@@ -29,6 +30,47 @@
         for k in range(c)
     ]
     return lax.ppermute(x, ("layer", "row", "col"), pairs)
+
+
+def power_of_two(k):
+    scale = jnp.ones(k.shape, jnp.float32)
+    for b in range(7):
+        factor = jnp.where(k < 0, 2.0 ** -(2**b), 2.0 ** (2**b))
+        scale = jnp.where((jnp.abs(k) >> b) & 1 == 1, scale * factor, scale)
+    return scale
+
+
+def pack(part, out_ref):
+    top = jnp.max(jnp.abs(part), axis=0, keepdims=True)
+    k = jnp.clip(jnp.ceil(jnp.log2(top)), -100.0, 125.0).astype(jnp.int32) + 1
+    q = jnp.floor(part * power_of_two(BITS - 1 - k) + 0.5).astype(jnp.int32)
+    rows = part.shape[0] // 4
+    a, b, c, d = (q[i * rows : (i + 1) * rows] for i in range(4))
+    out_ref[:rows] = (a << 8) | (d & 255)
+    out_ref[rows : 2 * rows] = (b << 8) | ((d >> 8) & 255)
+    out_ref[2 * rows : 3 * rows] = (c << 8) | ((d >> 16) & 255)
+    out_ref[3 * rows :] = jnp.broadcast_to(k, (8, part.shape[1]))
+
+
+def square_kernel(mine_ref, *refs):
+    coded_refs, (sq_ref, sum_ref) = refs[:-2], refs[-2:]
+    rows = mine_ref.shape[0] // 4
+    scales = [power_of_two(ref[3 * rows : 3 * rows + 1] - (BITS - 1)) for ref in coded_refs]
+    total = jnp.zeros(sum_ref.shape, jnp.float32)
+    for i in range(4):
+        at = slice(i * rows, (i + 1) * rows)
+        e = mine_ref[at]
+        for ref, scale in zip(coded_refs, scales):
+            if i < 3:
+                q = ref[at] >> 8
+            else:
+                w = [ref[j * rows : (j + 1) * rows] for j in range(3)]
+                q = (w[0] & 255) | ((w[1] & 255) << 8) | ((w[2] << 24) >> 8)
+            e = e + q.astype(jnp.float32) * scale
+        sq = e * e
+        sq_ref[at] = sq
+        total = total + jnp.sum(sq, axis=0, keepdims=True)
+    sum_ref[...] = total
 
 
 def product_kernel(masks, n_layer, n_row, n_col, ids_ref, *refs):
@@ -63,7 +105,11 @@
                 )
         out = jnp.dot(lhs_ref[slot], rhs, preferred_element_type=jnp.float32)
         for m in range(2):
-            out_refs[2 * slot + m][...] = out[:, m * width : (m + 1) * width]
+            part, out_ref = out[:, m * width : (m + 1) * width], out_refs[2 * slot + m]
+            if slot or m:
+                pack(part, out_ref)
+            else:
+                out_ref[...] = part
 
 
 def products(masks, ids, b_refs, panels):
@@ -73,7 +119,8 @@
     ins = [*b_refs, *panels]
     return pl.pallas_call(
         functools.partial(product_kernel, masks, n_layer, n_row, n_col),
-        out_shape=[pltpu.VMEM((rows, width), jnp.float32)] * (2 * n_slots),
+        out_shape=[pltpu.VMEM((rows, width), jnp.float32)]
+        + [pltpu.VMEM((rows // 4 * 3 + 8, width), jnp.int32)] * (2 * n_slots - 1),
         in_specs=[SMEM] + [VMEM] * len(ins),
         out_specs=[VMEM] * (2 * n_slots),
         scratch_shapes=[
@@ -121,11 +168,17 @@
     panels = [x for p in panels for x in (p, other(p))]
     parts = products(masks, ids, b_refs, panels)
 
-    expanded = parts[0]
-    for k in range(1, n_layer):
-        expanded = expanded + grid_permute(parts[k], 2 * (k // 2), 0, k % 2)
-    sq = expanded * expanded
-    col_sum = jnp.sum(sq, axis=0)[None]
+    parts = [parts[0]] + [grid_permute(parts[k], 2 * (k // 2), 0, k % 2) for k in range(1, n_layer)]
+    sq, col_sum = pl.pallas_call(
+        square_kernel,
+        out_shape=(
+            pltpu.VMEM(parts[0].shape, jnp.float32),
+            pltpu.VMEM((1, parts[0].shape[1]), jnp.float32),
+        ),
+        in_specs=[VMEM] * len(parts),
+        out_specs=(VMEM, VMEM),
+        name="squares",
+    )(*(pin(x) for x in parts))
 
     col_sum = col_sum + xor_permute(col_sum, "layer", 1)
     others = [

time: 45 us -> 42.7 us (0.949)
  waiting for transfers between devices: 24.4 us -> 21.7 us
  Pallas kernels: 1.3 us -> 1.76 us
    ppermute x6, waiting for transfers between devices: 14.5 us -> 11.9 us  [grid_permute(): return lax.ppermute(x, ('layer', 'row', 'col'), pairs)]
where the time goes in v4:
time: 42.7 us; the launch traced here: 42.5 us
  waiting for transfers between devices  21.7 us (51%)
  starting transfers between devices  15.5 us (36%)
  other arithmetic  2.19 us (5%)
  Pallas kernels  1.76 us (4%)
  between operations  0.72 us (2%)
  local copies, waits for them, and re-layouts  0.67 us (2%)
    ppermute x6, waiting for transfers between devices, grid_permute(): return lax.ppermute(x, ('layer', 'row', 'col'), pairs)  11.9 us
    ppermute x10, waiting for transfers between devices, xor_permute(): lax.ppermute(x, axis, [(i, i ^ mask) for i in range(lax.axis_size(axis))])  9.89 us
    ppermute x10, starting transfers between devices, xor_permute(): lax.ppermute(x, axis, [(i, i ^ mask) for i in range(lax.axis_size(axis))])  8.41 us
    ppermute x6, starting transfers between devices, grid_permute(): return lax.ppermute(x, ('layer', 'row', 'col'), pairs)  7.04 us
    pallas_call x1, Pallas kernels, products(): pl.pallas_call(functools.partial(product_kernel, masks, n_layer, n_row, n...  1.56 us
  transfers between devices with their start and end apart: 16, of which 10 were waited for; matrix products, arithmetic and copies ran while one was open for 3% of the time, Pallas kernels for 0%

profile of v4, /device:TPU:0, one launch (start us, length us, event | category | flops | bytes accessed | tf_op | source)
XLA Modules:
  0.0 42.5 jit_solution(10532788217589795362)
XLA Ops:
  0.0 0.5 %collective-permute-start.7 = (bf16[8,128,128]{2,1,0:T(8,128)(2,1)}, bf16[8,128,128]{2,1,0:T(8,128)(2,1)S(1)}, u32[]{:S(2)}, u32[]{:S(2)}) collective-permute-start(bf16[8,128,128]{2,1,0:T(8,128)(2,1)} %bitcast.14), channel_id=1, source_target_pairs={{0,8},{8,0},{16,24},{24,16},{1,9},{9,1},{17,25},{25,17},{2,10},{10... | collective-permute-start | bytes 786440 | tf_op jit(solution)/shard_map/ppermute | solution.py:21
  0.5 3.6 %collective-permute-start = (bf16[8,128,128]{2,1,0:T(8,128)(2,1)}, bf16[8,128,128]{2,1,0:T(8,128)(2,1)S(1)}, u32[]{:S(2)}, u32[]{:S(2)}) collective-permute-start(bf16[8,128,128]{2,1,0:T(8,128)(2,1)} %bitcast.15), channel_id=1, source_target_pairs={{0,2},{1,3},{2,0},{3,1},{4,6},{5,7},{6,4},{7,5},{8,10},{9,11},{10,... | collective-permute-start | bytes 786440 | tf_op jit(solution)/shard_map/ppermute | solution.py:21
  4.7 0.0 copy-start.1
  4.7 0.6 %copy-done.1 = s32[1,8]{1,0:T(1,128)S(1)} copy-done((s32[1,8]{1,0:T(1,128)S(1)}, s32[1,8]{1,0:T(1,128)}, u32[]{:S(2)}) %copy-start.1) | copy-done | bytes 56
  5.4 0.2 collective-permute-start.1
  5.6 1.5 %collective-permute-start.3 = (bf16[256,128]{1,0:T(8,128)(2,1)}, bf16[256,128]{1,0:T(8,128)(2,1)S(1)}, u32[]{:S(2)}, u32[]{:S(2)}) collective-permute-start(bf16[256,128]{1,0:T(8,128)(2,1)} %param.7), channel_id=1, source_target_pairs={{0,4},{4,0},{1,5},{5,1},{2,6},{6,2},{3,7},{7,3},{8,12},{12,8},{9,1... | collective-permute-start | bytes 196616 | tf_op jit(solution)/shard_map/ppermute | solution.py:21
  7.1 0.0 collective-permute-done.1
  7.1 0.0 copy-start
  7.1 0.4 collective-permute-start.2
  7.5 2.5 %collective-permute-done.3 = bf16[256,128]{1,0:T(8,128)(2,1)S(1)} collective-permute-done((bf16[256,128]{1,0:T(8,128)(2,1)}, bf16[256,128]{1,0:T(8,128)(2,1)S(1)}, u32[]{:S(2)}, u32[]{:S(2)}) %collective-permute-start.3) | collective-permute-done | bytes 65568 | tf_op jit(solution)/shard_map/ppermute | solution.py:21
  10.1 0.8 %pad_maximum_fusion = bf16[512,128]{1,0:T(8,128)(2,1)S(1)} fusion(bf16[256,128]{1,0:T(8,128)(2,1)S(1)} %collective-permute-done.3, bf16[256,128]{1,0:T(8,128)(2,1)} %param.7), kind=kLoop, calls=%fused_computation.1 | loop fusion | flops 262144 | bytes 262144 | tf_op jit(solution)/shard_map/concatenate | solution.py:157
  11.0 1.6 %collective-permute-start.5 = (bf16[256,128]{1,0:T(8,128)(2,1)S(1)}, bf16[256,128]{1,0:T(8,128)(2,1)S(1)}, u32[]{:S(2)}, u32[]{:S(2)}) collective-permute-start(bf16[256,128]{1,0:T(8,128)(2,1)S(1)} %bitcast.20), channel_id=1, source_target_pairs={{0,1},{1,0},{2,3},{3,2},{4,5},{5,4},{6,7},{7,6},{8,9},{9,8},{10,11... | collective-permute-start | bytes 196616 | tf_op jit(solution)/shard_map/ppermute | solution.py:21
  12.6 0.0 collective-permute-start.4
  12.6 4.4 %collective-permute-done.2 = s32[2,8]{1,0:T(2,128)S(1)} collective-permute-done((s32[2,8]{1,0:T(2,128)S(1)}, s32[2,8]{1,0:T(2,128)S(1)}, u32[]{:S(2)}, u32[]{:S(2)}) %collective-permute-start.2) | collective-permute-done | bytes 96 | tf_op jit(solution)/shard_map/ppermute | solution.py:21
  17.0 0.6 %pad_add_fusion.ids_ref = s32[4,8]{1,0:T(4,128)} fusion(s32[2,8]{1,0:T(2,128)S(1)} %collective-permute-done.2, s32[1,8]{1,0:T(1,128)S(1)} %collective-permute-done.1, s32[1,8]{1,0:T(1,128)S(1)} %compare_select_fusion), kind=kLoop, calls=%fused_computation.2 | loop fusion | flops 64 | bytes 256 | tf_op jit(solution)/shard_map/concatenate | solution.py:148
  17.6 0.7 %collective-permute-done.5.refs_2_ = bf16[256,128]{1,0:T(8,128)(2,1)S(1)} collective-permute-done((bf16[256,128]{1,0:T(8,128)(2,1)S(1)}, bf16[256,128]{1,0:T(8,128)(2,1)S(1)}, u32[]{:S(2)}, u32[]{:S(2)}) %collective-permute-start.5) | collective-permute-done | bytes 65568 | tf_op jit(solution)/shard_map/ppermute | solution.py:21
  18.3 0.0 collective-permute-done.4.refs_1_
  18.3 0.0 collective-permute-done.refs_6_
  18.3 0.0 collective-permute-start.8
  18.3 0.5 %collective-permute-start.6 = (bf16[256,128]{1,0:T(8,128)(2,1)S(1)}, bf16[256,128]{1,0:T(8,128)(2,1)S(1)}, u32[]{:S(2)}, u32[]{:S(2)}) collective-permute-start(bf16[256,128]{1,0:T(8,128)(2,1)S(1)} %collective-permute-done.5.refs_2_), channel_id=1, source_target_pairs={{0,8},{8,0},{16,24},{24,16},{1,9},{9,1},{17,25},{25,17},{2,10},{10... | collective-permute-start | bytes 196616 | tf_op jit(solution)/shard_map/ppermute | solution.py:21
  18.8 0.0 collective-permute-done.7.refs_5_
  18.8 1.1 %collective-permute-done.6.refs_3_ = bf16[256,128]{1,0:T(8,128)(2,1)S(1)} collective-permute-done((bf16[256,128]{1,0:T(8,128)(2,1)S(1)}, bf16[256,128]{1,0:T(8,128)(2,1)S(1)}, u32[]{:S(2)}, u32[]{:S(2)}) %collective-permute-start.6) | collective-permute-done | bytes 65568 | tf_op jit(solution)/shard_map/ppermute | solution.py:21
  19.9 0.0 collective-permute-done.8.refs_7_
  19.9 0.0 copy-done
  19.9 1.6 %partial_rows.1 = (f32[512,128]{1,0:T(8,128)S(1)}, s32[392,128]{1,0:T(8,128)S(1)}, s32[392,128]{1,0:T(8,128)S(1)}, s32[392,128]{1,0:T(8,128)S(1)}) custom-call(s32[4,8]{1,0:T(4,128)} %pad_add_fusion.ids_ref, bf16[256,128]{1,0:T(8,128)(2,1)S(1)} %bitcast.18, bf16[256,128]{1,0:T(8,128)(2,1)S(1)} %collective-permute-done.4.refs_1_, ...), custom_call_target="tpu_custom_call" | custom-call | tf_op jit(solution)/shard_map/partial_rows/pallas_call | solution.py:120
  21.5 0.2 collective-permute-start.9
  21.7 1.5 %collective-permute-start.10 = (s32[392,128]{1,0:T(8,128)S(1)}, s32[392,128]{1,0:T(8,128)S(1)}, u32[]{:S(2)}, u32[]{:S(2)}) collective-permute-start(s32[392,128]{1,0:T(8,128)S(1)} %get-tuple-element.23), channel_id=1, source_target_pairs={{0,16},{1,17},{2,18},{3,19},{4,20},{5,21},{6,22},{7,23},{8,24},{9,... | collective-permute-start | bytes 602120 | tf_op jit(solution)/shard_map/ppermute | solution.py:32
  23.2 1.9 %collective-permute-start.11 = (s32[392,128]{1,0:T(8,128)S(1)}, s32[392,128]{1,0:T(8,128)S(1)}, u32[]{:S(2)}, u32[]{:S(2)}) collective-permute-start(s32[392,128]{1,0:T(8,128)S(1)} %get-tuple-element.24), channel_id=1, source_target_pairs={{0,17},{1,16},{2,19},{3,18},{4,21},{5,20},{6,23},{7,22},{8,25},{9,... | collective-permute-start | bytes 602120 | tf_op jit(solution)/shard_map/ppermute | solution.py:32
  25.1 4.3 %collective-permute-done.9.refs_0_ = s32[392,128]{1,0:T(8,128)S(1)} collective-permute-done((s32[392,128]{1,0:T(8,128)S(1)}, s32[392,128]{1,0:T(8,128)S(1)}, u32[]{:S(2)}, u32[]{:S(2)}) %collective-permute-start.9) | collective-permute-done | bytes 200736 | tf_op jit(solution)/shard_map/ppermute | solution.py:32
  29.4 0.0 collective-permute-done.10.refs_1_
  29.4 4.5 %collective-permute-done.11.refs_2_ = s32[392,128]{1,0:T(8,128)S(1)} collective-permute-done((s32[392,128]{1,0:T(8,128)S(1)}, s32[392,128]{1,0:T(8,128)S(1)}, u32[]{:S(2)}, u32[]{:S(2)}) %collective-permute-start.11) | collective-permute-done | bytes 200736 | tf_op jit(solution)/shard_map/ppermute | solution.py:32
  33.9 0.2 squares.1
  34.1 0.1 collective-permute-start.12
  34.2 1.1 %collective-permute-done.12 = f32[1,128]{1,0:T(1,128)S(1)} collective-permute-done((f32[1,128]{1,0:T(1,128)S(1)}, f32[1,128]{1,0:T(1,128)S(1)}, u32[]{:S(2)}, u32[]{:S(2)}) %collective-permute-start.12) | collective-permute-done | bytes 544 | tf_op jit(solution)/shard_map/ppermute | solution.py:21
  35.3 1.6 %collective-permute-start.15 = (f32[1,128]{1,0:T(1,128)S(1)}, f32[1,128]{1,0:T(1,128)S(1)}, u32[]{:S(2)}, u32[]{:S(2)}) collective-permute-start(f32[1,128]{1,0:T(1,128)S(1)} %add.33), channel_id=1, source_target_pairs={{0,20},{1,21},{2,22},{3,23},{4,16},{5,17},{6,18},{7,19},{8,28},{9,... | collective-permute-start | bytes 1544 | tf_op jit(solution)/shard_map/ppermute | solution.py:32
  36.9 1.4 %collective-permute-start.14 = (f32[1,128]{1,0:T(1,128)S(1)}, f32[1,128]{1,0:T(1,128)S(1)}, u32[]{:S(2)}, u32[]{:S(2)}) collective-permute-start(f32[1,128]{1,0:T(1,128)S(1)} %add.33), channel_id=1, source_target_pairs={{0,16},{1,17},{2,18},{3,19},{4,20},{5,21},{6,22},{7,23},{8,24},{9,... | collective-permute-start | bytes 1544 | tf_op jit(solution)/shard_map/ppermute | solution.py:32
  38.3 0.5 %collective-permute-start.13 = (f32[1,128]{1,0:T(1,128)S(1)}, f32[1,128]{1,0:T(1,128)S(1)}, u32[]{:S(2)}, u32[]{:S(2)}) collective-permute-start(f32[1,128]{1,0:T(1,128)S(1)} %add.33), channel_id=1, source_target_pairs={{0,4},{1,5},{2,6},{3,7},{4,0},{5,1},{6,2},{7,3},{8,12},{9,13},{10,... | collective-permute-start | bytes 1544 | tf_op jit(solution)/shard_map/ppermute | solution.py:32
  38.8 0.9 %collective-permute-done.15 = f32[1,128]{1,0:T(1,128)S(1)} collective-permute-done((f32[1,128]{1,0:T(1,128)S(1)}, f32[1,128]{1,0:T(1,128)S(1)}, u32[]{:S(2)}, u32[]{:S(2)}) %collective-permute-start.15) | collective-permute-done | bytes 544 | tf_op jit(solution)/shard_map/ppermute | solution.py:32
  39.7 0.7 %collective-permute-done.14 = f32[1,128]{1,0:T(1,128)S(1)} collective-permute-done((f32[1,128]{1,0:T(1,128)S(1)}, f32[1,128]{1,0:T(1,128)S(1)}, u32[]{:S(2)}, u32[]{:S(2)}) %collective-permute-start.14) | collective-permute-done | bytes 544 | tf_op jit(solution)/shard_map/ppermute | solution.py:32
  40.4 1.4 %collective-permute-done.13 = f32[1,128]{1,0:T(1,128)S(1)} collective-permute-done((f32[1,128]{1,0:T(1,128)S(1)}, f32[1,128]{1,0:T(1,128)S(1)}, u32[]{:S(2)}, u32[]{:S(2)}) %collective-permute-start.13) | collective-permute-done | bytes 544 | tf_op jit(solution)/shard_map/ppermute | solution.py:32
  41.8 0.7 %multiply_bitcast_fusion = f32[1,512,128]{2,1,0:T(8,128)} fusion(f32[512,128]{1,0:T(8,128)S(1)} %get-tuple-element.25, f32[128]{0:T(128)S(1)} %divide_bitcast_fusion), kind=kLoop, calls=%fused_computation | loop fusion | flops 65536 | bytes 524800 | tf_op jit(solution)/shard_map/broadcast_in_dim | solution.py:193
  (5 shorter events, 0.0 us)
Async XLA Ops:
  0.0 18.8 %collective-permute-start.7 = (bf16[8,128,128]{2,1,0:T(8,128)(2,1)}, bf16[8,128,128]{2,1,0:T(8,128)(2,1)S(1)}, u32[]{:S(2)}, u32[]{:S(2)}) collective-permute-start(bf16[8,128,128]{2,1,0:T(8,128)(2,1)} %bitcast.14), channel_id=1, source_target_pairs={{0,8},{8,0},{16,24},{24,16},{1,9},{9,1},{17,25},{25,17},{2,10},{10... | collective-permute-start | bytes 786440 | tf_op jit(solution)/shard_map/ppermute | solution.py:21
  0.5 17.8 %collective-permute-start = (bf16[8,128,128]{2,1,0:T(8,128)(2,1)}, bf16[8,128,128]{2,1,0:T(8,128)(2,1)S(1)}, u32[]{:S(2)}, u32[]{:S(2)}) collective-permute-start(bf16[8,128,128]{2,1,0:T(8,128)(2,1)} %bitcast.15), channel_id=1, source_target_pairs={{0,2},{1,3},{2,0},{3,1},{4,6},{5,7},{6,4},{7,5},{8,10},{9,11},{10,... | collective-permute-start | bytes 786440 | tf_op jit(solution)/shard_map/ppermute | solution.py:21
  4.7 0.7 %copy-start.1 = (s32[1,8]{1,0:T(1,128)S(1)}, s32[1,8]{1,0:T(1,128)}, u32[]{:S(2)}) copy-start(s32[1,8]{1,0:T(1,128)} %param.5) | copy-start | bytes 100
  5.4 1.8 %collective-permute-start.1 = (s32[1,8]{1,0:T(1,128)S(1)}, s32[1,8]{1,0:T(1,128)S(1)}, u32[]{:S(2)}, u32[]{:S(2)}) collective-permute-start(s32[1,8]{1,0:T(1,128)S(1)} %compare_select_fusion), channel_id=1, source_target_pairs={{0,8},{8,0},{16,24},{24,16},{1,9},{9,1},{17,25},{25,17},{2,10},{10... | collective-permute-start | bytes 104 | tf_op jit(solution)/shard_map/ppermute | solution.py:21
  5.6 4.5 %collective-permute-start.3 = (bf16[256,128]{1,0:T(8,128)(2,1)}, bf16[256,128]{1,0:T(8,128)(2,1)S(1)}, u32[]{:S(2)}, u32[]{:S(2)}) collective-permute-start(bf16[256,128]{1,0:T(8,128)(2,1)} %param.7), channel_id=1, source_target_pairs={{0,4},{4,0},{1,5},{5,1},{2,6},{6,2},{3,7},{7,3},{8,12},{12,8},{9,1... | collective-permute-start | bytes 196616 | tf_op jit(solution)/shard_map/ppermute | solution.py:21
  7.1 12.8 %copy-start = (bf16[1,8,128,128]{3,2,1,0:T(8,128)(2,1)S(1)}, bf16[1,8,128,128]{3,2,1,0:T(8,128)(2,1)}, u32[]{:S(2)}) copy-start(bf16[1,8,128,128]{3,2,1,0:T(8,128)(2,1)} %param.4) | copy-start | bytes 786436
  7.1 9.9 %collective-permute-start.2 = (s32[2,8]{1,0:T(2,128)S(1)}, s32[2,8]{1,0:T(2,128)S(1)}, u32[]{:S(2)}, u32[]{:S(2)}) collective-permute-start(s32[2,8]{1,0:T(2,128)S(1)} %pad_add_fusion.1), channel_id=1, source_target_pairs={{0,2},{1,3},{2,0},{3,1},{4,6},{5,7},{6,4},{7,5},{8,10},{9,11},{10,... | collective-permute-start | bytes 200 | tf_op jit(solution)/shard_map/ppermute | solution.py:21
  11.0 7.3 %collective-permute-start.5 = (bf16[256,128]{1,0:T(8,128)(2,1)S(1)}, bf16[256,128]{1,0:T(8,128)(2,1)S(1)}, u32[]{:S(2)}, u32[]{:S(2)}) collective-permute-start(bf16[256,128]{1,0:T(8,128)(2,1)S(1)} %bitcast.20), channel_id=1, source_target_pairs={{0,1},{1,0},{2,3},{3,2},{4,5},{5,4},{6,7},{7,6},{8,9},{9,8},{10,11... | collective-permute-start | bytes 196616 | tf_op jit(solution)/shard_map/ppermute | solution.py:21
  12.6 5.7 %collective-permute-start.4 = (bf16[256,128]{1,0:T(8,128)(2,1)S(1)}, bf16[256,128]{1,0:T(8,128)(2,1)S(1)}, u32[]{:S(2)}, u32[]{:S(2)}) collective-permute-start(bf16[256,128]{1,0:T(8,128)(2,1)S(1)} %bitcast.17), channel_id=1, source_target_pairs={{0,8},{8,0},{16,24},{24,16},{1,9},{9,1},{17,25},{25,17},{2,10},{10... | collective-permute-start | bytes 196616 | tf_op jit(solution)/shard_map/ppermute | solution.py:21
  18.3 1.6 %collective-permute-start.8 = (bf16[8,128,128]{2,1,0:T(8,128)(2,1)S(1)}, bf16[8,128,128]{2,1,0:T(8,128)(2,1)S(1)}, u32[]{:S(2)}, u32[]{:S(2)}) collective-permute-start(bf16[8,128,128]{2,1,0:T(8,128)(2,1)S(1)} %collective-permute-done.refs_6_), channel_id=1, source_target_pairs={{0,8},{8,0},{16,24},{24,16},{1,9},{9,1},{17,25},{25,17},{2,10},{10... | collective-permute-start | bytes 786440 | tf_op jit(solution)/shard_map/ppermute | solution.py:21
  18.3 1.6 %collective-permute-start.6 = (bf16[256,128]{1,0:T(8,128)(2,1)S(1)}, bf16[256,128]{1,0:T(8,128)(2,1)S(1)}, u32[]{:S(2)}, u32[]{:S(2)}) collective-permute-start(bf16[256,128]{1,0:T(8,128)(2,1)S(1)} %collective-permute-done.5.refs_2_), channel_id=1, source_target_pairs={{0,8},{8,0},{16,24},{24,16},{1,9},{9,1},{17,25},{25,17},{2,10},{10... | collective-permute-start | bytes 196616 | tf_op jit(solution)/shard_map/ppermute | solution.py:21
  21.5 7.9 %collective-permute-start.9 = (s32[392,128]{1,0:T(8,128)S(1)}, s32[392,128]{1,0:T(8,128)S(1)}, u32[]{:S(2)}, u32[]{:S(2)}) collective-permute-start(s32[392,128]{1,0:T(8,128)S(1)} %get-tuple-element.22), channel_id=1, source_target_pairs={{0,1},{1,0},{2,3},{3,2},{4,5},{5,4},{6,7},{7,6},{8,9},{9,8},{10,11... | collective-permute-start | bytes 602120 | tf_op jit(solution)/shard_map/ppermute | solution.py:32
  21.7 7.7 %collective-permute-start.10 = (s32[392,128]{1,0:T(8,128)S(1)}, s32[392,128]{1,0:T(8,128)S(1)}, u32[]{:S(2)}, u32[]{:S(2)}) collective-permute-start(s32[392,128]{1,0:T(8,128)S(1)} %get-tuple-element.23), channel_id=1, source_target_pairs={{0,16},{1,17},{2,18},{3,19},{4,20},{5,21},{6,22},{7,23},{8,24},{9,... | collective-permute-start | bytes 602120 | tf_op jit(solution)/shard_map/ppermute | solution.py:32
  23.2 10.7 %collective-permute-start.11 = (s32[392,128]{1,0:T(8,128)S(1)}, s32[392,128]{1,0:T(8,128)S(1)}, u32[]{:S(2)}, u32[]{:S(2)}) collective-permute-start(s32[392,128]{1,0:T(8,128)S(1)} %get-tuple-element.24), channel_id=1, source_target_pairs={{0,17},{1,16},{2,19},{3,18},{4,21},{5,20},{6,23},{7,22},{8,25},{9,... | collective-permute-start | bytes 602120 | tf_op jit(solution)/shard_map/ppermute | solution.py:32
  34.1 1.2 %collective-permute-start.12 = (f32[1,128]{1,0:T(1,128)S(1)}, f32[1,128]{1,0:T(1,128)S(1)}, u32[]{:S(2)}, u32[]{:S(2)}) collective-permute-start(f32[1,128]{1,0:T(1,128)S(1)} %get-tuple-element.26), channel_id=1, source_target_pairs={{0,8},{8,0},{16,24},{24,16},{1,9},{9,1},{17,25},{25,17},{2,10},{10... | collective-permute-start | bytes 1544 | tf_op jit(solution)/shard_map/ppermute | solution.py:21
  35.3 4.4 %collective-permute-start.15 = (f32[1,128]{1,0:T(1,128)S(1)}, f32[1,128]{1,0:T(1,128)S(1)}, u32[]{:S(2)}, u32[]{:S(2)}) collective-permute-start(f32[1,128]{1,0:T(1,128)S(1)} %add.33), channel_id=1, source_target_pairs={{0,20},{1,21},{2,22},{3,23},{4,16},{5,17},{6,18},{7,19},{8,28},{9,... | collective-permute-start | bytes 1544 | tf_op jit(solution)/shard_map/ppermute | solution.py:32
  36.9 3.5 %collective-permute-start.14 = (f32[1,128]{1,0:T(1,128)S(1)}, f32[1,128]{1,0:T(1,128)S(1)}, u32[]{:S(2)}, u32[]{:S(2)}) collective-permute-start(f32[1,128]{1,0:T(1,128)S(1)} %add.33), channel_id=1, source_target_pairs={{0,16},{1,17},{2,18},{3,19},{4,20},{5,21},{6,22},{7,23},{8,24},{9,... | collective-permute-start | bytes 1544 | tf_op jit(solution)/shard_map/ppermute | solution.py:32
  38.3 3.5 %collective-permute-start.13 = (f32[1,128]{1,0:T(1,128)S(1)}, f32[1,128]{1,0:T(1,128)S(1)}, u32[]{:S(2)}, u32[]{:S(2)}) collective-permute-start(f32[1,128]{1,0:T(1,128)S(1)} %add.33), channel_id=1, source_target_pairs={{0,4},{1,5},{2,6},{3,7},{4,0},{5,1},{6,2},{7,3},{8,12},{9,13},{10,... | collective-permute-start | bytes 1544 | tf_op jit(solution)/shard_map/ppermute | solution.py:32

commit v5 on v4

--- a/solution.py
+++ b/solution.py
@@ -8,7 +8,7 @@
 from jax.sharding import PartitionSpec as P
 
 IB = 16
-BITS = 24
+BITS = 20
 VMEM = pl.BlockSpec(memory_space=pltpu.VMEM)
 SMEM = pl.BlockSpec(memory_space=pltpu.SMEM)
 
@@ -42,31 +42,43 @@
 
 def pack(part, out_ref):
     top = jnp.max(jnp.abs(part), axis=0, keepdims=True)
-    k = jnp.clip(jnp.ceil(jnp.log2(top)), -100.0, 125.0).astype(jnp.int32) + 1
+    k = jnp.clip(jnp.ceil(jnp.log2(top) + 0.01), -100.0, 126.0).astype(jnp.int32)
     q = jnp.floor(part * power_of_two(BITS - 1 - k) + 0.5).astype(jnp.int32)
-    rows = part.shape[0] // 4
-    a, b, c, d = (q[i * rows : (i + 1) * rows] for i in range(4))
-    out_ref[:rows] = (a << 8) | (d & 255)
-    out_ref[rows : 2 * rows] = (b << 8) | ((d >> 8) & 255)
-    out_ref[2 * rows : 3 * rows] = (c << 8) | ((d >> 16) & 255)
-    out_ref[3 * rows :] = jnp.broadcast_to(k, (8, part.shape[1]))
+    rows = part.shape[0] // 8
+    q = [q[i * rows : (i + 1) * rows] for i in range(8)]
+    low = [
+        q[5] & 4095,
+        ((q[5] >> 12) & 255) | ((q[6] & 15) << 8),
+        (q[6] >> 4) & 4095,
+        ((q[6] >> 16) & 15) | ((q[7] & 255) << 4),
+        (q[7] >> 8) & 4095,
+    ]
+    for i in range(5):
+        out_ref[i * rows : (i + 1) * rows] = (q[i] << 12) | low[i]
+    out_ref[5 * rows :] = jnp.broadcast_to(k, (8, part.shape[1]))
+
+
+def unpack(ref, rows, i):
+    w = [ref[j * rows : (j + 1) * rows] for j in ([i] if i < 5 else range(5))]
+    if i < 5:
+        return w[0] >> 12
+    if i == 5:
+        return (w[0] & 4095) | ((w[1] << 24) >> 12)
+    if i == 6:
+        return ((w[1] >> 8) & 15) | ((w[2] & 4095) << 4) | ((w[3] << 28) >> 12)
+    return ((w[3] >> 4) & 255) | ((w[4] << 20) >> 12)
 
 
 def square_kernel(mine_ref, *refs):
     coded_refs, (sq_ref, sum_ref) = refs[:-2], refs[-2:]
-    rows = mine_ref.shape[0] // 4
-    scales = [power_of_two(ref[3 * rows : 3 * rows + 1] - (BITS - 1)) for ref in coded_refs]
+    rows = mine_ref.shape[0] // 8
+    scales = [power_of_two(ref[5 * rows : 5 * rows + 1] - (BITS - 1)) for ref in coded_refs]
     total = jnp.zeros(sum_ref.shape, jnp.float32)
-    for i in range(4):
+    for i in range(8):
         at = slice(i * rows, (i + 1) * rows)
         e = mine_ref[at]
         for ref, scale in zip(coded_refs, scales):
-            if i < 3:
-                q = ref[at] >> 8
-            else:
-                w = [ref[j * rows : (j + 1) * rows] for j in range(3)]
-                q = (w[0] & 255) | ((w[1] & 255) << 8) | ((w[2] << 24) >> 8)
-            e = e + q.astype(jnp.float32) * scale
+            e = e + unpack(ref, rows, i).astype(jnp.float32) * scale
         sq = e * e
         sq_ref[at] = sq
         total = total + jnp.sum(sq, axis=0, keepdims=True)
@@ -120,7 +132,7 @@
     return pl.pallas_call(
         functools.partial(product_kernel, masks, n_layer, n_row, n_col),
         out_shape=[pltpu.VMEM((rows, width), jnp.float32)]
-        + [pltpu.VMEM((rows // 4 * 3 + 8, width), jnp.int32)] * (2 * n_slots - 1),
+        + [pltpu.VMEM((rows // 8 * 5 + 8, width), jnp.int32)] * (2 * n_slots - 1),
         in_specs=[SMEM] + [VMEM] * len(ins),
         out_specs=[VMEM] * (2 * n_slots),
         scratch_shapes=[

time: 42.7 us -> 41.4 us (0.970)
  waiting for transfers between devices: 21.7 us -> 20.3 us
    ppermute x6, waiting for transfers between devices: 11.9 us -> 10.4 us  [grid_permute(): return lax.ppermute(x, ('layer', 'row', 'col'), pairs)]
  transfers between devices with their start and end apart: 16 -> 16, of which waited for: 10 -> 10; matrix products, arithmetic and copies ran while one was open for 3% -> 4% of each run, Pallas kernels for 0% -> 0%
where the time goes in v5:
time: 41.4 us; the launch traced here: 41.2 us
  waiting for transfers between devices  20.3 us (49%)
  starting transfers between devices  15.5 us (37%)
  other arithmetic  2.19 us (5%)
  Pallas kernels  1.8 us (4%)
  between operations  0.72 us (2%)
  local copies, waits for them, and re-layouts  0.67 us (2%)
    ppermute x6, waiting for transfers between devices, grid_permute(): return lax.ppermute(x, ('layer', 'row', 'col'), pairs)  10.4 us
    ppermute x10, waiting for transfers between devices, xor_permute(): lax.ppermute(x, axis, [(i, i ^ mask) for i in range(lax.axis_size(axis))])  9.89 us
    ppermute x10, starting transfers between devices, xor_permute(): lax.ppermute(x, axis, [(i, i ^ mask) for i in range(lax.axis_size(axis))])  8.41 us
    ppermute x6, starting transfers between devices, grid_permute(): return lax.ppermute(x, ('layer', 'row', 'col'), pairs)  7.04 us
    pallas_call x1, Pallas kernels, products(): pl.pallas_call(functools.partial(product_kernel, masks, n_layer, n_row, n...  1.59 us
    concatenate x1, other arithmetic, body(): b_rows = jnp.concatenate(b_rows).reshape(-1, 2, *b_panel.shape[-1:] * 2)  0.85 us
  transfers between devices with their start and end apart: 16, of which 10 were waited for; matrix products, arithmetic and copies ran while one was open for 4% of the time, Pallas kernels for 0%

profile of v5, /device:TPU:0, one launch (start us, length us, event | category | flops | bytes accessed | tf_op | source)
XLA Modules:
  0.0 41.2 jit_solution(3576695523670661349)
XLA Ops:
  0.0 0.5 %collective-permute-start.7 = (bf16[8,128,128]{2,1,0:T(8,128)(2,1)}, bf16[8,128,128]{2,1,0:T(8,128)(2,1)S(1)}, u32[]{:S(2)}, u32[]{:S(2)}) collective-permute-start(bf16[8,128,128]{2,1,0:T(8,128)(2,1)} %bitcast.14), channel_id=1, source_target_pairs={{0,8},{8,0},{16,24},{24,16},{1,9},{9,1},{17,25},{25,17},{2,10},{10... | collective-permute-start | bytes 786440 | tf_op jit(solution)/shard_map/ppermute | solution.py:21
  0.5 3.6 %collective-permute-start = (bf16[8,128,128]{2,1,0:T(8,128)(2,1)}, bf16[8,128,128]{2,1,0:T(8,128)(2,1)S(1)}, u32[]{:S(2)}, u32[]{:S(2)}) collective-permute-start(bf16[8,128,128]{2,1,0:T(8,128)(2,1)} %bitcast.15), channel_id=1, source_target_pairs={{0,2},{1,3},{2,0},{3,1},{4,6},{5,7},{6,4},{7,5},{8,10},{9,11},{10,... | collective-permute-start | bytes 786440 | tf_op jit(solution)/shard_map/ppermute | solution.py:21
  4.7 0.0 copy-start.1
  4.7 0.6 %copy-done.1 = s32[1,8]{1,0:T(1,128)S(1)} copy-done((s32[1,8]{1,0:T(1,128)S(1)}, s32[1,8]{1,0:T(1,128)}, u32[]{:S(2)}) %copy-start.1) | copy-done | bytes 56
  5.4 0.2 collective-permute-start.1
  5.6 1.5 %collective-permute-start.3 = (bf16[256,128]{1,0:T(8,128)(2,1)}, bf16[256,128]{1,0:T(8,128)(2,1)S(1)}, u32[]{:S(2)}, u32[]{:S(2)}) collective-permute-start(bf16[256,128]{1,0:T(8,128)(2,1)} %param.7), channel_id=1, source_target_pairs={{0,4},{4,0},{1,5},{5,1},{2,6},{6,2},{3,7},{7,3},{8,12},{12,8},{9,1... | collective-permute-start | bytes 196616 | tf_op jit(solution)/shard_map/ppermute | solution.py:21
  7.1 0.0 collective-permute-done.1
  7.1 0.0 copy-start
  7.1 0.4 collective-permute-start.2
  7.5 2.5 %collective-permute-done.3 = bf16[256,128]{1,0:T(8,128)(2,1)S(1)} collective-permute-done((bf16[256,128]{1,0:T(8,128)(2,1)}, bf16[256,128]{1,0:T(8,128)(2,1)S(1)}, u32[]{:S(2)}, u32[]{:S(2)}) %collective-permute-start.3) | collective-permute-done | bytes 65568 | tf_op jit(solution)/shard_map/ppermute | solution.py:21
  10.1 0.8 %pad_maximum_fusion = bf16[512,128]{1,0:T(8,128)(2,1)S(1)} fusion(bf16[256,128]{1,0:T(8,128)(2,1)S(1)} %collective-permute-done.3, bf16[256,128]{1,0:T(8,128)(2,1)} %param.7), kind=kLoop, calls=%fused_computation.1 | loop fusion | flops 262144 | bytes 262144 | tf_op jit(solution)/shard_map/concatenate | solution.py:169
  11.0 1.6 %collective-permute-start.5 = (bf16[256,128]{1,0:T(8,128)(2,1)S(1)}, bf16[256,128]{1,0:T(8,128)(2,1)S(1)}, u32[]{:S(2)}, u32[]{:S(2)}) collective-permute-start(bf16[256,128]{1,0:T(8,128)(2,1)S(1)} %bitcast.20), channel_id=1, source_target_pairs={{0,1},{1,0},{2,3},{3,2},{4,5},{5,4},{6,7},{7,6},{8,9},{9,8},{10,11... | collective-permute-start | bytes 196616 | tf_op jit(solution)/shard_map/ppermute | solution.py:21
  12.6 0.0 collective-permute-start.4
  12.6 4.4 %collective-permute-done.2 = s32[2,8]{1,0:T(2,128)S(1)} collective-permute-done((s32[2,8]{1,0:T(2,128)S(1)}, s32[2,8]{1,0:T(2,128)S(1)}, u32[]{:S(2)}, u32[]{:S(2)}) %collective-permute-start.2) | collective-permute-done | bytes 96 | tf_op jit(solution)/shard_map/ppermute | solution.py:21
  17.0 0.6 %pad_add_fusion.ids_ref = s32[4,8]{1,0:T(4,128)} fusion(s32[2,8]{1,0:T(2,128)S(1)} %collective-permute-done.2, s32[1,8]{1,0:T(1,128)S(1)} %collective-permute-done.1, s32[1,8]{1,0:T(1,128)S(1)} %compare_select_fusion), kind=kLoop, calls=%fused_computation.2 | loop fusion | flops 64 | bytes 256 | tf_op jit(solution)/shard_map/concatenate | solution.py:160
  17.6 0.7 %collective-permute-done.5.refs_2_ = bf16[256,128]{1,0:T(8,128)(2,1)S(1)} collective-permute-done((bf16[256,128]{1,0:T(8,128)(2,1)S(1)}, bf16[256,128]{1,0:T(8,128)(2,1)S(1)}, u32[]{:S(2)}, u32[]{:S(2)}) %collective-permute-start.5) | collective-permute-done | bytes 65568 | tf_op jit(solution)/shard_map/ppermute | solution.py:21
  18.3 0.0 collective-permute-done.4.refs_1_
  18.3 0.0 collective-permute-done.refs_6_
  18.3 0.0 collective-permute-start.8
  18.3 0.5 %collective-permute-start.6 = (bf16[256,128]{1,0:T(8,128)(2,1)S(1)}, bf16[256,128]{1,0:T(8,128)(2,1)S(1)}, u32[]{:S(2)}, u32[]{:S(2)}) collective-permute-start(bf16[256,128]{1,0:T(8,128)(2,1)S(1)} %collective-permute-done.5.refs_2_), channel_id=1, source_target_pairs={{0,8},{8,0},{16,24},{24,16},{1,9},{9,1},{17,25},{25,17},{2,10},{10... | collective-permute-start | bytes 196616 | tf_op jit(solution)/shard_map/ppermute | solution.py:21
  18.8 0.0 collective-permute-done.7.refs_5_
  18.8 1.1 %collective-permute-done.6.refs_3_ = bf16[256,128]{1,0:T(8,128)(2,1)S(1)} collective-permute-done((bf16[256,128]{1,0:T(8,128)(2,1)S(1)}, bf16[256,128]{1,0:T(8,128)(2,1)S(1)}, u32[]{:S(2)}, u32[]{:S(2)}) %collective-permute-start.6) | collective-permute-done | bytes 65568 | tf_op jit(solution)/shard_map/ppermute | solution.py:21
  19.9 0.0 collective-permute-done.8.refs_7_
  19.9 0.0 copy-done
  19.9 1.6 %partial_rows.1 = (f32[512,128]{1,0:T(8,128)S(1)}, s32[328,128]{1,0:T(8,128)S(1)}, s32[328,128]{1,0:T(8,128)S(1)}, s32[328,128]{1,0:T(8,128)S(1)}) custom-call(s32[4,8]{1,0:T(4,128)} %pad_add_fusion.ids_ref, bf16[256,128]{1,0:T(8,128)(2,1)S(1)} %bitcast.18, bf16[256,128]{1,0:T(8,128)(2,1)S(1)} %collective-permute-done.4.refs_1_, ...), custom_call_target="tpu_custom_call" | custom-call | tf_op jit(solution)/shard_map/partial_rows/pallas_call | solution.py:132
  21.5 0.2 collective-permute-start.9
  21.7 1.5 %collective-permute-start.10 = (s32[328,128]{1,0:T(8,128)S(1)}, s32[328,128]{1,0:T(8,128)S(1)}, u32[]{:S(2)}, u32[]{:S(2)}) collective-permute-start(s32[328,128]{1,0:T(8,128)S(1)} %get-tuple-element.23), channel_id=1, source_target_pairs={{0,16},{1,17},{2,18},{3,19},{4,20},{5,21},{6,22},{7,23},{8,24},{9,... | collective-permute-start | bytes 503816 | tf_op jit(solution)/shard_map/ppermute | solution.py:32
  23.2 1.9 %collective-permute-start.11 = (s32[328,128]{1,0:T(8,128)S(1)}, s32[328,128]{1,0:T(8,128)S(1)}, u32[]{:S(2)}, u32[]{:S(2)}) collective-permute-start(s32[328,128]{1,0:T(8,128)S(1)} %get-tuple-element.24), channel_id=1, source_target_pairs={{0,17},{1,16},{2,19},{3,18},{4,21},{5,20},{6,23},{7,22},{8,25},{9,... | collective-permute-start | bytes 503816 | tf_op jit(solution)/shard_map/ppermute | solution.py:32
  25.1 3.6 %collective-permute-done.9.refs_0_ = s32[328,128]{1,0:T(8,128)S(1)} collective-permute-done((s32[328,128]{1,0:T(8,128)S(1)}, s32[328,128]{1,0:T(8,128)S(1)}, u32[]{:S(2)}, u32[]{:S(2)}) %collective-permute-start.9) | collective-permute-done | bytes 167968 | tf_op jit(solution)/shard_map/ppermute | solution.py:32
  28.7 0.0 collective-permute-done.10.refs_1_
  28.7 3.8 %collective-permute-done.11.refs_2_ = s32[328,128]{1,0:T(8,128)S(1)} collective-permute-done((s32[328,128]{1,0:T(8,128)S(1)}, s32[328,128]{1,0:T(8,128)S(1)}, u32[]{:S(2)}, u32[]{:S(2)}) %collective-permute-start.11) | collective-permute-done | bytes 167968 | tf_op jit(solution)/shard_map/ppermute | solution.py:32
  32.5 0.2 squares.1
  32.7 0.1 collective-permute-start.12
  32.8 1.1 %collective-permute-done.12 = f32[1,128]{1,0:T(1,128)S(1)} collective-permute-done((f32[1,128]{1,0:T(1,128)S(1)}, f32[1,128]{1,0:T(1,128)S(1)}, u32[]{:S(2)}, u32[]{:S(2)}) %collective-permute-start.12) | collective-permute-done | bytes 544 | tf_op jit(solution)/shard_map/ppermute | solution.py:21
  33.9 1.6 %collective-permute-start.15 = (f32[1,128]{1,0:T(1,128)S(1)}, f32[1,128]{1,0:T(1,128)S(1)}, u32[]{:S(2)}, u32[]{:S(2)}) collective-permute-start(f32[1,128]{1,0:T(1,128)S(1)} %add.33), channel_id=1, source_target_pairs={{0,20},{1,21},{2,22},{3,23},{4,16},{5,17},{6,18},{7,19},{8,28},{9,... | collective-permute-start | bytes 1544 | tf_op jit(solution)/shard_map/ppermute | solution.py:32
  35.5 1.4 %collective-permute-start.14 = (f32[1,128]{1,0:T(1,128)S(1)}, f32[1,128]{1,0:T(1,128)S(1)}, u32[]{:S(2)}, u32[]{:S(2)}) collective-permute-start(f32[1,128]{1,0:T(1,128)S(1)} %add.33), channel_id=1, source_target_pairs={{0,16},{1,17},{2,18},{3,19},{4,20},{5,21},{6,22},{7,23},{8,24},{9,... | collective-permute-start | bytes 1544 | tf_op jit(solution)/shard_map/ppermute | solution.py:32
  36.9 0.5 %collective-permute-start.13 = (f32[1,128]{1,0:T(1,128)S(1)}, f32[1,128]{1,0:T(1,128)S(1)}, u32[]{:S(2)}, u32[]{:S(2)}) collective-permute-start(f32[1,128]{1,0:T(1,128)S(1)} %add.33), channel_id=1, source_target_pairs={{0,4},{1,5},{2,6},{3,7},{4,0},{5,1},{6,2},{7,3},{8,12},{9,13},{10,... | collective-permute-start | bytes 1544 | tf_op jit(solution)/shard_map/ppermute | solution.py:32
  37.4 0.9 %collective-permute-done.15 = f32[1,128]{1,0:T(1,128)S(1)} collective-permute-done((f32[1,128]{1,0:T(1,128)S(1)}, f32[1,128]{1,0:T(1,128)S(1)}, u32[]{:S(2)}, u32[]{:S(2)}) %collective-permute-start.15) | collective-permute-done | bytes 544 | tf_op jit(solution)/shard_map/ppermute | solution.py:32
  38.3 0.7 %collective-permute-done.14 = f32[1,128]{1,0:T(1,128)S(1)} collective-permute-done((f32[1,128]{1,0:T(1,128)S(1)}, f32[1,128]{1,0:T(1,128)S(1)}, u32[]{:S(2)}, u32[]{:S(2)}) %collective-permute-start.14) | collective-permute-done | bytes 544 | tf_op jit(solution)/shard_map/ppermute | solution.py:32
  39.0 1.4 %collective-permute-done.13 = f32[1,128]{1,0:T(1,128)S(1)} collective-permute-done((f32[1,128]{1,0:T(1,128)S(1)}, f32[1,128]{1,0:T(1,128)S(1)}, u32[]{:S(2)}, u32[]{:S(2)}) %collective-permute-start.13) | collective-permute-done | bytes 544 | tf_op jit(solution)/shard_map/ppermute | solution.py:32
  40.4 0.7 %multiply_bitcast_fusion = f32[1,512,128]{2,1,0:T(8,128)} fusion(f32[512,128]{1,0:T(8,128)S(1)} %get-tuple-element.25, f32[128]{0:T(128)S(1)} %divide_bitcast_fusion), kind=kLoop, calls=%fused_computation | loop fusion | flops 65536 | bytes 524800 | tf_op jit(solution)/shard_map/broadcast_in_dim | solution.py:205
  (5 shorter events, 0.0 us)
Async XLA Ops:
  0.0 18.8 %collective-permute-start.7 = (bf16[8,128,128]{2,1,0:T(8,128)(2,1)}, bf16[8,128,128]{2,1,0:T(8,128)(2,1)S(1)}, u32[]{:S(2)}, u32[]{:S(2)}) collective-permute-start(bf16[8,128,128]{2,1,0:T(8,128)(2,1)} %bitcast.14), channel_id=1, source_target_pairs={{0,8},{8,0},{16,24},{24,16},{1,9},{9,1},{17,25},{25,17},{2,10},{10... | collective-permute-start | bytes 786440 | tf_op jit(solution)/shard_map/ppermute | solution.py:21
  0.5 17.8 %collective-permute-start = (bf16[8,128,128]{2,1,0:T(8,128)(2,1)}, bf16[8,128,128]{2,1,0:T(8,128)(2,1)S(1)}, u32[]{:S(2)}, u32[]{:S(2)}) collective-permute-start(bf16[8,128,128]{2,1,0:T(8,128)(2,1)} %bitcast.15), channel_id=1, source_target_pairs={{0,2},{1,3},{2,0},{3,1},{4,6},{5,7},{6,4},{7,5},{8,10},{9,11},{10,... | collective-permute-start | bytes 786440 | tf_op jit(solution)/shard_map/ppermute | solution.py:21
  4.7 0.7 %copy-start.1 = (s32[1,8]{1,0:T(1,128)S(1)}, s32[1,8]{1,0:T(1,128)}, u32[]{:S(2)}) copy-start(s32[1,8]{1,0:T(1,128)} %param.5) | copy-start | bytes 100
  5.4 1.8 %collective-permute-start.1 = (s32[1,8]{1,0:T(1,128)S(1)}, s32[1,8]{1,0:T(1,128)S(1)}, u32[]{:S(2)}, u32[]{:S(2)}) collective-permute-start(s32[1,8]{1,0:T(1,128)S(1)} %compare_select_fusion), channel_id=1, source_target_pairs={{0,8},{8,0},{16,24},{24,16},{1,9},{9,1},{17,25},{25,17},{2,10},{10... | collective-permute-start | bytes 104 | tf_op jit(solution)/shard_map/ppermute | solution.py:21
  5.6 4.5 %collective-permute-start.3 = (bf16[256,128]{1,0:T(8,128)(2,1)}, bf16[256,128]{1,0:T(8,128)(2,1)S(1)}, u32[]{:S(2)}, u32[]{:S(2)}) collective-permute-start(bf16[256,128]{1,0:T(8,128)(2,1)} %param.7), channel_id=1, source_target_pairs={{0,4},{4,0},{1,5},{5,1},{2,6},{6,2},{3,7},{7,3},{8,12},{12,8},{9,1... | collective-permute-start | bytes 196616 | tf_op jit(solution)/shard_map/ppermute | solution.py:21
  7.1 12.8 %copy-start = (bf16[1,8,128,128]{3,2,1,0:T(8,128)(2,1)S(1)}, bf16[1,8,128,128]{3,2,1,0:T(8,128)(2,1)}, u32[]{:S(2)}) copy-start(bf16[1,8,128,128]{3,2,1,0:T(8,128)(2,1)} %param.4) | copy-start | bytes 786436
  7.1 9.9 %collective-permute-start.2 = (s32[2,8]{1,0:T(2,128)S(1)}, s32[2,8]{1,0:T(2,128)S(1)}, u32[]{:S(2)}, u32[]{:S(2)}) collective-permute-start(s32[2,8]{1,0:T(2,128)S(1)} %pad_add_fusion.1), channel_id=1, source_target_pairs={{0,2},{1,3},{2,0},{3,1},{4,6},{5,7},{6,4},{7,5},{8,10},{9,11},{10,... | collective-permute-start | bytes 200 | tf_op jit(solution)/shard_map/ppermute | solution.py:21
  11.0 7.3 %collective-permute-start.5 = (bf16[256,128]{1,0:T(8,128)(2,1)S(1)}, bf16[256,128]{1,0:T(8,128)(2,1)S(1)}, u32[]{:S(2)}, u32[]{:S(2)}) collective-permute-start(bf16[256,128]{1,0:T(8,128)(2,1)S(1)} %bitcast.20), channel_id=1, source_target_pairs={{0,1},{1,0},{2,3},{3,2},{4,5},{5,4},{6,7},{7,6},{8,9},{9,8},{10,11... | collective-permute-start | bytes 196616 | tf_op jit(solution)/shard_map/ppermute | solution.py:21
  12.6 5.7 %collective-permute-start.4 = (bf16[256,128]{1,0:T(8,128)(2,1)S(1)}, bf16[256,128]{1,0:T(8,128)(2,1)S(1)}, u32[]{:S(2)}, u32[]{:S(2)}) collective-permute-start(bf16[256,128]{1,0:T(8,128)(2,1)S(1)} %bitcast.17), channel_id=1, source_target_pairs={{0,8},{8,0},{16,24},{24,16},{1,9},{9,1},{17,25},{25,17},{2,10},{10... | collective-permute-start | bytes 196616 | tf_op jit(solution)/shard_map/ppermute | solution.py:21
  18.3 1.6 %collective-permute-start.8 = (bf16[8,128,128]{2,1,0:T(8,128)(2,1)S(1)}, bf16[8,128,128]{2,1,0:T(8,128)(2,1)S(1)}, u32[]{:S(2)}, u32[]{:S(2)}) collective-permute-start(bf16[8,128,128]{2,1,0:T(8,128)(2,1)S(1)} %collective-permute-done.refs_6_), channel_id=1, source_target_pairs={{0,8},{8,0},{16,24},{24,16},{1,9},{9,1},{17,25},{25,17},{2,10},{10... | collective-permute-start | bytes 786440 | tf_op jit(solution)/shard_map/ppermute | solution.py:21
  18.3 1.6 %collective-permute-start.6 = (bf16[256,128]{1,0:T(8,128)(2,1)S(1)}, bf16[256,128]{1,0:T(8,128)(2,1)S(1)}, u32[]{:S(2)}, u32[]{:S(2)}) collective-permute-start(bf16[256,128]{1,0:T(8,128)(2,1)S(1)} %collective-permute-done.5.refs_2_), channel_id=1, source_target_pairs={{0,8},{8,0},{16,24},{24,16},{1,9},{9,1},{17,25},{25,17},{2,10},{10... | collective-permute-start | bytes 196616 | tf_op jit(solution)/shard_map/ppermute | solution.py:21
  21.5 7.2 %collective-permute-start.9 = (s32[328,128]{1,0:T(8,128)S(1)}, s32[328,128]{1,0:T(8,128)S(1)}, u32[]{:S(2)}, u32[]{:S(2)}) collective-permute-start(s32[328,128]{1,0:T(8,128)S(1)} %get-tuple-element.22), channel_id=1, source_target_pairs={{0,1},{1,0},{2,3},{3,2},{4,5},{5,4},{6,7},{7,6},{8,9},{9,8},{10,11... | collective-permute-start | bytes 503816 | tf_op jit(solution)/shard_map/ppermute | solution.py:32
  21.7 7.0 %collective-permute-start.10 = (s32[328,128]{1,0:T(8,128)S(1)}, s32[328,128]{1,0:T(8,128)S(1)}, u32[]{:S(2)}, u32[]{:S(2)}) collective-permute-start(s32[328,128]{1,0:T(8,128)S(1)} %get-tuple-element.23), channel_id=1, source_target_pairs={{0,16},{1,17},{2,18},{3,19},{4,20},{5,21},{6,22},{7,23},{8,24},{9,... | collective-permute-start | bytes 503816 | tf_op jit(solution)/shard_map/ppermute | solution.py:32
  23.2 9.3 %collective-permute-start.11 = (s32[328,128]{1,0:T(8,128)S(1)}, s32[328,128]{1,0:T(8,128)S(1)}, u32[]{:S(2)}, u32[]{:S(2)}) collective-permute-start(s32[328,128]{1,0:T(8,128)S(1)} %get-tuple-element.24), channel_id=1, source_target_pairs={{0,17},{1,16},{2,19},{3,18},{4,21},{5,20},{6,23},{7,22},{8,25},{9,... | collective-permute-start | bytes 503816 | tf_op jit(solution)/shard_map/ppermute | solution.py:32
  32.7 1.2 %collective-permute-start.12 = (f32[1,128]{1,0:T(1,128)S(1)}, f32[1,128]{1,0:T(1,128)S(1)}, u32[]{:S(2)}, u32[]{:S(2)}) collective-permute-start(f32[1,128]{1,0:T(1,128)S(1)} %get-tuple-element.26), channel_id=1, source_target_pairs={{0,8},{8,0},{16,24},{24,16},{1,9},{9,1},{17,25},{25,17},{2,10},{10... | collective-permute-start | bytes 1544 | tf_op jit(solution)/shard_map/ppermute | solution.py:21
  33.9 4.4 %collective-permute-start.15 = (f32[1,128]{1,0:T(1,128)S(1)}, f32[1,128]{1,0:T(1,128)S(1)}, u32[]{:S(2)}, u32[]{:S(2)}) collective-permute-start(f32[1,128]{1,0:T(1,128)S(1)} %add.33), channel_id=1, source_target_pairs={{0,20},{1,21},{2,22},{3,23},{4,16},{5,17},{6,18},{7,19},{8,28},{9,... | collective-permute-start | bytes 1544 | tf_op jit(solution)/shard_map/ppermute | solution.py:32
  35.5 3.5 %collective-permute-start.14 = (f32[1,128]{1,0:T(1,128)S(1)}, f32[1,128]{1,0:T(1,128)S(1)}, u32[]{:S(2)}, u32[]{:S(2)}) collective-permute-start(f32[1,128]{1,0:T(1,128)S(1)} %add.33), channel_id=1, source_target_pairs={{0,16},{1,17},{2,18},{3,19},{4,20},{5,21},{6,22},{7,23},{8,24},{9,... | collective-permute-start | bytes 1544 | tf_op jit(solution)/shard_map/ppermute | solution.py:32
  36.9 3.5 %collective-permute-start.13 = (f32[1,128]{1,0:T(1,128)S(1)}, f32[1,128]{1,0:T(1,128)S(1)}, u32[]{:S(2)}, u32[]{:S(2)}) collective-permute-start(f32[1,128]{1,0:T(1,128)S(1)} %add.33), channel_id=1, source_target_pairs={{0,4},{1,5},{2,6},{3,7},{4,0},{5,1},{6,2},{7,3},{8,12},{9,13},{10,... | collective-permute-start | bytes 1544 | tf_op jit(solution)/shard_map/ppermute | solution.py:32

commit v6 on v5

--- a/solution.py
+++ b/solution.py
@@ -2,12 +2,14 @@
 
 import jax
 import jax.numpy as jnp
+import numpy as np
 from jax import lax
 from jax.experimental import pallas as pl
 from jax.experimental.pallas import tpu as pltpu
 from jax.sharding import PartitionSpec as P
 
 IB = 16
+AXES = ("layer", "row", "col")
 BITS = 20
 VMEM = pl.BlockSpec(memory_space=pltpu.VMEM)
 SMEM = pl.BlockSpec(memory_space=pltpu.SMEM)
@@ -21,15 +23,24 @@
     return lax.ppermute(x, axis, [(i, i ^ mask) for i in range(lax.axis_size(axis))])
 
 
-def grid_permute(x, layer_mask, row_mask, col_mask):
-    n, m, c = (lax.axis_size(a) for a in ("layer", "row", "col"))
-    pairs = [
-        ((i * m + j) * c + k, ((i ^ layer_mask) * m + (j ^ row_mask)) * c + (k ^ col_mask))
-        for i in range(n)
-        for j in range(m)
-        for k in range(c)
-    ]
-    return lax.ppermute(x, ("layer", "row", "col"), pairs)
+def grid_permute(x, masks, other_masks=None):
+    sizes = [lax.axis_size(a) for a in AXES]
+    pairs = []
+    for source, at in enumerate(np.ndindex(*sizes)):
+        by = other_masks if other_masks and at[0] % 2 else masks
+        target = [i ^ m for i, m in zip(at, by, strict=True)]
+        pairs.append((source, int(np.ravel_multi_index(target, sizes))))
+    return lax.ppermute(x, AXES, pairs)
+
+
+def sum_over_devices(x):
+    n_layer, n_row, _ = (lax.axis_size(a) for a in AXES)
+    chips = [(i, j, 0) for i in range(0, n_layer, 2) for j in range(n_row)][:0:-1]
+    got = [grid_permute(x, chips.pop(0))] if len(chips) % 2 else []
+    x = x + xor_permute(x, "layer", 1)
+    got += [grid_permute(x, *chips[k : k + 2]) for k in range(0, len(chips), 2)]
+    got = sum(got)
+    return x + (got + xor_permute(got, "layer", 1))
 
 
 def power_of_two(k):
@@ -180,7 +191,7 @@
     panels = [x for p in panels for x in (p, other(p))]
     parts = products(masks, ids, b_refs, panels)
 
-    parts = [parts[0]] + [grid_permute(parts[k], 2 * (k // 2), 0, k % 2) for k in range(1, n_layer)]
+    parts = [parts[0]] + [grid_permute(parts[k], (2 * (k // 2), 0, k % 2)) for k in range(1, n_layer)]
     sq, col_sum = pl.pallas_call(
         square_kernel,
         out_shape=(
@@ -192,15 +203,7 @@
         name="squares",
     )(*(pin(x) for x in parts))
 
-    col_sum = col_sum + xor_permute(col_sum, "layer", 1)
-    others = [
-        grid_permute(col_sum, i, j, 0)
-        for i in range(0, n_layer, 2)
-        for j in range(n_row)
-        if i or j
-    ]
-    for other in others:
-        col_sum = col_sum + other
+    col_sum = sum_over_devices(col_sum)
     scale = 1.0 / (col_sum * (1.0 / (n_row * IB * block)) + 1e-06)
     return (sq * scale)[None]
 

time: 41.4 us -> 40.1 us (0.969)
  waiting for transfers between devices: 20.3 us -> 19.5 us
  starting transfers between devices: 15.5 us -> 15 us
    ppermute x6 -> x5, waiting for transfers between devices: 10.4 us -> 9.57 us  [grid_permute(): return lax.ppermute(x, AXES, pairs)]
    ppermute x6 -> x5, starting transfers between devices: 7.04 us -> 6.6 us  [grid_permute(): return lax.ppermute(x, AXES, pairs)]
    ppermute x10 -> x11, waiting for transfers between devices: 9.89 us -> 9.9 us  [xor_permute(): lax.ppermute(x, axis, [(i, i ^ mask) for i in range(lax.axis_size(axis))])]
    ppermute x10 -> x11, starting transfers between devices: 8.41 us -> 8.41 us  [xor_permute(): lax.ppermute(x, axis, [(i, i ^ mask) for i in range(lax.axis_size(axis))])]
  transfers between devices with their start and end apart: 16 -> 16, of which waited for: 10 -> 9; matrix products, arithmetic and copies ran while one was open for 4% -> 4% of each run, Pallas kernels for 0% -> 0%
where the time goes in v6:
time: 40.1 us; the launch traced here: 39.9 us
  waiting for transfers between devices  19.5 us (49%)
  starting transfers between devices  15 us (37%)
  other arithmetic  2.19 us (5%)
  Pallas kernels  1.8 us (4%)
  between operations  0.72 us (2%)
  local copies, waits for them, and re-layouts  0.67 us (2%)
    ppermute x11, waiting for transfers between devices, xor_permute(): lax.ppermute(x, axis, [(i, i ^ mask) for i in range(lax.axis_size(axis))])  9.9 us
    ppermute x5, waiting for transfers between devices, grid_permute(): return lax.ppermute(x, AXES, pairs)  9.57 us
    ppermute x11, starting transfers between devices, xor_permute(): lax.ppermute(x, axis, [(i, i ^ mask) for i in range(lax.axis_size(axis))])  8.41 us
    ppermute x5, starting transfers between devices, grid_permute(): return lax.ppermute(x, AXES, pairs)  6.6 us
    pallas_call x1, Pallas kernels, products(): pl.pallas_call(functools.partial(product_kernel, masks, n_layer, n_row, n...  1.59 us
    concatenate x1, other arithmetic, body(): b_rows = jnp.concatenate(b_rows).reshape(-1, 2, *b_panel.shape[-1:] * 2)  0.85 us
  transfers between devices with their start and end apart: 16, of which 9 were waited for; matrix products, arithmetic and copies ran while one was open for 4% of the time, Pallas kernels for 0%

profile of v6, /device:TPU:0, one launch (start us, length us, event | category | flops | bytes accessed | tf_op | source)
XLA Modules:
  0.0 39.9 jit_solution(16665736198176826360)
XLA Ops:
  0.0 0.5 %collective-permute-start.7 = (bf16[8,128,128]{2,1,0:T(8,128)(2,1)}, bf16[8,128,128]{2,1,0:T(8,128)(2,1)S(1)}, u32[]{:S(2)}, u32[]{:S(2)}) collective-permute-start(bf16[8,128,128]{2,1,0:T(8,128)(2,1)} %bitcast.14), channel_id=1, source_target_pairs={{0,8},{8,0},{16,24},{24,16},{1,9},{9,1},{17,25},{25,17},{2,10},{10... | collective-permute-start | bytes 786440 | tf_op jit(solution)/shard_map/ppermute | solution.py:23
  0.5 3.6 %collective-permute-start = (bf16[8,128,128]{2,1,0:T(8,128)(2,1)}, bf16[8,128,128]{2,1,0:T(8,128)(2,1)S(1)}, u32[]{:S(2)}, u32[]{:S(2)}) collective-permute-start(bf16[8,128,128]{2,1,0:T(8,128)(2,1)} %bitcast.15), channel_id=1, source_target_pairs={{0,2},{1,3},{2,0},{3,1},{4,6},{5,7},{6,4},{7,5},{8,10},{9,11},{10,... | collective-permute-start | bytes 786440 | tf_op jit(solution)/shard_map/ppermute | solution.py:23
  4.7 0.0 copy-start.1
  4.7 0.6 %copy-done.1 = s32[1,8]{1,0:T(1,128)S(1)} copy-done((s32[1,8]{1,0:T(1,128)S(1)}, s32[1,8]{1,0:T(1,128)}, u32[]{:S(2)}) %copy-start.1) | copy-done | bytes 56
  5.4 0.2 collective-permute-start.1
  5.6 1.5 %collective-permute-start.3 = (bf16[256,128]{1,0:T(8,128)(2,1)}, bf16[256,128]{1,0:T(8,128)(2,1)S(1)}, u32[]{:S(2)}, u32[]{:S(2)}) collective-permute-start(bf16[256,128]{1,0:T(8,128)(2,1)} %param.7), channel_id=1, source_target_pairs={{0,4},{4,0},{1,5},{5,1},{2,6},{6,2},{3,7},{7,3},{8,12},{12,8},{9,1... | collective-permute-start | bytes 196616 | tf_op jit(solution)/shard_map/ppermute | solution.py:23
  7.1 0.0 collective-permute-done.1
  7.1 0.0 copy-start
  7.1 0.4 %collective-permute-start.2 = (s32[2,8]{1,0:T(2,128)S(1)}, s32[2,8]{1,0:T(2,128)S(1)}, u32[]{:S(2)}, u32[]{:S(2)}) collective-permute-start(s32[2,8]{1,0:T(2,128)S(1)} %pad_add_fusion.1), channel_id=1, source_target_pairs={{0,2},{1,3},{2,0},{3,1},{4,6},{5,7},{6,4},{7,5},{8,10},{9,11},{10,... | collective-permute-start | bytes 200 | tf_op jit(solution)/shard_map/ppermute | solution.py:23
  7.5 2.5 %collective-permute-done.3 = bf16[256,128]{1,0:T(8,128)(2,1)S(1)} collective-permute-done((bf16[256,128]{1,0:T(8,128)(2,1)}, bf16[256,128]{1,0:T(8,128)(2,1)S(1)}, u32[]{:S(2)}, u32[]{:S(2)}) %collective-permute-start.3) | collective-permute-done | bytes 65568 | tf_op jit(solution)/shard_map/ppermute | solution.py:23
  10.1 0.8 %pad_maximum_fusion = bf16[512,128]{1,0:T(8,128)(2,1)S(1)} fusion(bf16[256,128]{1,0:T(8,128)(2,1)S(1)} %collective-permute-done.3, bf16[256,128]{1,0:T(8,128)(2,1)} %param.7), kind=kLoop, calls=%fused_computation.1 | loop fusion | flops 262144 | bytes 262144 | tf_op jit(solution)/shard_map/concatenate | solution.py:180
  11.0 1.6 %collective-permute-start.5 = (bf16[256,128]{1,0:T(8,128)(2,1)S(1)}, bf16[256,128]{1,0:T(8,128)(2,1)S(1)}, u32[]{:S(2)}, u32[]{:S(2)}) collective-permute-start(bf16[256,128]{1,0:T(8,128)(2,1)S(1)} %bitcast.20), channel_id=1, source_target_pairs={{0,1},{1,0},{2,3},{3,2},{4,5},{5,4},{6,7},{7,6},{8,9},{9,8},{10,11... | collective-permute-start | bytes 196616 | tf_op jit(solution)/shard_map/ppermute | solution.py:23
  12.6 0.0 collective-permute-start.4
  12.6 4.4 %collective-permute-done.2 = s32[2,8]{1,0:T(2,128)S(1)} collective-permute-done((s32[2,8]{1,0:T(2,128)S(1)}, s32[2,8]{1,0:T(2,128)S(1)}, u32[]{:S(2)}, u32[]{:S(2)}) %collective-permute-start.2) | collective-permute-done | bytes 96 | tf_op jit(solution)/shard_map/ppermute | solution.py:23
  17.0 0.6 %pad_add_fusion.ids_ref = s32[4,8]{1,0:T(4,128)} fusion(s32[2,8]{1,0:T(2,128)S(1)} %collective-permute-done.2, s32[1,8]{1,0:T(1,128)S(1)} %collective-permute-done.1, s32[1,8]{1,0:T(1,128)S(1)} %compare_select_fusion), kind=kLoop, calls=%fused_computation.2 | loop fusion | flops 64 | bytes 256 | tf_op jit(solution)/shard_map/concatenate | solution.py:171
  17.6 0.7 %collective-permute-done.5.refs_2_ = bf16[256,128]{1,0:T(8,128)(2,1)S(1)} collective-permute-done((bf16[256,128]{1,0:T(8,128)(2,1)S(1)}, bf16[256,128]{1,0:T(8,128)(2,1)S(1)}, u32[]{:S(2)}, u32[]{:S(2)}) %collective-permute-start.5) | collective-permute-done | bytes 65568 | tf_op jit(solution)/shard_map/ppermute | solution.py:23
  18.3 0.0 collective-permute-done.4.refs_1_
  18.3 0.0 collective-permute-done.refs_6_
  18.3 0.0 collective-permute-start.8
  18.3 0.5 %collective-permute-start.6 = (bf16[256,128]{1,0:T(8,128)(2,1)S(1)}, bf16[256,128]{1,0:T(8,128)(2,1)S(1)}, u32[]{:S(2)}, u32[]{:S(2)}) collective-permute-start(bf16[256,128]{1,0:T(8,128)(2,1)S(1)} %collective-permute-done.5.refs_2_), channel_id=1, source_target_pairs={{0,8},{8,0},{16,24},{24,16},{1,9},{9,1},{17,25},{25,17},{2,10},{10... | collective-permute-start | bytes 196616 | tf_op jit(solution)/shard_map/ppermute | solution.py:23
  18.8 0.0 collective-permute-done.7.refs_5_
  18.8 1.1 %collective-permute-done.6.refs_3_ = bf16[256,128]{1,0:T(8,128)(2,1)S(1)} collective-permute-done((bf16[256,128]{1,0:T(8,128)(2,1)S(1)}, bf16[256,128]{1,0:T(8,128)(2,1)S(1)}, u32[]{:S(2)}, u32[]{:S(2)}) %collective-permute-start.6) | collective-permute-done | bytes 65568 | tf_op jit(solution)/shard_map/ppermute | solution.py:23
  19.9 0.0 collective-permute-done.8.refs_7_
  19.9 0.0 copy-done
  19.9 1.6 %partial_rows.1 = (f32[512,128]{1,0:T(8,128)S(1)}, s32[328,128]{1,0:T(8,128)S(1)}, s32[328,128]{1,0:T(8,128)S(1)}, s32[328,128]{1,0:T(8,128)S(1)}) custom-call(s32[4,8]{1,0:T(4,128)} %pad_add_fusion.ids_ref, bf16[256,128]{1,0:T(8,128)(2,1)S(1)} %bitcast.18, bf16[256,128]{1,0:T(8,128)(2,1)S(1)} %collective-permute-done.4.refs_1_, ...), custom_call_target="tpu_custom_call" | custom-call | tf_op jit(solution)/shard_map/partial_rows/pallas_call | solution.py:143
  21.5 0.2 collective-permute-start.9
  21.7 1.5 %collective-permute-start.10 = (s32[328,128]{1,0:T(8,128)S(1)}, s32[328,128]{1,0:T(8,128)S(1)}, u32[]{:S(2)}, u32[]{:S(2)}) collective-permute-start(s32[328,128]{1,0:T(8,128)S(1)} %get-tuple-element.23), channel_id=1, source_target_pairs={{0,16},{1,17},{2,18},{3,19},{4,20},{5,21},{6,22},{7,23},{8,24},{9,... | collective-permute-start | bytes 503816 | tf_op jit(solution)/shard_map/ppermute | solution.py:33
  23.2 1.9 %collective-permute-start.11 = (s32[328,128]{1,0:T(8,128)S(1)}, s32[328,128]{1,0:T(8,128)S(1)}, u32[]{:S(2)}, u32[]{:S(2)}) collective-permute-start(s32[328,128]{1,0:T(8,128)S(1)} %get-tuple-element.24), channel_id=1, source_target_pairs={{0,17},{1,16},{2,19},{3,18},{4,21},{5,20},{6,23},{7,22},{8,25},{9,... | collective-permute-start | bytes 503816 | tf_op jit(solution)/shard_map/ppermute | solution.py:33
  25.1 3.6 %collective-permute-done.9.refs_0_ = s32[328,128]{1,0:T(8,128)S(1)} collective-permute-done((s32[328,128]{1,0:T(8,128)S(1)}, s32[328,128]{1,0:T(8,128)S(1)}, u32[]{:S(2)}, u32[]{:S(2)}) %collective-permute-start.9) | collective-permute-done | bytes 167968 | tf_op jit(solution)/shard_map/ppermute | solution.py:33
  28.7 0.0 collective-permute-done.10.refs_1_
  28.7 3.8 %collective-permute-done.11.refs_2_ = s32[328,128]{1,0:T(8,128)S(1)} collective-permute-done((s32[328,128]{1,0:T(8,128)S(1)}, s32[328,128]{1,0:T(8,128)S(1)}, u32[]{:S(2)}, u32[]{:S(2)}) %collective-permute-start.11) | collective-permute-done | bytes 167968 | tf_op jit(solution)/shard_map/ppermute | solution.py:33
  32.5 0.2 squares.1
  32.7 0.1 collective-permute-start.12
  32.8 1.7 %collective-permute-start.13 = (f32[1,128]{1,0:T(1,128)S(1)}, f32[1,128]{1,0:T(1,128)S(1)}, u32[]{:S(2)}, u32[]{:S(2)}) collective-permute-start(f32[1,128]{1,0:T(1,128)S(1)} %get-tuple-element.26), channel_id=1, source_target_pairs={{0,20},{1,21},{2,22},{3,23},{4,16},{5,17},{6,18},{7,19},{8,28},{9,... | collective-permute-start | bytes 1544 | tf_op jit(solution)/shard_map/ppermute | solution.py:33
  34.5 0.0 collective-permute-done.12
  34.5 1.4 %collective-permute-start.14 = (f32[1,128]{1,0:T(1,128)S(1)}, f32[1,128]{1,0:T(1,128)S(1)}, u32[]{:S(2)}, u32[]{:S(2)}) collective-permute-start(f32[1,128]{1,0:T(1,128)S(1)} %add.33), channel_id=1, source_target_pairs={{0,16},{1,17},{2,18},{3,19},{4,20},{5,21},{6,22},{7,23},{8,12},{9,... | collective-permute-start | bytes 1544 | tf_op jit(solution)/shard_map/ppermute | solution.py:33
  35.9 1.4 %collective-permute-done.13 = f32[1,128]{1,0:T(1,128)S(1)} collective-permute-done((f32[1,128]{1,0:T(1,128)S(1)}, f32[1,128]{1,0:T(1,128)S(1)}, u32[]{:S(2)}, u32[]{:S(2)}) %collective-permute-start.13) | collective-permute-done | bytes 544 | tf_op jit(solution)/shard_map/ppermute | solution.py:33
  37.3 0.7 %collective-permute-done.14 = f32[1,128]{1,0:T(1,128)S(1)} collective-permute-done((f32[1,128]{1,0:T(1,128)S(1)}, f32[1,128]{1,0:T(1,128)S(1)}, u32[]{:S(2)}, u32[]{:S(2)}) %collective-permute-start.14) | collective-permute-done | bytes 544 | tf_op jit(solution)/shard_map/ppermute | solution.py:33
  38.0 0.0 collective-permute-start.15
  38.0 1.1 %collective-permute-done.15 = f32[1,128]{1,0:T(1,128)S(1)} collective-permute-done((f32[1,128]{1,0:T(1,128)S(1)}, f32[1,128]{1,0:T(1,128)S(1)}, u32[]{:S(2)}, u32[]{:S(2)}) %collective-permute-start.15) | collective-permute-done | bytes 544 | tf_op jit(solution)/shard_map/ppermute | solution.py:23
  39.1 0.7 %multiply_bitcast_fusion = f32[1,512,128]{2,1,0:T(8,128)} fusion(f32[512,128]{1,0:T(8,128)S(1)} %get-tuple-element.25, f32[128]{0:T(128)S(1)} %divide_bitcast_fusion), kind=kLoop, calls=%fused_computation | loop fusion | flops 65536 | bytes 524800 | tf_op jit(solution)/shard_map/broadcast_in_dim | solution.py:208
  (6 shorter events, 0.0 us)
Async XLA Ops:
  0.0 18.8 %collective-permute-start.7 = (bf16[8,128,128]{2,1,0:T(8,128)(2,1)}, bf16[8,128,128]{2,1,0:T(8,128)(2,1)S(1)}, u32[]{:S(2)}, u32[]{:S(2)}) collective-permute-start(bf16[8,128,128]{2,1,0:T(8,128)(2,1)} %bitcast.14), channel_id=1, source_target_pairs={{0,8},{8,0},{16,24},{24,16},{1,9},{9,1},{17,25},{25,17},{2,10},{10... | collective-permute-start | bytes 786440 | tf_op jit(solution)/shard_map/ppermute | solution.py:23
  0.5 17.8 %collective-permute-start = (bf16[8,128,128]{2,1,0:T(8,128)(2,1)}, bf16[8,128,128]{2,1,0:T(8,128)(2,1)S(1)}, u32[]{:S(2)}, u32[]{:S(2)}) collective-permute-start(bf16[8,128,128]{2,1,0:T(8,128)(2,1)} %bitcast.15), channel_id=1, source_target_pairs={{0,2},{1,3},{2,0},{3,1},{4,6},{5,7},{6,4},{7,5},{8,10},{9,11},{10,... | collective-permute-start | bytes 786440 | tf_op jit(solution)/shard_map/ppermute | solution.py:23
  4.7 0.7 %copy-start.1 = (s32[1,8]{1,0:T(1,128)S(1)}, s32[1,8]{1,0:T(1,128)}, u32[]{:S(2)}) copy-start(s32[1,8]{1,0:T(1,128)} %param.5) | copy-start | bytes 100
  5.4 1.8 %collective-permute-start.1 = (s32[1,8]{1,0:T(1,128)S(1)}, s32[1,8]{1,0:T(1,128)S(1)}, u32[]{:S(2)}, u32[]{:S(2)}) collective-permute-start(s32[1,8]{1,0:T(1,128)S(1)} %compare_select_fusion), channel_id=1, source_target_pairs={{0,8},{8,0},{16,24},{24,16},{1,9},{9,1},{17,25},{25,17},{2,10},{10... | collective-permute-start | bytes 104 | tf_op jit(solution)/shard_map/ppermute | solution.py:23
  5.6 4.5 %collective-permute-start.3 = (bf16[256,128]{1,0:T(8,128)(2,1)}, bf16[256,128]{1,0:T(8,128)(2,1)S(1)}, u32[]{:S(2)}, u32[]{:S(2)}) collective-permute-start(bf16[256,128]{1,0:T(8,128)(2,1)} %param.7), channel_id=1, source_target_pairs={{0,4},{4,0},{1,5},{5,1},{2,6},{6,2},{3,7},{7,3},{8,12},{12,8},{9,1... | collective-permute-start | bytes 196616 | tf_op jit(solution)/shard_map/ppermute | solution.py:23
  7.1 12.8 %copy-start = (bf16[1,8,128,128]{3,2,1,0:T(8,128)(2,1)S(1)}, bf16[1,8,128,128]{3,2,1,0:T(8,128)(2,1)}, u32[]{:S(2)}) copy-start(bf16[1,8,128,128]{3,2,1,0:T(8,128)(2,1)} %param.4) | copy-start | bytes 786436
  7.1 9.9 %collective-permute-start.2 = (s32[2,8]{1,0:T(2,128)S(1)}, s32[2,8]{1,0:T(2,128)S(1)}, u32[]{:S(2)}, u32[]{:S(2)}) collective-permute-start(s32[2,8]{1,0:T(2,128)S(1)} %pad_add_fusion.1), channel_id=1, source_target_pairs={{0,2},{1,3},{2,0},{3,1},{4,6},{5,7},{6,4},{7,5},{8,10},{9,11},{10,... | collective-permute-start | bytes 200 | tf_op jit(solution)/shard_map/ppermute | solution.py:23
  11.0 7.3 %collective-permute-start.5 = (bf16[256,128]{1,0:T(8,128)(2,1)S(1)}, bf16[256,128]{1,0:T(8,128)(2,1)S(1)}, u32[]{:S(2)}, u32[]{:S(2)}) collective-permute-start(bf16[256,128]{1,0:T(8,128)(2,1)S(1)} %bitcast.20), channel_id=1, source_target_pairs={{0,1},{1,0},{2,3},{3,2},{4,5},{5,4},{6,7},{7,6},{8,9},{9,8},{10,11... | collective-permute-start | bytes 196616 | tf_op jit(solution)/shard_map/ppermute | solution.py:23
  12.6 5.7 %collective-permute-start.4 = (bf16[256,128]{1,0:T(8,128)(2,1)S(1)}, bf16[256,128]{1,0:T(8,128)(2,1)S(1)}, u32[]{:S(2)}, u32[]{:S(2)}) collective-permute-start(bf16[256,128]{1,0:T(8,128)(2,1)S(1)} %bitcast.17), channel_id=1, source_target_pairs={{0,8},{8,0},{16,24},{24,16},{1,9},{9,1},{17,25},{25,17},{2,10},{10... | collective-permute-start | bytes 196616 | tf_op jit(solution)/shard_map/ppermute | solution.py:23
  18.3 1.6 %collective-permute-start.8 = (bf16[8,128,128]{2,1,0:T(8,128)(2,1)S(1)}, bf16[8,128,128]{2,1,0:T(8,128)(2,1)S(1)}, u32[]{:S(2)}, u32[]{:S(2)}) collective-permute-start(bf16[8,128,128]{2,1,0:T(8,128)(2,1)S(1)} %collective-permute-done.refs_6_), channel_id=1, source_target_pairs={{0,8},{8,0},{16,24},{24,16},{1,9},{9,1},{17,25},{25,17},{2,10},{10... | collective-permute-start | bytes 786440 | tf_op jit(solution)/shard_map/ppermute | solution.py:23
  18.3 1.6 %collective-permute-start.6 = (bf16[256,128]{1,0:T(8,128)(2,1)S(1)}, bf16[256,128]{1,0:T(8,128)(2,1)S(1)}, u32[]{:S(2)}, u32[]{:S(2)}) collective-permute-start(bf16[256,128]{1,0:T(8,128)(2,1)S(1)} %collective-permute-done.5.refs_2_), channel_id=1, source_target_pairs={{0,8},{8,0},{16,24},{24,16},{1,9},{9,1},{17,25},{25,17},{2,10},{10... | collective-permute-start | bytes 196616 | tf_op jit(solution)/shard_map/ppermute | solution.py:23
  21.5 7.2 %collective-permute-start.9 = (s32[328,128]{1,0:T(8,128)S(1)}, s32[328,128]{1,0:T(8,128)S(1)}, u32[]{:S(2)}, u32[]{:S(2)}) collective-permute-start(s32[328,128]{1,0:T(8,128)S(1)} %get-tuple-element.22), channel_id=1, source_target_pairs={{0,1},{1,0},{2,3},{3,2},{4,5},{5,4},{6,7},{7,6},{8,9},{9,8},{10,11... | collective-permute-start | bytes 503816 | tf_op jit(solution)/shard_map/ppermute | solution.py:33
  21.7 7.0 %collective-permute-start.10 = (s32[328,128]{1,0:T(8,128)S(1)}, s32[328,128]{1,0:T(8,128)S(1)}, u32[]{:S(2)}, u32[]{:S(2)}) collective-permute-start(s32[328,128]{1,0:T(8,128)S(1)} %get-tuple-element.23), channel_id=1, source_target_pairs={{0,16},{1,17},{2,18},{3,19},{4,20},{5,21},{6,22},{7,23},{8,24},{9,... | collective-permute-start | bytes 503816 | tf_op jit(solution)/shard_map/ppermute | solution.py:33
  23.2 9.3 %collective-permute-start.11 = (s32[328,128]{1,0:T(8,128)S(1)}, s32[328,128]{1,0:T(8,128)S(1)}, u32[]{:S(2)}, u32[]{:S(2)}) collective-permute-start(s32[328,128]{1,0:T(8,128)S(1)} %get-tuple-element.24), channel_id=1, source_target_pairs={{0,17},{1,16},{2,19},{3,18},{4,21},{5,20},{6,23},{7,22},{8,25},{9,... | collective-permute-start | bytes 503816 | tf_op jit(solution)/shard_map/ppermute | solution.py:33
  32.7 1.7 %collective-permute-start.12 = (f32[1,128]{1,0:T(1,128)S(1)}, f32[1,128]{1,0:T(1,128)S(1)}, u32[]{:S(2)}, u32[]{:S(2)}) collective-permute-start(f32[1,128]{1,0:T(1,128)S(1)} %get-tuple-element.26), channel_id=1, source_target_pairs={{0,8},{8,0},{16,24},{24,16},{1,9},{9,1},{17,25},{25,17},{2,10},{10... | collective-permute-start | bytes 1544 | tf_op jit(solution)/shard_map/ppermute | solution.py:23
  32.8 4.5 %collective-permute-start.13 = (f32[1,128]{1,0:T(1,128)S(1)}, f32[1,128]{1,0:T(1,128)S(1)}, u32[]{:S(2)}, u32[]{:S(2)}) collective-permute-start(f32[1,128]{1,0:T(1,128)S(1)} %get-tuple-element.26), channel_id=1, source_target_pairs={{0,20},{1,21},{2,22},{3,23},{4,16},{5,17},{6,18},{7,19},{8,28},{9,... | collective-permute-start | bytes 1544 | tf_op jit(solution)/shard_map/ppermute | solution.py:33
  34.5 3.5 %collective-permute-start.14 = (f32[1,128]{1,0:T(1,128)S(1)}, f32[1,128]{1,0:T(1,128)S(1)}, u32[]{:S(2)}, u32[]{:S(2)}) collective-permute-start(f32[1,128]{1,0:T(1,128)S(1)} %add.33), channel_id=1, source_target_pairs={{0,16},{1,17},{2,18},{3,19},{4,20},{5,21},{6,22},{7,23},{8,12},{9,... | collective-permute-start | bytes 1544 | tf_op jit(solution)/shard_map/ppermute | solution.py:33
  38.0 1.1 %collective-permute-start.15 = (f32[1,128]{1,0:T(1,128)S(1)}, f32[1,128]{1,0:T(1,128)S(1)}, u32[]{:S(2)}, u32[]{:S(2)}) collective-permute-start(f32[1,128]{1,0:T(1,128)S(1)} %add.34), channel_id=1, source_target_pairs={{0,8},{8,0},{16,24},{24,16},{1,9},{9,1},{17,25},{25,17},{2,10},{10... | collective-permute-start | bytes 1544 | tf_op jit(solution)/shard_map/ppermute | solution.py:23

commit v7 on v6

--- a/solution.py
+++ b/solution.py
@@ -98,11 +98,11 @@
 
 def product_kernel(masks, n_layer, n_row, n_col, ids_ref, *refs):
     n_slots, n_held = n_layer // 2, 2 * len(masks)
-    b_refs, a_refs = refs[:4], refs[4 : 4 + n_held]
-    out_refs = refs[4 + n_held : -2]
+    mine_refs, near_refs = refs[:2], refs[2 : 2 + 2 * n_row]
+    a_refs, out_refs = refs[2 + 2 * n_row : 2 + 2 * n_row + n_held], refs[2 + 2 * n_row + n_held : -2]
     where_ref, lhs_ref = refs[-2:]
     layer, row, col = (lax.axis_index(n) for n in ("layer", "row", "col"))
-    per, per_row = IB // n_layer, n_col // n_row // 2
+    per, per_row = IB // n_layer, n_col // n_row
     capacity, block, depth = a_refs[0].shape
     rhs = []
     for k in range(n_held):
@@ -111,10 +111,16 @@
             where_ref[k, i] = -1
         for n in range(capacity):
             where_ref[k, ids_ref[k, n]] = n
-        pair = (col ^ masks[place]) // 2
-        start = (((pair // per_row) ^ row) * per_row + pair % per_row) * depth
-        at = pl.ds(pl.multiple_of(start, depth), depth)
-        rhs.append(jnp.concatenate([b_refs[2 * m + other][at, :] for m in range(2)], axis=1))
+        panel = col ^ masks[place]
+        at = panel % per_row * depth
+        owner = (panel // per_row) ^ row
+        start = pl.multiple_of(owner * (per_row * depth) + at, depth)
+        mine = mine_refs[other][pl.ds(start, depth), :]
+        at = pl.ds(pl.multiple_of(at, depth), depth)
+        near = near_refs[other][at, :]
+        for i in range(1, n_row):
+            near = jnp.where(owner == i, near_refs[2 * i + other][at, :], near)
+        rhs.append(jnp.concatenate([mine, near], axis=1))
     rhs = jnp.concatenate(rhs, axis=0)
     width = rhs.shape[1] // 2
     for slot in range(n_slots):
@@ -172,23 +178,25 @@
         masks = masks + [m ^ bit for m in masks]
         bit //= 2
 
-    b_rows = [b_panel]
+    own_other = other(panels[0])
+    b_panel, own_other = lax.optimization_barrier((b_panel, own_other))
+
+    b_rows = [[b_panel, xor_permute(b_panel, "col", 1)]]
     bit = 1
     while bit < n_row:
-        b_rows = b_rows + [xor_permute(b, "row", bit) for b in b_rows]
+        b_rows = b_rows + [[xor_permute(b, "row", bit) for b in pair] for pair in b_rows]
         bit *= 2
-    b_rows = jnp.concatenate(b_rows).reshape(-1, 2, *b_panel.shape[-1:] * 2)
-    parity = lax.axis_index("col") % 2
-    b_mine, b_near = (
-        lax.dynamic_index_in_dim(b_rows, p, 1, False).reshape(-1, b_panel.shape[1])
-        for p in (parity, 1 - parity)
+
+    mine = jnp.concatenate([pair[0] for pair in b_rows])
+    mine = [mine, other(mine)]
+    near = [pair[1] for pair in b_rows]
+    own = a_blocks[0]
+    far, ids, mine, near, own_other = lax.optimization_barrier(
+        (panels[1:], ids, mine, near, own_other)
     )
-    b_refs = [b_mine, other(b_mine), xor_permute(b_near, "col", 1)]
-
-    far, ids, b_refs = lax.optimization_barrier((panels[1:], ids, b_refs))
-    panels[1:] = far
-    b_refs.append(other(b_refs[2]))
-    panels = [x for p in panels for x in (p, other(p))]
+    near = [x for b in near for x in (b, other(b))]
+    panels = [own, own_other] + [x for p in far for x in (p, other(p))]
+    b_refs = mine + near
     parts = products(masks, ids, b_refs, panels)
 
     parts = [parts[0]] + [grid_permute(parts[k], (2 * (k // 2), 0, k % 2)) for k in range(1, n_layer)]

time: 40.1 us -> 40.2 us (level)
  starting transfers between devices: 15 us -> 16.7 us
  waiting for transfers between devices: 19.5 us -> 17.9 us
    ppermute x11 -> x13, waiting for transfers between devices: 9.9 us -> 7.64 us  [xor_permute(): lax.ppermute(x, axis, [(i, i ^ mask) for i in range(lax.axis_size(axis))])]
    ppermute x11 -> x13, starting transfers between devices: 8.41 us -> 10.1 us  [xor_permute(): lax.ppermute(x, axis, [(i, i ^ mask) for i in range(lax.axis_size(axis))])]
    concatenate x1 -> x0, other arithmetic: 0.85 us -> none  [body(): b_rows = jnp.concatenate(b_rows).reshape(-1, 2, *b_panel.shape[-1:] * 2)]
    ppermute x5, waiting for transfers between devices: 9.57 us -> 10.3 us  [grid_permute(): return lax.ppermute(x, AXES, pairs)]
    select_n x1, other arithmetic: 0.01 us -> 0.66 us  [body(): ids = jnp.where(valid, a_rows, IB)]
    unnamed x4 -> x3, local copies, waits for them, and re-layouts: 0.65 us -> 0.88 us
  transfers between devices with their start and end apart: 16 -> 18, of which waited for: 9 -> 10; matrix products, arithmetic and copies ran while one was open for 4% -> 5% of each run, Pallas kernels for 0% -> 0%
where the time goes in v7:
time: 40.2 us; the launch traced here: 40 us
  waiting for transfers between devices  17.9 us (45%)
  starting transfers between devices  16.7 us (42%)
  other arithmetic  2 us (5%)
  Pallas kernels  1.82 us (5%)
  local copies, waits for them, and re-layouts  0.89 us (2%)
  between operations  0.72 us (2%)
    ppermute x5, waiting for transfers between devices, grid_permute(): return lax.ppermute(x, AXES, pairs)  10.3 us
    ppermute x13, starting transfers between devices, xor_permute(): lax.ppermute(x, axis, [(i, i ^ mask) for i in range(lax.axis_size(axis))])  10.1 us
    ppermute x13, waiting for transfers between devices, xor_permute(): lax.ppermute(x, axis, [(i, i ^ mask) for i in range(lax.axis_size(axis))])  7.64 us
    ppermute x5, starting transfers between devices, grid_permute(): return lax.ppermute(x, AXES, pairs)  6.6 us
    pallas_call x1, Pallas kernels, products(): pl.pallas_call(functools.partial(product_kernel, masks, n_layer, n_row, n...  1.61 us
    unnamed x3, local copies, waits for them, and re-layouts  0.88 us
  transfers between devices with their start and end apart: 18, of which 10 were waited for; matrix products, arithmetic and copies ran while one was open for 5% of the time, Pallas kernels for 0%

profile of v7, /device:TPU:0, one launch (start us, length us, event | category | flops | bytes accessed | tf_op | source)
XLA Modules:
  0.0 40.0 jit_solution(764209538484367413)
XLA Ops:
  0.0 0.0 copy-start
  0.0 0.5 %collective-permute-start.3 = (bf16[8,128,128]{2,1,0:T(8,128)(2,1)}, bf16[8,128,128]{2,1,0:T(8,128)(2,1)S(1)}, u32[]{:S(2)}, u32[]{:S(2)}) collective-permute-start(bf16[8,128,128]{2,1,0:T(8,128)(2,1)} %bitcast.7), channel_id=1, source_target_pairs={{0,8},{8,0},{16,24},{24,16},{1,9},{9,1},{17,25},{25,17},{2,10},{10... | collective-permute-start | bytes 786440 | tf_op jit(solution)/shard_map/ppermute | solution.py:23
  0.5 3.6 %collective-permute-start = (bf16[8,128,128]{2,1,0:T(8,128)(2,1)}, bf16[8,128,128]{2,1,0:T(8,128)(2,1)S(1)}, u32[]{:S(2)}, u32[]{:S(2)}) collective-permute-start(bf16[8,128,128]{2,1,0:T(8,128)(2,1)} %bitcast.8), channel_id=1, source_target_pairs={{0,2},{1,3},{2,0},{3,1},{4,6},{5,7},{6,4},{7,5},{8,10},{9,11},{10,... | collective-permute-start | bytes 786440 | tf_op jit(solution)/shard_map/ppermute | solution.py:23
  4.8 0.7 %compare_select_fusion = s32[1,8]{1,0:T(1,128)S(1)} fusion(s32[1,8]{1,0:T(1,128)} %param.5, s32[]{:T(128)} %bitcast.6), kind=kLoop, calls=%fused_computation.4 | loop fusion | flops 16 | bytes 68 | tf_op jit(solution)/shard_map/jit(_where)/select_n | solution.py:172
  5.4 0.2 collective-permute-start.1
  5.6 0.0 collective-permute-done.3.refs_7_
  5.6 1.6 %collective-permute-start.6 = (bf16[256,128]{1,0:T(8,128)(2,1)}, bf16[256,128]{1,0:T(8,128)(2,1)S(1)}, u32[]{:S(2)}, u32[]{:S(2)}) collective-permute-start(bf16[256,128]{1,0:T(8,128)(2,1)} %param.7), channel_id=1, source_target_pairs={{0,1},{1,0},{2,3},{3,2},{4,5},{5,4},{6,7},{7,6},{8,9},{9,8},{10,11... | collective-permute-start | bytes 196616 | tf_op jit(solution)/shard_map/ppermute | solution.py:23
  7.2 1.5 %collective-permute-start.4 = (bf16[256,128]{1,0:T(8,128)(2,1)}, bf16[256,128]{1,0:T(8,128)(2,1)S(1)}, u32[]{:S(2)}, u32[]{:S(2)}) collective-permute-start(bf16[256,128]{1,0:T(8,128)(2,1)} %param.7), channel_id=1, source_target_pairs={{0,4},{4,0},{1,5},{5,1},{2,6},{6,2},{3,7},{7,3},{8,12},{12,8},{9,1... | collective-permute-start | bytes 196616 | tf_op jit(solution)/shard_map/ppermute | solution.py:23
  8.7 0.9 %constant_dynamic-update-slice_fusion.1 = bf16[512,128]{1,0:T(8,128)(2,1)S(1)} fusion(bf16[256,128]{1,0:T(8,128)(2,1)} %param.7), kind=kLoop, calls=%fused_computation.2 | loop fusion | bytes 131072
  9.6 2.1 %collective-permute-done.4 = bf16[256,128]{1,0:T(8,128)(2,1)S(1)} collective-permute-done((bf16[256,128]{1,0:T(8,128)(2,1)}, bf16[256,128]{1,0:T(8,128)(2,1)S(1)}, u32[]{:S(2)}, u32[]{:S(2)}) %collective-permute-start.4) | collective-permute-done | bytes 65568 | tf_op jit(solution)/shard_map/ppermute | solution.py:23
  11.7 0.1 collective-permute-start.5
  11.7 0.0 collective-permute-done.1
  11.8 0.4 %collective-permute-start.2 = (s32[2,8]{1,0:T(2,128)S(1)}, s32[2,8]{1,0:T(2,128)S(1)}, u32[]{:S(2)}, u32[]{:S(2)}) collective-permute-start(s32[2,8]{1,0:T(2,128)S(1)} %pad_add_fusion.1), channel_id=1, source_target_pairs={{0,2},{1,3},{2,0},{3,1},{4,6},{5,7},{6,4},{7,5},{8,10},{9,11},{10,... | collective-permute-start | bytes 200 | tf_op jit(solution)/shard_map/ppermute | solution.py:23
  12.2 0.0 collective-permute-done.6.refs_2_
  12.2 1.5 %collective-permute-start.7 = (bf16[256,128]{1,0:T(8,128)(2,1)S(1)}, bf16[256,128]{1,0:T(8,128)(2,1)S(1)}, u32[]{:S(2)}, u32[]{:S(2)}) collective-permute-start(bf16[256,128]{1,0:T(8,128)(2,1)S(1)} %collective-permute-done.6.refs_2_), channel_id=1, source_target_pairs={{0,4},{4,0},{1,5},{5,1},{2,6},{6,2},{3,7},{7,3},{8,12},{12,8},{9,1... | collective-permute-start | bytes 196616 | tf_op jit(solution)/shard_map/ppermute | solution.py:23
  13.7 3.2 %collective-permute-done.2 = s32[2,8]{1,0:T(2,128)S(1)} collective-permute-done((s32[2,8]{1,0:T(2,128)S(1)}, s32[2,8]{1,0:T(2,128)S(1)}, u32[]{:S(2)}, u32[]{:S(2)}) %collective-permute-start.2) | collective-permute-done | bytes 96 | tf_op jit(solution)/shard_map/ppermute | solution.py:23
  16.9 0.6 %pad_add_fusion.ids_ref = s32[4,8]{1,0:T(4,128)} fusion(s32[2,8]{1,0:T(2,128)S(1)} %collective-permute-done.2, s32[1,8]{1,0:T(1,128)S(1)} %collective-permute-done.1, s32[1,8]{1,0:T(1,128)S(1)} %compare_select_fusion), kind=kLoop, calls=%fused_computation.3 | loop fusion | flops 64 | bytes 256 | tf_op jit(solution)/shard_map/concatenate | solution.py:177
  17.5 0.0 collective-permute-done.refs_8_
  17.5 0.0 collective-permute-done.7.refs_4_
  17.5 0.0 collective-permute-done.5.refs_1_
  17.5 0.1 collective-permute-start.10
  17.6 0.5 %collective-permute-start.8 = (bf16[256,128]{1,0:T(8,128)(2,1)S(1)}, bf16[256,128]{1,0:T(8,128)(2,1)S(1)}, u32[]{:S(2)}, u32[]{:S(2)}) collective-permute-start(bf16[256,128]{1,0:T(8,128)(2,1)S(1)} %collective-permute-done.6.refs_2_), channel_id=1, source_target_pairs={{0,8},{8,0},{16,24},{24,16},{1,9},{9,1},{17,25},{25,17},{2,10},{10... | collective-permute-start | bytes 196616 | tf_op jit(solution)/shard_map/ppermute | solution.py:23
  18.1 0.1 collective-permute-start.9
  18.2 1.0 %collective-permute-done.8.refs_3_ = bf16[256,128]{1,0:T(8,128)(2,1)S(1)} collective-permute-done((bf16[256,128]{1,0:T(8,128)(2,1)S(1)}, bf16[256,128]{1,0:T(8,128)(2,1)S(1)}, u32[]{:S(2)}, u32[]{:S(2)}) %collective-permute-start.8) | collective-permute-done | bytes 65568 | tf_op jit(solution)/shard_map/ppermute | solution.py:23
  19.2 0.1 collective-permute-done.9.refs_5_
  19.4 0.0 collective-permute-done.10.refs_9_
  19.4 0.0 copy-done
  19.4 1.6 %partial_rows.1 = (f32[512,128]{1,0:T(8,128)S(1)}, s32[328,128]{1,0:T(8,128)S(1)}, s32[328,128]{1,0:T(8,128)S(1)}, s32[328,128]{1,0:T(8,128)S(1)}) custom-call(s32[4,8]{1,0:T(4,128)} %pad_add_fusion.ids_ref, bf16[512,128]{1,0:T(8,128)(2,1)S(1)} %constant_dynamic-update-slice_fusion.refs_0_, bf16[512,128]{1,0:T(8,128)(2,1)S(1)} %collective-permute-done.5.refs_1_, ...), custom_call_target="tpu_custom_call" | custom-call | tf_op jit(solution)/shard_map/partial_rows/pallas_call | solution.py:149
  21.0 1.2 %collective-permute-start.11 = (s32[328,128]{1,0:T(8,128)S(1)}, s32[328,128]{1,0:T(8,128)S(1)}, u32[]{:S(2)}, u32[]{:S(2)}) collective-permute-start(s32[328,128]{1,0:T(8,128)S(1)} %get-tuple-element.30), channel_id=1, source_target_pairs={{0,1},{1,0},{2,3},{3,2},{4,5},{5,4},{6,7},{7,6},{8,9},{9,8},{10,11... | collective-permute-start | bytes 503816 | tf_op jit(solution)/shard_map/ppermute | solution.py:33
  22.1 1.5 %collective-permute-start.12 = (s32[328,128]{1,0:T(8,128)S(1)}, s32[328,128]{1,0:T(8,128)S(1)}, u32[]{:S(2)}, u32[]{:S(2)}) collective-permute-start(s32[328,128]{1,0:T(8,128)S(1)} %get-tuple-element.31), channel_id=1, source_target_pairs={{0,16},{1,17},{2,18},{3,19},{4,20},{5,21},{6,22},{7,23},{8,24},{9,... | collective-permute-start | bytes 503816 | tf_op jit(solution)/shard_map/ppermute | solution.py:33
  23.6 0.9 %collective-permute-start.13 = (s32[328,128]{1,0:T(8,128)S(1)}, s32[328,128]{1,0:T(8,128)S(1)}, u32[]{:S(2)}, u32[]{:S(2)}) collective-permute-start(s32[328,128]{1,0:T(8,128)S(1)} %get-tuple-element.32), channel_id=1, source_target_pairs={{0,17},{1,16},{2,19},{3,18},{4,21},{5,20},{6,23},{7,22},{8,25},{9,... | collective-permute-start | bytes 503816 | tf_op jit(solution)/shard_map/ppermute | solution.py:33
  24.5 3.6 %collective-permute-done.11.refs_0_ = s32[328,128]{1,0:T(8,128)S(1)} collective-permute-done((s32[328,128]{1,0:T(8,128)S(1)}, s32[328,128]{1,0:T(8,128)S(1)}, u32[]{:S(2)}, u32[]{:S(2)}) %collective-permute-start.11) | collective-permute-done | bytes 167968 | tf_op jit(solution)/shard_map/ppermute | solution.py:33
  28.2 2.6 %collective-permute-done.12.refs_1_ = s32[328,128]{1,0:T(8,128)S(1)} collective-permute-done((s32[328,128]{1,0:T(8,128)S(1)}, s32[328,128]{1,0:T(8,128)S(1)}, u32[]{:S(2)}, u32[]{:S(2)}) %collective-permute-start.12) | collective-permute-done | bytes 167968 | tf_op jit(solution)/shard_map/ppermute | solution.py:33
  30.8 1.2 %collective-permute-done.13.refs_2_ = s32[328,128]{1,0:T(8,128)S(1)} collective-permute-done((s32[328,128]{1,0:T(8,128)S(1)}, s32[328,128]{1,0:T(8,128)S(1)}, u32[]{:S(2)}, u32[]{:S(2)}) %collective-permute-start.13) | collective-permute-done | bytes 167968 | tf_op jit(solution)/shard_map/ppermute | solution.py:33
  32.0 0.2 squares.1
  32.2 0.1 collective-permute-start.14
  32.3 2.4 %collective-permute-start.15 = (f32[1,128]{1,0:T(1,128)S(1)}, f32[1,128]{1,0:T(1,128)S(1)}, u32[]{:S(2)}, u32[]{:S(2)}) collective-permute-start(f32[1,128]{1,0:T(1,128)S(1)} %get-tuple-element.34), channel_id=1, source_target_pairs={{0,20},{1,21},{2,22},{3,23},{4,16},{5,17},{6,18},{7,19},{8,28},{9,... | collective-permute-start | bytes 1544 | tf_op jit(solution)/shard_map/ppermute | solution.py:33
  34.6 0.0 collective-permute-done.14
  34.6 0.7 %collective-permute-start.16 = (f32[1,128]{1,0:T(1,128)S(1)}, f32[1,128]{1,0:T(1,128)S(1)}, u32[]{:S(2)}, u32[]{:S(2)}) collective-permute-start(f32[1,128]{1,0:T(1,128)S(1)} %add.18), channel_id=1, source_target_pairs={{0,16},{1,17},{2,18},{3,19},{4,20},{5,21},{6,22},{7,23},{8,12},{9,... | collective-permute-start | bytes 1544 | tf_op jit(solution)/shard_map/ppermute | solution.py:33
  35.3 1.4 %collective-permute-done.15 = f32[1,128]{1,0:T(1,128)S(1)} collective-permute-done((f32[1,128]{1,0:T(1,128)S(1)}, f32[1,128]{1,0:T(1,128)S(1)}, u32[]{:S(2)}, u32[]{:S(2)}) %collective-permute-start.15) | collective-permute-done | bytes 544 | tf_op jit(solution)/shard_map/ppermute | solution.py:33
  36.8 1.4 %collective-permute-done.16 = f32[1,128]{1,0:T(1,128)S(1)} collective-permute-done((f32[1,128]{1,0:T(1,128)S(1)}, f32[1,128]{1,0:T(1,128)S(1)}, u32[]{:S(2)}, u32[]{:S(2)}) %collective-permute-start.16) | collective-permute-done | bytes 544 | tf_op jit(solution)/shard_map/ppermute | solution.py:33
  38.2 0.0 collective-permute-start.17
  38.2 1.1 %collective-permute-done.17 = f32[1,128]{1,0:T(1,128)S(1)} collective-permute-done((f32[1,128]{1,0:T(1,128)S(1)}, f32[1,128]{1,0:T(1,128)S(1)}, u32[]{:S(2)}, u32[]{:S(2)}) %collective-permute-start.17) | collective-permute-done | bytes 544 | tf_op jit(solution)/shard_map/ppermute | solution.py:23
  39.3 0.7 %multiply_bitcast_fusion = f32[1,512,128]{2,1,0:T(8,128)} fusion(f32[512,128]{1,0:T(8,128)S(1)} %get-tuple-element.33, f32[128]{0:T(128)S(1)} %divide_bitcast_fusion), kind=kLoop, calls=%fused_computation | loop fusion | flops 65536 | bytes 524800 | tf_op jit(solution)/shard_map/broadcast_in_dim | solution.py:216
  (5 shorter events, 0.0 us)
Async XLA Ops:
  0.0 19.4 %copy-start = (bf16[1,8,128,128]{3,2,1,0:T(8,128)(2,1)S(1)}, bf16[1,8,128,128]{3,2,1,0:T(8,128)(2,1)}, u32[]{:S(2)}) copy-start(bf16[1,8,128,128]{3,2,1,0:T(8,128)(2,1)} %param.4) | copy-start | bytes 786436
  0.0 5.6 %collective-permute-start.3 = (bf16[8,128,128]{2,1,0:T(8,128)(2,1)}, bf16[8,128,128]{2,1,0:T(8,128)(2,1)S(1)}, u32[]{:S(2)}, u32[]{:S(2)}) collective-permute-start(bf16[8,128,128]{2,1,0:T(8,128)(2,1)} %bitcast.7), channel_id=1, source_target_pairs={{0,8},{8,0},{16,24},{24,16},{1,9},{9,1},{17,25},{25,17},{2,10},{10... | collective-permute-start | bytes 786440 | tf_op jit(solution)/shard_map/ppermute | solution.py:23
  0.5 17.1 %collective-permute-start = (bf16[8,128,128]{2,1,0:T(8,128)(2,1)}, bf16[8,128,128]{2,1,0:T(8,128)(2,1)S(1)}, u32[]{:S(2)}, u32[]{:S(2)}) collective-permute-start(bf16[8,128,128]{2,1,0:T(8,128)(2,1)} %bitcast.8), channel_id=1, source_target_pairs={{0,2},{1,3},{2,0},{3,1},{4,6},{5,7},{6,4},{7,5},{8,10},{9,11},{10,... | collective-permute-start | bytes 786440 | tf_op jit(solution)/shard_map/ppermute | solution.py:23
  5.4 6.3 %collective-permute-start.1 = (s32[1,8]{1,0:T(1,128)S(1)}, s32[1,8]{1,0:T(1,128)S(1)}, u32[]{:S(2)}, u32[]{:S(2)}) collective-permute-start(s32[1,8]{1,0:T(1,128)S(1)} %compare_select_fusion), channel_id=1, source_target_pairs={{0,8},{8,0},{16,24},{24,16},{1,9},{9,1},{17,25},{25,17},{2,10},{10... | collective-permute-start | bytes 104 | tf_op jit(solution)/shard_map/ppermute | solution.py:23
  5.6 6.6 %collective-permute-start.6 = (bf16[256,128]{1,0:T(8,128)(2,1)}, bf16[256,128]{1,0:T(8,128)(2,1)S(1)}, u32[]{:S(2)}, u32[]{:S(2)}) collective-permute-start(bf16[256,128]{1,0:T(8,128)(2,1)} %param.7), channel_id=1, source_target_pairs={{0,1},{1,0},{2,3},{3,2},{4,5},{5,4},{6,7},{7,6},{8,9},{9,8},{10,11... | collective-permute-start | bytes 196616 | tf_op jit(solution)/shard_map/ppermute | solution.py:23
  7.2 4.5 %collective-permute-start.4 = (bf16[256,128]{1,0:T(8,128)(2,1)}, bf16[256,128]{1,0:T(8,128)(2,1)S(1)}, u32[]{:S(2)}, u32[]{:S(2)}) collective-permute-start(bf16[256,128]{1,0:T(8,128)(2,1)} %param.7), channel_id=1, source_target_pairs={{0,4},{4,0},{1,5},{5,1},{2,6},{6,2},{3,7},{7,3},{8,12},{12,8},{9,1... | collective-permute-start | bytes 196616 | tf_op jit(solution)/shard_map/ppermute | solution.py:23
  11.7 5.9 %collective-permute-start.5 = (bf16[512,128]{1,0:T(8,128)(2,1)S(1)}, bf16[512,128]{1,0:T(8,128)(2,1)S(1)}, u32[]{:S(2)}, u32[]{:S(2)}) collective-permute-start(bf16[512,128]{1,0:T(8,128)(2,1)S(1)} %constant_dynamic-update-slice_fusion.refs_0_), channel_id=1, source_target_pairs={{0,8},{8,0},{16,24},{24,16},{1,9},{9,1},{17,25},{25,17},{2,10},{10... | collective-permute-start | bytes 393224 | tf_op jit(solution)/shard_map/ppermute | solution.py:23
  11.8 5.2 %collective-permute-start.2 = (s32[2,8]{1,0:T(2,128)S(1)}, s32[2,8]{1,0:T(2,128)S(1)}, u32[]{:S(2)}, u32[]{:S(2)}) collective-permute-start(s32[2,8]{1,0:T(2,128)S(1)} %pad_add_fusion.1), channel_id=1, source_target_pairs={{0,2},{1,3},{2,0},{3,1},{4,6},{5,7},{6,4},{7,5},{8,10},{9,11},{10,... | collective-permute-start | bytes 200 | tf_op jit(solution)/shard_map/ppermute | solution.py:23
  12.2 5.4 %collective-permute-start.7 = (bf16[256,128]{1,0:T(8,128)(2,1)S(1)}, bf16[256,128]{1,0:T(8,128)(2,1)S(1)}, u32[]{:S(2)}, u32[]{:S(2)}) collective-permute-start(bf16[256,128]{1,0:T(8,128)(2,1)S(1)} %collective-permute-done.6.refs_2_), channel_id=1, source_target_pairs={{0,4},{4,0},{1,5},{5,1},{2,6},{6,2},{3,7},{7,3},{8,12},{12,8},{9,1... | collective-permute-start | bytes 196616 | tf_op jit(solution)/shard_map/ppermute | solution.py:23
  17.5 1.8 %collective-permute-start.10 = (bf16[8,128,128]{2,1,0:T(8,128)(2,1)S(1)}, bf16[8,128,128]{2,1,0:T(8,128)(2,1)S(1)}, u32[]{:S(2)}, u32[]{:S(2)}) collective-permute-start(bf16[8,128,128]{2,1,0:T(8,128)(2,1)S(1)} %collective-permute-done.refs_8_), channel_id=1, source_target_pairs={{0,8},{8,0},{16,24},{24,16},{1,9},{9,1},{17,25},{25,17},{2,10},{10... | collective-permute-start | bytes 786440 | tf_op jit(solution)/shard_map/ppermute | solution.py:23
  17.6 1.6 %collective-permute-start.8 = (bf16[256,128]{1,0:T(8,128)(2,1)S(1)}, bf16[256,128]{1,0:T(8,128)(2,1)S(1)}, u32[]{:S(2)}, u32[]{:S(2)}) collective-permute-start(bf16[256,128]{1,0:T(8,128)(2,1)S(1)} %collective-permute-done.6.refs_2_), channel_id=1, source_target_pairs={{0,8},{8,0},{16,24},{24,16},{1,9},{9,1},{17,25},{25,17},{2,10},{10... | collective-permute-start | bytes 196616 | tf_op jit(solution)/shard_map/ppermute | solution.py:23
  18.1 1.3 %collective-permute-start.9 = (bf16[256,128]{1,0:T(8,128)(2,1)S(1)}, bf16[256,128]{1,0:T(8,128)(2,1)S(1)}, u32[]{:S(2)}, u32[]{:S(2)}) collective-permute-start(bf16[256,128]{1,0:T(8,128)(2,1)S(1)} %collective-permute-done.7.refs_4_), channel_id=1, source_target_pairs={{0,8},{8,0},{16,24},{24,16},{1,9},{9,1},{17,25},{25,17},{2,10},{10... | collective-permute-start | bytes 196616 | tf_op jit(solution)/shard_map/ppermute | solution.py:23
  21.0 7.2 %collective-permute-start.11 = (s32[328,128]{1,0:T(8,128)S(1)}, s32[328,128]{1,0:T(8,128)S(1)}, u32[]{:S(2)}, u32[]{:S(2)}) collective-permute-start(s32[328,128]{1,0:T(8,128)S(1)} %get-tuple-element.30), channel_id=1, source_target_pairs={{0,1},{1,0},{2,3},{3,2},{4,5},{5,4},{6,7},{7,6},{8,9},{9,8},{10,11... | collective-permute-start | bytes 503816 | tf_op jit(solution)/shard_map/ppermute | solution.py:33
  22.1 8.7 %collective-permute-start.12 = (s32[328,128]{1,0:T(8,128)S(1)}, s32[328,128]{1,0:T(8,128)S(1)}, u32[]{:S(2)}, u32[]{:S(2)}) collective-permute-start(s32[328,128]{1,0:T(8,128)S(1)} %get-tuple-element.31), channel_id=1, source_target_pairs={{0,16},{1,17},{2,18},{3,19},{4,20},{5,21},{6,22},{7,23},{8,24},{9,... | collective-permute-start | bytes 503816 | tf_op jit(solution)/shard_map/ppermute | solution.py:33
  23.6 8.3 %collective-permute-start.13 = (s32[328,128]{1,0:T(8,128)S(1)}, s32[328,128]{1,0:T(8,128)S(1)}, u32[]{:S(2)}, u32[]{:S(2)}) collective-permute-start(s32[328,128]{1,0:T(8,128)S(1)} %get-tuple-element.32), channel_id=1, source_target_pairs={{0,17},{1,16},{2,19},{3,18},{4,21},{5,20},{6,23},{7,22},{8,25},{9,... | collective-permute-start | bytes 503816 | tf_op jit(solution)/shard_map/ppermute | solution.py:33
  32.2 2.4 %collective-permute-start.14 = (f32[1,128]{1,0:T(1,128)S(1)}, f32[1,128]{1,0:T(1,128)S(1)}, u32[]{:S(2)}, u32[]{:S(2)}) collective-permute-start(f32[1,128]{1,0:T(1,128)S(1)} %get-tuple-element.34), channel_id=1, source_target_pairs={{0,8},{8,0},{16,24},{24,16},{1,9},{9,1},{17,25},{25,17},{2,10},{10... | collective-permute-start | bytes 1544 | tf_op jit(solution)/shard_map/ppermute | solution.py:23
  32.3 4.5 %collective-permute-start.15 = (f32[1,128]{1,0:T(1,128)S(1)}, f32[1,128]{1,0:T(1,128)S(1)}, u32[]{:S(2)}, u32[]{:S(2)}) collective-permute-start(f32[1,128]{1,0:T(1,128)S(1)} %get-tuple-element.34), channel_id=1, source_target_pairs={{0,20},{1,21},{2,22},{3,23},{4,16},{5,17},{6,18},{7,19},{8,28},{9,... | collective-permute-start | bytes 1544 | tf_op jit(solution)/shard_map/ppermute | solution.py:33
  34.6 3.5 %collective-permute-start.16 = (f32[1,128]{1,0:T(1,128)S(1)}, f32[1,128]{1,0:T(1,128)S(1)}, u32[]{:S(2)}, u32[]{:S(2)}) collective-permute-start(f32[1,128]{1,0:T(1,128)S(1)} %add.18), channel_id=1, source_target_pairs={{0,16},{1,17},{2,18},{3,19},{4,20},{5,21},{6,22},{7,23},{8,12},{9,... | collective-permute-start | bytes 1544 | tf_op jit(solution)/shard_map/ppermute | solution.py:33
  38.2 1.1 %collective-permute-start.17 = (f32[1,128]{1,0:T(1,128)S(1)}, f32[1,128]{1,0:T(1,128)S(1)}, u32[]{:S(2)}, u32[]{:S(2)}) collective-permute-start(f32[1,128]{1,0:T(1,128)S(1)} %add.19), channel_id=1, source_target_pairs={{0,8},{8,0},{16,24},{24,16},{1,9},{9,1},{17,25},{25,17},{2,10},{10... | collective-permute-start | bytes 1544 | tf_op jit(solution)/shard_map/ppermute | solution.py:23

commit v8 on v7

--- a/solution.py
+++ b/solution.py
@@ -10,7 +10,7 @@
 
 IB = 16
 AXES = ("layer", "row", "col")
-BITS = 20
+BITS, VALUES, WORDS = 18, 16, 9
 VMEM = pl.BlockSpec(memory_space=pltpu.VMEM)
 SMEM = pl.BlockSpec(memory_space=pltpu.SMEM)
 
@@ -51,41 +51,51 @@
     return scale
 
 
+def low_fields(i):
+    fields, at, bit = [], (i - WORDS) * BITS, 0
+    while bit < BITS:
+        word, to = divmod(at, 32 - BITS)
+        bits = min(BITS - bit, 32 - BITS - to)
+        fields.append((bit, word, to, bits))
+        at, bit = at + bits, bit + bits
+    return fields
+
+
 def pack(part, out_ref):
     top = jnp.max(jnp.abs(part), axis=0, keepdims=True)
     k = jnp.clip(jnp.ceil(jnp.log2(top) + 0.01), -100.0, 126.0).astype(jnp.int32)
     q = jnp.floor(part * power_of_two(BITS - 1 - k) + 0.5).astype(jnp.int32)
-    rows = part.shape[0] // 8
-    q = [q[i * rows : (i + 1) * rows] for i in range(8)]
-    low = [
-        q[5] & 4095,
-        ((q[5] >> 12) & 255) | ((q[6] & 15) << 8),
-        (q[6] >> 4) & 4095,
-        ((q[6] >> 16) & 15) | ((q[7] & 255) << 4),
-        (q[7] >> 8) & 4095,
-    ]
-    for i in range(5):
-        out_ref[i * rows : (i + 1) * rows] = (q[i] << 12) | low[i]
-    out_ref[5 * rows :] = jnp.broadcast_to(k, (8, part.shape[1]))
+    rows = part.shape[0] // VALUES
+    q = [q[i * rows : (i + 1) * rows] for i in range(VALUES)]
+    words = [q[j] << (32 - BITS) for j in range(WORDS)]
+    for i in range(WORDS, VALUES):
+        for bit, word, to, bits in low_fields(i):
+            words[word] = words[word] | (((q[i] >> bit) & ((1 << bits) - 1)) << to)
+    for j in range(WORDS):
+        out_ref[j * rows : (j + 1) * rows] = words[j]
+    out_ref[WORDS * rows :] = jnp.broadcast_to(k, (8, part.shape[1]))
 
 
 def unpack(ref, rows, i):
-    w = [ref[j * rows : (j + 1) * rows] for j in ([i] if i < 5 else range(5))]
-    if i < 5:
-        return w[0] >> 12
-    if i == 5:
-        return (w[0] & 4095) | ((w[1] << 24) >> 12)
-    if i == 6:
-        return ((w[1] >> 8) & 15) | ((w[2] & 4095) << 4) | ((w[3] << 28) >> 12)
-    return ((w[3] >> 4) & 255) | ((w[4] << 20) >> 12)
+    if i < WORDS:
+        return ref[i * rows : (i + 1) * rows] >> (32 - BITS)
+    total = None
+    for bit, word, to, bits in low_fields(i):
+        w = ref[word * rows : (word + 1) * rows]
+        if bit + bits == BITS:
+            w = ((w << (32 - to - bits)) >> (32 - bits)) << bit
+        else:
+            w = ((w >> to) & ((1 << bits) - 1)) << bit
+        total = w if total is None else total | w
+    return total
 
 
 def square_kernel(mine_ref, *refs):
     coded_refs, (sq_ref, sum_ref) = refs[:-2], refs[-2:]
-    rows = mine_ref.shape[0] // 8
-    scales = [power_of_two(ref[5 * rows : 5 * rows + 1] - (BITS - 1)) for ref in coded_refs]
+    rows = mine_ref.shape[0] // VALUES
+    scales = [power_of_two(ref[WORDS * rows : WORDS * rows + 1] - (BITS - 1)) for ref in coded_refs]
     total = jnp.zeros(sum_ref.shape, jnp.float32)
-    for i in range(8):
+    for i in range(VALUES):
         at = slice(i * rows, (i + 1) * rows)
         e = mine_ref[at]
         for ref, scale in zip(coded_refs, scales):
@@ -149,7 +159,7 @@
     return pl.pallas_call(
         functools.partial(product_kernel, masks, n_layer, n_row, n_col),
         out_shape=[pltpu.VMEM((rows, width), jnp.float32)]
-        + [pltpu.VMEM((rows // 8 * 5 + 8, width), jnp.int32)] * (2 * n_slots - 1),
+        + [pltpu.VMEM((rows // VALUES * WORDS + 8, width), jnp.int32)] * (2 * n_slots - 1),
         in_specs=[SMEM] + [VMEM] * len(ins),
         out_specs=[VMEM] * (2 * n_slots),
         scratch_shapes=[

time: 40.2 us -> 39.5 us (0.983)
  waiting for transfers between devices: 17.9 us -> 17.2 us
    ppermute x5, waiting for transfers between devices: 10.3 us -> 9.58 us  [grid_permute(): return lax.ppermute(x, AXES, pairs)]
where the time goes in v8:
time: 39.5 us; the launch traced here: 39.4 us
  waiting for transfers between devices  17.2 us (44%)
  starting transfers between devices  16.7 us (42%)
  other arithmetic  2 us (5%)
  Pallas kernels  1.84 us (5%)
  local copies, waits for them, and re-layouts  0.89 us (2%)
  between operations  0.72 us (2%)
    ppermute x13, starting transfers between devices, xor_permute(): lax.ppermute(x, axis, [(i, i ^ mask) for i in range(lax.axis_size(axis))])  10.1 us
    ppermute x5, waiting for transfers between devices, grid_permute(): return lax.ppermute(x, AXES, pairs)  9.58 us
    ppermute x13, waiting for transfers between devices, xor_permute(): lax.ppermute(x, axis, [(i, i ^ mask) for i in range(lax.axis_size(axis))])  7.64 us
    ppermute x5, starting transfers between devices, grid_permute(): return lax.ppermute(x, AXES, pairs)  6.6 us
    pallas_call x1, Pallas kernels, products(): pl.pallas_call(functools.partial(product_kernel, masks, n_layer, n_row, n...  1.62 us
    unnamed x3, local copies, waits for them, and re-layouts  0.88 us
  transfers between devices with their start and end apart: 18, of which 10 were waited for; matrix products, arithmetic and copies ran while one was open for 5% of the time, Pallas kernels for 0%

profile of v8, /device:TPU:0, one launch (start us, length us, event | category | flops | bytes accessed | tf_op | source)
XLA Modules:
  0.0 39.4 jit_solution(13709110609209614274)
XLA Ops:
  0.0 0.0 copy-start
  0.0 0.5 %collective-permute-start.3 = (bf16[8,128,128]{2,1,0:T(8,128)(2,1)}, bf16[8,128,128]{2,1,0:T(8,128)(2,1)S(1)}, u32[]{:S(2)}, u32[]{:S(2)}) collective-permute-start(bf16[8,128,128]{2,1,0:T(8,128)(2,1)} %bitcast.7), channel_id=1, source_target_pairs={{0,8},{8,0},{16,24},{24,16},{1,9},{9,1},{17,25},{25,17},{2,10},{10... | collective-permute-start | bytes 786440 | tf_op jit(solution)/shard_map/ppermute | solution.py:23
  0.5 3.6 %collective-permute-start = (bf16[8,128,128]{2,1,0:T(8,128)(2,1)}, bf16[8,128,128]{2,1,0:T(8,128)(2,1)S(1)}, u32[]{:S(2)}, u32[]{:S(2)}) collective-permute-start(bf16[8,128,128]{2,1,0:T(8,128)(2,1)} %bitcast.8), channel_id=1, source_target_pairs={{0,2},{1,3},{2,0},{3,1},{4,6},{5,7},{6,4},{7,5},{8,10},{9,11},{10,... | collective-permute-start | bytes 786440 | tf_op jit(solution)/shard_map/ppermute | solution.py:23
  4.8 0.7 %compare_select_fusion = s32[1,8]{1,0:T(1,128)S(1)} fusion(s32[1,8]{1,0:T(1,128)} %param.5, s32[]{:T(128)} %bitcast.6), kind=kLoop, calls=%fused_computation.4 | loop fusion | flops 16 | bytes 68 | tf_op jit(solution)/shard_map/jit(_where)/select_n | solution.py:182
  5.4 0.2 collective-permute-start.1
  5.6 0.0 collective-permute-done.3.refs_7_
  5.6 1.6 %collective-permute-start.6 = (bf16[256,128]{1,0:T(8,128)(2,1)}, bf16[256,128]{1,0:T(8,128)(2,1)S(1)}, u32[]{:S(2)}, u32[]{:S(2)}) collective-permute-start(bf16[256,128]{1,0:T(8,128)(2,1)} %param.7), channel_id=1, source_target_pairs={{0,1},{1,0},{2,3},{3,2},{4,5},{5,4},{6,7},{7,6},{8,9},{9,8},{10,11... | collective-permute-start | bytes 196616 | tf_op jit(solution)/shard_map/ppermute | solution.py:23
  7.2 1.5 %collective-permute-start.4 = (bf16[256,128]{1,0:T(8,128)(2,1)}, bf16[256,128]{1,0:T(8,128)(2,1)S(1)}, u32[]{:S(2)}, u32[]{:S(2)}) collective-permute-start(bf16[256,128]{1,0:T(8,128)(2,1)} %param.7), channel_id=1, source_target_pairs={{0,4},{4,0},{1,5},{5,1},{2,6},{6,2},{3,7},{7,3},{8,12},{12,8},{9,1... | collective-permute-start | bytes 196616 | tf_op jit(solution)/shard_map/ppermute | solution.py:23
  8.7 0.9 %constant_dynamic-update-slice_fusion.1 = bf16[512,128]{1,0:T(8,128)(2,1)S(1)} fusion(bf16[256,128]{1,0:T(8,128)(2,1)} %param.7), kind=kLoop, calls=%fused_computation.2 | loop fusion | bytes 131072
  9.6 2.1 %collective-permute-done.4 = bf16[256,128]{1,0:T(8,128)(2,1)S(1)} collective-permute-done((bf16[256,128]{1,0:T(8,128)(2,1)}, bf16[256,128]{1,0:T(8,128)(2,1)S(1)}, u32[]{:S(2)}, u32[]{:S(2)}) %collective-permute-start.4) | collective-permute-done | bytes 65568 | tf_op jit(solution)/shard_map/ppermute | solution.py:23
  11.7 0.1 collective-permute-start.5
  11.7 0.0 collective-permute-done.1
  11.8 0.4 %collective-permute-start.2 = (s32[2,8]{1,0:T(2,128)S(1)}, s32[2,8]{1,0:T(2,128)S(1)}, u32[]{:S(2)}, u32[]{:S(2)}) collective-permute-start(s32[2,8]{1,0:T(2,128)S(1)} %pad_add_fusion.1), channel_id=1, source_target_pairs={{0,2},{1,3},{2,0},{3,1},{4,6},{5,7},{6,4},{7,5},{8,10},{9,11},{10,... | collective-permute-start | bytes 200 | tf_op jit(solution)/shard_map/ppermute | solution.py:23
  12.2 0.0 collective-permute-done.6.refs_2_
  12.2 1.5 %collective-permute-start.7 = (bf16[256,128]{1,0:T(8,128)(2,1)S(1)}, bf16[256,128]{1,0:T(8,128)(2,1)S(1)}, u32[]{:S(2)}, u32[]{:S(2)}) collective-permute-start(bf16[256,128]{1,0:T(8,128)(2,1)S(1)} %collective-permute-done.6.refs_2_), channel_id=1, source_target_pairs={{0,4},{4,0},{1,5},{5,1},{2,6},{6,2},{3,7},{7,3},{8,12},{12,8},{9,1... | collective-permute-start | bytes 196616 | tf_op jit(solution)/shard_map/ppermute | solution.py:23
  13.7 3.2 %collective-permute-done.2 = s32[2,8]{1,0:T(2,128)S(1)} collective-permute-done((s32[2,8]{1,0:T(2,128)S(1)}, s32[2,8]{1,0:T(2,128)S(1)}, u32[]{:S(2)}, u32[]{:S(2)}) %collective-permute-start.2) | collective-permute-done | bytes 96 | tf_op jit(solution)/shard_map/ppermute | solution.py:23
  16.9 0.6 %pad_add_fusion.ids_ref = s32[4,8]{1,0:T(4,128)} fusion(s32[2,8]{1,0:T(2,128)S(1)} %collective-permute-done.2, s32[1,8]{1,0:T(1,128)S(1)} %collective-permute-done.1, s32[1,8]{1,0:T(1,128)S(1)} %compare_select_fusion), kind=kLoop, calls=%fused_computation.3 | loop fusion | flops 64 | bytes 256 | tf_op jit(solution)/shard_map/concatenate | solution.py:187
  17.5 0.0 collective-permute-done.refs_8_
  17.5 0.0 collective-permute-done.7.refs_4_
  17.5 0.0 collective-permute-done.5.refs_1_
  17.5 0.1 collective-permute-start.10
  17.6 0.5 %collective-permute-start.8 = (bf16[256,128]{1,0:T(8,128)(2,1)S(1)}, bf16[256,128]{1,0:T(8,128)(2,1)S(1)}, u32[]{:S(2)}, u32[]{:S(2)}) collective-permute-start(bf16[256,128]{1,0:T(8,128)(2,1)S(1)} %collective-permute-done.6.refs_2_), channel_id=1, source_target_pairs={{0,8},{8,0},{16,24},{24,16},{1,9},{9,1},{17,25},{25,17},{2,10},{10... | collective-permute-start | bytes 196616 | tf_op jit(solution)/shard_map/ppermute | solution.py:23
  18.1 0.1 collective-permute-start.9
  18.2 1.0 %collective-permute-done.8.refs_3_ = bf16[256,128]{1,0:T(8,128)(2,1)S(1)} collective-permute-done((bf16[256,128]{1,0:T(8,128)(2,1)S(1)}, bf16[256,128]{1,0:T(8,128)(2,1)S(1)}, u32[]{:S(2)}, u32[]{:S(2)}) %collective-permute-start.8) | collective-permute-done | bytes 65568 | tf_op jit(solution)/shard_map/ppermute | solution.py:23
  19.2 0.1 collective-permute-done.9.refs_5_
  19.4 0.0 collective-permute-done.10.refs_9_
  19.4 0.0 copy-done
  19.4 1.6 %partial_rows.1 = (f32[512,128]{1,0:T(8,128)S(1)}, s32[296,128]{1,0:T(8,128)S(1)}, s32[296,128]{1,0:T(8,128)S(1)}, s32[296,128]{1,0:T(8,128)S(1)}) custom-call(s32[4,8]{1,0:T(4,128)} %pad_add_fusion.ids_ref, bf16[512,128]{1,0:T(8,128)(2,1)S(1)} %constant_dynamic-update-slice_fusion.refs_0_, bf16[512,128]{1,0:T(8,128)(2,1)S(1)} %collective-permute-done.5.refs_1_, ...), custom_call_target="tpu_custom_call" | custom-call | tf_op jit(solution)/shard_map/partial_rows/pallas_call | solution.py:159
  21.0 1.2 %collective-permute-start.11 = (s32[296,128]{1,0:T(8,128)S(1)}, s32[296,128]{1,0:T(8,128)S(1)}, u32[]{:S(2)}, u32[]{:S(2)}) collective-permute-start(s32[296,128]{1,0:T(8,128)S(1)} %get-tuple-element.30), channel_id=1, source_target_pairs={{0,1},{1,0},{2,3},{3,2},{4,5},{5,4},{6,7},{7,6},{8,9},{9,8},{10,11... | collective-permute-start | bytes 454664 | tf_op jit(solution)/shard_map/ppermute | solution.py:33
  22.2 1.5 %collective-permute-start.12 = (s32[296,128]{1,0:T(8,128)S(1)}, s32[296,128]{1,0:T(8,128)S(1)}, u32[]{:S(2)}, u32[]{:S(2)}) collective-permute-start(s32[296,128]{1,0:T(8,128)S(1)} %get-tuple-element.31), channel_id=1, source_target_pairs={{0,16},{1,17},{2,18},{3,19},{4,20},{5,21},{6,22},{7,23},{8,24},{9,... | collective-permute-start | bytes 454664 | tf_op jit(solution)/shard_map/ppermute | solution.py:33
  23.6 0.9 %collective-permute-start.13 = (s32[296,128]{1,0:T(8,128)S(1)}, s32[296,128]{1,0:T(8,128)S(1)}, u32[]{:S(2)}, u32[]{:S(2)}) collective-permute-start(s32[296,128]{1,0:T(8,128)S(1)} %get-tuple-element.32), channel_id=1, source_target_pairs={{0,17},{1,16},{2,19},{3,18},{4,21},{5,20},{6,23},{7,22},{8,25},{9,... | collective-permute-start | bytes 454664 | tf_op jit(solution)/shard_map/ppermute | solution.py:33
  24.5 3.3 %collective-permute-done.11.refs_0_ = s32[296,128]{1,0:T(8,128)S(1)} collective-permute-done((s32[296,128]{1,0:T(8,128)S(1)}, s32[296,128]{1,0:T(8,128)S(1)}, u32[]{:S(2)}, u32[]{:S(2)}) %collective-permute-start.11) | collective-permute-done | bytes 151584 | tf_op jit(solution)/shard_map/ppermute | solution.py:33
  27.8 2.3 %collective-permute-done.12.refs_1_ = s32[296,128]{1,0:T(8,128)S(1)} collective-permute-done((s32[296,128]{1,0:T(8,128)S(1)}, s32[296,128]{1,0:T(8,128)S(1)}, u32[]{:S(2)}, u32[]{:S(2)}) %collective-permute-start.12) | collective-permute-done | bytes 151584 | tf_op jit(solution)/shard_map/ppermute | solution.py:33
  30.1 1.2 %collective-permute-done.13.refs_2_ = s32[296,128]{1,0:T(8,128)S(1)} collective-permute-done((s32[296,128]{1,0:T(8,128)S(1)}, s32[296,128]{1,0:T(8,128)S(1)}, u32[]{:S(2)}, u32[]{:S(2)}) %collective-permute-start.13) | collective-permute-done | bytes 151584 | tf_op jit(solution)/shard_map/ppermute | solution.py:33
  31.3 0.2 squares.1
  31.5 0.1 collective-permute-start.14
  31.6 2.4 %collective-permute-start.15 = (f32[1,128]{1,0:T(1,128)S(1)}, f32[1,128]{1,0:T(1,128)S(1)}, u32[]{:S(2)}, u32[]{:S(2)}) collective-permute-start(f32[1,128]{1,0:T(1,128)S(1)} %get-tuple-element.34), channel_id=1, source_target_pairs={{0,20},{1,21},{2,22},{3,23},{4,16},{5,17},{6,18},{7,19},{8,28},{9,... | collective-permute-start | bytes 1544 | tf_op jit(solution)/shard_map/ppermute | solution.py:33
  33.9 0.0 collective-permute-done.14
  33.9 0.7 %collective-permute-start.16 = (f32[1,128]{1,0:T(1,128)S(1)}, f32[1,128]{1,0:T(1,128)S(1)}, u32[]{:S(2)}, u32[]{:S(2)}) collective-permute-start(f32[1,128]{1,0:T(1,128)S(1)} %add.18), channel_id=1, source_target_pairs={{0,16},{1,17},{2,18},{3,19},{4,20},{5,21},{6,22},{7,23},{8,12},{9,... | collective-permute-start | bytes 1544 | tf_op jit(solution)/shard_map/ppermute | solution.py:33
  34.6 1.4 %collective-permute-done.15 = f32[1,128]{1,0:T(1,128)S(1)} collective-permute-done((f32[1,128]{1,0:T(1,128)S(1)}, f32[1,128]{1,0:T(1,128)S(1)}, u32[]{:S(2)}, u32[]{:S(2)}) %collective-permute-start.15) | collective-permute-done | bytes 544 | tf_op jit(solution)/shard_map/ppermute | solution.py:33
  36.1 1.4 %collective-permute-done.16 = f32[1,128]{1,0:T(1,128)S(1)} collective-permute-done((f32[1,128]{1,0:T(1,128)S(1)}, f32[1,128]{1,0:T(1,128)S(1)}, u32[]{:S(2)}, u32[]{:S(2)}) %collective-permute-start.16) | collective-permute-done | bytes 544 | tf_op jit(solution)/shard_map/ppermute | solution.py:33
  37.5 0.0 collective-permute-start.17
  37.5 1.1 %collective-permute-done.17 = f32[1,128]{1,0:T(1,128)S(1)} collective-permute-done((f32[1,128]{1,0:T(1,128)S(1)}, f32[1,128]{1,0:T(1,128)S(1)}, u32[]{:S(2)}, u32[]{:S(2)}) %collective-permute-start.17) | collective-permute-done | bytes 544 | tf_op jit(solution)/shard_map/ppermute | solution.py:23
  38.6 0.7 %multiply_bitcast_fusion = f32[1,512,128]{2,1,0:T(8,128)} fusion(f32[512,128]{1,0:T(8,128)S(1)} %get-tuple-element.33, f32[128]{0:T(128)S(1)} %divide_bitcast_fusion), kind=kLoop, calls=%fused_computation | loop fusion | flops 65536 | bytes 524800 | tf_op jit(solution)/shard_map/broadcast_in_dim | solution.py:226
  (5 shorter events, 0.0 us)
Async XLA Ops:
  0.0 19.4 %copy-start = (bf16[1,8,128,128]{3,2,1,0:T(8,128)(2,1)S(1)}, bf16[1,8,128,128]{3,2,1,0:T(8,128)(2,1)}, u32[]{:S(2)}) copy-start(bf16[1,8,128,128]{3,2,1,0:T(8,128)(2,1)} %param.4) | copy-start | bytes 786436
  0.0 5.6 %collective-permute-start.3 = (bf16[8,128,128]{2,1,0:T(8,128)(2,1)}, bf16[8,128,128]{2,1,0:T(8,128)(2,1)S(1)}, u32[]{:S(2)}, u32[]{:S(2)}) collective-permute-start(bf16[8,128,128]{2,1,0:T(8,128)(2,1)} %bitcast.7), channel_id=1, source_target_pairs={{0,8},{8,0},{16,24},{24,16},{1,9},{9,1},{17,25},{25,17},{2,10},{10... | collective-permute-start | bytes 786440 | tf_op jit(solution)/shard_map/ppermute | solution.py:23
  0.5 17.1 %collective-permute-start = (bf16[8,128,128]{2,1,0:T(8,128)(2,1)}, bf16[8,128,128]{2,1,0:T(8,128)(2,1)S(1)}, u32[]{:S(2)}, u32[]{:S(2)}) collective-permute-start(bf16[8,128,128]{2,1,0:T(8,128)(2,1)} %bitcast.8), channel_id=1, source_target_pairs={{0,2},{1,3},{2,0},{3,1},{4,6},{5,7},{6,4},{7,5},{8,10},{9,11},{10,... | collective-permute-start | bytes 786440 | tf_op jit(solution)/shard_map/ppermute | solution.py:23
  5.4 6.3 %collective-permute-start.1 = (s32[1,8]{1,0:T(1,128)S(1)}, s32[1,8]{1,0:T(1,128)S(1)}, u32[]{:S(2)}, u32[]{:S(2)}) collective-permute-start(s32[1,8]{1,0:T(1,128)S(1)} %compare_select_fusion), channel_id=1, source_target_pairs={{0,8},{8,0},{16,24},{24,16},{1,9},{9,1},{17,25},{25,17},{2,10},{10... | collective-permute-start | bytes 104 | tf_op jit(solution)/shard_map/ppermute | solution.py:23
  5.6 6.6 %collective-permute-start.6 = (bf16[256,128]{1,0:T(8,128)(2,1)}, bf16[256,128]{1,0:T(8,128)(2,1)S(1)}, u32[]{:S(2)}, u32[]{:S(2)}) collective-permute-start(bf16[256,128]{1,0:T(8,128)(2,1)} %param.7), channel_id=1, source_target_pairs={{0,1},{1,0},{2,3},{3,2},{4,5},{5,4},{6,7},{7,6},{8,9},{9,8},{10,11... | collective-permute-start | bytes 196616 | tf_op jit(solution)/shard_map/ppermute | solution.py:23
  7.2 4.5 %collective-permute-start.4 = (bf16[256,128]{1,0:T(8,128)(2,1)}, bf16[256,128]{1,0:T(8,128)(2,1)S(1)}, u32[]{:S(2)}, u32[]{:S(2)}) collective-permute-start(bf16[256,128]{1,0:T(8,128)(2,1)} %param.7), channel_id=1, source_target_pairs={{0,4},{4,0},{1,5},{5,1},{2,6},{6,2},{3,7},{7,3},{8,12},{12,8},{9,1... | collective-permute-start | bytes 196616 | tf_op jit(solution)/shard_map/ppermute | solution.py:23
  11.7 5.9 %collective-permute-start.5 = (bf16[512,128]{1,0:T(8,128)(2,1)S(1)}, bf16[512,128]{1,0:T(8,128)(2,1)S(1)}, u32[]{:S(2)}, u32[]{:S(2)}) collective-permute-start(bf16[512,128]{1,0:T(8,128)(2,1)S(1)} %constant_dynamic-update-slice_fusion.refs_0_), channel_id=1, source_target_pairs={{0,8},{8,0},{16,24},{24,16},{1,9},{9,1},{17,25},{25,17},{2,10},{10... | collective-permute-start | bytes 393224 | tf_op jit(solution)/shard_map/ppermute | solution.py:23
  11.8 5.2 %collective-permute-start.2 = (s32[2,8]{1,0:T(2,128)S(1)}, s32[2,8]{1,0:T(2,128)S(1)}, u32[]{:S(2)}, u32[]{:S(2)}) collective-permute-start(s32[2,8]{1,0:T(2,128)S(1)} %pad_add_fusion.1), channel_id=1, source_target_pairs={{0,2},{1,3},{2,0},{3,1},{4,6},{5,7},{6,4},{7,5},{8,10},{9,11},{10,... | collective-permute-start | bytes 200 | tf_op jit(solution)/shard_map/ppermute | solution.py:23
  12.2 5.4 %collective-permute-start.7 = (bf16[256,128]{1,0:T(8,128)(2,1)S(1)}, bf16[256,128]{1,0:T(8,128)(2,1)S(1)}, u32[]{:S(2)}, u32[]{:S(2)}) collective-permute-start(bf16[256,128]{1,0:T(8,128)(2,1)S(1)} %collective-permute-done.6.refs_2_), channel_id=1, source_target_pairs={{0,4},{4,0},{1,5},{5,1},{2,6},{6,2},{3,7},{7,3},{8,12},{12,8},{9,1... | collective-permute-start | bytes 196616 | tf_op jit(solution)/shard_map/ppermute | solution.py:23
  17.5 1.8 %collective-permute-start.10 = (bf16[8,128,128]{2,1,0:T(8,128)(2,1)S(1)}, bf16[8,128,128]{2,1,0:T(8,128)(2,1)S(1)}, u32[]{:S(2)}, u32[]{:S(2)}) collective-permute-start(bf16[8,128,128]{2,1,0:T(8,128)(2,1)S(1)} %collective-permute-done.refs_8_), channel_id=1, source_target_pairs={{0,8},{8,0},{16,24},{24,16},{1,9},{9,1},{17,25},{25,17},{2,10},{10... | collective-permute-start | bytes 786440 | tf_op jit(solution)/shard_map/ppermute | solution.py:23
  17.6 1.6 %collective-permute-start.8 = (bf16[256,128]{1,0:T(8,128)(2,1)S(1)}, bf16[256,128]{1,0:T(8,128)(2,1)S(1)}, u32[]{:S(2)}, u32[]{:S(2)}) collective-permute-start(bf16[256,128]{1,0:T(8,128)(2,1)S(1)} %collective-permute-done.6.refs_2_), channel_id=1, source_target_pairs={{0,8},{8,0},{16,24},{24,16},{1,9},{9,1},{17,25},{25,17},{2,10},{10... | collective-permute-start | bytes 196616 | tf_op jit(solution)/shard_map/ppermute | solution.py:23
  18.1 1.3 %collective-permute-start.9 = (bf16[256,128]{1,0:T(8,128)(2,1)S(1)}, bf16[256,128]{1,0:T(8,128)(2,1)S(1)}, u32[]{:S(2)}, u32[]{:S(2)}) collective-permute-start(bf16[256,128]{1,0:T(8,128)(2,1)S(1)} %collective-permute-done.7.refs_4_), channel_id=1, source_target_pairs={{0,8},{8,0},{16,24},{24,16},{1,9},{9,1},{17,25},{25,17},{2,10},{10... | collective-permute-start | bytes 196616 | tf_op jit(solution)/shard_map/ppermute | solution.py:23
  21.0 6.8 %collective-permute-start.11 = (s32[296,128]{1,0:T(8,128)S(1)}, s32[296,128]{1,0:T(8,128)S(1)}, u32[]{:S(2)}, u32[]{:S(2)}) collective-permute-start(s32[296,128]{1,0:T(8,128)S(1)} %get-tuple-element.30), channel_id=1, source_target_pairs={{0,1},{1,0},{2,3},{3,2},{4,5},{5,4},{6,7},{7,6},{8,9},{9,8},{10,11... | collective-permute-start | bytes 454664 | tf_op jit(solution)/shard_map/ppermute | solution.py:33
  22.2 8.0 %collective-permute-start.12 = (s32[296,128]{1,0:T(8,128)S(1)}, s32[296,128]{1,0:T(8,128)S(1)}, u32[]{:S(2)}, u32[]{:S(2)}) collective-permute-start(s32[296,128]{1,0:T(8,128)S(1)} %get-tuple-element.31), channel_id=1, source_target_pairs={{0,16},{1,17},{2,18},{3,19},{4,20},{5,21},{6,22},{7,23},{8,24},{9,... | collective-permute-start | bytes 454664 | tf_op jit(solution)/shard_map/ppermute | solution.py:33
  23.6 7.6 %collective-permute-start.13 = (s32[296,128]{1,0:T(8,128)S(1)}, s32[296,128]{1,0:T(8,128)S(1)}, u32[]{:S(2)}, u32[]{:S(2)}) collective-permute-start(s32[296,128]{1,0:T(8,128)S(1)} %get-tuple-element.32), channel_id=1, source_target_pairs={{0,17},{1,16},{2,19},{3,18},{4,21},{5,20},{6,23},{7,22},{8,25},{9,... | collective-permute-start | bytes 454664 | tf_op jit(solution)/shard_map/ppermute | solution.py:33
  31.5 2.4 %collective-permute-start.14 = (f32[1,128]{1,0:T(1,128)S(1)}, f32[1,128]{1,0:T(1,128)S(1)}, u32[]{:S(2)}, u32[]{:S(2)}) collective-permute-start(f32[1,128]{1,0:T(1,128)S(1)} %get-tuple-element.34), channel_id=1, source_target_pairs={{0,8},{8,0},{16,24},{24,16},{1,9},{9,1},{17,25},{25,17},{2,10},{10... | collective-permute-start | bytes 1544 | tf_op jit(solution)/shard_map/ppermute | solution.py:23
  31.6 4.5 %collective-permute-start.15 = (f32[1,128]{1,0:T(1,128)S(1)}, f32[1,128]{1,0:T(1,128)S(1)}, u32[]{:S(2)}, u32[]{:S(2)}) collective-permute-start(f32[1,128]{1,0:T(1,128)S(1)} %get-tuple-element.34), channel_id=1, source_target_pairs={{0,20},{1,21},{2,22},{3,23},{4,16},{5,17},{6,18},{7,19},{8,28},{9,... | collective-permute-start | bytes 1544 | tf_op jit(solution)/shard_map/ppermute | solution.py:33
  33.9 3.5 %collective-permute-start.16 = (f32[1,128]{1,0:T(1,128)S(1)}, f32[1,128]{1,0:T(1,128)S(1)}, u32[]{:S(2)}, u32[]{:S(2)}) collective-permute-start(f32[1,128]{1,0:T(1,128)S(1)} %add.18), channel_id=1, source_target_pairs={{0,16},{1,17},{2,18},{3,19},{4,20},{5,21},{6,22},{7,23},{8,12},{9,... | collective-permute-start | bytes 1544 | tf_op jit(solution)/shard_map/ppermute | solution.py:33
  37.5 1.1 %collective-permute-start.17 = (f32[1,128]{1,0:T(1,128)S(1)}, f32[1,128]{1,0:T(1,128)S(1)}, u32[]{:S(2)}, u32[]{:S(2)}) collective-permute-start(f32[1,128]{1,0:T(1,128)S(1)} %add.19), channel_id=1, source_target_pairs={{0,8},{8,0},{16,24},{24,16},{1,9},{9,1},{17,25},{25,17},{2,10},{10... | collective-permute-start | bytes 1544 | tf_op jit(solution)/shard_map/ppermute | solution.py:23

commit v9 on v8

--- a/solution.py
+++ b/solution.py
@@ -12,7 +12,6 @@
 AXES = ("layer", "row", "col")
 BITS, VALUES, WORDS = 18, 16, 9
 VMEM = pl.BlockSpec(memory_space=pltpu.VMEM)
-SMEM = pl.BlockSpec(memory_space=pltpu.SMEM)
 
 
 def pin(x):
@@ -106,21 +105,19 @@
     sum_ref[...] = total
 
 
-def product_kernel(masks, n_layer, n_row, n_col, ids_ref, *refs):
+def product_kernel(masks, n_layer, n_row, n_col, lists_ref, *refs):
     n_slots, n_held = n_layer // 2, 2 * len(masks)
     mine_refs, near_refs = refs[:2], refs[2 : 2 + 2 * n_row]
-    a_refs, out_refs = refs[2 + 2 * n_row : 2 + 2 * n_row + n_held], refs[2 + 2 * n_row + n_held : -2]
-    where_ref, lhs_ref = refs[-2:]
+    a_refs, out_refs = refs[2 + 2 * n_row : 2 + 2 * n_row + n_held], refs[2 + 2 * n_row + n_held : -1]
+    lhs_ref = refs[-1]
     layer, row, col = (lax.axis_index(n) for n in ("layer", "row", "col"))
     per, per_row = IB // n_layer, n_col // n_row
     capacity, block, depth = a_refs[0].shape
+    lists = lists_ref[...]
+    lists = [[lists[k, h] for h in range(lists.shape[1])] for k in range(n_held)]
     rhs = []
     for k in range(n_held):
         other, place = k % 2, k // 2
-        for i in range(IB + 1):
-            where_ref[k, i] = -1
-        for n in range(capacity):
-            where_ref[k, ids_ref[k, n]] = n
         panel = col ^ masks[place]
         at = panel % per_row * depth
         owner = (panel // per_row) ^ row
@@ -132,42 +129,55 @@
             near = jnp.where(owner == i, near_refs[2 * i + other][at, :], near)
         rhs.append(jnp.concatenate([mine, near], axis=1))
     rhs = jnp.concatenate(rhs, axis=0)
-    width = rhs.shape[1] // 2
+    width, parts = rhs.shape[1] // 2, []
     for slot in range(n_slots):
         for sub in range(per):
             block_row = (layer ^ (2 * slot)) * per + sub
             for k in range(n_held):
-                n = where_ref[k, block_row]
-                a = a_refs[k][jnp.maximum(n, 0)]
+                word = lists[k][0]
+                for h in range(1, len(lists[k])):
+                    word = jnp.where(block_row // 8 == h, lists[k][h], word)
+                n = (word >> (block_row % 8 * 4)) & 15
+                a = a_refs[k][jnp.minimum(n, capacity - 1)]
                 lhs_ref[slot, sub * block : (sub + 1) * block, k * depth : (k + 1) * depth] = (
-                    jnp.where(n >= 0, a, jnp.zeros_like(a))
+                    jnp.where(n < capacity, a, jnp.zeros_like(a))
                 )
         out = jnp.dot(lhs_ref[slot], rhs, preferred_element_type=jnp.float32)
-        for m in range(2):
-            part, out_ref = out[:, m * width : (m + 1) * width], out_refs[2 * slot + m]
-            if slot or m:
-                pack(part, out_ref)
-            else:
-                out_ref[...] = part
-
-
-def products(masks, ids, b_refs, panels):
+        parts += [out[:, m * width : (m + 1) * width] for m in range(2)]
+    out_refs[0][...] = parts[0]
+    for k in range(1, 2 * n_slots - 1, 2):
+        one, two = parts[k : k + 2]
+        pack(jnp.where(layer % 2 == 0, one, two), out_refs[k])
+        pack(jnp.where(layer % 2 == 0, two, one), out_refs[k + 1])
+    pack(parts[-1], out_refs[-1])
+
+
+def products(masks, lists, b_refs, panels):
     n_layer, n_row, n_col = (lax.axis_size(a) for a in ("layer", "row", "col"))
     _, block, depth = panels[0].shape
     rows, n_slots, width = IB // n_layer * block, n_layer // 2, b_refs[0].shape[1]
-    ins = [*b_refs, *panels]
+    ins = [lists, *b_refs, *panels]
     return pl.pallas_call(
         functools.partial(product_kernel, masks, n_layer, n_row, n_col),
         out_shape=[pltpu.VMEM((rows, width), jnp.float32)]
         + [pltpu.VMEM((rows // VALUES * WORDS + 8, width), jnp.int32)] * (2 * n_slots - 1),
-        in_specs=[SMEM] + [VMEM] * len(ins),
+        in_specs=[VMEM] * len(ins),
         out_specs=[VMEM] * (2 * n_slots),
         scratch_shapes=[
-            pltpu.SMEM((len(panels), IB + 1), jnp.int32),
             pltpu.VMEM((n_slots, rows, len(panels) * depth), jnp.bfloat16),
         ],
         name="partial_rows",
-    )(ids, *(pin(x) for x in ins))
+    )(*(pin(x) for x in ins))
+
+
+def whereabouts(a_rows, a_count):
+    panels, capacity = a_rows.shape
+    place = jnp.arange(capacity, dtype=jnp.int32)
+    valid = place[None, :] < a_count[:, None]
+    block_rows = jnp.arange(IB, dtype=jnp.int32)
+    listed = (a_rows[:, :, None] == block_rows) & valid[:, :, None]
+    places = capacity + jnp.sum(jnp.where(listed, place[:, None] - capacity, 0), axis=1)
+    return jnp.sum((places << (block_rows % 8 * 4)).reshape(panels, IB // 8, 8), axis=2)
 
 
 def body(a_blocks, a_rows, a_count, b_panel):
@@ -178,13 +188,12 @@
         return xor_permute(x, "layer", 1)
 
     masks, panels = [0], [a_blocks[0]]
-    valid = jnp.arange(capacity, dtype=jnp.int32)[None, :] < a_count[:, None]
-    ids = jnp.where(valid, a_rows, IB)
-    ids = jnp.concatenate([ids, other(ids)])
+    lists = whereabouts(a_rows, a_count)
+    lists = jnp.concatenate([lists, other(lists)])
     bit = n_col // 2
     while bit > 1:
         panels = panels + [xor_permute(p, "col", bit) for p in panels]
-        ids = jnp.concatenate([ids, xor_permute(ids, "col", bit)])
+        lists = jnp.concatenate([lists, xor_permute(lists, "col", bit)])
         masks = masks + [m ^ bit for m in masks]
         bit //= 2
 
@@ -201,15 +210,19 @@
     mine = [mine, other(mine)]
     near = [pair[1] for pair in b_rows]
     own = a_blocks[0]
-    far, ids, mine, near, own_other = lax.optimization_barrier(
-        (panels[1:], ids, mine, near, own_other)
+    far, lists, mine, near, own_other = lax.optimization_barrier(
+        (panels[1:], lists, mine, near, own_other)
     )
     near = [x for b in near for x in (b, other(b))]
     panels = [own, own_other] + [x for p in far for x in (p, other(p))]
     b_refs = mine + near
-    parts = products(masks, ids, b_refs, panels)
-
-    parts = [parts[0]] + [grid_permute(parts[k], (2 * (k // 2), 0, k % 2)) for k in range(1, n_layer)]
+    parts = products(masks, lists, b_refs, panels)
+
+    masks = [(2 * (k // 2), 0, k % 2) for k in range(n_layer)]
+    swaps = [0] + [k + 1 if k % 2 else k - 1 for k in range(1, n_layer - 1)] + [n_layer - 1]
+    parts = [parts[0]] + [
+        grid_permute(parts[k], masks[k], masks[swaps[k]]) for k in range(1, n_layer)
+    ]
     sq, col_sum = pl.pallas_call(
         square_kernel,
         out_shape=(

time: 39.5 us -> 38.2 us (0.967)
  Pallas kernels: 1.84 us -> 1.14 us
  waiting for transfers between devices: 17.2 us -> 16.7 us
    reduce_sum x0 -> x2, other arithmetic: none -> 0.87 us  [the longest x1 0.74 us: whereabouts(): jnp.sum(jnp.where(listed, place[:, None] - capacity, 0), axis=1)]
    pallas_call x1, Pallas kernels: 1.62 us -> 0.92 us  [products(): pl.pallas_call(functools.partial(product_kernel, masks, n_layer, n_row, n...]
    select_n x1 -> x0, other arithmetic: 0.66 us -> none  [body(): ids = jnp.where(valid, a_rows, IB)]
    concatenate x2, other arithmetic: 0.6 us -> 0.02 us  [the longest x1 0.01 us: body(): lists = jnp.concatenate([lists, other(lists)])]
where the time goes in v9:
time: 38.2 us; the launch traced here: 38 us
  starting transfers between devices  16.8 us (44%)
  waiting for transfers between devices  16.7 us (44%)
  other arithmetic  1.65 us (4%)
  Pallas kernels  1.14 us (3%)
  local copies, waits for them, and re-layouts  0.98 us (3%)
  between operations  0.75 us (2%)
    ppermute x13, starting transfers between devices, xor_permute(): lax.ppermute(x, axis, [(i, i ^ mask) for i in range(lax.axis_size(axis))])  10.1 us
    ppermute x5, waiting for transfers between devices, grid_permute(): return lax.ppermute(x, AXES, pairs)  9.45 us
    ppermute x13, waiting for transfers between devices, xor_permute(): lax.ppermute(x, axis, [(i, i ^ mask) for i in range(lax.axis_size(axis))])  7.26 us
    ppermute x5, starting transfers between devices, grid_permute(): return lax.ppermute(x, AXES, pairs)  6.67 us
    pallas_call x1, Pallas kernels, products(): pl.pallas_call(functools.partial(product_kernel, masks, n_layer, n_row, n...  0.92 us
    unnamed x3, local copies, waits for them, and re-layouts  0.88 us
  transfers between devices with their start and end apart: 18, of which 10 were waited for; matrix products, arithmetic and copies ran while one was open for 5% of the time, Pallas kernels for 0%

profile of v9, /device:TPU:0, one launch (start us, length us, event | category | flops | bytes accessed | tf_op | source)
XLA Modules:
  0.0 38.0 jit_solution(5628569135685435055)
XLA Ops:
  0.0 0.0 copy-start
  0.0 0.5 %collective-permute-start.3 = (bf16[8,128,128]{2,1,0:T(8,128)(2,1)}, bf16[8,128,128]{2,1,0:T(8,128)(2,1)S(1)}, u32[]{:S(2)}, u32[]{:S(2)}) collective-permute-start(bf16[8,128,128]{2,1,0:T(8,128)(2,1)} %bitcast.9), channel_id=1, source_target_pairs={{0,8},{8,0},{16,24},{24,16},{1,9},{9,1},{17,25},{25,17},{2,10},{10... | collective-permute-start | bytes 786440 | tf_op jit(solution)/shard_map/ppermute | solution.py:22
  0.5 3.6 %collective-permute-start = (bf16[8,128,128]{2,1,0:T(8,128)(2,1)}, bf16[8,128,128]{2,1,0:T(8,128)(2,1)S(1)}, u32[]{:S(2)}, u32[]{:S(2)}) collective-permute-start(bf16[8,128,128]{2,1,0:T(8,128)(2,1)} %bitcast.10), channel_id=1, source_target_pairs={{0,2},{1,3},{2,0},{3,1},{4,6},{5,7},{6,4},{7,5},{8,10},{9,11},{10,... | collective-permute-start | bytes 786440 | tf_op jit(solution)/shard_map/ppermute | solution.py:22
  4.8 0.7 %select_reduce_fusion = s32[16]{0:T(128)S(1)} fusion(s32[8]{0:T(128)S(1)} %iota_add_fusion, s32[8]{0:T(128)} %bitcast.15, pred[8]{0:T(512)(128)(4,1)S(1)} %iota_compare_fusion.1), kind=kLoop, calls=%fused_computation.3 | loop fusion | flops 496 | bytes 136 | tf_op jit(solution)/shard_map/reduce_sum | solution.py:179
  5.5 0.1 add.60
  5.6 0.1 fusion.4
  5.7 0.2 collective-permute-start.1
  6.0 0.0 collective-permute-done.3.refs_7_
  6.0 1.6 %collective-permute-start.6 = (bf16[256,128]{1,0:T(8,128)(2,1)}, bf16[256,128]{1,0:T(8,128)(2,1)S(1)}, u32[]{:S(2)}, u32[]{:S(2)}) collective-permute-start(bf16[256,128]{1,0:T(8,128)(2,1)} %param.7), channel_id=1, source_target_pairs={{0,1},{1,0},{2,3},{3,2},{4,5},{5,4},{6,7},{7,6},{8,9},{9,8},{10,11... | collective-permute-start | bytes 196616 | tf_op jit(solution)/shard_map/ppermute | solution.py:22
  7.5 1.5 %collective-permute-start.4 = (bf16[256,128]{1,0:T(8,128)(2,1)}, bf16[256,128]{1,0:T(8,128)(2,1)S(1)}, u32[]{:S(2)}, u32[]{:S(2)}) collective-permute-start(bf16[256,128]{1,0:T(8,128)(2,1)} %param.7), channel_id=1, source_target_pairs={{0,4},{4,0},{1,5},{5,1},{2,6},{6,2},{3,7},{7,3},{8,12},{12,8},{9,1... | collective-permute-start | bytes 196616 | tf_op jit(solution)/shard_map/ppermute | solution.py:22
  9.1 0.9 %constant_dynamic-update-slice_fusion.1 = bf16[512,128]{1,0:T(8,128)(2,1)S(1)} fusion(bf16[256,128]{1,0:T(8,128)(2,1)} %param.7), kind=kLoop, calls=%fused_computation.2 | loop fusion | bytes 131072
  9.9 2.1 %collective-permute-done.4 = bf16[256,128]{1,0:T(8,128)(2,1)S(1)} collective-permute-done((bf16[256,128]{1,0:T(8,128)(2,1)}, bf16[256,128]{1,0:T(8,128)(2,1)S(1)}, u32[]{:S(2)}, u32[]{:S(2)}) %collective-permute-start.4) | collective-permute-done | bytes 65568 | tf_op jit(solution)/shard_map/ppermute | solution.py:22
  12.0 0.1 collective-permute-start.5
  12.1 0.0 collective-permute-done.1
  12.1 0.4 %collective-permute-start.2 = (s32[2,2]{1,0:T(2,128)S(1)}, s32[2,2]{1,0:T(2,128)S(1)}, u32[]{:S(2)}, u32[]{:S(2)}) collective-permute-start(s32[2,2]{1,0:T(2,128)S(1)} %pad_add_fusion.1), channel_id=1, source_target_pairs={{0,2},{1,3},{2,0},{3,1},{4,6},{5,7},{6,4},{7,5},{8,10},{9,11},{10,... | collective-permute-start | bytes 56 | tf_op jit(solution)/shard_map/ppermute | solution.py:22
  12.5 0.0 collective-permute-done.6.refs_2_
  12.5 1.5 %collective-permute-start.7 = (bf16[256,128]{1,0:T(8,128)(2,1)S(1)}, bf16[256,128]{1,0:T(8,128)(2,1)S(1)}, u32[]{:S(2)}, u32[]{:S(2)}) collective-permute-start(bf16[256,128]{1,0:T(8,128)(2,1)S(1)} %collective-permute-done.6.refs_2_), channel_id=1, source_target_pairs={{0,4},{4,0},{1,5},{5,1},{2,6},{6,2},{3,7},{7,3},{8,12},{12,8},{9,1... | collective-permute-start | bytes 196616 | tf_op jit(solution)/shard_map/ppermute | solution.py:22
  14.1 2.9 %collective-permute-done.2 = s32[2,2]{1,0:T(2,128)S(1)} collective-permute-done((s32[2,2]{1,0:T(2,128)S(1)}, s32[2,2]{1,0:T(2,128)S(1)}, u32[]{:S(2)}, u32[]{:S(2)}) %collective-permute-start.2) | collective-permute-done | bytes 48 | tf_op jit(solution)/shard_map/ppermute | solution.py:22
  16.9 0.0 collective-permute-done.refs_8_
  16.9 0.0 collective-permute-done.7.refs_4_
  17.0 0.0 collective-permute-done.5.refs_1_
  17.0 0.1 collective-permute-start.10
  17.0 0.5 %collective-permute-start.8 = (bf16[256,128]{1,0:T(8,128)(2,1)S(1)}, bf16[256,128]{1,0:T(8,128)(2,1)S(1)}, u32[]{:S(2)}, u32[]{:S(2)}) collective-permute-start(bf16[256,128]{1,0:T(8,128)(2,1)S(1)} %collective-permute-done.6.refs_2_), channel_id=1, source_target_pairs={{0,8},{8,0},{16,24},{24,16},{1,9},{9,1},{17,25},{25,17},{2,10},{10... | collective-permute-start | bytes 196616 | tf_op jit(solution)/shard_map/ppermute | solution.py:22
  17.5 0.1 collective-permute-start.9
  17.6 1.0 %collective-permute-done.8.refs_3_ = bf16[256,128]{1,0:T(8,128)(2,1)S(1)} collective-permute-done((bf16[256,128]{1,0:T(8,128)(2,1)S(1)}, bf16[256,128]{1,0:T(8,128)(2,1)S(1)}, u32[]{:S(2)}, u32[]{:S(2)}) %collective-permute-start.8) | collective-permute-done | bytes 65568 | tf_op jit(solution)/shard_map/ppermute | solution.py:22
  18.7 0.1 collective-permute-done.9.refs_5_
  18.8 0.0 collective-permute-done.10.refs_9_
  18.8 0.0 copy-done
  18.8 0.9 %partial_rows.1 = (f32[512,128]{1,0:T(8,128)S(1)}, s32[296,128]{1,0:T(8,128)S(1)}, s32[296,128]{1,0:T(8,128)S(1)}, s32[296,128]{1,0:T(8,128)S(1)}) custom-call(s32[4,2]{1,0:T(4,128)S(1)} %pad_add_fusion.lists_ref, bf16[512,128]{1,0:T(8,128)(2,1)S(1)} %constant_dynamic-update-slice_fusion.refs_0_, bf16[512,128]{1,0:T(8,128)(2,1)S(1)} %collective-permute-done.5.refs_1_, ...), custom_call_target="tpu_custom_call" | custom-call | tf_op jit(solution)/shard_map/partial_rows/pallas_call | solution.py:160
  19.7 1.7 %collective-permute-start.11 = (s32[296,128]{1,0:T(8,128)S(1)}, s32[296,128]{1,0:T(8,128)S(1)}, u32[]{:S(2)}, u32[]{:S(2)}) collective-permute-start(s32[296,128]{1,0:T(8,128)S(1)} %get-tuple-element.30), channel_id=1, source_target_pairs={{0,1},{1,0},{2,3},{3,2},{4,5},{5,4},{6,7},{7,6},{8,24},{9,25},{10,... | collective-permute-start | bytes 454664 | tf_op jit(solution)/shard_map/ppermute | solution.py:32
  21.4 1.5 %collective-permute-start.12 = (s32[296,128]{1,0:T(8,128)S(1)}, s32[296,128]{1,0:T(8,128)S(1)}, u32[]{:S(2)}, u32[]{:S(2)}) collective-permute-start(s32[296,128]{1,0:T(8,128)S(1)} %get-tuple-element.31), channel_id=1, source_target_pairs={{0,16},{1,17},{2,18},{3,19},{4,20},{5,21},{6,22},{7,23},{8,9},{9,8... | collective-permute-start | bytes 454664 | tf_op jit(solution)/shard_map/ppermute | solution.py:32
  22.9 0.3 collective-permute-start.13
  23.3 3.0 %collective-permute-done.11.refs_0_ = s32[296,128]{1,0:T(8,128)S(1)} collective-permute-done((s32[296,128]{1,0:T(8,128)S(1)}, s32[296,128]{1,0:T(8,128)S(1)}, u32[]{:S(2)}, u32[]{:S(2)}) %collective-permute-start.11) | collective-permute-done | bytes 151584 | tf_op jit(solution)/shard_map/ppermute | solution.py:32
  26.2 0.6 %collective-permute-done.12.refs_1_ = s32[296,128]{1,0:T(8,128)S(1)} collective-permute-done((s32[296,128]{1,0:T(8,128)S(1)}, s32[296,128]{1,0:T(8,128)S(1)}, u32[]{:S(2)}, u32[]{:S(2)}) %collective-permute-start.12) | collective-permute-done | bytes 151584 | tf_op jit(solution)/shard_map/ppermute | solution.py:32
  26.9 3.4 %collective-permute-done.13.refs_2_ = s32[296,128]{1,0:T(8,128)S(1)} collective-permute-done((s32[296,128]{1,0:T(8,128)S(1)}, s32[296,128]{1,0:T(8,128)S(1)}, u32[]{:S(2)}, u32[]{:S(2)}) %collective-permute-start.13) | collective-permute-done | bytes 151584 | tf_op jit(solution)/shard_map/ppermute | solution.py:32
  30.2 0.2 squares.1
  30.5 0.1 collective-permute-start.14
  30.5 2.1 %collective-permute-start.15 = (f32[1,128]{1,0:T(1,128)S(1)}, f32[1,128]{1,0:T(1,128)S(1)}, u32[]{:S(2)}, u32[]{:S(2)}) collective-permute-start(f32[1,128]{1,0:T(1,128)S(1)} %get-tuple-element.34), channel_id=1, source_target_pairs={{0,20},{1,21},{2,22},{3,23},{4,16},{5,17},{6,18},{7,19},{8,28},{9,... | collective-permute-start | bytes 1544 | tf_op jit(solution)/shard_map/ppermute | solution.py:32
  32.6 0.0 collective-permute-done.14
  32.6 1.0 %collective-permute-start.16 = (f32[1,128]{1,0:T(1,128)S(1)}, f32[1,128]{1,0:T(1,128)S(1)}, u32[]{:S(2)}, u32[]{:S(2)}) collective-permute-start(f32[1,128]{1,0:T(1,128)S(1)} %add.62), channel_id=1, source_target_pairs={{0,16},{1,17},{2,18},{3,19},{4,20},{5,21},{6,22},{7,23},{8,12},{9,... | collective-permute-start | bytes 1544 | tf_op jit(solution)/shard_map/ppermute | solution.py:32
  33.7 1.4 %collective-permute-done.15 = f32[1,128]{1,0:T(1,128)S(1)} collective-permute-done((f32[1,128]{1,0:T(1,128)S(1)}, f32[1,128]{1,0:T(1,128)S(1)}, u32[]{:S(2)}, u32[]{:S(2)}) %collective-permute-start.15) | collective-permute-done | bytes 544 | tf_op jit(solution)/shard_map/ppermute | solution.py:32
  35.0 1.1 %collective-permute-done.16 = f32[1,128]{1,0:T(1,128)S(1)} collective-permute-done((f32[1,128]{1,0:T(1,128)S(1)}, f32[1,128]{1,0:T(1,128)S(1)}, u32[]{:S(2)}, u32[]{:S(2)}) %collective-permute-start.16) | collective-permute-done | bytes 544 | tf_op jit(solution)/shard_map/ppermute | solution.py:32
  36.2 0.0 collective-permute-start.17
  36.2 1.1 %collective-permute-done.17 = f32[1,128]{1,0:T(1,128)S(1)} collective-permute-done((f32[1,128]{1,0:T(1,128)S(1)}, f32[1,128]{1,0:T(1,128)S(1)}, u32[]{:S(2)}, u32[]{:S(2)}) %collective-permute-start.17) | collective-permute-done | bytes 544 | tf_op jit(solution)/shard_map/ppermute | solution.py:22
  37.3 0.7 %multiply_bitcast_fusion = f32[1,512,128]{2,1,0:T(8,128)} fusion(f32[512,128]{1,0:T(8,128)S(1)} %get-tuple-element.33, f32[128]{0:T(128)S(1)} %divide_bitcast_fusion), kind=kLoop, calls=%fused_computation | loop fusion | flops 65536 | bytes 524800 | tf_op jit(solution)/shard_map/broadcast_in_dim | solution.py:239
  (9 shorter events, 0.1 us)
Async XLA Ops:
  0.0 18.8 %copy-start = (bf16[1,8,128,128]{3,2,1,0:T(8,128)(2,1)S(1)}, bf16[1,8,128,128]{3,2,1,0:T(8,128)(2,1)}, u32[]{:S(2)}) copy-start(bf16[1,8,128,128]{3,2,1,0:T(8,128)(2,1)} %param.4) | copy-start | bytes 786436
  0.0 6.0 %collective-permute-start.3 = (bf16[8,128,128]{2,1,0:T(8,128)(2,1)}, bf16[8,128,128]{2,1,0:T(8,128)(2,1)S(1)}, u32[]{:S(2)}, u32[]{:S(2)}) collective-permute-start(bf16[8,128,128]{2,1,0:T(8,128)(2,1)} %bitcast.9), channel_id=1, source_target_pairs={{0,8},{8,0},{16,24},{24,16},{1,9},{9,1},{17,25},{25,17},{2,10},{10... | collective-permute-start | bytes 786440 | tf_op jit(solution)/shard_map/ppermute | solution.py:22
  0.5 16.5 %collective-permute-start = (bf16[8,128,128]{2,1,0:T(8,128)(2,1)}, bf16[8,128,128]{2,1,0:T(8,128)(2,1)S(1)}, u32[]{:S(2)}, u32[]{:S(2)}) collective-permute-start(bf16[8,128,128]{2,1,0:T(8,128)(2,1)} %bitcast.10), channel_id=1, source_target_pairs={{0,2},{1,3},{2,0},{3,1},{4,6},{5,7},{6,4},{7,5},{8,10},{9,11},{10,... | collective-permute-start | bytes 786440 | tf_op jit(solution)/shard_map/ppermute | solution.py:22
  5.7 6.4 %collective-permute-start.1 = (s32[1,2]{1,0:T(1,128)S(1)}, s32[1,2]{1,0:T(1,128)S(1)}, u32[]{:S(2)}, u32[]{:S(2)}) collective-permute-start(s32[1,2]{1,0:T(1,128)S(1)} %bitcast.12), channel_id=1, source_target_pairs={{0,8},{8,0},{16,24},{24,16},{1,9},{9,1},{17,25},{25,17},{2,10},{10... | collective-permute-start | bytes 32 | tf_op jit(solution)/shard_map/ppermute | solution.py:22
  6.0 6.6 %collective-permute-start.6 = (bf16[256,128]{1,0:T(8,128)(2,1)}, bf16[256,128]{1,0:T(8,128)(2,1)S(1)}, u32[]{:S(2)}, u32[]{:S(2)}) collective-permute-start(bf16[256,128]{1,0:T(8,128)(2,1)} %param.7), channel_id=1, source_target_pairs={{0,1},{1,0},{2,3},{3,2},{4,5},{5,4},{6,7},{7,6},{8,9},{9,8},{10,11... | collective-permute-start | bytes 196616 | tf_op jit(solution)/shard_map/ppermute | solution.py:22
  7.5 4.5 %collective-permute-start.4 = (bf16[256,128]{1,0:T(8,128)(2,1)}, bf16[256,128]{1,0:T(8,128)(2,1)S(1)}, u32[]{:S(2)}, u32[]{:S(2)}) collective-permute-start(bf16[256,128]{1,0:T(8,128)(2,1)} %param.7), channel_id=1, source_target_pairs={{0,4},{4,0},{1,5},{5,1},{2,6},{6,2},{3,7},{7,3},{8,12},{12,8},{9,1... | collective-permute-start | bytes 196616 | tf_op jit(solution)/shard_map/ppermute | solution.py:22
  12.0 4.9 %collective-permute-start.5 = (bf16[512,128]{1,0:T(8,128)(2,1)S(1)}, bf16[512,128]{1,0:T(8,128)(2,1)S(1)}, u32[]{:S(2)}, u32[]{:S(2)}) collective-permute-start(bf16[512,128]{1,0:T(8,128)(2,1)S(1)} %constant_dynamic-update-slice_fusion.refs_0_), channel_id=1, source_target_pairs={{0,8},{8,0},{16,24},{24,16},{1,9},{9,1},{17,25},{25,17},{2,10},{10... | collective-permute-start | bytes 393224 | tf_op jit(solution)/shard_map/ppermute | solution.py:22
  12.1 4.8 %collective-permute-start.2 = (s32[2,2]{1,0:T(2,128)S(1)}, s32[2,2]{1,0:T(2,128)S(1)}, u32[]{:S(2)}, u32[]{:S(2)}) collective-permute-start(s32[2,2]{1,0:T(2,128)S(1)} %pad_add_fusion.1), channel_id=1, source_target_pairs={{0,2},{1,3},{2,0},{3,1},{4,6},{5,7},{6,4},{7,5},{8,10},{9,11},{10,... | collective-permute-start | bytes 56 | tf_op jit(solution)/shard_map/ppermute | solution.py:22
  12.5 4.4 %collective-permute-start.7 = (bf16[256,128]{1,0:T(8,128)(2,1)S(1)}, bf16[256,128]{1,0:T(8,128)(2,1)S(1)}, u32[]{:S(2)}, u32[]{:S(2)}) collective-permute-start(bf16[256,128]{1,0:T(8,128)(2,1)S(1)} %collective-permute-done.6.refs_2_), channel_id=1, source_target_pairs={{0,4},{4,0},{1,5},{5,1},{2,6},{6,2},{3,7},{7,3},{8,12},{12,8},{9,1... | collective-permute-start | bytes 196616 | tf_op jit(solution)/shard_map/ppermute | solution.py:22
  17.0 1.8 %collective-permute-start.10 = (bf16[8,128,128]{2,1,0:T(8,128)(2,1)S(1)}, bf16[8,128,128]{2,1,0:T(8,128)(2,1)S(1)}, u32[]{:S(2)}, u32[]{:S(2)}) collective-permute-start(bf16[8,128,128]{2,1,0:T(8,128)(2,1)S(1)} %collective-permute-done.refs_8_), channel_id=1, source_target_pairs={{0,8},{8,0},{16,24},{24,16},{1,9},{9,1},{17,25},{25,17},{2,10},{10... | collective-permute-start | bytes 786440 | tf_op jit(solution)/shard_map/ppermute | solution.py:22
  17.0 1.6 %collective-permute-start.8 = (bf16[256,128]{1,0:T(8,128)(2,1)S(1)}, bf16[256,128]{1,0:T(8,128)(2,1)S(1)}, u32[]{:S(2)}, u32[]{:S(2)}) collective-permute-start(bf16[256,128]{1,0:T(8,128)(2,1)S(1)} %collective-permute-done.6.refs_2_), channel_id=1, source_target_pairs={{0,8},{8,0},{16,24},{24,16},{1,9},{9,1},{17,25},{25,17},{2,10},{10... | collective-permute-start | bytes 196616 | tf_op jit(solution)/shard_map/ppermute | solution.py:22
  17.5 1.3 %collective-permute-start.9 = (bf16[256,128]{1,0:T(8,128)(2,1)S(1)}, bf16[256,128]{1,0:T(8,128)(2,1)S(1)}, u32[]{:S(2)}, u32[]{:S(2)}) collective-permute-start(bf16[256,128]{1,0:T(8,128)(2,1)S(1)} %collective-permute-done.7.refs_4_), channel_id=1, source_target_pairs={{0,8},{8,0},{16,24},{24,16},{1,9},{9,1},{17,25},{25,17},{2,10},{10... | collective-permute-start | bytes 196616 | tf_op jit(solution)/shard_map/ppermute | solution.py:22
  19.7 6.5 %collective-permute-start.11 = (s32[296,128]{1,0:T(8,128)S(1)}, s32[296,128]{1,0:T(8,128)S(1)}, u32[]{:S(2)}, u32[]{:S(2)}) collective-permute-start(s32[296,128]{1,0:T(8,128)S(1)} %get-tuple-element.30), channel_id=1, source_target_pairs={{0,1},{1,0},{2,3},{3,2},{4,5},{5,4},{6,7},{7,6},{8,24},{9,25},{10,... | collective-permute-start | bytes 454664 | tf_op jit(solution)/shard_map/ppermute | solution.py:32
  21.4 5.4 %collective-permute-start.12 = (s32[296,128]{1,0:T(8,128)S(1)}, s32[296,128]{1,0:T(8,128)S(1)}, u32[]{:S(2)}, u32[]{:S(2)}) collective-permute-start(s32[296,128]{1,0:T(8,128)S(1)} %get-tuple-element.31), channel_id=1, source_target_pairs={{0,16},{1,17},{2,18},{3,19},{4,20},{5,21},{6,22},{7,23},{8,9},{9,8... | collective-permute-start | bytes 454664 | tf_op jit(solution)/shard_map/ppermute | solution.py:32
  22.9 7.3 %collective-permute-start.13 = (s32[296,128]{1,0:T(8,128)S(1)}, s32[296,128]{1,0:T(8,128)S(1)}, u32[]{:S(2)}, u32[]{:S(2)}) collective-permute-start(s32[296,128]{1,0:T(8,128)S(1)} %get-tuple-element.32), channel_id=1, source_target_pairs={{0,17},{1,16},{2,19},{3,18},{4,21},{5,20},{6,23},{7,22},{8,25},{9,... | collective-permute-start | bytes 454664 | tf_op jit(solution)/shard_map/ppermute | solution.py:32
  30.5 2.2 %collective-permute-start.14 = (f32[1,128]{1,0:T(1,128)S(1)}, f32[1,128]{1,0:T(1,128)S(1)}, u32[]{:S(2)}, u32[]{:S(2)}) collective-permute-start(f32[1,128]{1,0:T(1,128)S(1)} %get-tuple-element.34), channel_id=1, source_target_pairs={{0,8},{8,0},{16,24},{24,16},{1,9},{9,1},{17,25},{25,17},{2,10},{10... | collective-permute-start | bytes 1544 | tf_op jit(solution)/shard_map/ppermute | solution.py:22
  30.5 4.5 %collective-permute-start.15 = (f32[1,128]{1,0:T(1,128)S(1)}, f32[1,128]{1,0:T(1,128)S(1)}, u32[]{:S(2)}, u32[]{:S(2)}) collective-permute-start(f32[1,128]{1,0:T(1,128)S(1)} %get-tuple-element.34), channel_id=1, source_target_pairs={{0,20},{1,21},{2,22},{3,23},{4,16},{5,17},{6,18},{7,19},{8,28},{9,... | collective-permute-start | bytes 1544 | tf_op jit(solution)/shard_map/ppermute | solution.py:32
  32.6 3.5 %collective-permute-start.16 = (f32[1,128]{1,0:T(1,128)S(1)}, f32[1,128]{1,0:T(1,128)S(1)}, u32[]{:S(2)}, u32[]{:S(2)}) collective-permute-start(f32[1,128]{1,0:T(1,128)S(1)} %add.62), channel_id=1, source_target_pairs={{0,16},{1,17},{2,18},{3,19},{4,20},{5,21},{6,22},{7,23},{8,12},{9,... | collective-permute-start | bytes 1544 | tf_op jit(solution)/shard_map/ppermute | solution.py:32
  36.2 1.1 %collective-permute-start.17 = (f32[1,128]{1,0:T(1,128)S(1)}, f32[1,128]{1,0:T(1,128)S(1)}, u32[]{:S(2)}, u32[]{:S(2)}) collective-permute-start(f32[1,128]{1,0:T(1,128)S(1)} %add.63), channel_id=1, source_target_pairs={{0,8},{8,0},{16,24},{24,16},{1,9},{9,1},{17,25},{25,17},{2,10},{10... | collective-permute-start | bytes 1544 | tf_op jit(solution)/shard_map/ppermute | solution.py:22

commit v10 on v9

--- a/solution.py
+++ b/solution.py
@@ -105,6 +105,17 @@
     sum_ref[...] = total
 
 
+def places(listed):
+    words = []
+    for h in range(IB // 8):
+        word = sum(8 << (4 * i) for i in range(8)) - (1 << 32)
+        for n, block_row in enumerate(listed):
+            bits = (n ^ 8) << (block_row % 8 * 4)
+            word = word ^ jnp.where(block_row // 8 == h, bits, 0)
+        words.append(word)
+    return words
+
+
 def product_kernel(masks, n_layer, n_row, n_col, lists_ref, *refs):
     n_slots, n_held = n_layer // 2, 2 * len(masks)
     mine_refs, near_refs = refs[:2], refs[2 : 2 + 2 * n_row]
@@ -114,7 +125,7 @@
     per, per_row = IB // n_layer, n_col // n_row
     capacity, block, depth = a_refs[0].shape
     lists = lists_ref[...]
-    lists = [[lists[k, h] for h in range(lists.shape[1])] for k in range(n_held)]
+    lists = [places([lists[k, n] for n in range(capacity)]) for k in range(n_held)]
     rhs = []
     for k in range(n_held):
         other, place = k % 2, k // 2
@@ -170,16 +181,6 @@
     )(*(pin(x) for x in ins))
 
 
-def whereabouts(a_rows, a_count):
-    panels, capacity = a_rows.shape
-    place = jnp.arange(capacity, dtype=jnp.int32)
-    valid = place[None, :] < a_count[:, None]
-    block_rows = jnp.arange(IB, dtype=jnp.int32)
-    listed = (a_rows[:, :, None] == block_rows) & valid[:, :, None]
-    places = capacity + jnp.sum(jnp.where(listed, place[:, None] - capacity, 0), axis=1)
-    return jnp.sum((places << (block_rows % 8 * 4)).reshape(panels, IB // 8, 8), axis=2)
-
-
 def body(a_blocks, a_rows, a_count, b_panel):
     n_layer, n_row, n_col = (lax.axis_size(a) for a in ("layer", "row", "col"))
     _, capacity, block, _ = a_blocks.shape
@@ -188,7 +189,8 @@
         return xor_permute(x, "layer", 1)
 
     masks, panels = [0], [a_blocks[0]]
-    lists = whereabouts(a_rows, a_count)
+    valid = jnp.arange(capacity, dtype=jnp.int32)[None, :] < a_count[:, None]
+    lists = jnp.where(valid, a_rows, IB)
     lists = jnp.concatenate([lists, other(lists)])
     bit = n_col // 2
     while bit > 1:

time: 38.2 us -> 38.4 us (level)
  waiting for transfers between devices: 16.7 us -> 17.1 us
    reduce_sum x2 -> x0, other arithmetic: 0.87 us -> none  [the longest x1 0.74 us: whereabouts(): jnp.sum(jnp.where(listed, place[:, None] - capacity, 0), axis=1)]
    select_n x0 -> x1, other arithmetic: none -> 0.66 us  [body(): lists = jnp.where(valid, a_rows, IB)]
  transfers between devices with their start and end apart: 18 -> 18, of which waited for: 10 -> 10; matrix products, arithmetic and copies ran while one was open for 5% -> 4% of each run, Pallas kernels for 0% -> 0%
where the time goes in v10:
time: 38.4 us; the launch traced here: 38.3 us
  waiting for transfers between devices  17.1 us (45%)
  starting transfers between devices  16.7 us (43%)
  other arithmetic  1.42 us (4%)
  Pallas kernels  1.38 us (4%)
  local copies, waits for them, and re-layouts  0.89 us (2%)
  between operations  0.74 us (2%)
    ppermute x13, starting transfers between devices, xor_permute(): lax.ppermute(x, axis, [(i, i ^ mask) for i in range(lax.axis_size(axis))])  10.1 us
    ppermute x5, waiting for transfers between devices, grid_permute(): return lax.ppermute(x, AXES, pairs)  9.45 us
    ppermute x13, waiting for transfers between devices, xor_permute(): lax.ppermute(x, axis, [(i, i ^ mask) for i in range(lax.axis_size(axis))])  7.64 us
    ppermute x5, starting transfers between devices, grid_permute(): return lax.ppermute(x, AXES, pairs)  6.67 us
    pallas_call x1, Pallas kernels, products(): pl.pallas_call(functools.partial(product_kernel, masks, n_layer, n_row, n...  1.16 us
    unnamed x3, local copies, waits for them, and re-layouts  0.88 us
  transfers between devices with their start and end apart: 18, of which 10 were waited for; matrix products, arithmetic and copies ran while one was open for 4% of the time, Pallas kernels for 0%

profile of v10, /device:TPU:0, one launch (start us, length us, event | category | flops | bytes accessed | tf_op | source)
XLA Modules:
  0.0 38.3 jit_solution(15115043583267142814)
XLA Ops:
  0.0 0.0 copy-start
  0.0 0.5 %collective-permute-start.3 = (bf16[8,128,128]{2,1,0:T(8,128)(2,1)}, bf16[8,128,128]{2,1,0:T(8,128)(2,1)S(1)}, u32[]{:S(2)}, u32[]{:S(2)}) collective-permute-start(bf16[8,128,128]{2,1,0:T(8,128)(2,1)} %bitcast.7), channel_id=1, source_target_pairs={{0,8},{8,0},{16,24},{24,16},{1,9},{9,1},{17,25},{25,17},{2,10},{10... | collective-permute-start | bytes 786440 | tf_op jit(solution)/shard_map/ppermute | solution.py:22
  0.5 3.6 %collective-permute-start = (bf16[8,128,128]{2,1,0:T(8,128)(2,1)}, bf16[8,128,128]{2,1,0:T(8,128)(2,1)S(1)}, u32[]{:S(2)}, u32[]{:S(2)}) collective-permute-start(bf16[8,128,128]{2,1,0:T(8,128)(2,1)} %bitcast.8), channel_id=1, source_target_pairs={{0,2},{1,3},{2,0},{3,1},{4,6},{5,7},{6,4},{7,5},{8,10},{9,11},{10,... | collective-permute-start | bytes 786440 | tf_op jit(solution)/shard_map/ppermute | solution.py:22
  4.8 0.7 %compare_select_fusion = s32[1,8]{1,0:T(1,128)S(1)} fusion(s32[1,8]{1,0:T(1,128)} %param.5, s32[]{:T(128)} %bitcast.6), kind=kLoop, calls=%fused_computation.4 | loop fusion | flops 16 | bytes 68 | tf_op jit(solution)/shard_map/jit(_where)/select_n | solution.py:193
  5.4 0.2 collective-permute-start.1
  5.6 0.0 collective-permute-done.3.refs_7_
  5.6 1.6 %collective-permute-start.6 = (bf16[256,128]{1,0:T(8,128)(2,1)}, bf16[256,128]{1,0:T(8,128)(2,1)S(1)}, u32[]{:S(2)}, u32[]{:S(2)}) collective-permute-start(bf16[256,128]{1,0:T(8,128)(2,1)} %param.7), channel_id=1, source_target_pairs={{0,1},{1,0},{2,3},{3,2},{4,5},{5,4},{6,7},{7,6},{8,9},{9,8},{10,11... | collective-permute-start | bytes 196616 | tf_op jit(solution)/shard_map/ppermute | solution.py:22
  7.2 1.5 %collective-permute-start.4 = (bf16[256,128]{1,0:T(8,128)(2,1)}, bf16[256,128]{1,0:T(8,128)(2,1)S(1)}, u32[]{:S(2)}, u32[]{:S(2)}) collective-permute-start(bf16[256,128]{1,0:T(8,128)(2,1)} %param.7), channel_id=1, source_target_pairs={{0,4},{4,0},{1,5},{5,1},{2,6},{6,2},{3,7},{7,3},{8,12},{12,8},{9,1... | collective-permute-start | bytes 196616 | tf_op jit(solution)/shard_map/ppermute | solution.py:22
  8.7 0.9 %constant_dynamic-update-slice_fusion.1 = bf16[512,128]{1,0:T(8,128)(2,1)S(1)} fusion(bf16[256,128]{1,0:T(8,128)(2,1)} %param.7), kind=kLoop, calls=%fused_computation.2 | loop fusion | bytes 131072
  9.6 2.1 %collective-permute-done.4 = bf16[256,128]{1,0:T(8,128)(2,1)S(1)} collective-permute-done((bf16[256,128]{1,0:T(8,128)(2,1)}, bf16[256,128]{1,0:T(8,128)(2,1)S(1)}, u32[]{:S(2)}, u32[]{:S(2)}) %collective-permute-start.4) | collective-permute-done | bytes 65568 | tf_op jit(solution)/shard_map/ppermute | solution.py:22
  11.7 0.1 collective-permute-start.5
  11.7 0.0 collective-permute-done.1
  11.8 0.4 %collective-permute-start.2 = (s32[2,8]{1,0:T(2,128)S(1)}, s32[2,8]{1,0:T(2,128)S(1)}, u32[]{:S(2)}, u32[]{:S(2)}) collective-permute-start(s32[2,8]{1,0:T(2,128)S(1)} %pad_add_fusion.1), channel_id=1, source_target_pairs={{0,2},{1,3},{2,0},{3,1},{4,6},{5,7},{6,4},{7,5},{8,10},{9,11},{10,... | collective-permute-start | bytes 200 | tf_op jit(solution)/shard_map/ppermute | solution.py:22
  12.2 0.0 collective-permute-done.6.refs_2_
  12.2 1.5 %collective-permute-start.7 = (bf16[256,128]{1,0:T(8,128)(2,1)S(1)}, bf16[256,128]{1,0:T(8,128)(2,1)S(1)}, u32[]{:S(2)}, u32[]{:S(2)}) collective-permute-start(bf16[256,128]{1,0:T(8,128)(2,1)S(1)} %collective-permute-done.6.refs_2_), channel_id=1, source_target_pairs={{0,4},{4,0},{1,5},{5,1},{2,6},{6,2},{3,7},{7,3},{8,12},{12,8},{9,1... | collective-permute-start | bytes 196616 | tf_op jit(solution)/shard_map/ppermute | solution.py:22
  13.7 3.2 %collective-permute-done.2 = s32[2,8]{1,0:T(2,128)S(1)} collective-permute-done((s32[2,8]{1,0:T(2,128)S(1)}, s32[2,8]{1,0:T(2,128)S(1)}, u32[]{:S(2)}, u32[]{:S(2)}) %collective-permute-start.2) | collective-permute-done | bytes 96 | tf_op jit(solution)/shard_map/ppermute | solution.py:22
  16.9 0.0 collective-permute-done.refs_8_
  16.9 0.0 collective-permute-done.7.refs_4_
  17.0 0.0 collective-permute-done.5.refs_1_
  17.0 0.1 collective-permute-start.10
  17.0 0.5 %collective-permute-start.8 = (bf16[256,128]{1,0:T(8,128)(2,1)S(1)}, bf16[256,128]{1,0:T(8,128)(2,1)S(1)}, u32[]{:S(2)}, u32[]{:S(2)}) collective-permute-start(bf16[256,128]{1,0:T(8,128)(2,1)S(1)} %collective-permute-done.6.refs_2_), channel_id=1, source_target_pairs={{0,8},{8,0},{16,24},{24,16},{1,9},{9,1},{17,25},{25,17},{2,10},{10... | collective-permute-start | bytes 196616 | tf_op jit(solution)/shard_map/ppermute | solution.py:22
  17.5 0.1 collective-permute-start.9
  17.6 1.0 %collective-permute-done.8.refs_3_ = bf16[256,128]{1,0:T(8,128)(2,1)S(1)} collective-permute-done((bf16[256,128]{1,0:T(8,128)(2,1)S(1)}, bf16[256,128]{1,0:T(8,128)(2,1)S(1)}, u32[]{:S(2)}, u32[]{:S(2)}) %collective-permute-start.8) | collective-permute-done | bytes 65568 | tf_op jit(solution)/shard_map/ppermute | solution.py:22
  18.7 0.1 collective-permute-done.9.refs_5_
  18.8 0.0 collective-permute-done.10.refs_9_
  18.8 0.0 copy-done
  18.8 1.2 %partial_rows.1 = (f32[512,128]{1,0:T(8,128)S(1)}, s32[296,128]{1,0:T(8,128)S(1)}, s32[296,128]{1,0:T(8,128)S(1)}, s32[296,128]{1,0:T(8,128)S(1)}) custom-call(s32[4,8]{1,0:T(4,128)S(1)} %pad_add_fusion.lists_ref, bf16[512,128]{1,0:T(8,128)(2,1)S(1)} %constant_dynamic-update-slice_fusion.refs_0_, bf16[512,128]{1,0:T(8,128)(2,1)S(1)} %collective-permute-done.5.refs_1_, ...), custom_call_target="tpu_custom_call" | custom-call | tf_op jit(solution)/shard_map/partial_rows/pallas_call | solution.py:171
  20.0 1.7 %collective-permute-start.11 = (s32[296,128]{1,0:T(8,128)S(1)}, s32[296,128]{1,0:T(8,128)S(1)}, u32[]{:S(2)}, u32[]{:S(2)}) collective-permute-start(s32[296,128]{1,0:T(8,128)S(1)} %get-tuple-element.30), channel_id=1, source_target_pairs={{0,1},{1,0},{2,3},{3,2},{4,5},{5,4},{6,7},{7,6},{8,24},{9,25},{10,... | collective-permute-start | bytes 454664 | tf_op jit(solution)/shard_map/ppermute | solution.py:32
  21.7 1.5 %collective-permute-start.12 = (s32[296,128]{1,0:T(8,128)S(1)}, s32[296,128]{1,0:T(8,128)S(1)}, u32[]{:S(2)}, u32[]{:S(2)}) collective-permute-start(s32[296,128]{1,0:T(8,128)S(1)} %get-tuple-element.31), channel_id=1, source_target_pairs={{0,16},{1,17},{2,18},{3,19},{4,20},{5,21},{6,22},{7,23},{8,9},{9,8... | collective-permute-start | bytes 454664 | tf_op jit(solution)/shard_map/ppermute | solution.py:32
  23.2 0.3 collective-permute-start.13
  23.5 2.9 %collective-permute-done.11.refs_0_ = s32[296,128]{1,0:T(8,128)S(1)} collective-permute-done((s32[296,128]{1,0:T(8,128)S(1)}, s32[296,128]{1,0:T(8,128)S(1)}, u32[]{:S(2)}, u32[]{:S(2)}) %collective-permute-start.11) | collective-permute-done | bytes 151584 | tf_op jit(solution)/shard_map/ppermute | solution.py:32
  26.5 0.6 %collective-permute-done.12.refs_1_ = s32[296,128]{1,0:T(8,128)S(1)} collective-permute-done((s32[296,128]{1,0:T(8,128)S(1)}, s32[296,128]{1,0:T(8,128)S(1)}, u32[]{:S(2)}, u32[]{:S(2)}) %collective-permute-start.12) | collective-permute-done | bytes 151584 | tf_op jit(solution)/shard_map/ppermute | solution.py:32
  27.1 3.4 %collective-permute-done.13.refs_2_ = s32[296,128]{1,0:T(8,128)S(1)} collective-permute-done((s32[296,128]{1,0:T(8,128)S(1)}, s32[296,128]{1,0:T(8,128)S(1)}, u32[]{:S(2)}, u32[]{:S(2)}) %collective-permute-start.13) | collective-permute-done | bytes 151584 | tf_op jit(solution)/shard_map/ppermute | solution.py:32
  30.5 0.2 squares.1
  30.7 0.1 collective-permute-start.14
  30.8 2.1 %collective-permute-start.15 = (f32[1,128]{1,0:T(1,128)S(1)}, f32[1,128]{1,0:T(1,128)S(1)}, u32[]{:S(2)}, u32[]{:S(2)}) collective-permute-start(f32[1,128]{1,0:T(1,128)S(1)} %get-tuple-element.34), channel_id=1, source_target_pairs={{0,20},{1,21},{2,22},{3,23},{4,16},{5,17},{6,18},{7,19},{8,28},{9,... | collective-permute-start | bytes 1544 | tf_op jit(solution)/shard_map/ppermute | solution.py:32
  32.9 0.0 collective-permute-done.14
  32.9 1.0 %collective-permute-start.16 = (f32[1,128]{1,0:T(1,128)S(1)}, f32[1,128]{1,0:T(1,128)S(1)}, u32[]{:S(2)}, u32[]{:S(2)}) collective-permute-start(f32[1,128]{1,0:T(1,128)S(1)} %add.18), channel_id=1, source_target_pairs={{0,16},{1,17},{2,18},{3,19},{4,20},{5,21},{6,22},{7,23},{8,12},{9,... | collective-permute-start | bytes 1544 | tf_op jit(solution)/shard_map/ppermute | solution.py:32
  33.9 1.4 %collective-permute-done.15 = f32[1,128]{1,0:T(1,128)S(1)} collective-permute-done((f32[1,128]{1,0:T(1,128)S(1)}, f32[1,128]{1,0:T(1,128)S(1)}, u32[]{:S(2)}, u32[]{:S(2)}) %collective-permute-start.15) | collective-permute-done | bytes 544 | tf_op jit(solution)/shard_map/ppermute | solution.py:32
  35.3 1.1 %collective-permute-done.16 = f32[1,128]{1,0:T(1,128)S(1)} collective-permute-done((f32[1,128]{1,0:T(1,128)S(1)}, f32[1,128]{1,0:T(1,128)S(1)}, u32[]{:S(2)}, u32[]{:S(2)}) %collective-permute-start.16) | collective-permute-done | bytes 544 | tf_op jit(solution)/shard_map/ppermute | solution.py:32
  36.4 0.0 collective-permute-start.17
  36.4 1.1 %collective-permute-done.17 = f32[1,128]{1,0:T(1,128)S(1)} collective-permute-done((f32[1,128]{1,0:T(1,128)S(1)}, f32[1,128]{1,0:T(1,128)S(1)}, u32[]{:S(2)}, u32[]{:S(2)}) %collective-permute-start.17) | collective-permute-done | bytes 544 | tf_op jit(solution)/shard_map/ppermute | solution.py:22
  37.5 0.7 %multiply_bitcast_fusion = f32[1,512,128]{2,1,0:T(8,128)} fusion(f32[512,128]{1,0:T(8,128)S(1)} %get-tuple-element.33, f32[128]{0:T(128)S(1)} %divide_bitcast_fusion), kind=kLoop, calls=%fused_computation | loop fusion | flops 65536 | bytes 524800 | tf_op jit(solution)/shard_map/broadcast_in_dim | solution.py:241
  (6 shorter events, 0.0 us)
Async XLA Ops:
  0.0 18.8 %copy-start = (bf16[1,8,128,128]{3,2,1,0:T(8,128)(2,1)S(1)}, bf16[1,8,128,128]{3,2,1,0:T(8,128)(2,1)}, u32[]{:S(2)}) copy-start(bf16[1,8,128,128]{3,2,1,0:T(8,128)(2,1)} %param.4) | copy-start | bytes 786436
  0.0 5.6 %collective-permute-start.3 = (bf16[8,128,128]{2,1,0:T(8,128)(2,1)}, bf16[8,128,128]{2,1,0:T(8,128)(2,1)S(1)}, u32[]{:S(2)}, u32[]{:S(2)}) collective-permute-start(bf16[8,128,128]{2,1,0:T(8,128)(2,1)} %bitcast.7), channel_id=1, source_target_pairs={{0,8},{8,0},{16,24},{24,16},{1,9},{9,1},{17,25},{25,17},{2,10},{10... | collective-permute-start | bytes 786440 | tf_op jit(solution)/shard_map/ppermute | solution.py:22
  0.5 16.5 %collective-permute-start = (bf16[8,128,128]{2,1,0:T(8,128)(2,1)}, bf16[8,128,128]{2,1,0:T(8,128)(2,1)S(1)}, u32[]{:S(2)}, u32[]{:S(2)}) collective-permute-start(bf16[8,128,128]{2,1,0:T(8,128)(2,1)} %bitcast.8), channel_id=1, source_target_pairs={{0,2},{1,3},{2,0},{3,1},{4,6},{5,7},{6,4},{7,5},{8,10},{9,11},{10,... | collective-permute-start | bytes 786440 | tf_op jit(solution)/shard_map/ppermute | solution.py:22
  5.4 6.3 %collective-permute-start.1 = (s32[1,8]{1,0:T(1,128)S(1)}, s32[1,8]{1,0:T(1,128)S(1)}, u32[]{:S(2)}, u32[]{:S(2)}) collective-permute-start(s32[1,8]{1,0:T(1,128)S(1)} %compare_select_fusion), channel_id=1, source_target_pairs={{0,8},{8,0},{16,24},{24,16},{1,9},{9,1},{17,25},{25,17},{2,10},{10... | collective-permute-start | bytes 104 | tf_op jit(solution)/shard_map/ppermute | solution.py:22
  5.6 6.6 %collective-permute-start.6 = (bf16[256,128]{1,0:T(8,128)(2,1)}, bf16[256,128]{1,0:T(8,128)(2,1)S(1)}, u32[]{:S(2)}, u32[]{:S(2)}) collective-permute-start(bf16[256,128]{1,0:T(8,128)(2,1)} %param.7), channel_id=1, source_target_pairs={{0,1},{1,0},{2,3},{3,2},{4,5},{5,4},{6,7},{7,6},{8,9},{9,8},{10,11... | collective-permute-start | bytes 196616 | tf_op jit(solution)/shard_map/ppermute | solution.py:22
  7.2 4.5 %collective-permute-start.4 = (bf16[256,128]{1,0:T(8,128)(2,1)}, bf16[256,128]{1,0:T(8,128)(2,1)S(1)}, u32[]{:S(2)}, u32[]{:S(2)}) collective-permute-start(bf16[256,128]{1,0:T(8,128)(2,1)} %param.7), channel_id=1, source_target_pairs={{0,4},{4,0},{1,5},{5,1},{2,6},{6,2},{3,7},{7,3},{8,12},{12,8},{9,1... | collective-permute-start | bytes 196616 | tf_op jit(solution)/shard_map/ppermute | solution.py:22
  11.7 5.3 %collective-permute-start.5 = (bf16[512,128]{1,0:T(8,128)(2,1)S(1)}, bf16[512,128]{1,0:T(8,128)(2,1)S(1)}, u32[]{:S(2)}, u32[]{:S(2)}) collective-permute-start(bf16[512,128]{1,0:T(8,128)(2,1)S(1)} %constant_dynamic-update-slice_fusion.refs_0_), channel_id=1, source_target_pairs={{0,8},{8,0},{16,24},{24,16},{1,9},{9,1},{17,25},{25,17},{2,10},{10... | collective-permute-start | bytes 393224 | tf_op jit(solution)/shard_map/ppermute | solution.py:22
  11.8 5.2 %collective-permute-start.2 = (s32[2,8]{1,0:T(2,128)S(1)}, s32[2,8]{1,0:T(2,128)S(1)}, u32[]{:S(2)}, u32[]{:S(2)}) collective-permute-start(s32[2,8]{1,0:T(2,128)S(1)} %pad_add_fusion.1), channel_id=1, source_target_pairs={{0,2},{1,3},{2,0},{3,1},{4,6},{5,7},{6,4},{7,5},{8,10},{9,11},{10,... | collective-permute-start | bytes 200 | tf_op jit(solution)/shard_map/ppermute | solution.py:22
  12.2 4.8 %collective-permute-start.7 = (bf16[256,128]{1,0:T(8,128)(2,1)S(1)}, bf16[256,128]{1,0:T(8,128)(2,1)S(1)}, u32[]{:S(2)}, u32[]{:S(2)}) collective-permute-start(bf16[256,128]{1,0:T(8,128)(2,1)S(1)} %collective-permute-done.6.refs_2_), channel_id=1, source_target_pairs={{0,4},{4,0},{1,5},{5,1},{2,6},{6,2},{3,7},{7,3},{8,12},{12,8},{9,1... | collective-permute-start | bytes 196616 | tf_op jit(solution)/shard_map/ppermute | solution.py:22
  17.0 1.8 %collective-permute-start.10 = (bf16[8,128,128]{2,1,0:T(8,128)(2,1)S(1)}, bf16[8,128,128]{2,1,0:T(8,128)(2,1)S(1)}, u32[]{:S(2)}, u32[]{:S(2)}) collective-permute-start(bf16[8,128,128]{2,1,0:T(8,128)(2,1)S(1)} %collective-permute-done.refs_8_), channel_id=1, source_target_pairs={{0,8},{8,0},{16,24},{24,16},{1,9},{9,1},{17,25},{25,17},{2,10},{10... | collective-permute-start | bytes 786440 | tf_op jit(solution)/shard_map/ppermute | solution.py:22
  17.0 1.6 %collective-permute-start.8 = (bf16[256,128]{1,0:T(8,128)(2,1)S(1)}, bf16[256,128]{1,0:T(8,128)(2,1)S(1)}, u32[]{:S(2)}, u32[]{:S(2)}) collective-permute-start(bf16[256,128]{1,0:T(8,128)(2,1)S(1)} %collective-permute-done.6.refs_2_), channel_id=1, source_target_pairs={{0,8},{8,0},{16,24},{24,16},{1,9},{9,1},{17,25},{25,17},{2,10},{10... | collective-permute-start | bytes 196616 | tf_op jit(solution)/shard_map/ppermute | solution.py:22
  17.5 1.3 %collective-permute-start.9 = (bf16[256,128]{1,0:T(8,128)(2,1)S(1)}, bf16[256,128]{1,0:T(8,128)(2,1)S(1)}, u32[]{:S(2)}, u32[]{:S(2)}) collective-permute-start(bf16[256,128]{1,0:T(8,128)(2,1)S(1)} %collective-permute-done.7.refs_4_), channel_id=1, source_target_pairs={{0,8},{8,0},{16,24},{24,16},{1,9},{9,1},{17,25},{25,17},{2,10},{10... | collective-permute-start | bytes 196616 | tf_op jit(solution)/shard_map/ppermute | solution.py:22
  20.0 6.5 %collective-permute-start.11 = (s32[296,128]{1,0:T(8,128)S(1)}, s32[296,128]{1,0:T(8,128)S(1)}, u32[]{:S(2)}, u32[]{:S(2)}) collective-permute-start(s32[296,128]{1,0:T(8,128)S(1)} %get-tuple-element.30), channel_id=1, source_target_pairs={{0,1},{1,0},{2,3},{3,2},{4,5},{5,4},{6,7},{7,6},{8,24},{9,25},{10,... | collective-permute-start | bytes 454664 | tf_op jit(solution)/shard_map/ppermute | solution.py:32
  21.7 5.4 %collective-permute-start.12 = (s32[296,128]{1,0:T(8,128)S(1)}, s32[296,128]{1,0:T(8,128)S(1)}, u32[]{:S(2)}, u32[]{:S(2)}) collective-permute-start(s32[296,128]{1,0:T(8,128)S(1)} %get-tuple-element.31), channel_id=1, source_target_pairs={{0,16},{1,17},{2,18},{3,19},{4,20},{5,21},{6,22},{7,23},{8,9},{9,8... | collective-permute-start | bytes 454664 | tf_op jit(solution)/shard_map/ppermute | solution.py:32
  23.2 7.3 %collective-permute-start.13 = (s32[296,128]{1,0:T(8,128)S(1)}, s32[296,128]{1,0:T(8,128)S(1)}, u32[]{:S(2)}, u32[]{:S(2)}) collective-permute-start(s32[296,128]{1,0:T(8,128)S(1)} %get-tuple-element.32), channel_id=1, source_target_pairs={{0,17},{1,16},{2,19},{3,18},{4,21},{5,20},{6,23},{7,22},{8,25},{9,... | collective-permute-start | bytes 454664 | tf_op jit(solution)/shard_map/ppermute | solution.py:32
  30.7 2.2 %collective-permute-start.14 = (f32[1,128]{1,0:T(1,128)S(1)}, f32[1,128]{1,0:T(1,128)S(1)}, u32[]{:S(2)}, u32[]{:S(2)}) collective-permute-start(f32[1,128]{1,0:T(1,128)S(1)} %get-tuple-element.34), channel_id=1, source_target_pairs={{0,8},{8,0},{16,24},{24,16},{1,9},{9,1},{17,25},{25,17},{2,10},{10... | collective-permute-start | bytes 1544 | tf_op jit(solution)/shard_map/ppermute | solution.py:22
  30.8 4.5 %collective-permute-start.15 = (f32[1,128]{1,0:T(1,128)S(1)}, f32[1,128]{1,0:T(1,128)S(1)}, u32[]{:S(2)}, u32[]{:S(2)}) collective-permute-start(f32[1,128]{1,0:T(1,128)S(1)} %get-tuple-element.34), channel_id=1, source_target_pairs={{0,20},{1,21},{2,22},{3,23},{4,16},{5,17},{6,18},{7,19},{8,28},{9,... | collective-permute-start | bytes 1544 | tf_op jit(solution)/shard_map/ppermute | solution.py:32
  32.9 3.5 %collective-permute-start.16 = (f32[1,128]{1,0:T(1,128)S(1)}, f32[1,128]{1,0:T(1,128)S(1)}, u32[]{:S(2)}, u32[]{:S(2)}) collective-permute-start(f32[1,128]{1,0:T(1,128)S(1)} %add.18), channel_id=1, source_target_pairs={{0,16},{1,17},{2,18},{3,19},{4,20},{5,21},{6,22},{7,23},{8,12},{9,... | collective-permute-start | bytes 1544 | tf_op jit(solution)/shard_map/ppermute | solution.py:32
  36.4 1.1 %collective-permute-start.17 = (f32[1,128]{1,0:T(1,128)S(1)}, f32[1,128]{1,0:T(1,128)S(1)}, u32[]{:S(2)}, u32[]{:S(2)}) collective-permute-start(f32[1,128]{1,0:T(1,128)S(1)} %add.19), channel_id=1, source_target_pairs={{0,8},{8,0},{16,24},{24,16},{1,9},{9,1},{17,25},{25,17},{2,10},{10... | collective-permute-start | bytes 1544 | tf_op jit(solution)/shard_map/ppermute | solution.py:22

commit v11 on v10

--- a/solution.py
+++ b/solution.py
@@ -105,15 +105,15 @@
     sum_ref[...] = total
 
 
-def places(listed):
-    words = []
-    for h in range(IB // 8):
-        word = sum(8 << (4 * i) for i in range(8)) - (1 << 32)
-        for n, block_row in enumerate(listed):
-            bits = (n ^ 8) << (block_row % 8 * 4)
-            word = word ^ jnp.where(block_row // 8 == h, bits, 0)
-        words.append(word)
-    return words
+def places(lists):
+    place = lax.broadcasted_iota(jnp.int32, lists.shape, 1)
+    bits = (place ^ 8) << ((lists & 7) * 4)
+    none = sum(8 << (4 * i) for i in range(8)) - (1 << 32)
+    words = [
+        jnp.sum(jnp.where(lists >> 3 == h, bits, 0), axis=1, keepdims=True) ^ none
+        for h in range(IB // 8)
+    ]
+    return [[word[k, 0] for word in words] for k in range(lists.shape[0])]
 
 
 def product_kernel(masks, n_layer, n_row, n_col, lists_ref, *refs):
@@ -124,8 +124,7 @@
     layer, row, col = (lax.axis_index(n) for n in ("layer", "row", "col"))
     per, per_row = IB // n_layer, n_col // n_row
     capacity, block, depth = a_refs[0].shape
-    lists = lists_ref[...]
-    lists = [places([lists[k, n] for n in range(capacity)]) for k in range(n_held)]
+    lists = places(lists_ref[...])
     rhs = []
     for k in range(n_held):
         other, place = k % 2, k // 2

time: 38.4 us -> 38.3 us (level)
  no operation moved by 1% of the time
where the time goes in v11:
time: 38.3 us; the launch traced here: 38.1 us
  waiting for transfers between devices  17.1 us (45%)
  starting transfers between devices  16.7 us (44%)
  other arithmetic  1.42 us (4%)
  Pallas kernels  1.21 us (3%)
  local copies, waits for them, and re-layouts  0.89 us (2%)
  between operations  0.74 us (2%)
    ppermute x13, starting transfers between devices, xor_permute(): lax.ppermute(x, axis, [(i, i ^ mask) for i in range(lax.axis_size(axis))])  10.1 us
    ppermute x5, waiting for transfers between devices, grid_permute(): return lax.ppermute(x, AXES, pairs)  9.44 us
    ppermute x13, waiting for transfers between devices, xor_permute(): lax.ppermute(x, axis, [(i, i ^ mask) for i in range(lax.axis_size(axis))])  7.64 us
    ppermute x5, starting transfers between devices, grid_permute(): return lax.ppermute(x, AXES, pairs)  6.67 us
    pallas_call x1, Pallas kernels, products(): pl.pallas_call(functools.partial(product_kernel, masks, n_layer, n_row, n...  0.98 us
    unnamed x3, local copies, waits for them, and re-layouts  0.88 us
  transfers between devices with their start and end apart: 18, of which 10 were waited for; matrix products, arithmetic and copies ran while one was open for 4% of the time, Pallas kernels for 0%

profile of v11, /device:TPU:0, one launch (start us, length us, event | category | flops | bytes accessed | tf_op | source)
XLA Modules:
  0.0 38.1 jit_solution(17951125580487577829)
XLA Ops:
  0.0 0.0 copy-start
  0.0 0.5 %collective-permute-start.3 = (bf16[8,128,128]{2,1,0:T(8,128)(2,1)}, bf16[8,128,128]{2,1,0:T(8,128)(2,1)S(1)}, u32[]{:S(2)}, u32[]{:S(2)}) collective-permute-start(bf16[8,128,128]{2,1,0:T(8,128)(2,1)} %bitcast.7), channel_id=1, source_target_pairs={{0,8},{8,0},{16,24},{24,16},{1,9},{9,1},{17,25},{25,17},{2,10},{10... | collective-permute-start | bytes 786440 | tf_op jit(solution)/shard_map/ppermute | solution.py:22
  0.5 3.6 %collective-permute-start = (bf16[8,128,128]{2,1,0:T(8,128)(2,1)}, bf16[8,128,128]{2,1,0:T(8,128)(2,1)S(1)}, u32[]{:S(2)}, u32[]{:S(2)}) collective-permute-start(bf16[8,128,128]{2,1,0:T(8,128)(2,1)} %bitcast.8), channel_id=1, source_target_pairs={{0,2},{1,3},{2,0},{3,1},{4,6},{5,7},{6,4},{7,5},{8,10},{9,11},{10,... | collective-permute-start | bytes 786440 | tf_op jit(solution)/shard_map/ppermute | solution.py:22
  4.8 0.7 %compare_select_fusion = s32[1,8]{1,0:T(1,128)S(1)} fusion(s32[1,8]{1,0:T(1,128)} %param.5, s32[]{:T(128)} %bitcast.6), kind=kLoop, calls=%fused_computation.4 | loop fusion | flops 16 | bytes 68 | tf_op jit(solution)/shard_map/jit(_where)/select_n | solution.py:192
  5.4 0.2 collective-permute-start.1
  5.6 0.0 collective-permute-done.3.refs_7_
  5.6 1.6 %collective-permute-start.6 = (bf16[256,128]{1,0:T(8,128)(2,1)}, bf16[256,128]{1,0:T(8,128)(2,1)S(1)}, u32[]{:S(2)}, u32[]{:S(2)}) collective-permute-start(bf16[256,128]{1,0:T(8,128)(2,1)} %param.7), channel_id=1, source_target_pairs={{0,1},{1,0},{2,3},{3,2},{4,5},{5,4},{6,7},{7,6},{8,9},{9,8},{10,11... | collective-permute-start | bytes 196616 | tf_op jit(solution)/shard_map/ppermute | solution.py:22
  7.2 1.5 %collective-permute-start.4 = (bf16[256,128]{1,0:T(8,128)(2,1)}, bf16[256,128]{1,0:T(8,128)(2,1)S(1)}, u32[]{:S(2)}, u32[]{:S(2)}) collective-permute-start(bf16[256,128]{1,0:T(8,128)(2,1)} %param.7), channel_id=1, source_target_pairs={{0,4},{4,0},{1,5},{5,1},{2,6},{6,2},{3,7},{7,3},{8,12},{12,8},{9,1... | collective-permute-start | bytes 196616 | tf_op jit(solution)/shard_map/ppermute | solution.py:22
  8.7 0.9 %constant_dynamic-update-slice_fusion.1 = bf16[512,128]{1,0:T(8,128)(2,1)S(1)} fusion(bf16[256,128]{1,0:T(8,128)(2,1)} %param.7), kind=kLoop, calls=%fused_computation.2 | loop fusion | bytes 131072
  9.6 2.1 %collective-permute-done.4 = bf16[256,128]{1,0:T(8,128)(2,1)S(1)} collective-permute-done((bf16[256,128]{1,0:T(8,128)(2,1)}, bf16[256,128]{1,0:T(8,128)(2,1)S(1)}, u32[]{:S(2)}, u32[]{:S(2)}) %collective-permute-start.4) | collective-permute-done | bytes 65568 | tf_op jit(solution)/shard_map/ppermute | solution.py:22
  11.7 0.1 collective-permute-start.5
  11.7 0.0 collective-permute-done.1
  11.8 0.4 %collective-permute-start.2 = (s32[2,8]{1,0:T(2,128)S(1)}, s32[2,8]{1,0:T(2,128)S(1)}, u32[]{:S(2)}, u32[]{:S(2)}) collective-permute-start(s32[2,8]{1,0:T(2,128)S(1)} %pad_add_fusion.1), channel_id=1, source_target_pairs={{0,2},{1,3},{2,0},{3,1},{4,6},{5,7},{6,4},{7,5},{8,10},{9,11},{10,... | collective-permute-start | bytes 200 | tf_op jit(solution)/shard_map/ppermute | solution.py:22
  12.2 0.0 collective-permute-done.6.refs_2_
  12.2 1.5 %collective-permute-start.7 = (bf16[256,128]{1,0:T(8,128)(2,1)S(1)}, bf16[256,128]{1,0:T(8,128)(2,1)S(1)}, u32[]{:S(2)}, u32[]{:S(2)}) collective-permute-start(bf16[256,128]{1,0:T(8,128)(2,1)S(1)} %collective-permute-done.6.refs_2_), channel_id=1, source_target_pairs={{0,4},{4,0},{1,5},{5,1},{2,6},{6,2},{3,7},{7,3},{8,12},{12,8},{9,1... | collective-permute-start | bytes 196616 | tf_op jit(solution)/shard_map/ppermute | solution.py:22
  13.7 3.2 %collective-permute-done.2 = s32[2,8]{1,0:T(2,128)S(1)} collective-permute-done((s32[2,8]{1,0:T(2,128)S(1)}, s32[2,8]{1,0:T(2,128)S(1)}, u32[]{:S(2)}, u32[]{:S(2)}) %collective-permute-start.2) | collective-permute-done | bytes 96 | tf_op jit(solution)/shard_map/ppermute | solution.py:22
  16.9 0.0 collective-permute-done.refs_8_
  16.9 0.0 collective-permute-done.7.refs_4_
  17.0 0.0 collective-permute-done.5.refs_1_
  17.0 0.1 collective-permute-start.10
  17.0 0.5 %collective-permute-start.8 = (bf16[256,128]{1,0:T(8,128)(2,1)S(1)}, bf16[256,128]{1,0:T(8,128)(2,1)S(1)}, u32[]{:S(2)}, u32[]{:S(2)}) collective-permute-start(bf16[256,128]{1,0:T(8,128)(2,1)S(1)} %collective-permute-done.6.refs_2_), channel_id=1, source_target_pairs={{0,8},{8,0},{16,24},{24,16},{1,9},{9,1},{17,25},{25,17},{2,10},{10... | collective-permute-start | bytes 196616 | tf_op jit(solution)/shard_map/ppermute | solution.py:22
  17.5 0.1 collective-permute-start.9
  17.6 1.0 %collective-permute-done.8.refs_3_ = bf16[256,128]{1,0:T(8,128)(2,1)S(1)} collective-permute-done((bf16[256,128]{1,0:T(8,128)(2,1)S(1)}, bf16[256,128]{1,0:T(8,128)(2,1)S(1)}, u32[]{:S(2)}, u32[]{:S(2)}) %collective-permute-start.8) | collective-permute-done | bytes 65568 | tf_op jit(solution)/shard_map/ppermute | solution.py:22
  18.7 0.1 collective-permute-done.9.refs_5_
  18.8 0.0 collective-permute-done.10.refs_9_
  18.8 0.0 copy-done
  18.8 1.0 %partial_rows.1 = (f32[512,128]{1,0:T(8,128)S(1)}, s32[296,128]{1,0:T(8,128)S(1)}, s32[296,128]{1,0:T(8,128)S(1)}, s32[296,128]{1,0:T(8,128)S(1)}) custom-call(s32[4,8]{1,0:T(4,128)S(1)} %pad_add_fusion.lists_ref, bf16[512,128]{1,0:T(8,128)(2,1)S(1)} %constant_dynamic-update-slice_fusion.refs_0_, bf16[512,128]{1,0:T(8,128)(2,1)S(1)} %collective-permute-done.5.refs_1_, ...), custom_call_target="tpu_custom_call" | custom-call | tf_op jit(solution)/shard_map/partial_rows/pallas_call | solution.py:170
  19.8 1.7 %collective-permute-start.11 = (s32[296,128]{1,0:T(8,128)S(1)}, s32[296,128]{1,0:T(8,128)S(1)}, u32[]{:S(2)}, u32[]{:S(2)}) collective-permute-start(s32[296,128]{1,0:T(8,128)S(1)} %get-tuple-element.30), channel_id=1, source_target_pairs={{0,1},{1,0},{2,3},{3,2},{4,5},{5,4},{6,7},{7,6},{8,24},{9,25},{10,... | collective-permute-start | bytes 454664 | tf_op jit(solution)/shard_map/ppermute | solution.py:32
  21.5 1.5 %collective-permute-start.12 = (s32[296,128]{1,0:T(8,128)S(1)}, s32[296,128]{1,0:T(8,128)S(1)}, u32[]{:S(2)}, u32[]{:S(2)}) collective-permute-start(s32[296,128]{1,0:T(8,128)S(1)} %get-tuple-element.31), channel_id=1, source_target_pairs={{0,16},{1,17},{2,18},{3,19},{4,20},{5,21},{6,22},{7,23},{8,9},{9,8... | collective-permute-start | bytes 454664 | tf_op jit(solution)/shard_map/ppermute | solution.py:32
  23.0 0.3 collective-permute-start.13
  23.4 2.9 %collective-permute-done.11.refs_0_ = s32[296,128]{1,0:T(8,128)S(1)} collective-permute-done((s32[296,128]{1,0:T(8,128)S(1)}, s32[296,128]{1,0:T(8,128)S(1)}, u32[]{:S(2)}, u32[]{:S(2)}) %collective-permute-start.11) | collective-permute-done | bytes 151584 | tf_op jit(solution)/shard_map/ppermute | solution.py:32
  26.3 0.6 %collective-permute-done.12.refs_1_ = s32[296,128]{1,0:T(8,128)S(1)} collective-permute-done((s32[296,128]{1,0:T(8,128)S(1)}, s32[296,128]{1,0:T(8,128)S(1)}, u32[]{:S(2)}, u32[]{:S(2)}) %collective-permute-start.12) | collective-permute-done | bytes 151584 | tf_op jit(solution)/shard_map/ppermute | solution.py:32
  26.9 3.4 %collective-permute-done.13.refs_2_ = s32[296,128]{1,0:T(8,128)S(1)} collective-permute-done((s32[296,128]{1,0:T(8,128)S(1)}, s32[296,128]{1,0:T(8,128)S(1)}, u32[]{:S(2)}, u32[]{:S(2)}) %collective-permute-start.13) | collective-permute-done | bytes 151584 | tf_op jit(solution)/shard_map/ppermute | solution.py:32
  30.3 0.2 squares.1
  30.5 0.1 collective-permute-start.14
  30.6 2.1 %collective-permute-start.15 = (f32[1,128]{1,0:T(1,128)S(1)}, f32[1,128]{1,0:T(1,128)S(1)}, u32[]{:S(2)}, u32[]{:S(2)}) collective-permute-start(f32[1,128]{1,0:T(1,128)S(1)} %get-tuple-element.34), channel_id=1, source_target_pairs={{0,20},{1,21},{2,22},{3,23},{4,16},{5,17},{6,18},{7,19},{8,28},{9,... | collective-permute-start | bytes 1544 | tf_op jit(solution)/shard_map/ppermute | solution.py:32
  32.7 0.0 collective-permute-done.14
  32.7 1.0 %collective-permute-start.16 = (f32[1,128]{1,0:T(1,128)S(1)}, f32[1,128]{1,0:T(1,128)S(1)}, u32[]{:S(2)}, u32[]{:S(2)}) collective-permute-start(f32[1,128]{1,0:T(1,128)S(1)} %add.18), channel_id=1, source_target_pairs={{0,16},{1,17},{2,18},{3,19},{4,20},{5,21},{6,22},{7,23},{8,12},{9,... | collective-permute-start | bytes 1544 | tf_op jit(solution)/shard_map/ppermute | solution.py:32
  33.7 1.4 %collective-permute-done.15 = f32[1,128]{1,0:T(1,128)S(1)} collective-permute-done((f32[1,128]{1,0:T(1,128)S(1)}, f32[1,128]{1,0:T(1,128)S(1)}, u32[]{:S(2)}, u32[]{:S(2)}) %collective-permute-start.15) | collective-permute-done | bytes 544 | tf_op jit(solution)/shard_map/ppermute | solution.py:32
  35.1 1.1 %collective-permute-done.16 = f32[1,128]{1,0:T(1,128)S(1)} collective-permute-done((f32[1,128]{1,0:T(1,128)S(1)}, f32[1,128]{1,0:T(1,128)S(1)}, u32[]{:S(2)}, u32[]{:S(2)}) %collective-permute-start.16) | collective-permute-done | bytes 544 | tf_op jit(solution)/shard_map/ppermute | solution.py:32
  36.2 0.0 collective-permute-start.17
  36.2 1.1 %collective-permute-done.17 = f32[1,128]{1,0:T(1,128)S(1)} collective-permute-done((f32[1,128]{1,0:T(1,128)S(1)}, f32[1,128]{1,0:T(1,128)S(1)}, u32[]{:S(2)}, u32[]{:S(2)}) %collective-permute-start.17) | collective-permute-done | bytes 544 | tf_op jit(solution)/shard_map/ppermute | solution.py:22
  37.4 0.7 %multiply_bitcast_fusion = f32[1,512,128]{2,1,0:T(8,128)} fusion(f32[512,128]{1,0:T(8,128)S(1)} %get-tuple-element.33, f32[128]{0:T(128)S(1)} %divide_bitcast_fusion), kind=kLoop, calls=%fused_computation | loop fusion | flops 65536 | bytes 524800 | tf_op jit(solution)/shard_map/broadcast_in_dim | solution.py:240
  (6 shorter events, 0.0 us)
Async XLA Ops:
  0.0 18.8 %copy-start = (bf16[1,8,128,128]{3,2,1,0:T(8,128)(2,1)S(1)}, bf16[1,8,128,128]{3,2,1,0:T(8,128)(2,1)}, u32[]{:S(2)}) copy-start(bf16[1,8,128,128]{3,2,1,0:T(8,128)(2,1)} %param.4) | copy-start | bytes 786436
  0.0 5.6 %collective-permute-start.3 = (bf16[8,128,128]{2,1,0:T(8,128)(2,1)}, bf16[8,128,128]{2,1,0:T(8,128)(2,1)S(1)}, u32[]{:S(2)}, u32[]{:S(2)}) collective-permute-start(bf16[8,128,128]{2,1,0:T(8,128)(2,1)} %bitcast.7), channel_id=1, source_target_pairs={{0,8},{8,0},{16,24},{24,16},{1,9},{9,1},{17,25},{25,17},{2,10},{10... | collective-permute-start | bytes 786440 | tf_op jit(solution)/shard_map/ppermute | solution.py:22
  0.5 16.5 %collective-permute-start = (bf16[8,128,128]{2,1,0:T(8,128)(2,1)}, bf16[8,128,128]{2,1,0:T(8,128)(2,1)S(1)}, u32[]{:S(2)}, u32[]{:S(2)}) collective-permute-start(bf16[8,128,128]{2,1,0:T(8,128)(2,1)} %bitcast.8), channel_id=1, source_target_pairs={{0,2},{1,3},{2,0},{3,1},{4,6},{5,7},{6,4},{7,5},{8,10},{9,11},{10,... | collective-permute-start | bytes 786440 | tf_op jit(solution)/shard_map/ppermute | solution.py:22
  5.4 6.3 %collective-permute-start.1 = (s32[1,8]{1,0:T(1,128)S(1)}, s32[1,8]{1,0:T(1,128)S(1)}, u32[]{:S(2)}, u32[]{:S(2)}) collective-permute-start(s32[1,8]{1,0:T(1,128)S(1)} %compare_select_fusion), channel_id=1, source_target_pairs={{0,8},{8,0},{16,24},{24,16},{1,9},{9,1},{17,25},{25,17},{2,10},{10... | collective-permute-start | bytes 104 | tf_op jit(solution)/shard_map/ppermute | solution.py:22
  5.6 6.6 %collective-permute-start.6 = (bf16[256,128]{1,0:T(8,128)(2,1)}, bf16[256,128]{1,0:T(8,128)(2,1)S(1)}, u32[]{:S(2)}, u32[]{:S(2)}) collective-permute-start(bf16[256,128]{1,0:T(8,128)(2,1)} %param.7), channel_id=1, source_target_pairs={{0,1},{1,0},{2,3},{3,2},{4,5},{5,4},{6,7},{7,6},{8,9},{9,8},{10,11... | collective-permute-start | bytes 196616 | tf_op jit(solution)/shard_map/ppermute | solution.py:22
  7.2 4.5 %collective-permute-start.4 = (bf16[256,128]{1,0:T(8,128)(2,1)}, bf16[256,128]{1,0:T(8,128)(2,1)S(1)}, u32[]{:S(2)}, u32[]{:S(2)}) collective-permute-start(bf16[256,128]{1,0:T(8,128)(2,1)} %param.7), channel_id=1, source_target_pairs={{0,4},{4,0},{1,5},{5,1},{2,6},{6,2},{3,7},{7,3},{8,12},{12,8},{9,1... | collective-permute-start | bytes 196616 | tf_op jit(solution)/shard_map/ppermute | solution.py:22
  11.7 5.3 %collective-permute-start.5 = (bf16[512,128]{1,0:T(8,128)(2,1)S(1)}, bf16[512,128]{1,0:T(8,128)(2,1)S(1)}, u32[]{:S(2)}, u32[]{:S(2)}) collective-permute-start(bf16[512,128]{1,0:T(8,128)(2,1)S(1)} %constant_dynamic-update-slice_fusion.refs_0_), channel_id=1, source_target_pairs={{0,8},{8,0},{16,24},{24,16},{1,9},{9,1},{17,25},{25,17},{2,10},{10... | collective-permute-start | bytes 393224 | tf_op jit(solution)/shard_map/ppermute | solution.py:22
  11.8 5.2 %collective-permute-start.2 = (s32[2,8]{1,0:T(2,128)S(1)}, s32[2,8]{1,0:T(2,128)S(1)}, u32[]{:S(2)}, u32[]{:S(2)}) collective-permute-start(s32[2,8]{1,0:T(2,128)S(1)} %pad_add_fusion.1), channel_id=1, source_target_pairs={{0,2},{1,3},{2,0},{3,1},{4,6},{5,7},{6,4},{7,5},{8,10},{9,11},{10,... | collective-permute-start | bytes 200 | tf_op jit(solution)/shard_map/ppermute | solution.py:22
  12.2 4.8 %collective-permute-start.7 = (bf16[256,128]{1,0:T(8,128)(2,1)S(1)}, bf16[256,128]{1,0:T(8,128)(2,1)S(1)}, u32[]{:S(2)}, u32[]{:S(2)}) collective-permute-start(bf16[256,128]{1,0:T(8,128)(2,1)S(1)} %collective-permute-done.6.refs_2_), channel_id=1, source_target_pairs={{0,4},{4,0},{1,5},{5,1},{2,6},{6,2},{3,7},{7,3},{8,12},{12,8},{9,1... | collective-permute-start | bytes 196616 | tf_op jit(solution)/shard_map/ppermute | solution.py:22
  17.0 1.8 %collective-permute-start.10 = (bf16[8,128,128]{2,1,0:T(8,128)(2,1)S(1)}, bf16[8,128,128]{2,1,0:T(8,128)(2,1)S(1)}, u32[]{:S(2)}, u32[]{:S(2)}) collective-permute-start(bf16[8,128,128]{2,1,0:T(8,128)(2,1)S(1)} %collective-permute-done.refs_8_), channel_id=1, source_target_pairs={{0,8},{8,0},{16,24},{24,16},{1,9},{9,1},{17,25},{25,17},{2,10},{10... | collective-permute-start | bytes 786440 | tf_op jit(solution)/shard_map/ppermute | solution.py:22
  17.0 1.6 %collective-permute-start.8 = (bf16[256,128]{1,0:T(8,128)(2,1)S(1)}, bf16[256,128]{1,0:T(8,128)(2,1)S(1)}, u32[]{:S(2)}, u32[]{:S(2)}) collective-permute-start(bf16[256,128]{1,0:T(8,128)(2,1)S(1)} %collective-permute-done.6.refs_2_), channel_id=1, source_target_pairs={{0,8},{8,0},{16,24},{24,16},{1,9},{9,1},{17,25},{25,17},{2,10},{10... | collective-permute-start | bytes 196616 | tf_op jit(solution)/shard_map/ppermute | solution.py:22
  17.5 1.3 %collective-permute-start.9 = (bf16[256,128]{1,0:T(8,128)(2,1)S(1)}, bf16[256,128]{1,0:T(8,128)(2,1)S(1)}, u32[]{:S(2)}, u32[]{:S(2)}) collective-permute-start(bf16[256,128]{1,0:T(8,128)(2,1)S(1)} %collective-permute-done.7.refs_4_), channel_id=1, source_target_pairs={{0,8},{8,0},{16,24},{24,16},{1,9},{9,1},{17,25},{25,17},{2,10},{10... | collective-permute-start | bytes 196616 | tf_op jit(solution)/shard_map/ppermute | solution.py:22
  19.8 6.5 %collective-permute-start.11 = (s32[296,128]{1,0:T(8,128)S(1)}, s32[296,128]{1,0:T(8,128)S(1)}, u32[]{:S(2)}, u32[]{:S(2)}) collective-permute-start(s32[296,128]{1,0:T(8,128)S(1)} %get-tuple-element.30), channel_id=1, source_target_pairs={{0,1},{1,0},{2,3},{3,2},{4,5},{5,4},{6,7},{7,6},{8,24},{9,25},{10,... | collective-permute-start | bytes 454664 | tf_op jit(solution)/shard_map/ppermute | solution.py:32
  21.5 5.4 %collective-permute-start.12 = (s32[296,128]{1,0:T(8,128)S(1)}, s32[296,128]{1,0:T(8,128)S(1)}, u32[]{:S(2)}, u32[]{:S(2)}) collective-permute-start(s32[296,128]{1,0:T(8,128)S(1)} %get-tuple-element.31), channel_id=1, source_target_pairs={{0,16},{1,17},{2,18},{3,19},{4,20},{5,21},{6,22},{7,23},{8,9},{9,8... | collective-permute-start | bytes 454664 | tf_op jit(solution)/shard_map/ppermute | solution.py:32
  23.0 7.3 %collective-permute-start.13 = (s32[296,128]{1,0:T(8,128)S(1)}, s32[296,128]{1,0:T(8,128)S(1)}, u32[]{:S(2)}, u32[]{:S(2)}) collective-permute-start(s32[296,128]{1,0:T(8,128)S(1)} %get-tuple-element.32), channel_id=1, source_target_pairs={{0,17},{1,16},{2,19},{3,18},{4,21},{5,20},{6,23},{7,22},{8,25},{9,... | collective-permute-start | bytes 454664 | tf_op jit(solution)/shard_map/ppermute | solution.py:32
  30.5 2.2 %collective-permute-start.14 = (f32[1,128]{1,0:T(1,128)S(1)}, f32[1,128]{1,0:T(1,128)S(1)}, u32[]{:S(2)}, u32[]{:S(2)}) collective-permute-start(f32[1,128]{1,0:T(1,128)S(1)} %get-tuple-element.34), channel_id=1, source_target_pairs={{0,8},{8,0},{16,24},{24,16},{1,9},{9,1},{17,25},{25,17},{2,10},{10... | collective-permute-start | bytes 1544 | tf_op jit(solution)/shard_map/ppermute | solution.py:22
  30.6 4.5 %collective-permute-start.15 = (f32[1,128]{1,0:T(1,128)S(1)}, f32[1,128]{1,0:T(1,128)S(1)}, u32[]{:S(2)}, u32[]{:S(2)}) collective-permute-start(f32[1,128]{1,0:T(1,128)S(1)} %get-tuple-element.34), channel_id=1, source_target_pairs={{0,20},{1,21},{2,22},{3,23},{4,16},{5,17},{6,18},{7,19},{8,28},{9,... | collective-permute-start | bytes 1544 | tf_op jit(solution)/shard_map/ppermute | solution.py:32
  32.7 3.5 %collective-permute-start.16 = (f32[1,128]{1,0:T(1,128)S(1)}, f32[1,128]{1,0:T(1,128)S(1)}, u32[]{:S(2)}, u32[]{:S(2)}) collective-permute-start(f32[1,128]{1,0:T(1,128)S(1)} %add.18), channel_id=1, source_target_pairs={{0,16},{1,17},{2,18},{3,19},{4,20},{5,21},{6,22},{7,23},{8,12},{9,... | collective-permute-start | bytes 1544 | tf_op jit(solution)/shard_map/ppermute | solution.py:32
  36.2 1.1 %collective-permute-start.17 = (f32[1,128]{1,0:T(1,128)S(1)}, f32[1,128]{1,0:T(1,128)S(1)}, u32[]{:S(2)}, u32[]{:S(2)}) collective-permute-start(f32[1,128]{1,0:T(1,128)S(1)} %add.19), channel_id=1, source_target_pairs={{0,8},{8,0},{16,24},{24,16},{1,9},{9,1},{17,25},{25,17},{2,10},{10... | collective-permute-start | bytes 1544 | tf_op jit(solution)/shard_map/ppermute | solution.py:22

commit v12 on v11

--- a/solution.py
+++ b/solution.py
@@ -60,19 +60,21 @@
     return fields
 
 
-def pack(part, out_ref):
-    top = jnp.max(jnp.abs(part), axis=0, keepdims=True)
+def pack(parts, out_refs):
+    top = jnp.concatenate([jnp.max(jnp.abs(p), axis=0, keepdims=True) for p in parts])
     k = jnp.clip(jnp.ceil(jnp.log2(top) + 0.01), -100.0, 126.0).astype(jnp.int32)
-    q = jnp.floor(part * power_of_two(BITS - 1 - k) + 0.5).astype(jnp.int32)
-    rows = part.shape[0] // VALUES
-    q = [q[i * rows : (i + 1) * rows] for i in range(VALUES)]
-    words = [q[j] << (32 - BITS) for j in range(WORDS)]
-    for i in range(WORDS, VALUES):
-        for bit, word, to, bits in low_fields(i):
-            words[word] = words[word] | (((q[i] >> bit) & ((1 << bits) - 1)) << to)
-    for j in range(WORDS):
-        out_ref[j * rows : (j + 1) * rows] = words[j]
-    out_ref[WORDS * rows :] = jnp.broadcast_to(k, (8, part.shape[1]))
+    steps = power_of_two(BITS - 1 - k)
+    for p, (part, out_ref) in enumerate(zip(parts, out_refs, strict=True)):
+        q = jnp.floor(part * steps[p : p + 1] + 0.5).astype(jnp.int32)
+        rows = part.shape[0] // VALUES
+        q = [q[i * rows : (i + 1) * rows] for i in range(VALUES)]
+        words = [q[j] << (32 - BITS) for j in range(WORDS)]
+        for i in range(WORDS, VALUES):
+            for bit, word, to, bits in low_fields(i):
+                words[word] = words[word] | (((q[i] >> bit) & ((1 << bits) - 1)) << to)
+        for j in range(WORDS):
+            out_ref[j * rows : (j + 1) * rows] = words[j]
+        out_ref[WORDS * rows :] = jnp.broadcast_to(k[p : p + 1], (8, part.shape[1]))
 
 
 def unpack(ref, rows, i):
@@ -157,9 +159,9 @@
     out_refs[0][...] = parts[0]
     for k in range(1, 2 * n_slots - 1, 2):
         one, two = parts[k : k + 2]
-        pack(jnp.where(layer % 2 == 0, one, two), out_refs[k])
-        pack(jnp.where(layer % 2 == 0, two, one), out_refs[k + 1])
-    pack(parts[-1], out_refs[-1])
+        parts[k] = jnp.where(layer % 2 == 0, one, two)
+        parts[k + 1] = jnp.where(layer % 2 == 0, two, one)
+    pack(parts[1:], out_refs[1:])
 
 
 def products(masks, lists, b_refs, panels):

time: 38.3 us -> 38.2 us (level)
  no operation moved by 1% of the time
where the time goes in v12:
time: 38.2 us; the launch traced here: 38 us
  waiting for transfers between devices  17.1 us (45%)
  starting transfers between devices  16.7 us (44%)
  other arithmetic  1.42 us (4%)
  Pallas kernels  1.15 us (3%)
  local copies, waits for them, and re-layouts  0.89 us (2%)
  between operations  0.74 us (2%)
    ppermute x13, starting transfers between devices, xor_permute(): lax.ppermute(x, axis, [(i, i ^ mask) for i in range(lax.axis_size(axis))])  10.1 us
    ppermute x5, waiting for transfers between devices, grid_permute(): return lax.ppermute(x, AXES, pairs)  9.44 us
    ppermute x13, waiting for transfers between devices, xor_permute(): lax.ppermute(x, axis, [(i, i ^ mask) for i in range(lax.axis_size(axis))])  7.64 us
    ppermute x5, starting transfers between devices, grid_permute(): return lax.ppermute(x, AXES, pairs)  6.67 us
    pallas_call x1, Pallas kernels, products(): pl.pallas_call(functools.partial(product_kernel, masks, n_layer, n_row, n...  0.92 us
    unnamed x3, local copies, waits for them, and re-layouts  0.88 us
  transfers between devices with their start and end apart: 18, of which 10 were waited for; matrix products, arithmetic and copies ran while one was open for 4% of the time, Pallas kernels for 0%

profile of v12, /device:TPU:0, one launch (start us, length us, event | category | flops | bytes accessed | tf_op | source)
XLA Modules:
  0.0 38.0 jit_solution(7478889459472647410)
XLA Ops:
  0.0 0.0 copy-start
  0.0 0.5 %collective-permute-start.3 = (bf16[8,128,128]{2,1,0:T(8,128)(2,1)}, bf16[8,128,128]{2,1,0:T(8,128)(2,1)S(1)}, u32[]{:S(2)}, u32[]{:S(2)}) collective-permute-start(bf16[8,128,128]{2,1,0:T(8,128)(2,1)} %bitcast.7), channel_id=1, source_target_pairs={{0,8},{8,0},{16,24},{24,16},{1,9},{9,1},{17,25},{25,17},{2,10},{10... | collective-permute-start | bytes 786440 | tf_op jit(solution)/shard_map/ppermute | solution.py:22
  0.5 3.6 %collective-permute-start = (bf16[8,128,128]{2,1,0:T(8,128)(2,1)}, bf16[8,128,128]{2,1,0:T(8,128)(2,1)S(1)}, u32[]{:S(2)}, u32[]{:S(2)}) collective-permute-start(bf16[8,128,128]{2,1,0:T(8,128)(2,1)} %bitcast.8), channel_id=1, source_target_pairs={{0,2},{1,3},{2,0},{3,1},{4,6},{5,7},{6,4},{7,5},{8,10},{9,11},{10,... | collective-permute-start | bytes 786440 | tf_op jit(solution)/shard_map/ppermute | solution.py:22
  4.8 0.7 %compare_select_fusion = s32[1,8]{1,0:T(1,128)S(1)} fusion(s32[1,8]{1,0:T(1,128)} %param.5, s32[]{:T(128)} %bitcast.6), kind=kLoop, calls=%fused_computation.4 | loop fusion | flops 16 | bytes 68 | tf_op jit(solution)/shard_map/jit(_where)/select_n | solution.py:194
  5.4 0.2 collective-permute-start.1
  5.6 0.0 collective-permute-done.3.refs_7_
  5.6 1.6 %collective-permute-start.6 = (bf16[256,128]{1,0:T(8,128)(2,1)}, bf16[256,128]{1,0:T(8,128)(2,1)S(1)}, u32[]{:S(2)}, u32[]{:S(2)}) collective-permute-start(bf16[256,128]{1,0:T(8,128)(2,1)} %param.7), channel_id=1, source_target_pairs={{0,1},{1,0},{2,3},{3,2},{4,5},{5,4},{6,7},{7,6},{8,9},{9,8},{10,11... | collective-permute-start | bytes 196616 | tf_op jit(solution)/shard_map/ppermute | solution.py:22
  7.2 1.5 %collective-permute-start.4 = (bf16[256,128]{1,0:T(8,128)(2,1)}, bf16[256,128]{1,0:T(8,128)(2,1)S(1)}, u32[]{:S(2)}, u32[]{:S(2)}) collective-permute-start(bf16[256,128]{1,0:T(8,128)(2,1)} %param.7), channel_id=1, source_target_pairs={{0,4},{4,0},{1,5},{5,1},{2,6},{6,2},{3,7},{7,3},{8,12},{12,8},{9,1... | collective-permute-start | bytes 196616 | tf_op jit(solution)/shard_map/ppermute | solution.py:22
  8.7 0.9 %constant_dynamic-update-slice_fusion.1 = bf16[512,128]{1,0:T(8,128)(2,1)S(1)} fusion(bf16[256,128]{1,0:T(8,128)(2,1)} %param.7), kind=kLoop, calls=%fused_computation.2 | loop fusion | bytes 131072
  9.6 2.1 %collective-permute-done.4 = bf16[256,128]{1,0:T(8,128)(2,1)S(1)} collective-permute-done((bf16[256,128]{1,0:T(8,128)(2,1)}, bf16[256,128]{1,0:T(8,128)(2,1)S(1)}, u32[]{:S(2)}, u32[]{:S(2)}) %collective-permute-start.4) | collective-permute-done | bytes 65568 | tf_op jit(solution)/shard_map/ppermute | solution.py:22
  11.7 0.1 collective-permute-start.5
  11.7 0.0 collective-permute-done.1
  11.8 0.4 %collective-permute-start.2 = (s32[2,8]{1,0:T(2,128)S(1)}, s32[2,8]{1,0:T(2,128)S(1)}, u32[]{:S(2)}, u32[]{:S(2)}) collective-permute-start(s32[2,8]{1,0:T(2,128)S(1)} %pad_add_fusion.1), channel_id=1, source_target_pairs={{0,2},{1,3},{2,0},{3,1},{4,6},{5,7},{6,4},{7,5},{8,10},{9,11},{10,... | collective-permute-start | bytes 200 | tf_op jit(solution)/shard_map/ppermute | solution.py:22
  12.2 0.0 collective-permute-done.6.refs_2_
  12.2 1.5 %collective-permute-start.7 = (bf16[256,128]{1,0:T(8,128)(2,1)S(1)}, bf16[256,128]{1,0:T(8,128)(2,1)S(1)}, u32[]{:S(2)}, u32[]{:S(2)}) collective-permute-start(bf16[256,128]{1,0:T(8,128)(2,1)S(1)} %collective-permute-done.6.refs_2_), channel_id=1, source_target_pairs={{0,4},{4,0},{1,5},{5,1},{2,6},{6,2},{3,7},{7,3},{8,12},{12,8},{9,1... | collective-permute-start | bytes 196616 | tf_op jit(solution)/shard_map/ppermute | solution.py:22
  13.7 3.2 %collective-permute-done.2 = s32[2,8]{1,0:T(2,128)S(1)} collective-permute-done((s32[2,8]{1,0:T(2,128)S(1)}, s32[2,8]{1,0:T(2,128)S(1)}, u32[]{:S(2)}, u32[]{:S(2)}) %collective-permute-start.2) | collective-permute-done | bytes 96 | tf_op jit(solution)/shard_map/ppermute | solution.py:22
  16.9 0.0 collective-permute-done.refs_8_
  16.9 0.0 collective-permute-done.7.refs_4_
  17.0 0.0 collective-permute-done.5.refs_1_
  17.0 0.1 collective-permute-start.10
  17.0 0.5 %collective-permute-start.8 = (bf16[256,128]{1,0:T(8,128)(2,1)S(1)}, bf16[256,128]{1,0:T(8,128)(2,1)S(1)}, u32[]{:S(2)}, u32[]{:S(2)}) collective-permute-start(bf16[256,128]{1,0:T(8,128)(2,1)S(1)} %collective-permute-done.6.refs_2_), channel_id=1, source_target_pairs={{0,8},{8,0},{16,24},{24,16},{1,9},{9,1},{17,25},{25,17},{2,10},{10... | collective-permute-start | bytes 196616 | tf_op jit(solution)/shard_map/ppermute | solution.py:22
  17.5 0.1 collective-permute-start.9
  17.6 1.0 %collective-permute-done.8.refs_3_ = bf16[256,128]{1,0:T(8,128)(2,1)S(1)} collective-permute-done((bf16[256,128]{1,0:T(8,128)(2,1)S(1)}, bf16[256,128]{1,0:T(8,128)(2,1)S(1)}, u32[]{:S(2)}, u32[]{:S(2)}) %collective-permute-start.8) | collective-permute-done | bytes 65568 | tf_op jit(solution)/shard_map/ppermute | solution.py:22
  18.7 0.1 collective-permute-done.9.refs_5_
  18.8 0.0 collective-permute-done.10.refs_9_
  18.8 0.0 copy-done
  18.8 0.9 %partial_rows.1 = (f32[512,128]{1,0:T(8,128)S(1)}, s32[296,128]{1,0:T(8,128)S(1)}, s32[296,128]{1,0:T(8,128)S(1)}, s32[296,128]{1,0:T(8,128)S(1)}) custom-call(s32[4,8]{1,0:T(4,128)S(1)} %pad_add_fusion.lists_ref, bf16[512,128]{1,0:T(8,128)(2,1)S(1)} %constant_dynamic-update-slice_fusion.refs_0_, bf16[512,128]{1,0:T(8,128)(2,1)S(1)} %collective-permute-done.5.refs_1_, ...), custom_call_target="tpu_custom_call" | custom-call | tf_op jit(solution)/shard_map/partial_rows/pallas_call | solution.py:172
  19.7 1.7 %collective-permute-start.11 = (s32[296,128]{1,0:T(8,128)S(1)}, s32[296,128]{1,0:T(8,128)S(1)}, u32[]{:S(2)}, u32[]{:S(2)}) collective-permute-start(s32[296,128]{1,0:T(8,128)S(1)} %get-tuple-element.30), channel_id=1, source_target_pairs={{0,1},{1,0},{2,3},{3,2},{4,5},{5,4},{6,7},{7,6},{8,24},{9,25},{10,... | collective-permute-start | bytes 454664 | tf_op jit(solution)/shard_map/ppermute | solution.py:32
  21.5 1.5 %collective-permute-start.12 = (s32[296,128]{1,0:T(8,128)S(1)}, s32[296,128]{1,0:T(8,128)S(1)}, u32[]{:S(2)}, u32[]{:S(2)}) collective-permute-start(s32[296,128]{1,0:T(8,128)S(1)} %get-tuple-element.31), channel_id=1, source_target_pairs={{0,16},{1,17},{2,18},{3,19},{4,20},{5,21},{6,22},{7,23},{8,9},{9,8... | collective-permute-start | bytes 454664 | tf_op jit(solution)/shard_map/ppermute | solution.py:32
  23.0 0.3 collective-permute-start.13
  23.3 2.9 %collective-permute-done.11.refs_0_ = s32[296,128]{1,0:T(8,128)S(1)} collective-permute-done((s32[296,128]{1,0:T(8,128)S(1)}, s32[296,128]{1,0:T(8,128)S(1)}, u32[]{:S(2)}, u32[]{:S(2)}) %collective-permute-start.11) | collective-permute-done | bytes 151584 | tf_op jit(solution)/shard_map/ppermute | solution.py:32
  26.2 0.6 %collective-permute-done.12.refs_1_ = s32[296,128]{1,0:T(8,128)S(1)} collective-permute-done((s32[296,128]{1,0:T(8,128)S(1)}, s32[296,128]{1,0:T(8,128)S(1)}, u32[]{:S(2)}, u32[]{:S(2)}) %collective-permute-start.12) | collective-permute-done | bytes 151584 | tf_op jit(solution)/shard_map/ppermute | solution.py:32
  26.9 3.4 %collective-permute-done.13.refs_2_ = s32[296,128]{1,0:T(8,128)S(1)} collective-permute-done((s32[296,128]{1,0:T(8,128)S(1)}, s32[296,128]{1,0:T(8,128)S(1)}, u32[]{:S(2)}, u32[]{:S(2)}) %collective-permute-start.13) | collective-permute-done | bytes 151584 | tf_op jit(solution)/shard_map/ppermute | solution.py:32
  30.2 0.2 squares.1
  30.5 0.1 collective-permute-start.14
  30.5 2.1 %collective-permute-start.15 = (f32[1,128]{1,0:T(1,128)S(1)}, f32[1,128]{1,0:T(1,128)S(1)}, u32[]{:S(2)}, u32[]{:S(2)}) collective-permute-start(f32[1,128]{1,0:T(1,128)S(1)} %get-tuple-element.34), channel_id=1, source_target_pairs={{0,20},{1,21},{2,22},{3,23},{4,16},{5,17},{6,18},{7,19},{8,28},{9,... | collective-permute-start | bytes 1544 | tf_op jit(solution)/shard_map/ppermute | solution.py:32
  32.6 0.0 collective-permute-done.14
  32.6 1.0 %collective-permute-start.16 = (f32[1,128]{1,0:T(1,128)S(1)}, f32[1,128]{1,0:T(1,128)S(1)}, u32[]{:S(2)}, u32[]{:S(2)}) collective-permute-start(f32[1,128]{1,0:T(1,128)S(1)} %add.18), channel_id=1, source_target_pairs={{0,16},{1,17},{2,18},{3,19},{4,20},{5,21},{6,22},{7,23},{8,12},{9,... | collective-permute-start | bytes 1544 | tf_op jit(solution)/shard_map/ppermute | solution.py:32
  33.7 1.4 %collective-permute-done.15 = f32[1,128]{1,0:T(1,128)S(1)} collective-permute-done((f32[1,128]{1,0:T(1,128)S(1)}, f32[1,128]{1,0:T(1,128)S(1)}, u32[]{:S(2)}, u32[]{:S(2)}) %collective-permute-start.15) | collective-permute-done | bytes 544 | tf_op jit(solution)/shard_map/ppermute | solution.py:32
  35.0 1.1 %collective-permute-done.16 = f32[1,128]{1,0:T(1,128)S(1)} collective-permute-done((f32[1,128]{1,0:T(1,128)S(1)}, f32[1,128]{1,0:T(1,128)S(1)}, u32[]{:S(2)}, u32[]{:S(2)}) %collective-permute-start.16) | collective-permute-done | bytes 544 | tf_op jit(solution)/shard_map/ppermute | solution.py:32
  36.2 0.0 collective-permute-start.17
  36.2 1.1 %collective-permute-done.17 = f32[1,128]{1,0:T(1,128)S(1)} collective-permute-done((f32[1,128]{1,0:T(1,128)S(1)}, f32[1,128]{1,0:T(1,128)S(1)}, u32[]{:S(2)}, u32[]{:S(2)}) %collective-permute-start.17) | collective-permute-done | bytes 544 | tf_op jit(solution)/shard_map/ppermute | solution.py:22
  37.3 0.7 %multiply_bitcast_fusion = f32[1,512,128]{2,1,0:T(8,128)} fusion(f32[512,128]{1,0:T(8,128)S(1)} %get-tuple-element.33, f32[128]{0:T(128)S(1)} %divide_bitcast_fusion), kind=kLoop, calls=%fused_computation | loop fusion | flops 65536 | bytes 524800 | tf_op jit(solution)/shard_map/broadcast_in_dim | solution.py:242
  (6 shorter events, 0.0 us)
Async XLA Ops:
  0.0 18.8 %copy-start = (bf16[1,8,128,128]{3,2,1,0:T(8,128)(2,1)S(1)}, bf16[1,8,128,128]{3,2,1,0:T(8,128)(2,1)}, u32[]{:S(2)}) copy-start(bf16[1,8,128,128]{3,2,1,0:T(8,128)(2,1)} %param.4) | copy-start | bytes 786436
  0.0 5.6 %collective-permute-start.3 = (bf16[8,128,128]{2,1,0:T(8,128)(2,1)}, bf16[8,128,128]{2,1,0:T(8,128)(2,1)S(1)}, u32[]{:S(2)}, u32[]{:S(2)}) collective-permute-start(bf16[8,128,128]{2,1,0:T(8,128)(2,1)} %bitcast.7), channel_id=1, source_target_pairs={{0,8},{8,0},{16,24},{24,16},{1,9},{9,1},{17,25},{25,17},{2,10},{10... | collective-permute-start | bytes 786440 | tf_op jit(solution)/shard_map/ppermute | solution.py:22
  0.5 16.5 %collective-permute-start = (bf16[8,128,128]{2,1,0:T(8,128)(2,1)}, bf16[8,128,128]{2,1,0:T(8,128)(2,1)S(1)}, u32[]{:S(2)}, u32[]{:S(2)}) collective-permute-start(bf16[8,128,128]{2,1,0:T(8,128)(2,1)} %bitcast.8), channel_id=1, source_target_pairs={{0,2},{1,3},{2,0},{3,1},{4,6},{5,7},{6,4},{7,5},{8,10},{9,11},{10,... | collective-permute-start | bytes 786440 | tf_op jit(solution)/shard_map/ppermute | solution.py:22
  5.4 6.3 %collective-permute-start.1 = (s32[1,8]{1,0:T(1,128)S(1)}, s32[1,8]{1,0:T(1,128)S(1)}, u32[]{:S(2)}, u32[]{:S(2)}) collective-permute-start(s32[1,8]{1,0:T(1,128)S(1)} %compare_select_fusion), channel_id=1, source_target_pairs={{0,8},{8,0},{16,24},{24,16},{1,9},{9,1},{17,25},{25,17},{2,10},{10... | collective-permute-start | bytes 104 | tf_op jit(solution)/shard_map/ppermute | solution.py:22
  5.6 6.6 %collective-permute-start.6 = (bf16[256,128]{1,0:T(8,128)(2,1)}, bf16[256,128]{1,0:T(8,128)(2,1)S(1)}, u32[]{:S(2)}, u32[]{:S(2)}) collective-permute-start(bf16[256,128]{1,0:T(8,128)(2,1)} %param.7), channel_id=1, source_target_pairs={{0,1},{1,0},{2,3},{3,2},{4,5},{5,4},{6,7},{7,6},{8,9},{9,8},{10,11... | collective-permute-start | bytes 196616 | tf_op jit(solution)/shard_map/ppermute | solution.py:22
  7.2 4.5 %collective-permute-start.4 = (bf16[256,128]{1,0:T(8,128)(2,1)}, bf16[256,128]{1,0:T(8,128)(2,1)S(1)}, u32[]{:S(2)}, u32[]{:S(2)}) collective-permute-start(bf16[256,128]{1,0:T(8,128)(2,1)} %param.7), channel_id=1, source_target_pairs={{0,4},{4,0},{1,5},{5,1},{2,6},{6,2},{3,7},{7,3},{8,12},{12,8},{9,1... | collective-permute-start | bytes 196616 | tf_op jit(solution)/shard_map/ppermute | solution.py:22
  11.7 5.3 %collective-permute-start.5 = (bf16[512,128]{1,0:T(8,128)(2,1)S(1)}, bf16[512,128]{1,0:T(8,128)(2,1)S(1)}, u32[]{:S(2)}, u32[]{:S(2)}) collective-permute-start(bf16[512,128]{1,0:T(8,128)(2,1)S(1)} %constant_dynamic-update-slice_fusion.refs_0_), channel_id=1, source_target_pairs={{0,8},{8,0},{16,24},{24,16},{1,9},{9,1},{17,25},{25,17},{2,10},{10... | collective-permute-start | bytes 393224 | tf_op jit(solution)/shard_map/ppermute | solution.py:22
  11.8 5.2 %collective-permute-start.2 = (s32[2,8]{1,0:T(2,128)S(1)}, s32[2,8]{1,0:T(2,128)S(1)}, u32[]{:S(2)}, u32[]{:S(2)}) collective-permute-start(s32[2,8]{1,0:T(2,128)S(1)} %pad_add_fusion.1), channel_id=1, source_target_pairs={{0,2},{1,3},{2,0},{3,1},{4,6},{5,7},{6,4},{7,5},{8,10},{9,11},{10,... | collective-permute-start | bytes 200 | tf_op jit(solution)/shard_map/ppermute | solution.py:22
  12.2 4.8 %collective-permute-start.7 = (bf16[256,128]{1,0:T(8,128)(2,1)S(1)}, bf16[256,128]{1,0:T(8,128)(2,1)S(1)}, u32[]{:S(2)}, u32[]{:S(2)}) collective-permute-start(bf16[256,128]{1,0:T(8,128)(2,1)S(1)} %collective-permute-done.6.refs_2_), channel_id=1, source_target_pairs={{0,4},{4,0},{1,5},{5,1},{2,6},{6,2},{3,7},{7,3},{8,12},{12,8},{9,1... | collective-permute-start | bytes 196616 | tf_op jit(solution)/shard_map/ppermute | solution.py:22
  17.0 1.8 %collective-permute-start.10 = (bf16[8,128,128]{2,1,0:T(8,128)(2,1)S(1)}, bf16[8,128,128]{2,1,0:T(8,128)(2,1)S(1)}, u32[]{:S(2)}, u32[]{:S(2)}) collective-permute-start(bf16[8,128,128]{2,1,0:T(8,128)(2,1)S(1)} %collective-permute-done.refs_8_), channel_id=1, source_target_pairs={{0,8},{8,0},{16,24},{24,16},{1,9},{9,1},{17,25},{25,17},{2,10},{10... | collective-permute-start | bytes 786440 | tf_op jit(solution)/shard_map/ppermute | solution.py:22
  17.0 1.6 %collective-permute-start.8 = (bf16[256,128]{1,0:T(8,128)(2,1)S(1)}, bf16[256,128]{1,0:T(8,128)(2,1)S(1)}, u32[]{:S(2)}, u32[]{:S(2)}) collective-permute-start(bf16[256,128]{1,0:T(8,128)(2,1)S(1)} %collective-permute-done.6.refs_2_), channel_id=1, source_target_pairs={{0,8},{8,0},{16,24},{24,16},{1,9},{9,1},{17,25},{25,17},{2,10},{10... | collective-permute-start | bytes 196616 | tf_op jit(solution)/shard_map/ppermute | solution.py:22
  17.5 1.3 %collective-permute-start.9 = (bf16[256,128]{1,0:T(8,128)(2,1)S(1)}, bf16[256,128]{1,0:T(8,128)(2,1)S(1)}, u32[]{:S(2)}, u32[]{:S(2)}) collective-permute-start(bf16[256,128]{1,0:T(8,128)(2,1)S(1)} %collective-permute-done.7.refs_4_), channel_id=1, source_target_pairs={{0,8},{8,0},{16,24},{24,16},{1,9},{9,1},{17,25},{25,17},{2,10},{10... | collective-permute-start | bytes 196616 | tf_op jit(solution)/shard_map/ppermute | solution.py:22
  19.7 6.5 %collective-permute-start.11 = (s32[296,128]{1,0:T(8,128)S(1)}, s32[296,128]{1,0:T(8,128)S(1)}, u32[]{:S(2)}, u32[]{:S(2)}) collective-permute-start(s32[296,128]{1,0:T(8,128)S(1)} %get-tuple-element.30), channel_id=1, source_target_pairs={{0,1},{1,0},{2,3},{3,2},{4,5},{5,4},{6,7},{7,6},{8,24},{9,25},{10,... | collective-permute-start | bytes 454664 | tf_op jit(solution)/shard_map/ppermute | solution.py:32
  21.5 5.4 %collective-permute-start.12 = (s32[296,128]{1,0:T(8,128)S(1)}, s32[296,128]{1,0:T(8,128)S(1)}, u32[]{:S(2)}, u32[]{:S(2)}) collective-permute-start(s32[296,128]{1,0:T(8,128)S(1)} %get-tuple-element.31), channel_id=1, source_target_pairs={{0,16},{1,17},{2,18},{3,19},{4,20},{5,21},{6,22},{7,23},{8,9},{9,8... | collective-permute-start | bytes 454664 | tf_op jit(solution)/shard_map/ppermute | solution.py:32
  23.0 7.3 %collective-permute-start.13 = (s32[296,128]{1,0:T(8,128)S(1)}, s32[296,128]{1,0:T(8,128)S(1)}, u32[]{:S(2)}, u32[]{:S(2)}) collective-permute-start(s32[296,128]{1,0:T(8,128)S(1)} %get-tuple-element.32), channel_id=1, source_target_pairs={{0,17},{1,16},{2,19},{3,18},{4,21},{5,20},{6,23},{7,22},{8,25},{9,... | collective-permute-start | bytes 454664 | tf_op jit(solution)/shard_map/ppermute | solution.py:32
  30.5 2.2 %collective-permute-start.14 = (f32[1,128]{1,0:T(1,128)S(1)}, f32[1,128]{1,0:T(1,128)S(1)}, u32[]{:S(2)}, u32[]{:S(2)}) collective-permute-start(f32[1,128]{1,0:T(1,128)S(1)} %get-tuple-element.34), channel_id=1, source_target_pairs={{0,8},{8,0},{16,24},{24,16},{1,9},{9,1},{17,25},{25,17},{2,10},{10... | collective-permute-start | bytes 1544 | tf_op jit(solution)/shard_map/ppermute | solution.py:22
  30.5 4.5 %collective-permute-start.15 = (f32[1,128]{1,0:T(1,128)S(1)}, f32[1,128]{1,0:T(1,128)S(1)}, u32[]{:S(2)}, u32[]{:S(2)}) collective-permute-start(f32[1,128]{1,0:T(1,128)S(1)} %get-tuple-element.34), channel_id=1, source_target_pairs={{0,20},{1,21},{2,22},{3,23},{4,16},{5,17},{6,18},{7,19},{8,28},{9,... | collective-permute-start | bytes 1544 | tf_op jit(solution)/shard_map/ppermute | solution.py:32
  32.6 3.5 %collective-permute-start.16 = (f32[1,128]{1,0:T(1,128)S(1)}, f32[1,128]{1,0:T(1,128)S(1)}, u32[]{:S(2)}, u32[]{:S(2)}) collective-permute-start(f32[1,128]{1,0:T(1,128)S(1)} %add.18), channel_id=1, source_target_pairs={{0,16},{1,17},{2,18},{3,19},{4,20},{5,21},{6,22},{7,23},{8,12},{9,... | collective-permute-start | bytes 1544 | tf_op jit(solution)/shard_map/ppermute | solution.py:32
  36.2 1.1 %collective-permute-start.17 = (f32[1,128]{1,0:T(1,128)S(1)}, f32[1,128]{1,0:T(1,128)S(1)}, u32[]{:S(2)}, u32[]{:S(2)}) collective-permute-start(f32[1,128]{1,0:T(1,128)S(1)} %add.19), channel_id=1, source_target_pairs={{0,8},{8,0},{16,24},{24,16},{1,9},{9,1},{17,25},{25,17},{2,10},{10... | collective-permute-start | bytes 1544 | tf_op jit(solution)/shard_map/ppermute | solution.py:22

commit v13 on v12

--- a/solution.py
+++ b/solution.py
@@ -116,6 +116,18 @@
         for h in range(IB // 8)
     ]
     return [[word[k, 0] for word in words] for k in range(lists.shape[0])]
+
+
+def scale_kernel(share, sq_ref, sum_ref, out_ref, held_ref, sems):
+    scale = 1.0 / (sum_ref[...] * share + 1e-06)
+    half, copies = sq_ref.shape[0] // 2, []
+    for i in range(2):
+        at = pl.ds(i * half, half)
+        held_ref[at, :] = sq_ref[at, :] * scale
+        copies.append(pltpu.make_async_copy(held_ref.at[at], out_ref.at[at], sems.at[i]))
+        copies[i].start()
+    for copy in copies:
+        copy.wait()
 
 
 def product_kernel(masks, n_layer, n_row, n_col, lists_ref, *refs):
@@ -238,8 +250,15 @@
     )(*(pin(x) for x in parts))
 
     col_sum = sum_over_devices(col_sum)
-    scale = 1.0 / (col_sum * (1.0 / (n_row * IB * block)) + 1e-06)
-    return (sq * scale)[None]
+    flow = pl.pallas_call(
+        functools.partial(scale_kernel, 1.0 / (n_row * IB * block)),
+        out_shape=jax.ShapeDtypeStruct(sq.shape, jnp.float32),
+        in_specs=[VMEM] * 2,
+        out_specs=pl.BlockSpec(memory_space=pl.ANY),
+        scratch_shapes=[pltpu.VMEM(sq.shape, jnp.float32), pltpu.SemaphoreType.DMA((2,))],
+        name="scale",
+    )(pin(sq), pin(col_sum))
+    return flow[None]
 
 
 def solution(mesh):

time: 38.2 us -> 38.2 us (level)
  Pallas kernels: 1.15 us -> 1.89 us
  other arithmetic: 1.42 us -> 0.69 us
    pallas_call x0 -> x1, Pallas kernels: none -> 0.74 us  [body(): pl.pallas_call(functools.partial(scale_kernel, 1.0 / (n_row * IB * block)...]
    broadcast_in_dim x1 -> x0, other arithmetic: 0.73 us -> none  [body(): return (sq * scale)[None]]
where the time goes in v13:
time: 38.2 us; the launch traced here: 38 us
  waiting for transfers between devices  17.1 us (45%)
  starting transfers between devices  16.7 us (44%)
  Pallas kernels  1.89 us (5%)
  local copies, waits for them, and re-layouts  0.89 us (2%)
  between operations  0.74 us (2%)
  other arithmetic  0.69 us (2%)
    ppermute x13, starting transfers between devices, xor_permute(): lax.ppermute(x, axis, [(i, i ^ mask) for i in range(lax.axis_size(axis))])  10.1 us
    ppermute x5, waiting for transfers between devices, grid_permute(): return lax.ppermute(x, AXES, pairs)  9.44 us
    ppermute x13, waiting for transfers between devices, xor_permute(): lax.ppermute(x, axis, [(i, i ^ mask) for i in range(lax.axis_size(axis))])  7.64 us
    ppermute x5, starting transfers between devices, grid_permute(): return lax.ppermute(x, AXES, pairs)  6.67 us
    pallas_call x1, Pallas kernels, products(): pl.pallas_call(functools.partial(product_kernel, masks, n_layer, n_row, n...  0.92 us
    unnamed x3, local copies, waits for them, and re-layouts  0.88 us
  transfers between devices with their start and end apart: 18, of which 10 were waited for; matrix products, arithmetic and copies ran while one was open for 4% of the time, Pallas kernels for 0%

profile of v13, /device:TPU:0, one launch (start us, length us, event | category | flops | bytes accessed | tf_op | source)
XLA Modules:
  0.0 38.0 jit_solution(11356819387221101691)
XLA Ops:
  0.0 0.0 copy-start
  0.0 0.5 %collective-permute-start.3 = (bf16[8,128,128]{2,1,0:T(8,128)(2,1)}, bf16[8,128,128]{2,1,0:T(8,128)(2,1)S(1)}, u32[]{:S(2)}, u32[]{:S(2)}) collective-permute-start(bf16[8,128,128]{2,1,0:T(8,128)(2,1)} %bitcast.4), channel_id=1, source_target_pairs={{0,8},{8,0},{16,24},{24,16},{1,9},{9,1},{17,25},{25,17},{2,10},{10... | collective-permute-start | bytes 786440 | tf_op jit(solution)/shard_map/ppermute | solution.py:22
  0.5 3.6 %collective-permute-start = (bf16[8,128,128]{2,1,0:T(8,128)(2,1)}, bf16[8,128,128]{2,1,0:T(8,128)(2,1)S(1)}, u32[]{:S(2)}, u32[]{:S(2)}) collective-permute-start(bf16[8,128,128]{2,1,0:T(8,128)(2,1)} %bitcast.5), channel_id=1, source_target_pairs={{0,2},{1,3},{2,0},{3,1},{4,6},{5,7},{6,4},{7,5},{8,10},{9,11},{10,... | collective-permute-start | bytes 786440 | tf_op jit(solution)/shard_map/ppermute | solution.py:22
  4.8 0.7 %compare_select_fusion = s32[1,8]{1,0:T(1,128)S(1)} fusion(s32[1,8]{1,0:T(1,128)} %param.5, s32[]{:T(128)} %bitcast.3), kind=kLoop, calls=%fused_computation.3 | loop fusion | flops 16 | bytes 68 | tf_op jit(solution)/shard_map/jit(_where)/select_n | solution.py:206
  5.4 0.2 collective-permute-start.1
  5.6 0.0 collective-permute-done.3.refs_7_
  5.6 1.6 %collective-permute-start.6 = (bf16[256,128]{1,0:T(8,128)(2,1)}, bf16[256,128]{1,0:T(8,128)(2,1)S(1)}, u32[]{:S(2)}, u32[]{:S(2)}) collective-permute-start(bf16[256,128]{1,0:T(8,128)(2,1)} %param.7), channel_id=1, source_target_pairs={{0,1},{1,0},{2,3},{3,2},{4,5},{5,4},{6,7},{7,6},{8,9},{9,8},{10,11... | collective-permute-start | bytes 196616 | tf_op jit(solution)/shard_map/ppermute | solution.py:22
  7.2 1.5 %collective-permute-start.4 = (bf16[256,128]{1,0:T(8,128)(2,1)}, bf16[256,128]{1,0:T(8,128)(2,1)S(1)}, u32[]{:S(2)}, u32[]{:S(2)}) collective-permute-start(bf16[256,128]{1,0:T(8,128)(2,1)} %param.7), channel_id=1, source_target_pairs={{0,4},{4,0},{1,5},{5,1},{2,6},{6,2},{3,7},{7,3},{8,12},{12,8},{9,1... | collective-permute-start | bytes 196616 | tf_op jit(solution)/shard_map/ppermute | solution.py:22
  8.7 0.9 %constant_dynamic-update-slice_fusion.1 = bf16[512,128]{1,0:T(8,128)(2,1)S(1)} fusion(bf16[256,128]{1,0:T(8,128)(2,1)} %param.7), kind=kLoop, calls=%fused_computation.1 | loop fusion | bytes 131072
  9.6 2.1 %collective-permute-done.4 = bf16[256,128]{1,0:T(8,128)(2,1)S(1)} collective-permute-done((bf16[256,128]{1,0:T(8,128)(2,1)}, bf16[256,128]{1,0:T(8,128)(2,1)S(1)}, u32[]{:S(2)}, u32[]{:S(2)}) %collective-permute-start.4) | collective-permute-done | bytes 65568 | tf_op jit(solution)/shard_map/ppermute | solution.py:22
  11.7 0.1 collective-permute-start.5
  11.7 0.0 collective-permute-done.1
  11.8 0.4 %collective-permute-start.2 = (s32[2,8]{1,0:T(2,128)S(1)}, s32[2,8]{1,0:T(2,128)S(1)}, u32[]{:S(2)}, u32[]{:S(2)}) collective-permute-start(s32[2,8]{1,0:T(2,128)S(1)} %pad_add_fusion.1), channel_id=1, source_target_pairs={{0,2},{1,3},{2,0},{3,1},{4,6},{5,7},{6,4},{7,5},{8,10},{9,11},{10,... | collective-permute-start | bytes 200 | tf_op jit(solution)/shard_map/ppermute | solution.py:22
  12.2 0.0 collective-permute-done.6.refs_2_
  12.2 1.5 %collective-permute-start.7 = (bf16[256,128]{1,0:T(8,128)(2,1)S(1)}, bf16[256,128]{1,0:T(8,128)(2,1)S(1)}, u32[]{:S(2)}, u32[]{:S(2)}) collective-permute-start(bf16[256,128]{1,0:T(8,128)(2,1)S(1)} %collective-permute-done.6.refs_2_), channel_id=1, source_target_pairs={{0,4},{4,0},{1,5},{5,1},{2,6},{6,2},{3,7},{7,3},{8,12},{12,8},{9,1... | collective-permute-start | bytes 196616 | tf_op jit(solution)/shard_map/ppermute | solution.py:22
  13.7 3.2 %collective-permute-done.2 = s32[2,8]{1,0:T(2,128)S(1)} collective-permute-done((s32[2,8]{1,0:T(2,128)S(1)}, s32[2,8]{1,0:T(2,128)S(1)}, u32[]{:S(2)}, u32[]{:S(2)}) %collective-permute-start.2) | collective-permute-done | bytes 96 | tf_op jit(solution)/shard_map/ppermute | solution.py:22
  16.9 0.0 collective-permute-done.refs_8_
  16.9 0.0 collective-permute-done.7.refs_4_
  17.0 0.0 collective-permute-done.5.refs_1_
  17.0 0.1 collective-permute-start.10
  17.0 0.5 %collective-permute-start.8 = (bf16[256,128]{1,0:T(8,128)(2,1)S(1)}, bf16[256,128]{1,0:T(8,128)(2,1)S(1)}, u32[]{:S(2)}, u32[]{:S(2)}) collective-permute-start(bf16[256,128]{1,0:T(8,128)(2,1)S(1)} %collective-permute-done.6.refs_2_), channel_id=1, source_target_pairs={{0,8},{8,0},{16,24},{24,16},{1,9},{9,1},{17,25},{25,17},{2,10},{10... | collective-permute-start | bytes 196616 | tf_op jit(solution)/shard_map/ppermute | solution.py:22
  17.5 0.1 collective-permute-start.9
  17.6 1.0 %collective-permute-done.8.refs_3_ = bf16[256,128]{1,0:T(8,128)(2,1)S(1)} collective-permute-done((bf16[256,128]{1,0:T(8,128)(2,1)S(1)}, bf16[256,128]{1,0:T(8,128)(2,1)S(1)}, u32[]{:S(2)}, u32[]{:S(2)}) %collective-permute-start.8) | collective-permute-done | bytes 65568 | tf_op jit(solution)/shard_map/ppermute | solution.py:22
  18.7 0.1 collective-permute-done.9.refs_5_
  18.8 0.0 collective-permute-done.10.refs_9_
  18.8 0.0 copy-done
  18.8 0.9 %partial_rows.1 = (f32[512,128]{1,0:T(8,128)S(1)}, s32[296,128]{1,0:T(8,128)S(1)}, s32[296,128]{1,0:T(8,128)S(1)}, s32[296,128]{1,0:T(8,128)S(1)}) custom-call(s32[4,8]{1,0:T(4,128)S(1)} %pad_add_fusion.lists_ref, bf16[512,128]{1,0:T(8,128)(2,1)S(1)} %constant_dynamic-update-slice_fusion.refs_0_, bf16[512,128]{1,0:T(8,128)(2,1)S(1)} %collective-permute-done.5.refs_1_, ...), custom_call_target="tpu_custom_call" | custom-call | tf_op jit(solution)/shard_map/partial_rows/pallas_call | solution.py:184
  19.7 1.7 %collective-permute-start.11 = (s32[296,128]{1,0:T(8,128)S(1)}, s32[296,128]{1,0:T(8,128)S(1)}, u32[]{:S(2)}, u32[]{:S(2)}) collective-permute-start(s32[296,128]{1,0:T(8,128)S(1)} %get-tuple-element.30), channel_id=1, source_target_pairs={{0,1},{1,0},{2,3},{3,2},{4,5},{5,4},{6,7},{7,6},{8,24},{9,25},{10,... | collective-permute-start | bytes 454664 | tf_op jit(solution)/shard_map/ppermute | solution.py:32
  21.5 1.5 %collective-permute-start.12 = (s32[296,128]{1,0:T(8,128)S(1)}, s32[296,128]{1,0:T(8,128)S(1)}, u32[]{:S(2)}, u32[]{:S(2)}) collective-permute-start(s32[296,128]{1,0:T(8,128)S(1)} %get-tuple-element.31), channel_id=1, source_target_pairs={{0,16},{1,17},{2,18},{3,19},{4,20},{5,21},{6,22},{7,23},{8,9},{9,8... | collective-permute-start | bytes 454664 | tf_op jit(solution)/shard_map/ppermute | solution.py:32
  23.0 0.3 collective-permute-start.13
  23.3 2.9 %collective-permute-done.11.refs_0_ = s32[296,128]{1,0:T(8,128)S(1)} collective-permute-done((s32[296,128]{1,0:T(8,128)S(1)}, s32[296,128]{1,0:T(8,128)S(1)}, u32[]{:S(2)}, u32[]{:S(2)}) %collective-permute-start.11) | collective-permute-done | bytes 151584 | tf_op jit(solution)/shard_map/ppermute | solution.py:32
  26.2 0.6 %collective-permute-done.12.refs_1_ = s32[296,128]{1,0:T(8,128)S(1)} collective-permute-done((s32[296,128]{1,0:T(8,128)S(1)}, s32[296,128]{1,0:T(8,128)S(1)}, u32[]{:S(2)}, u32[]{:S(2)}) %collective-permute-start.12) | collective-permute-done | bytes 151584 | tf_op jit(solution)/shard_map/ppermute | solution.py:32
  26.9 3.4 %collective-permute-done.13.refs_2_ = s32[296,128]{1,0:T(8,128)S(1)} collective-permute-done((s32[296,128]{1,0:T(8,128)S(1)}, s32[296,128]{1,0:T(8,128)S(1)}, u32[]{:S(2)}, u32[]{:S(2)}) %collective-permute-start.13) | collective-permute-done | bytes 151584 | tf_op jit(solution)/shard_map/ppermute | solution.py:32
  30.2 0.2 squares.1
  30.5 0.1 collective-permute-start.14
  30.5 2.1 %collective-permute-start.15 = (f32[1,128]{1,0:T(1,128)S(1)}, f32[1,128]{1,0:T(1,128)S(1)}, u32[]{:S(2)}, u32[]{:S(2)}) collective-permute-start(f32[1,128]{1,0:T(1,128)S(1)} %get-tuple-element.34), channel_id=1, source_target_pairs={{0,20},{1,21},{2,22},{3,23},{4,16},{5,17},{6,18},{7,19},{8,28},{9,... | collective-permute-start | bytes 1544 | tf_op jit(solution)/shard_map/ppermute | solution.py:32
  32.6 0.0 collective-permute-done.14
  32.6 1.0 %collective-permute-start.16 = (f32[1,128]{1,0:T(1,128)S(1)}, f32[1,128]{1,0:T(1,128)S(1)}, u32[]{:S(2)}, u32[]{:S(2)}) collective-permute-start(f32[1,128]{1,0:T(1,128)S(1)} %add.12), channel_id=1, source_target_pairs={{0,16},{1,17},{2,18},{3,19},{4,20},{5,21},{6,22},{7,23},{8,12},{9,... | collective-permute-start | bytes 1544 | tf_op jit(solution)/shard_map/ppermute | solution.py:32
  33.7 1.4 %collective-permute-done.15 = f32[1,128]{1,0:T(1,128)S(1)} collective-permute-done((f32[1,128]{1,0:T(1,128)S(1)}, f32[1,128]{1,0:T(1,128)S(1)}, u32[]{:S(2)}, u32[]{:S(2)}) %collective-permute-start.15) | collective-permute-done | bytes 544 | tf_op jit(solution)/shard_map/ppermute | solution.py:32
  35.0 1.1 %collective-permute-done.16 = f32[1,128]{1,0:T(1,128)S(1)} collective-permute-done((f32[1,128]{1,0:T(1,128)S(1)}, f32[1,128]{1,0:T(1,128)S(1)}, u32[]{:S(2)}, u32[]{:S(2)}) %collective-permute-start.16) | collective-permute-done | bytes 544 | tf_op jit(solution)/shard_map/ppermute | solution.py:32
  36.2 0.0 collective-permute-start.17
  36.2 1.1 %collective-permute-done.17 = f32[1,128]{1,0:T(1,128)S(1)} collective-permute-done((f32[1,128]{1,0:T(1,128)S(1)}, f32[1,128]{1,0:T(1,128)S(1)}, u32[]{:S(2)}, u32[]{:S(2)}) %collective-permute-start.17) | collective-permute-done | bytes 544 | tf_op jit(solution)/shard_map/ppermute | solution.py:22
  37.3 0.7 %scale.1 = f32[512,128]{1,0:T(8,128)} custom-call(f32[512,128]{1,0:T(8,128)S(1)} %get-tuple-element.33.sq_ref, f32[1,128]{1,0:T(1,128)S(1)} %add_add_fusion.sum_ref), custom_call_target="tpu_custom_call" | custom-call | tf_op jit(solution)/shard_map/scale/pallas_call | solution.py:253
  (6 shorter events, 0.0 us)
Async XLA Ops:
  0.0 18.8 %copy-start = (bf16[1,8,128,128]{3,2,1,0:T(8,128)(2,1)S(1)}, bf16[1,8,128,128]{3,2,1,0:T(8,128)(2,1)}, u32[]{:S(2)}) copy-start(bf16[1,8,128,128]{3,2,1,0:T(8,128)(2,1)} %param.4) | copy-start | bytes 786436
  0.0 5.6 %collective-permute-start.3 = (bf16[8,128,128]{2,1,0:T(8,128)(2,1)}, bf16[8,128,128]{2,1,0:T(8,128)(2,1)S(1)}, u32[]{:S(2)}, u32[]{:S(2)}) collective-permute-start(bf16[8,128,128]{2,1,0:T(8,128)(2,1)} %bitcast.4), channel_id=1, source_target_pairs={{0,8},{8,0},{16,24},{24,16},{1,9},{9,1},{17,25},{25,17},{2,10},{10... | collective-permute-start | bytes 786440 | tf_op jit(solution)/shard_map/ppermute | solution.py:22
  0.5 16.5 %collective-permute-start = (bf16[8,128,128]{2,1,0:T(8,128)(2,1)}, bf16[8,128,128]{2,1,0:T(8,128)(2,1)S(1)}, u32[]{:S(2)}, u32[]{:S(2)}) collective-permute-start(bf16[8,128,128]{2,1,0:T(8,128)(2,1)} %bitcast.5), channel_id=1, source_target_pairs={{0,2},{1,3},{2,0},{3,1},{4,6},{5,7},{6,4},{7,5},{8,10},{9,11},{10,... | collective-permute-start | bytes 786440 | tf_op jit(solution)/shard_map/ppermute | solution.py:22
  5.4 6.3 %collective-permute-start.1 = (s32[1,8]{1,0:T(1,128)S(1)}, s32[1,8]{1,0:T(1,128)S(1)}, u32[]{:S(2)}, u32[]{:S(2)}) collective-permute-start(s32[1,8]{1,0:T(1,128)S(1)} %compare_select_fusion), channel_id=1, source_target_pairs={{0,8},{8,0},{16,24},{24,16},{1,9},{9,1},{17,25},{25,17},{2,10},{10... | collective-permute-start | bytes 104 | tf_op jit(solution)/shard_map/ppermute | solution.py:22
  5.6 6.6 %collective-permute-start.6 = (bf16[256,128]{1,0:T(8,128)(2,1)}, bf16[256,128]{1,0:T(8,128)(2,1)S(1)}, u32[]{:S(2)}, u32[]{:S(2)}) collective-permute-start(bf16[256,128]{1,0:T(8,128)(2,1)} %param.7), channel_id=1, source_target_pairs={{0,1},{1,0},{2,3},{3,2},{4,5},{5,4},{6,7},{7,6},{8,9},{9,8},{10,11... | collective-permute-start | bytes 196616 | tf_op jit(solution)/shard_map/ppermute | solution.py:22
  7.2 4.5 %collective-permute-start.4 = (bf16[256,128]{1,0:T(8,128)(2,1)}, bf16[256,128]{1,0:T(8,128)(2,1)S(1)}, u32[]{:S(2)}, u32[]{:S(2)}) collective-permute-start(bf16[256,128]{1,0:T(8,128)(2,1)} %param.7), channel_id=1, source_target_pairs={{0,4},{4,0},{1,5},{5,1},{2,6},{6,2},{3,7},{7,3},{8,12},{12,8},{9,1... | collective-permute-start | bytes 196616 | tf_op jit(solution)/shard_map/ppermute | solution.py:22
  11.7 5.3 %collective-permute-start.5 = (bf16[512,128]{1,0:T(8,128)(2,1)S(1)}, bf16[512,128]{1,0:T(8,128)(2,1)S(1)}, u32[]{:S(2)}, u32[]{:S(2)}) collective-permute-start(bf16[512,128]{1,0:T(8,128)(2,1)S(1)} %constant_dynamic-update-slice_fusion.refs_0_), channel_id=1, source_target_pairs={{0,8},{8,0},{16,24},{24,16},{1,9},{9,1},{17,25},{25,17},{2,10},{10... | collective-permute-start | bytes 393224 | tf_op jit(solution)/shard_map/ppermute | solution.py:22
  11.8 5.2 %collective-permute-start.2 = (s32[2,8]{1,0:T(2,128)S(1)}, s32[2,8]{1,0:T(2,128)S(1)}, u32[]{:S(2)}, u32[]{:S(2)}) collective-permute-start(s32[2,8]{1,0:T(2,128)S(1)} %pad_add_fusion.1), channel_id=1, source_target_pairs={{0,2},{1,3},{2,0},{3,1},{4,6},{5,7},{6,4},{7,5},{8,10},{9,11},{10,... | collective-permute-start | bytes 200 | tf_op jit(solution)/shard_map/ppermute | solution.py:22
  12.2 4.8 %collective-permute-start.7 = (bf16[256,128]{1,0:T(8,128)(2,1)S(1)}, bf16[256,128]{1,0:T(8,128)(2,1)S(1)}, u32[]{:S(2)}, u32[]{:S(2)}) collective-permute-start(bf16[256,128]{1,0:T(8,128)(2,1)S(1)} %collective-permute-done.6.refs_2_), channel_id=1, source_target_pairs={{0,4},{4,0},{1,5},{5,1},{2,6},{6,2},{3,7},{7,3},{8,12},{12,8},{9,1... | collective-permute-start | bytes 196616 | tf_op jit(solution)/shard_map/ppermute | solution.py:22
  17.0 1.8 %collective-permute-start.10 = (bf16[8,128,128]{2,1,0:T(8,128)(2,1)S(1)}, bf16[8,128,128]{2,1,0:T(8,128)(2,1)S(1)}, u32[]{:S(2)}, u32[]{:S(2)}) collective-permute-start(bf16[8,128,128]{2,1,0:T(8,128)(2,1)S(1)} %collective-permute-done.refs_8_), channel_id=1, source_target_pairs={{0,8},{8,0},{16,24},{24,16},{1,9},{9,1},{17,25},{25,17},{2,10},{10... | collective-permute-start | bytes 786440 | tf_op jit(solution)/shard_map/ppermute | solution.py:22
  17.0 1.6 %collective-permute-start.8 = (bf16[256,128]{1,0:T(8,128)(2,1)S(1)}, bf16[256,128]{1,0:T(8,128)(2,1)S(1)}, u32[]{:S(2)}, u32[]{:S(2)}) collective-permute-start(bf16[256,128]{1,0:T(8,128)(2,1)S(1)} %collective-permute-done.6.refs_2_), channel_id=1, source_target_pairs={{0,8},{8,0},{16,24},{24,16},{1,9},{9,1},{17,25},{25,17},{2,10},{10... | collective-permute-start | bytes 196616 | tf_op jit(solution)/shard_map/ppermute | solution.py:22
  17.5 1.3 %collective-permute-start.9 = (bf16[256,128]{1,0:T(8,128)(2,1)S(1)}, bf16[256,128]{1,0:T(8,128)(2,1)S(1)}, u32[]{:S(2)}, u32[]{:S(2)}) collective-permute-start(bf16[256,128]{1,0:T(8,128)(2,1)S(1)} %collective-permute-done.7.refs_4_), channel_id=1, source_target_pairs={{0,8},{8,0},{16,24},{24,16},{1,9},{9,1},{17,25},{25,17},{2,10},{10... | collective-permute-start | bytes 196616 | tf_op jit(solution)/shard_map/ppermute | solution.py:22
  19.7 6.5 %collective-permute-start.11 = (s32[296,128]{1,0:T(8,128)S(1)}, s32[296,128]{1,0:T(8,128)S(1)}, u32[]{:S(2)}, u32[]{:S(2)}) collective-permute-start(s32[296,128]{1,0:T(8,128)S(1)} %get-tuple-element.30), channel_id=1, source_target_pairs={{0,1},{1,0},{2,3},{3,2},{4,5},{5,4},{6,7},{7,6},{8,24},{9,25},{10,... | collective-permute-start | bytes 454664 | tf_op jit(solution)/shard_map/ppermute | solution.py:32
  21.5 5.4 %collective-permute-start.12 = (s32[296,128]{1,0:T(8,128)S(1)}, s32[296,128]{1,0:T(8,128)S(1)}, u32[]{:S(2)}, u32[]{:S(2)}) collective-permute-start(s32[296,128]{1,0:T(8,128)S(1)} %get-tuple-element.31), channel_id=1, source_target_pairs={{0,16},{1,17},{2,18},{3,19},{4,20},{5,21},{6,22},{7,23},{8,9},{9,8... | collective-permute-start | bytes 454664 | tf_op jit(solution)/shard_map/ppermute | solution.py:32
  23.0 7.3 %collective-permute-start.13 = (s32[296,128]{1,0:T(8,128)S(1)}, s32[296,128]{1,0:T(8,128)S(1)}, u32[]{:S(2)}, u32[]{:S(2)}) collective-permute-start(s32[296,128]{1,0:T(8,128)S(1)} %get-tuple-element.32), channel_id=1, source_target_pairs={{0,17},{1,16},{2,19},{3,18},{4,21},{5,20},{6,23},{7,22},{8,25},{9,... | collective-permute-start | bytes 454664 | tf_op jit(solution)/shard_map/ppermute | solution.py:32
  30.5 2.2 %collective-permute-start.14 = (f32[1,128]{1,0:T(1,128)S(1)}, f32[1,128]{1,0:T(1,128)S(1)}, u32[]{:S(2)}, u32[]{:S(2)}) collective-permute-start(f32[1,128]{1,0:T(1,128)S(1)} %get-tuple-element.34), channel_id=1, source_target_pairs={{0,8},{8,0},{16,24},{24,16},{1,9},{9,1},{17,25},{25,17},{2,10},{10... | collective-permute-start | bytes 1544 | tf_op jit(solution)/shard_map/ppermute | solution.py:22
  30.5 4.5 %collective-permute-start.15 = (f32[1,128]{1,0:T(1,128)S(1)}, f32[1,128]{1,0:T(1,128)S(1)}, u32[]{:S(2)}, u32[]{:S(2)}) collective-permute-start(f32[1,128]{1,0:T(1,128)S(1)} %get-tuple-element.34), channel_id=1, source_target_pairs={{0,20},{1,21},{2,22},{3,23},{4,16},{5,17},{6,18},{7,19},{8,28},{9,... | collective-permute-start | bytes 1544 | tf_op jit(solution)/shard_map/ppermute | solution.py:32
  32.6 3.5 %collective-permute-start.16 = (f32[1,128]{1,0:T(1,128)S(1)}, f32[1,128]{1,0:T(1,128)S(1)}, u32[]{:S(2)}, u32[]{:S(2)}) collective-permute-start(f32[1,128]{1,0:T(1,128)S(1)} %add.12), channel_id=1, source_target_pairs={{0,16},{1,17},{2,18},{3,19},{4,20},{5,21},{6,22},{7,23},{8,12},{9,... | collective-permute-start | bytes 1544 | tf_op jit(solution)/shard_map/ppermute | solution.py:32
  36.2 1.1 %collective-permute-start.17 = (f32[1,128]{1,0:T(1,128)S(1)}, f32[1,128]{1,0:T(1,128)S(1)}, u32[]{:S(2)}, u32[]{:S(2)}) collective-permute-start(f32[1,128]{1,0:T(1,128)S(1)} %add.13), channel_id=1, source_target_pairs={{0,8},{8,0},{16,24},{24,16},{1,9},{9,1},{17,25},{25,17},{2,10},{10... | collective-permute-start | bytes 1544 | tf_op jit(solution)/shard_map/ppermute | solution.py:22

commit v14 on v12

--- a/solution.py
+++ b/solution.py
@@ -213,10 +213,11 @@
     mine = [mine, other(mine)]
     near = [pair[1] for pair in b_rows]
     own = a_blocks[0]
-    far, lists, mine, near, own_other = lax.optimization_barrier(
-        (panels[1:], lists, mine, near, own_other)
+    first_other = other(near[0])
+    far, lists, mine, near, own_other, first_other = lax.optimization_barrier(
+        (panels[1:], lists, mine, near, own_other, first_other)
     )
-    near = [x for b in near for x in (b, other(b))]
+    near = [near[0], first_other] + [x for b in near[1:] for x in (b, other(b))]
     panels = [own, own_other] + [x for p in far for x in (p, other(p))]
     b_refs = mine + near
     parts = products(masks, lists, b_refs, panels)

time: 38.2 us -> 38.4 us (level)
    ppermute x5, waiting for transfers between devices: 9.44 us -> 9.87 us  [grid_permute(): return lax.ppermute(x, AXES, pairs)]
  transfers between devices with their start and end apart: 18 -> 18, of which waited for: 10 -> 9; matrix products, arithmetic and copies ran while one was open for 4% -> 4% of each run, Pallas kernels for 0% -> 0%
where the time goes in v14:
time: 38.4 us; the launch traced here: 38.3 us
  waiting for transfers between devices  17.2 us (45%)
  starting transfers between devices  16.8 us (44%)
  other arithmetic  1.42 us (4%)
  Pallas kernels  1.15 us (3%)
  local copies, waits for them, and re-layouts  0.89 us (2%)
  between operations  0.75 us (2%)
    ppermute x13, starting transfers between devices, xor_permute(): lax.ppermute(x, axis, [(i, i ^ mask) for i in range(lax.axis_size(axis))])  10.2 us
    ppermute x5, waiting for transfers between devices, grid_permute(): return lax.ppermute(x, AXES, pairs)  9.87 us
    ppermute x13, waiting for transfers between devices, xor_permute(): lax.ppermute(x, axis, [(i, i ^ mask) for i in range(lax.axis_size(axis))])  7.35 us
    ppermute x5, starting transfers between devices, grid_permute(): return lax.ppermute(x, AXES, pairs)  6.6 us
    pallas_call x1, Pallas kernels, products(): pl.pallas_call(functools.partial(product_kernel, masks, n_layer, n_row, n...  0.92 us
    unnamed x3, local copies, waits for them, and re-layouts  0.88 us
  transfers between devices with their start and end apart: 18, of which 9 were waited for; matrix products, arithmetic and copies ran while one was open for 4% of the time, Pallas kernels for 0%

profile of v14, /device:TPU:0, one launch (start us, length us, event | category | flops | bytes accessed | tf_op | source)
XLA Modules:
  0.0 38.3 jit_solution(3914072104202042384)
XLA Ops:
  0.0 0.0 copy-start
  0.0 0.5 %collective-permute-start.3 = (bf16[8,128,128]{2,1,0:T(8,128)(2,1)}, bf16[8,128,128]{2,1,0:T(8,128)(2,1)S(1)}, u32[]{:S(2)}, u32[]{:S(2)}) collective-permute-start(bf16[8,128,128]{2,1,0:T(8,128)(2,1)} %bitcast.7), channel_id=1, source_target_pairs={{0,8},{8,0},{16,24},{24,16},{1,9},{9,1},{17,25},{25,17},{2,10},{10... | collective-permute-start | bytes 786440 | tf_op jit(solution)/shard_map/ppermute | solution.py:22
  0.5 3.6 %collective-permute-start = (bf16[8,128,128]{2,1,0:T(8,128)(2,1)}, bf16[8,128,128]{2,1,0:T(8,128)(2,1)S(1)}, u32[]{:S(2)}, u32[]{:S(2)}) collective-permute-start(bf16[8,128,128]{2,1,0:T(8,128)(2,1)} %bitcast.8), channel_id=1, source_target_pairs={{0,2},{1,3},{2,0},{3,1},{4,6},{5,7},{6,4},{7,5},{8,10},{9,11},{10,... | collective-permute-start | bytes 786440 | tf_op jit(solution)/shard_map/ppermute | solution.py:22
  4.8 0.7 %compare_select_fusion = s32[1,8]{1,0:T(1,128)S(1)} fusion(s32[1,8]{1,0:T(1,128)} %param.5, s32[]{:T(128)} %bitcast.6), kind=kLoop, calls=%fused_computation.4 | loop fusion | flops 16 | bytes 68 | tf_op jit(solution)/shard_map/jit(_where)/select_n | solution.py:194
  5.4 0.2 collective-permute-start.1
  5.6 0.0 collective-permute-done.3.refs_7_
  5.6 1.6 %collective-permute-start.6 = (bf16[256,128]{1,0:T(8,128)(2,1)}, bf16[256,128]{1,0:T(8,128)(2,1)S(1)}, u32[]{:S(2)}, u32[]{:S(2)}) collective-permute-start(bf16[256,128]{1,0:T(8,128)(2,1)} %param.7), channel_id=1, source_target_pairs={{0,1},{1,0},{2,3},{3,2},{4,5},{5,4},{6,7},{7,6},{8,9},{9,8},{10,11... | collective-permute-start | bytes 196616 | tf_op jit(solution)/shard_map/ppermute | solution.py:22
  7.2 1.5 %collective-permute-start.4 = (bf16[256,128]{1,0:T(8,128)(2,1)}, bf16[256,128]{1,0:T(8,128)(2,1)S(1)}, u32[]{:S(2)}, u32[]{:S(2)}) collective-permute-start(bf16[256,128]{1,0:T(8,128)(2,1)} %param.7), channel_id=1, source_target_pairs={{0,4},{4,0},{1,5},{5,1},{2,6},{6,2},{3,7},{7,3},{8,12},{12,8},{9,1... | collective-permute-start | bytes 196616 | tf_op jit(solution)/shard_map/ppermute | solution.py:22
  8.7 0.9 %constant_dynamic-update-slice_fusion.1 = bf16[512,128]{1,0:T(8,128)(2,1)S(1)} fusion(bf16[256,128]{1,0:T(8,128)(2,1)} %param.7), kind=kLoop, calls=%fused_computation.2 | loop fusion | bytes 131072
  9.6 2.1 %collective-permute-done.4 = bf16[256,128]{1,0:T(8,128)(2,1)S(1)} collective-permute-done((bf16[256,128]{1,0:T(8,128)(2,1)}, bf16[256,128]{1,0:T(8,128)(2,1)S(1)}, u32[]{:S(2)}, u32[]{:S(2)}) %collective-permute-start.4) | collective-permute-done | bytes 65568 | tf_op jit(solution)/shard_map/ppermute | solution.py:22
  11.7 0.1 collective-permute-start.5
  11.7 0.0 collective-permute-done.1
  11.8 0.4 %collective-permute-start.2 = (s32[2,8]{1,0:T(2,128)S(1)}, s32[2,8]{1,0:T(2,128)S(1)}, u32[]{:S(2)}, u32[]{:S(2)}) collective-permute-start(s32[2,8]{1,0:T(2,128)S(1)} %pad_add_fusion.1), channel_id=1, source_target_pairs={{0,2},{1,3},{2,0},{3,1},{4,6},{5,7},{6,4},{7,5},{8,10},{9,11},{10,... | collective-permute-start | bytes 200 | tf_op jit(solution)/shard_map/ppermute | solution.py:22
  12.2 0.0 collective-permute-done.6.refs_2_
  12.2 0.2 collective-permute-start.8
  12.4 1.5 %collective-permute-start.7 = (bf16[256,128]{1,0:T(8,128)(2,1)S(1)}, bf16[256,128]{1,0:T(8,128)(2,1)S(1)}, u32[]{:S(2)}, u32[]{:S(2)}) collective-permute-start(bf16[256,128]{1,0:T(8,128)(2,1)S(1)} %collective-permute-done.6.refs_2_), channel_id=1, source_target_pairs={{0,4},{4,0},{1,5},{5,1},{2,6},{6,2},{3,7},{7,3},{8,12},{12,8},{9,1... | collective-permute-start | bytes 196616 | tf_op jit(solution)/shard_map/ppermute | solution.py:22
  13.9 3.0 %collective-permute-done.2 = s32[2,8]{1,0:T(2,128)S(1)} collective-permute-done((s32[2,8]{1,0:T(2,128)S(1)}, s32[2,8]{1,0:T(2,128)S(1)}, u32[]{:S(2)}, u32[]{:S(2)}) %collective-permute-start.2) | collective-permute-done | bytes 96 | tf_op jit(solution)/shard_map/ppermute | solution.py:22
  16.9 0.0 collective-permute-done.refs_8_
  16.9 0.0 collective-permute-done.8.refs_3_
  17.0 0.0 collective-permute-done.7.refs_4_
  17.0 0.0 collective-permute-done.5.refs_1_
  17.0 0.1 collective-permute-start.10
  17.1 0.5 %collective-permute-start.9 = (bf16[256,128]{1,0:T(8,128)(2,1)S(1)}, bf16[256,128]{1,0:T(8,128)(2,1)S(1)}, u32[]{:S(2)}, u32[]{:S(2)}) collective-permute-start(bf16[256,128]{1,0:T(8,128)(2,1)S(1)} %collective-permute-done.7.refs_4_), channel_id=1, source_target_pairs={{0,8},{8,0},{16,24},{24,16},{1,9},{9,1},{17,25},{25,17},{2,10},{10... | collective-permute-start | bytes 196616 | tf_op jit(solution)/shard_map/ppermute | solution.py:22
  17.6 1.1 %collective-permute-done.9.refs_5_ = bf16[256,128]{1,0:T(8,128)(2,1)S(1)} collective-permute-done((bf16[256,128]{1,0:T(8,128)(2,1)S(1)}, bf16[256,128]{1,0:T(8,128)(2,1)S(1)}, u32[]{:S(2)}, u32[]{:S(2)}) %collective-permute-start.9) | collective-permute-done | bytes 65568 | tf_op jit(solution)/shard_map/ppermute | solution.py:22
  18.7 0.0 collective-permute-done.10.refs_9_
  18.7 0.0 copy-done
  18.7 0.9 %partial_rows.1 = (f32[512,128]{1,0:T(8,128)S(1)}, s32[296,128]{1,0:T(8,128)S(1)}, s32[296,128]{1,0:T(8,128)S(1)}, s32[296,128]{1,0:T(8,128)S(1)}) custom-call(s32[4,8]{1,0:T(4,128)S(1)} %pad_add_fusion.lists_ref, bf16[512,128]{1,0:T(8,128)(2,1)S(1)} %constant_dynamic-update-slice_fusion.refs_0_, bf16[512,128]{1,0:T(8,128)(2,1)S(1)} %collective-permute-done.5.refs_1_, ...), custom_call_target="tpu_custom_call" | custom-call | tf_op jit(solution)/shard_map/partial_rows/pallas_call | solution.py:172
  19.6 2.0 %collective-permute-start.11 = (s32[296,128]{1,0:T(8,128)S(1)}, s32[296,128]{1,0:T(8,128)S(1)}, u32[]{:S(2)}, u32[]{:S(2)}) collective-permute-start(s32[296,128]{1,0:T(8,128)S(1)} %get-tuple-element.32), channel_id=1, source_target_pairs={{0,1},{1,0},{2,3},{3,2},{4,5},{5,4},{6,7},{7,6},{8,24},{9,25},{10,... | collective-permute-start | bytes 454664 | tf_op jit(solution)/shard_map/ppermute | solution.py:32
  21.6 1.5 %collective-permute-start.12 = (s32[296,128]{1,0:T(8,128)S(1)}, s32[296,128]{1,0:T(8,128)S(1)}, u32[]{:S(2)}, u32[]{:S(2)}) collective-permute-start(s32[296,128]{1,0:T(8,128)S(1)} %get-tuple-element.33), channel_id=1, source_target_pairs={{0,16},{1,17},{2,18},{3,19},{4,20},{5,21},{6,22},{7,23},{8,9},{9,8... | collective-permute-start | bytes 454664 | tf_op jit(solution)/shard_map/ppermute | solution.py:32
  23.1 0.1 collective-permute-start.13
  23.2 2.9 %collective-permute-done.11.refs_0_ = s32[296,128]{1,0:T(8,128)S(1)} collective-permute-done((s32[296,128]{1,0:T(8,128)S(1)}, s32[296,128]{1,0:T(8,128)S(1)}, u32[]{:S(2)}, u32[]{:S(2)}) %collective-permute-start.11) | collective-permute-done | bytes 151584 | tf_op jit(solution)/shard_map/ppermute | solution.py:32
  26.0 3.0 %collective-permute-done.12.refs_1_ = s32[296,128]{1,0:T(8,128)S(1)} collective-permute-done((s32[296,128]{1,0:T(8,128)S(1)}, s32[296,128]{1,0:T(8,128)S(1)}, u32[]{:S(2)}, u32[]{:S(2)}) %collective-permute-start.12) | collective-permute-done | bytes 151584 | tf_op jit(solution)/shard_map/ppermute | solution.py:32
  29.1 1.2 %collective-permute-done.13.refs_2_ = s32[296,128]{1,0:T(8,128)S(1)} collective-permute-done((s32[296,128]{1,0:T(8,128)S(1)}, s32[296,128]{1,0:T(8,128)S(1)}, u32[]{:S(2)}, u32[]{:S(2)}) %collective-permute-start.13) | collective-permute-done | bytes 151584 | tf_op jit(solution)/shard_map/ppermute | solution.py:32
  30.2 0.2 squares.1
  30.5 0.1 collective-permute-start.14
  30.5 2.3 %collective-permute-start.15 = (f32[1,128]{1,0:T(1,128)S(1)}, f32[1,128]{1,0:T(1,128)S(1)}, u32[]{:S(2)}, u32[]{:S(2)}) collective-permute-start(f32[1,128]{1,0:T(1,128)S(1)} %get-tuple-element.36), channel_id=1, source_target_pairs={{0,20},{1,21},{2,22},{3,23},{4,16},{5,17},{6,18},{7,19},{8,28},{9,... | collective-permute-start | bytes 1544 | tf_op jit(solution)/shard_map/ppermute | solution.py:32
  32.8 0.0 collective-permute-done.14
  32.9 0.7 %collective-permute-start.16 = (f32[1,128]{1,0:T(1,128)S(1)}, f32[1,128]{1,0:T(1,128)S(1)}, u32[]{:S(2)}, u32[]{:S(2)}) collective-permute-start(f32[1,128]{1,0:T(1,128)S(1)} %add.18), channel_id=1, source_target_pairs={{0,16},{1,17},{2,18},{3,19},{4,20},{5,21},{6,22},{7,23},{8,12},{9,... | collective-permute-start | bytes 1544 | tf_op jit(solution)/shard_map/ppermute | solution.py:32
  33.6 1.4 %collective-permute-done.15 = f32[1,128]{1,0:T(1,128)S(1)} collective-permute-done((f32[1,128]{1,0:T(1,128)S(1)}, f32[1,128]{1,0:T(1,128)S(1)}, u32[]{:S(2)}, u32[]{:S(2)}) %collective-permute-start.15) | collective-permute-done | bytes 544 | tf_op jit(solution)/shard_map/ppermute | solution.py:32
  35.0 1.4 %collective-permute-done.16 = f32[1,128]{1,0:T(1,128)S(1)} collective-permute-done((f32[1,128]{1,0:T(1,128)S(1)}, f32[1,128]{1,0:T(1,128)S(1)}, u32[]{:S(2)}, u32[]{:S(2)}) %collective-permute-start.16) | collective-permute-done | bytes 544 | tf_op jit(solution)/shard_map/ppermute | solution.py:32
  36.4 0.0 collective-permute-start.17
  36.4 1.1 %collective-permute-done.17 = f32[1,128]{1,0:T(1,128)S(1)} collective-permute-done((f32[1,128]{1,0:T(1,128)S(1)}, f32[1,128]{1,0:T(1,128)S(1)}, u32[]{:S(2)}, u32[]{:S(2)}) %collective-permute-start.17) | collective-permute-done | bytes 544 | tf_op jit(solution)/shard_map/ppermute | solution.py:22
  37.5 0.7 %multiply_bitcast_fusion = f32[1,512,128]{2,1,0:T(8,128)} fusion(f32[512,128]{1,0:T(8,128)S(1)} %get-tuple-element.35, f32[128]{0:T(128)S(1)} %divide_bitcast_fusion), kind=kLoop, calls=%fused_computation | loop fusion | flops 65536 | bytes 524800 | tf_op jit(solution)/shard_map/broadcast_in_dim | solution.py:243
  (6 shorter events, 0.0 us)
Async XLA Ops:
  0.0 18.7 %copy-start = (bf16[1,8,128,128]{3,2,1,0:T(8,128)(2,1)S(1)}, bf16[1,8,128,128]{3,2,1,0:T(8,128)(2,1)}, u32[]{:S(2)}) copy-start(bf16[1,8,128,128]{3,2,1,0:T(8,128)(2,1)} %param.4) | copy-start | bytes 786436
  0.0 5.6 %collective-permute-start.3 = (bf16[8,128,128]{2,1,0:T(8,128)(2,1)}, bf16[8,128,128]{2,1,0:T(8,128)(2,1)S(1)}, u32[]{:S(2)}, u32[]{:S(2)}) collective-permute-start(bf16[8,128,128]{2,1,0:T(8,128)(2,1)} %bitcast.7), channel_id=1, source_target_pairs={{0,8},{8,0},{16,24},{24,16},{1,9},{9,1},{17,25},{25,17},{2,10},{10... | collective-permute-start | bytes 786440 | tf_op jit(solution)/shard_map/ppermute | solution.py:22
  0.5 16.5 %collective-permute-start = (bf16[8,128,128]{2,1,0:T(8,128)(2,1)}, bf16[8,128,128]{2,1,0:T(8,128)(2,1)S(1)}, u32[]{:S(2)}, u32[]{:S(2)}) collective-permute-start(bf16[8,128,128]{2,1,0:T(8,128)(2,1)} %bitcast.8), channel_id=1, source_target_pairs={{0,2},{1,3},{2,0},{3,1},{4,6},{5,7},{6,4},{7,5},{8,10},{9,11},{10,... | collective-permute-start | bytes 786440 | tf_op jit(solution)/shard_map/ppermute | solution.py:22
  5.4 6.3 %collective-permute-start.1 = (s32[1,8]{1,0:T(1,128)S(1)}, s32[1,8]{1,0:T(1,128)S(1)}, u32[]{:S(2)}, u32[]{:S(2)}) collective-permute-start(s32[1,8]{1,0:T(1,128)S(1)} %compare_select_fusion), channel_id=1, source_target_pairs={{0,8},{8,0},{16,24},{24,16},{1,9},{9,1},{17,25},{25,17},{2,10},{10... | collective-permute-start | bytes 104 | tf_op jit(solution)/shard_map/ppermute | solution.py:22
  5.6 6.6 %collective-permute-start.6 = (bf16[256,128]{1,0:T(8,128)(2,1)}, bf16[256,128]{1,0:T(8,128)(2,1)S(1)}, u32[]{:S(2)}, u32[]{:S(2)}) collective-permute-start(bf16[256,128]{1,0:T(8,128)(2,1)} %param.7), channel_id=1, source_target_pairs={{0,1},{1,0},{2,3},{3,2},{4,5},{5,4},{6,7},{7,6},{8,9},{9,8},{10,11... | collective-permute-start | bytes 196616 | tf_op jit(solution)/shard_map/ppermute | solution.py:22
  7.2 4.5 %collective-permute-start.4 = (bf16[256,128]{1,0:T(8,128)(2,1)}, bf16[256,128]{1,0:T(8,128)(2,1)S(1)}, u32[]{:S(2)}, u32[]{:S(2)}) collective-permute-start(bf16[256,128]{1,0:T(8,128)(2,1)} %param.7), channel_id=1, source_target_pairs={{0,4},{4,0},{1,5},{5,1},{2,6},{6,2},{3,7},{7,3},{8,12},{12,8},{9,1... | collective-permute-start | bytes 196616 | tf_op jit(solution)/shard_map/ppermute | solution.py:22
  11.7 5.3 %collective-permute-start.5 = (bf16[512,128]{1,0:T(8,128)(2,1)S(1)}, bf16[512,128]{1,0:T(8,128)(2,1)S(1)}, u32[]{:S(2)}, u32[]{:S(2)}) collective-permute-start(bf16[512,128]{1,0:T(8,128)(2,1)S(1)} %constant_dynamic-update-slice_fusion.refs_0_), channel_id=1, source_target_pairs={{0,8},{8,0},{16,24},{24,16},{1,9},{9,1},{17,25},{25,17},{2,10},{10... | collective-permute-start | bytes 393224 | tf_op jit(solution)/shard_map/ppermute | solution.py:22
  11.8 5.2 %collective-permute-start.2 = (s32[2,8]{1,0:T(2,128)S(1)}, s32[2,8]{1,0:T(2,128)S(1)}, u32[]{:S(2)}, u32[]{:S(2)}) collective-permute-start(s32[2,8]{1,0:T(2,128)S(1)} %pad_add_fusion.1), channel_id=1, source_target_pairs={{0,2},{1,3},{2,0},{3,1},{4,6},{5,7},{6,4},{7,5},{8,10},{9,11},{10,... | collective-permute-start | bytes 200 | tf_op jit(solution)/shard_map/ppermute | solution.py:22
  12.2 4.8 %collective-permute-start.8 = (bf16[256,128]{1,0:T(8,128)(2,1)S(1)}, bf16[256,128]{1,0:T(8,128)(2,1)S(1)}, u32[]{:S(2)}, u32[]{:S(2)}) collective-permute-start(bf16[256,128]{1,0:T(8,128)(2,1)S(1)} %collective-permute-done.6.refs_2_), channel_id=1, source_target_pairs={{0,8},{8,0},{16,24},{24,16},{1,9},{9,1},{17,25},{25,17},{2,10},{10... | collective-permute-start | bytes 196616 | tf_op jit(solution)/shard_map/ppermute | solution.py:22
  12.4 4.6 %collective-permute-start.7 = (bf16[256,128]{1,0:T(8,128)(2,1)S(1)}, bf16[256,128]{1,0:T(8,128)(2,1)S(1)}, u32[]{:S(2)}, u32[]{:S(2)}) collective-permute-start(bf16[256,128]{1,0:T(8,128)(2,1)S(1)} %collective-permute-done.6.refs_2_), channel_id=1, source_target_pairs={{0,4},{4,0},{1,5},{5,1},{2,6},{6,2},{3,7},{7,3},{8,12},{12,8},{9,1... | collective-permute-start | bytes 196616 | tf_op jit(solution)/shard_map/ppermute | solution.py:22
  17.0 1.7 %collective-permute-start.10 = (bf16[8,128,128]{2,1,0:T(8,128)(2,1)S(1)}, bf16[8,128,128]{2,1,0:T(8,128)(2,1)S(1)}, u32[]{:S(2)}, u32[]{:S(2)}) collective-permute-start(bf16[8,128,128]{2,1,0:T(8,128)(2,1)S(1)} %collective-permute-done.refs_8_), channel_id=1, source_target_pairs={{0,8},{8,0},{16,24},{24,16},{1,9},{9,1},{17,25},{25,17},{2,10},{10... | collective-permute-start | bytes 786440 | tf_op jit(solution)/shard_map/ppermute | solution.py:22
  17.1 1.6 %collective-permute-start.9 = (bf16[256,128]{1,0:T(8,128)(2,1)S(1)}, bf16[256,128]{1,0:T(8,128)(2,1)S(1)}, u32[]{:S(2)}, u32[]{:S(2)}) collective-permute-start(bf16[256,128]{1,0:T(8,128)(2,1)S(1)} %collective-permute-done.7.refs_4_), channel_id=1, source_target_pairs={{0,8},{8,0},{16,24},{24,16},{1,9},{9,1},{17,25},{25,17},{2,10},{10... | collective-permute-start | bytes 196616 | tf_op jit(solution)/shard_map/ppermute | solution.py:22
  19.6 6.4 %collective-permute-start.11 = (s32[296,128]{1,0:T(8,128)S(1)}, s32[296,128]{1,0:T(8,128)S(1)}, u32[]{:S(2)}, u32[]{:S(2)}) collective-permute-start(s32[296,128]{1,0:T(8,128)S(1)} %get-tuple-element.32), channel_id=1, source_target_pairs={{0,1},{1,0},{2,3},{3,2},{4,5},{5,4},{6,7},{7,6},{8,24},{9,25},{10,... | collective-permute-start | bytes 454664 | tf_op jit(solution)/shard_map/ppermute | solution.py:32
  21.6 7.5 %collective-permute-start.12 = (s32[296,128]{1,0:T(8,128)S(1)}, s32[296,128]{1,0:T(8,128)S(1)}, u32[]{:S(2)}, u32[]{:S(2)}) collective-permute-start(s32[296,128]{1,0:T(8,128)S(1)} %get-tuple-element.33), channel_id=1, source_target_pairs={{0,16},{1,17},{2,18},{3,19},{4,20},{5,21},{6,22},{7,23},{8,9},{9,8... | collective-permute-start | bytes 454664 | tf_op jit(solution)/shard_map/ppermute | solution.py:32
  23.1 7.1 %collective-permute-start.13 = (s32[296,128]{1,0:T(8,128)S(1)}, s32[296,128]{1,0:T(8,128)S(1)}, u32[]{:S(2)}, u32[]{:S(2)}) collective-permute-start(s32[296,128]{1,0:T(8,128)S(1)} %get-tuple-element.34), channel_id=1, source_target_pairs={{0,17},{1,16},{2,19},{3,18},{4,21},{5,20},{6,23},{7,22},{8,25},{9,... | collective-permute-start | bytes 454664 | tf_op jit(solution)/shard_map/ppermute | solution.py:32
  30.5 2.4 %collective-permute-start.14 = (f32[1,128]{1,0:T(1,128)S(1)}, f32[1,128]{1,0:T(1,128)S(1)}, u32[]{:S(2)}, u32[]{:S(2)}) collective-permute-start(f32[1,128]{1,0:T(1,128)S(1)} %get-tuple-element.36), channel_id=1, source_target_pairs={{0,8},{8,0},{16,24},{24,16},{1,9},{9,1},{17,25},{25,17},{2,10},{10... | collective-permute-start | bytes 1544 | tf_op jit(solution)/shard_map/ppermute | solution.py:22
  30.5 4.5 %collective-permute-start.15 = (f32[1,128]{1,0:T(1,128)S(1)}, f32[1,128]{1,0:T(1,128)S(1)}, u32[]{:S(2)}, u32[]{:S(2)}) collective-permute-start(f32[1,128]{1,0:T(1,128)S(1)} %get-tuple-element.36), channel_id=1, source_target_pairs={{0,20},{1,21},{2,22},{3,23},{4,16},{5,17},{6,18},{7,19},{8,28},{9,... | collective-permute-start | bytes 1544 | tf_op jit(solution)/shard_map/ppermute | solution.py:32
  32.9 3.5 %collective-permute-start.16 = (f32[1,128]{1,0:T(1,128)S(1)}, f32[1,128]{1,0:T(1,128)S(1)}, u32[]{:S(2)}, u32[]{:S(2)}) collective-permute-start(f32[1,128]{1,0:T(1,128)S(1)} %add.18), channel_id=1, source_target_pairs={{0,16},{1,17},{2,18},{3,19},{4,20},{5,21},{6,22},{7,23},{8,12},{9,... | collective-permute-start | bytes 1544 | tf_op jit(solution)/shard_map/ppermute | solution.py:32
  36.4 1.1 %collective-permute-start.17 = (f32[1,128]{1,0:T(1,128)S(1)}, f32[1,128]{1,0:T(1,128)S(1)}, u32[]{:S(2)}, u32[]{:S(2)}) collective-permute-start(f32[1,128]{1,0:T(1,128)S(1)} %add.19), channel_id=1, source_target_pairs={{0,8},{8,0},{16,24},{24,16},{1,9},{9,1},{17,25},{25,17},{2,10},{10... | collective-permute-start | bytes 1544 | tf_op jit(solution)/shard_map/ppermute | solution.py:22
